TPU v7x, 32 devices: a whole 2x2x4 slice. The times are simulated.
32 devices in a mesh: dp: 8 (over z, x), mp: 4 (over y, core).
Axes of the slice: x: 2, y: 2, z: 4, core: 2. Of those that a mesh axis runs over, the one named last changes fastest.
Arguments:
- tokens: bfloat16 [16384, 512], P('dp'), may hold values from -6 to 6
- cotangent: bfloat16 [16384, 512], P('dp'), may hold values from -6 to 6
- memory_init: bfloat16 [20, 512], P(None, ('dp', 'mp')), may hold values from -6 to 6
- query_weight: bfloat16 [512, 512], P(('dp', 'mp')), may hold values from -0.25 to 0.25
- key_weight: bfloat16 [512, 512], P(('dp', 'mp')), may hold values from -0.25 to 0.25
- value_weight: bfloat16 [512, 512], P(('dp', 'mp')), may hold values from -0.25 to 0.25
- output_weight: bfloat16 [512, 512], P(('dp', 'mp')), may hold values from -2 to 2
- first_gain: bfloat16 [512], P(('dp', 'mp')), may hold values from 0.5 to 1.5
- first_bias: bfloat16 [512], P(('dp', 'mp')), may hold values from -2 to 2
- inner_weight: bfloat16 [512, 2048], P(None, 'mp'), may hold values from -0.25 to 0.25
- inner_bias: bfloat16 [2048], P('mp'), may hold values from -3 to 3
- outer_weight: bfloat16 [2048, 512], P('mp'), may hold values from -0.125 to 0.125
- outer_bias: bfloat16 [512], P(('dp', 'mp')), may hold values from -3 to 3
- second_gain: bfloat16 [512], P(('dp', 'mp')), may hold values from 0.5 to 1.5
- second_bias: bfloat16 [512], P(('dp', 'mp')), may hold values from -2 to 2
Outputs:
- layer_out: bfloat16 [16384, 512], P('dp')
- grad_tokens: bfloat16 [16384, 512], P('dp')
- grad_memory: float32 [20, 512], P(None, ('dp', 'mp'))
- grad_query: float32 [512, 512], P(('dp', 'mp'))
- grad_key: float32 [512, 512], P(('dp', 'mp'))
- grad_value: float32 [512, 512], P(('dp', 'mp'))
- grad_output: float32 [512, 512], P(('dp', 'mp'))
- grad_first_gain: float32 [512], P(('dp', 'mp'))
- grad_first_bias: float32 [512], P(('dp', 'mp'))
- grad_inner: float32 [512, 2048], P(None, 'mp')
- grad_inner_bias: float32 [2048], P('mp')
- grad_outer: float32 [2048, 512], P('mp')
- grad_outer_bias: float32 [512], P(('dp', 'mp'))
- grad_second_gain: float32 [512], P(('dp', 'mp'))
- grad_second_bias: float32 [512], P(('dp', 'mp'))
All inputs are finite; a program needn't handle non-finite values.
Results may differ from a plain program's by a relative error of at most 0.019.
Values may be sent and summed in bfloat16 or wider, within the bound.
No kernel may reach another device: no remote copies, remote signals or barrier semaphores. Data moves between devices by JAX's collectives and lax.ppermute only.
A program may use at most 192 MiB of HBM per device.

v0:
```python
import jax
import jax.numpy as jnp
from jax import lax
from jax.sharding import PartitionSpec as P

D = 512
HEADS = 8
HEAD = 64
MEM = 20
SPAN = 512
SPANS = 2


norm_eps = 1e-05


def layer_norm(values, scales, shifts):
    center = values - jnp.mean(values, axis=-1, keepdims=True)
    spread = jnp.mean(center * center, axis=-1, keepdims=True)
    return center * lax.rsqrt(spread + norm_eps) * scales + shifts


def add_all(earlier, another):
    return jax.tree.map(lambda augend, addend: augend + addend, earlier, another)


def shards(
    tokens,
    cotangent,
    memory_init,
    query_weight,
    key_weight,
    value_weight,
    output_weight,
    first_gain,
    first_bias,
    inner_weight,
    inner_bias,
    outer_weight,
    outer_bias,
    second_gain,
    second_bias,
):
    gathered = (
        lax.all_gather(query_weight, ("dp", "mp"), axis=0, tiled=True),
        lax.all_gather(key_weight, ("dp", "mp"), axis=0, tiled=True),
        lax.all_gather(value_weight, ("dp", "mp"), axis=0, tiled=True),
        lax.all_gather(output_weight, ("dp", "mp"), axis=0, tiled=True),
        lax.all_gather(memory_init, ("dp", "mp"), axis=1, tiled=True),
        lax.all_gather(first_gain, ("dp", "mp"), axis=0, tiled=True),
        lax.all_gather(first_bias, ("dp", "mp"), axis=0, tiled=True),
        lax.all_gather(outer_bias, ("dp", "mp"), axis=0, tiled=True),
        lax.all_gather(second_gain, ("dp", "mp"), axis=0, tiled=True),
        lax.all_gather(second_bias, ("dp", "mp"), axis=0, tiled=True),
    )
    packed_weight = jnp.concatenate([gathered[0], gathered[1], gathered[2]], axis=1)
    mixer_weight = gathered[3]
    start_memory = gathered[4].astype(jnp.float32)
    first_scale = gathered[5].astype(jnp.float32)
    first_shift = gathered[6].astype(jnp.float32)
    outer_shift = gathered[7].astype(jnp.float32)
    second_scale = gathered[8].astype(jnp.float32)
    second_shift = gathered[9].astype(jnp.float32)
    inner_shift = inner_bias.astype(jnp.float32)
    score_scale = HEAD ** (-0.5)
    documents = tokens.reshape(-1, SPANS, SPAN, D)
    cotangents = cotangent.reshape(-1, SPANS, SPAN, D)

    def span_pass(joined, cot_rows):
        row_count = joined.shape[0]
        joined_low = joined.astype(jnp.bfloat16)
        packed = jnp.dot(joined_low, packed_weight, preferred_element_type=jnp.float32).astype(
            jnp.bfloat16
        )
        queries = packed[:, :D].reshape(row_count, HEADS, HEAD)
        key_rows = packed[:, D : 2 * D].reshape(row_count, HEADS, HEAD)
        value_rows = packed[:, 2 * D :].reshape(row_count, HEADS, HEAD)
        scores = (
            jnp.einsum("qhd,khd->hqk", queries, key_rows, preferred_element_type=jnp.float32)
            * score_scale
        )
        log_total = jax.nn.logsumexp(scores, axis=-1, keepdims=True)
        attend_low = jnp.exp(scores - log_total).astype(jnp.bfloat16)
        mixed_heads = jnp.einsum(
            "hqk,khd->qhd", attend_low, value_rows, preferred_element_type=jnp.float32
        )
        mixed_heads = mixed_heads.reshape(row_count, D).astype(jnp.bfloat16)
        branch = jnp.dot(mixed_heads, mixer_weight, preferred_element_type=jnp.float32)
        normed, first_pull = jax.vjp(layer_norm, joined + branch, first_scale, first_shift)
        normed_low = normed.astype(jnp.bfloat16)
        inner_act = (
            jnp.dot(normed_low, inner_weight, preferred_element_type=jnp.float32) + inner_shift
        )
        hidden, gelu_pull = jax.vjp(jax.nn.gelu, inner_act)
        hidden_low = hidden.astype(jnp.bfloat16)
        upstream = jnp.concatenate(
            [jnp.zeros((MEM, D), jnp.float32), cot_rows.astype(jnp.float32)], axis=0
        )
        partial_out = jnp.dot(hidden_low, outer_weight, preferred_element_type=jnp.float32)
        outer_act = (
            lax.psum(partial_out.astype(jnp.bfloat16), "mp").astype(jnp.float32) + outer_shift
        )
        result, second_pull = jax.vjp(layer_norm, normed + outer_act, second_scale, second_shift)
        grad_sum, grad_second_scale, grad_second_shift = second_pull(upstream)
        grad_ffn_out = grad_sum.astype(jnp.bfloat16)
        grad_outer_w = jnp.einsum(
            "rf,rd->fd", hidden_low, grad_ffn_out, preferred_element_type=jnp.float32
        )
        grad_outer_shift = jnp.sum(grad_sum, axis=0)
        grad_hidden = jnp.einsum(
            "rd,fd->rf", grad_ffn_out, outer_weight, preferred_element_type=jnp.float32
        )
        (grad_inner_act,) = gelu_pull(grad_hidden)
        grad_inner_low = grad_inner_act.astype(jnp.bfloat16)
        grad_inner_shift = jnp.sum(grad_inner_low.astype(jnp.float32), axis=0)
        grad_inner_w = jnp.einsum(
            "rd,rf->df", normed_low, grad_inner_low, preferred_element_type=jnp.float32
        )
        grad_normed = grad_sum + lax.psum(
            jnp.einsum(
                "rf,df->rd", grad_inner_low, inner_weight, preferred_element_type=jnp.float32
            ).astype(jnp.bfloat16),
            "mp",
        ).astype(jnp.float32)
        grad_resid, grad_first_scale, grad_first_shift = first_pull(grad_normed)
        grad_branch = grad_resid.astype(jnp.bfloat16)
        grad_mixer_w = jnp.einsum(
            "rk,rd->kd", mixed_heads, grad_branch, preferred_element_type=jnp.float32
        )
        grad_mixed = jnp.einsum(
            "rd,kd->rk", grad_branch, mixer_weight, preferred_element_type=jnp.float32
        )
        grad_mixed = grad_mixed.astype(jnp.bfloat16).reshape(row_count, HEADS, HEAD)
        scores_again = (
            jnp.einsum("qhd,khd->hqk", queries, key_rows, preferred_element_type=jnp.float32)
            * score_scale
        )
        attend = jnp.exp(scores_again - log_total)
        attend_again_low = attend.astype(jnp.bfloat16)
        grad_attend = jnp.einsum(
            "qhd,khd->hqk", grad_mixed, value_rows, preferred_element_type=jnp.float32
        )
        grad_attend = lax.optimization_barrier(grad_attend.astype(jnp.bfloat16)).astype(jnp.float32)
        grad_scores = attend * (grad_attend - jnp.sum(grad_attend * attend, axis=-1, keepdims=True))
        grad_logits = (grad_scores * score_scale).astype(jnp.bfloat16)
        grad_values = jnp.einsum(
            "hqk,qhd->khd", attend_again_low, grad_mixed, preferred_element_type=jnp.float32
        )
        grad_queries = jnp.einsum(
            "hqk,khd->qhd", grad_logits, key_rows, preferred_element_type=jnp.float32
        )
        grad_keys = jnp.einsum(
            "hqk,qhd->khd", grad_logits, queries, preferred_element_type=jnp.float32
        )
        grad_packed = jnp.concatenate(
            [
                grad_queries.reshape(row_count, D),
                grad_keys.reshape(row_count, D),
                grad_values.reshape(row_count, D),
            ],
            axis=1,
        ).astype(jnp.bfloat16)
        grad_packed_w = jnp.einsum(
            "rd,rk->dk", joined_low, grad_packed, preferred_element_type=jnp.float32
        )
        grad_joined = grad_resid + jnp.einsum(
            "rk,dk->rd", grad_packed, packed_weight, preferred_element_type=jnp.float32
        )
        attn_terms = (
            grad_packed_w,
            grad_mixer_w,
            grad_first_scale,
            grad_first_shift,
            grad_outer_shift,
            grad_second_scale,
            grad_second_shift,
        )
        ffn_terms = (grad_inner_w, grad_inner_shift, grad_outer_w)
        return (result, grad_joined, attn_terms, ffn_terms)

    def one_document(totals, document_pair):
        attn_totals, ffn_totals, memory_total = totals
        document_rows, document_cot = document_pair
        current = start_memory
        ffn_local = jax.tree.map(jnp.zeros_like, ffn_totals)
        outputs = []
        grad_rows = []
        for span_index in range(SPANS):
            joined = jnp.concatenate(
                [current, document_rows[span_index].astype(jnp.float32)], axis=0
            )
            result, grad_joined, attn_terms, ffn_terms = span_pass(joined, document_cot[span_index])
            attn_totals = add_all(attn_totals, attn_terms)
            ffn_local = add_all(ffn_local, ffn_terms)
            if span_index == 0:
                memory_total = memory_total + grad_joined[:MEM]
            outputs.append(result[MEM:].astype(jnp.bfloat16))
            grad_rows.append(grad_joined[MEM:].astype(jnp.bfloat16))
            current = result[:MEM]
        ffn_totals = add_all(ffn_totals, ffn_local)
        return ((attn_totals, ffn_totals, memory_total), (jnp.stack(outputs), jnp.stack(grad_rows)))

    attn_initial = (
        jnp.zeros((D, 3 * D), jnp.float32),
        jnp.zeros((D, D), jnp.float32),
        jnp.zeros((D,), jnp.float32),
        jnp.zeros((D,), jnp.float32),
        jnp.zeros((D,), jnp.float32),
        jnp.zeros((D,), jnp.float32),
        jnp.zeros((D,), jnp.float32),
    )
    ffn_initial = (
        jnp.zeros(inner_weight.shape, jnp.float32),
        jnp.zeros(inner_bias.shape, jnp.float32),
        jnp.zeros(outer_weight.shape, jnp.float32),
    )
    initial = (attn_initial, ffn_initial, jnp.zeros((MEM, D), jnp.float32))
    totals, (outputs, grad_rows) = lax.scan(one_document, initial, (documents, cotangents))
    attn_totals, ffn_totals, memory_total = totals
    ffn_totals = lax.psum((ffn_totals[0], ffn_totals[1], ffn_totals[2]), "dp")
    packed_grad = attn_totals[0]
    full = (
        packed_grad[:, :D],
        packed_grad[:, D : 2 * D],
        packed_grad[:, 2 * D :],
        attn_totals[1],
        memory_total,
        attn_totals[2],
        attn_totals[3],
        attn_totals[4],
        attn_totals[5],
        attn_totals[6],
    )
    fraction = 1.0 / lax.axis_size("mp")
    reduced = (
        lax.psum_scatter(full[0] * fraction, ("dp", "mp"), scatter_dimension=0, tiled=True),
        lax.psum_scatter(full[1] * fraction, ("dp", "mp"), scatter_dimension=0, tiled=True),
        lax.psum_scatter(full[2] * fraction, ("dp", "mp"), scatter_dimension=0, tiled=True),
        lax.psum_scatter(full[3] * fraction, ("dp", "mp"), scatter_dimension=0, tiled=True),
        lax.psum_scatter(full[4] * fraction, ("dp", "mp"), scatter_dimension=1, tiled=True),
        lax.psum_scatter(full[5] * fraction, ("dp", "mp"), scatter_dimension=0, tiled=True),
        lax.psum_scatter(full[6] * fraction, ("dp", "mp"), scatter_dimension=0, tiled=True),
        lax.psum_scatter(full[7] * fraction, ("dp", "mp"), scatter_dimension=0, tiled=True),
        lax.psum_scatter(full[8] * fraction, ("dp", "mp"), scatter_dimension=0, tiled=True),
        lax.psum_scatter(full[9] * fraction, ("dp", "mp"), scatter_dimension=0, tiled=True),
    )
    return (
        outputs.reshape(-1, D),
        grad_rows.reshape(-1, D),
        reduced[4],
        reduced[0],
        reduced[1],
        reduced[2],
        reduced[3],
        reduced[5],
        reduced[6],
        ffn_totals[0],
        ffn_totals[1],
        ffn_totals[2],
        reduced[7],
        reduced[8],
        reduced[9],
    )


def solution(mesh):
    in_specs = (
        P("dp", None),
        P("dp", None),
        P(None, ("dp", "mp")),
        P(("dp", "mp"), None),
        P(("dp", "mp"), None),
        P(("dp", "mp"), None),
        P(("dp", "mp"), None),
        P(("dp", "mp")),
        P(("dp", "mp")),
        P(None, "mp"),
        P("mp"),
        P("mp", None),
        P(("dp", "mp")),
        P(("dp", "mp")),
        P(("dp", "mp")),
    )
    out_specs = (
        P("dp", None),
        P("dp", None),
        P(None, ("dp", "mp")),
        P(("dp", "mp"), None),
        P(("dp", "mp"), None),
        P(("dp", "mp"), None),
        P(("dp", "mp"), None),
        P(("dp", "mp")),
        P(("dp", "mp")),
        P(None, "mp"),
        P("mp"),
        P("mp", None),
        P(("dp", "mp")),
        P(("dp", "mp")),
        P(("dp", "mp")),
    )
    return jax.shard_map(shards, mesh=mesh, in_specs=in_specs, out_specs=out_specs, check_vma=False)
```

profile of v0, /device:TPU:0, one launch (start us, length us, event | category | flops | bytes accessed | tf_op | source)
XLA Modules:
  0.0 1666.1 jit_solution(3178349153771887752)
XLA Ops:
  12.4 42.1 %all-reduce.15 = (bf16[512]{0:T(512)(128)(2,1)S(1)}, bf16[512]{0:T(512)(128)(2,1)S(1)}, bf16[512]{0:T(512)(128)(2,1)S(1)}, bf16[512]{0:T(512)(128)(2,1)S(1)}, bf16[512]{0:T(512)(128)(2,1)S(1)}) all-reduce(bf16[512]{0:T(512)(128)(2,1)S(1)} %dynamic-update-slice, ...), channel_id=1, replica_groups=mesh['dp'=8,'mp'=4] {'dp','mp'}, use_global_device_ids=true, to_apply=%add.2 | all-reduce | flops 2560 | bytes 10240
  55.2 40.8 %all_gather.30 = bf16[20,512]{0,1:T(8,128)(2,1)S(1)} all-gather(bf16[20,16]{0,1:T(8,128)(2,1)} %param.19), channel_id=1, replica_groups=mesh['dp'=8,'mp'=4] {'dp','mp'}, dimensions={1}, use_global_device_ids=true | all-gather | bytes 21120 | tf_op jit(solution)/shard_map/all_gather | solution.py:49
  96.1 38.3 %all_gather.31 = bf16[512,512]{1,0:T(8,128)(2,1)S(1)} all-gather(bf16[16,512]{1,0:T(8,128)(2,1)} %param.20), channel_id=1, replica_groups=mesh['dp'=8,'mp'=4] {'dp','mp'}, dimensions={0}, use_global_device_ids=true | all-gather | bytes 540672 | tf_op jit(solution)/shard_map/all_gather | solution.py:45
  134.4 39.6 %all_gather.32 = bf16[512,512]{1,0:T(8,128)(2,1)S(1)} all-gather(bf16[16,512]{1,0:T(8,128)(2,1)} %param.21), channel_id=1, replica_groups=mesh['dp'=8,'mp'=4] {'dp','mp'}, dimensions={0}, use_global_device_ids=true | all-gather | bytes 540672 | tf_op jit(solution)/shard_map/all_gather | solution.py:46
  174.0 38.0 %all_gather.33 = bf16[512,512]{1,0:T(8,128)(2,1)S(1)} all-gather(bf16[16,512]{1,0:T(8,128)(2,1)S(1)} %copy-done.61), channel_id=1, replica_groups=mesh['dp'=8,'mp'=4] {'dp','mp'}, dimensions={0}, use_global_device_ids=true | all-gather | bytes 540672 | tf_op jit(solution)/shard_map/all_gather | solution.py:47
  212.1 39.4 %all_gather.35 = bf16[512,512]{1,0:T(8,128)(2,1)S(1)} all-gather(bf16[16,512]{1,0:T(8,128)(2,1)S(1)} %copy-done.62), channel_id=1, replica_groups=mesh['dp'=8,'mp'=4] {'dp','mp'}, dimensions={0}, use_global_device_ids=true | all-gather | bytes 540672 | tf_op jit(solution)/shard_map/all_gather | solution.py:48
  252.7 705.7 %while.38 = (s32[]{:T(128)}, f32[512,1536]{1,0:T(8,128)}, f32[512,512]{1,0:T(8,128)}, f32[512]{0:T(512)S(1)}, f32[512]{0:T(512)S(1)}, /*index=5*/f32[512]{0:T(51...) while((s32[]{:T(128)}, f32[512,1536]{1,0:T(8,128)}, ...), condition=%wide.region_39.0_spmd.clone, body=%wide.region_0.39_spmd.clone.sunk | while | flops 13709531136 | bytes 771561344 | solution.py:218
  256.8 2.1 copy.208
  260.8 6.1 fusion.346
  266.9 14.8 copy.211
  281.7 5.1 multiply_reduce_fusion.17
  288.9 7.6 exponential_reduce_fusion.4
  308.6 26.9 %all-reduce.25.cloned.1.call-done = bf16[532,512]{1,0:T(8,128)(2,1)} async-done(((bf16[532,512]{1,0:T(8,128)(2,1)}), bf16[532,512]{1,0:T(8,128)(2,1)}) %all-reduce.25.cloned.1.call-update) | async-done | bytes 544784 | tf_op jit(solution)/shard_map/while/body/eval_jaxpr/psum | solution.py:101
  343.7 2.4 copy.214
  346.1 7.2 fusion.355
  353.2 14.8 copy.215
  368.0 5.1 multiply_reduce_fusion.20
  375.2 7.6 exponential_reduce_fusion.5
  393.4 2.2 fusion.381
  395.6 31.0 %all-reduce.27.cloned.1.call-done = bf16[532,512]{1,0:T(8,128)(2,1)} async-done(((bf16[532,512]{1,0:T(8,128)(2,1)}), bf16[532,512]{1,0:T(8,128)(2,1)}) %all-reduce.27.cloned.1.call-update) | async-done | bytes 544784 | tf_op jit(solution)/shard_map/while/body/eval_jaxpr/psum | solution.py:101
  441.8 3.4 fusion.377
  448.8 30.0 %all-reduce.29.cloned.1.call-done = (bf16[532,512]{1,0:T(8,128)(2,1)}, bf16[532,512]{1,0:T(8,128)(2,1)}) async-done(((bf16[532,512]{1,0:T(8,128)(2,1)}, bf16[532,512]{1,0:T(8,128)(2,1)}), (bf16[532,512]{1,0:T(8,128)(2,1)}, bf16[532,512]{1,0:T(8,128)(2,1)})) %all-reduce.29.cloned.1.call-update) | async-done | bytes 1089552 | tf_op jit(solution)/shard_map/while/body/eval_jaxpr/psum | solution.py:119
  478.8 2.9 multiply_reduce_fusion.23
  486.4 5.6 fusion.364
  494.9 34.0 %fusion.366 = bf16[8,532,532]{2,0,1:T(8,128)(2,1)} fusion(bf16[8,532,532]{2,0,1:T(8,128)(2,1)S(1)} %copy.217, f32[8,532,532]{2,0,1:T(8,128)} %copy.211, f32[8,532]{0,1:T(8,128)S(1)} %copy-done.49), kind=kOutput, calls=%fused_computation.8.clone.1 | output fusion | flops 24910900 | bytes 18130560 | tf_op jit(solution)/shard_map/while/body/eval_jaxpr/sub | solution.py:144
  529.0 5.4 fusion.368
  534.4 2.8 fusion.367
  539.2 4.5 fusion.369
  546.7 33.8 %fusion.371 = bf16[8,532,532]{2,0,1:T(8,128)(2,1)} fusion(bf16[8,532,532]{2,0,1:T(8,128)(2,1)S(1)} %copy.219, f32[8,532,532]{2,0,1:T(8,128)} %copy.215, f32[8,532]{0,1:T(8,128)S(1)} %copy-done.51), kind=kOutput, calls=%fused_computation.11.clone.1 | output fusion | flops 24910900 | bytes 18130560 | tf_op jit(solution)/shard_map/while/body/eval_jaxpr/sub | solution.py:144
  580.5 4.6 fusion.373
  596.1 3.1 convolution_add_fusion.21
  610.6 6.1 fusion.346
  616.6 14.8 copy.211
  631.4 5.1 multiply_reduce_fusion.17
  638.6 7.6 exponential_reduce_fusion.4
  658.3 31.1 %all-reduce.25.cloned.1.call-done = bf16[532,512]{1,0:T(8,128)(2,1)} async-done(((bf16[532,512]{1,0:T(8,128)(2,1)}), bf16[532,512]{1,0:T(8,128)(2,1)}) %all-reduce.25.cloned.1.call-update) | async-done | bytes 544784 | tf_op jit(solution)/shard_map/while/body/eval_jaxpr/psum | solution.py:101
  697.6 2.4 copy.214
  700.0 7.2 fusion.355
  707.1 14.8 copy.215
  721.9 5.1 multiply_reduce_fusion.20
  729.1 7.6 exponential_reduce_fusion.5
  747.3 2.2 fusion.381
  749.5 31.0 %all-reduce.27.cloned.1.call-done = bf16[532,512]{1,0:T(8,128)(2,1)} async-done(((bf16[532,512]{1,0:T(8,128)(2,1)}), bf16[532,512]{1,0:T(8,128)(2,1)}) %all-reduce.27.cloned.1.call-update) | async-done | bytes 544784 | tf_op jit(solution)/shard_map/while/body/eval_jaxpr/psum | solution.py:101
  795.7 3.7 fusion.377
  801.1 3.1 fusion.379
  804.2 28.4 %all-reduce.29.cloned.1.call-done = (bf16[532,512]{1,0:T(8,128)(2,1)}, bf16[532,512]{1,0:T(8,128)(2,1)}) async-done(((bf16[532,512]{1,0:T(8,128)(2,1)}, bf16[532,512]{1,0:T(8,128)(2,1)}), (bf16[532,512]{1,0:T(8,128)(2,1)}, bf16[532,512]{1,0:T(8,128)(2,1)})) %all-reduce.29.cloned.1.call-update) | async-done | bytes 1089552 | tf_op jit(solution)/shard_map/while/body/eval_jaxpr/psum | solution.py:119
  832.6 2.9 multiply_reduce_fusion.23
  840.3 5.6 fusion.364
  848.8 34.0 %fusion.366 = bf16[8,532,532]{2,0,1:T(8,128)(2,1)} fusion(bf16[8,532,532]{2,0,1:T(8,128)(2,1)S(1)} %copy.217, f32[8,532,532]{2,0,1:T(8,128)} %copy.211, f32[8,532]{0,1:T(8,128)S(1)} %copy-done.49), kind=kOutput, calls=%fused_computation.8.clone.1 | output fusion | flops 24910900 | bytes 18130560 | tf_op jit(solution)/shard_map/while/body/eval_jaxpr/sub | solution.py:144
  882.9 5.4 fusion.368
  888.3 2.8 fusion.367
  893.1 4.5 fusion.369
  900.6 33.8 %fusion.371 = bf16[8,532,532]{2,0,1:T(8,128)(2,1)} fusion(bf16[8,532,532]{2,0,1:T(8,128)(2,1)S(1)} %copy.219, f32[8,532,532]{2,0,1:T(8,128)} %copy.215, f32[8,532]{0,1:T(8,128)S(1)} %copy-done.51), kind=kOutput, calls=%fused_computation.11.clone.1 | output fusion | flops 24910900 | bytes 18130560 | tf_op jit(solution)/shard_map/while/body/eval_jaxpr/sub | solution.py:144
  934.4 4.6 fusion.373
  949.9 3.1 convolution_add_fusion.21
  961.8 3.6 slice_multiply_fusion.1
  967.0 42.1 %all-reduce.13 = (f32[512]{0:T(512)S(1)}, f32[512]{0:T(512)S(1)}, f32[512]{0:T(512)S(1)}, f32[512]{0:T(512)S(1)}, f32[512]{0:T(512)S(1)}) all-reduce(f32[512]{0:T(512)S(1)} %broadcast_multiply_fusion.10, f32[512]{0:T(512)S(1)} %get-tuple-element.765, ...), channel_id=7, replica_groups=mesh['dp'=8,'mp'=4] {'dp','mp'}, use_global_device_ids=true, to_apply=%region_45.0.clone | all-reduce | flops 2560 | bytes 20480
  1011.9 21.3 %psum.66 = f32[512]{0:T(512)} all-reduce(f32[512]{0:T(512)S(1)} %get-tuple-element.424), channel_id=1, replica_groups=mesh['dp'=8,'mp'=4] {'dp'}, use_global_device_ids=true, to_apply=%region_48.0 | all-reduce | flops 512 | bytes 4096 | tf_op jit(solution)/shard_map/psum | solution.py:220
  1033.2 87.7 %reduce-scatter.16.cloned.1.call-done = f32[16,20]{1,0:T(8,128)} async-done(((f32[512,20]{1,0:T(8,128)}), f32[16,20]{1,0:T(8,128)}) %reduce-scatter.16.cloned.1.call-update) | async-done | bytes 1296
  1120.9 133.3 %reduce-scatter.14.cloned.1.call-done = f32[16,512]{1,0:T(8,128)} async-done(((f32[512,512]{1,0:T(8,128)}), f32[16,512]{1,0:T(8,128)}) %reduce-scatter.14.cloned.1.call-update) | async-done | bytes 32784 | tf_op jit(solution)/shard_map/reduce_scatter | solution.py:239
  1254.3 133.8 %reduce-scatter.12.cloned.1.call-done = f32[16,512]{1,0:T(8,128)} async-done(((f32[512,512]{1,0:T(8,128)}), f32[16,512]{1,0:T(8,128)}) %reduce-scatter.12.cloned.1.call-update) | async-done | bytes 32784 | tf_op jit(solution)/shard_map/reduce_scatter | solution.py:238
  1388.1 133.5 %reduce-scatter.8.cloned.1.call-done = f32[16,512]{1,0:T(8,128)} async-done(((f32[512,512]{1,0:T(8,128)}), f32[16,512]{1,0:T(8,128)}) %reduce-scatter.8.cloned.1.call-update) | async-done | bytes 32784 | tf_op jit(solution)/shard_map/reduce_scatter | solution.py:236
  1521.6 133.4 %reduce-scatter.10.cloned.1.call-done = f32[16,512]{1,0:T(8,128)} async-done(((f32[512,512]{1,0:T(8,128)}), f32[16,512]{1,0:T(8,128)}) %reduce-scatter.10.cloned.1.call-update) | async-done | bytes 32784 | tf_op jit(solution)/shard_map/reduce_scatter | solution.py:237
  1655.0 2.3 copy.275
  (526 shorter events, 186.7 us)
Async XLA Ops:
  8.0 166.0 %copy-start.61 = (bf16[16,512]{1,0:T(8,128)(2,1)S(1)}, bf16[16,512]{1,0:T(8,128)(2,1)}, u32[]{:S(2)}) copy-start(bf16[16,512]{1,0:T(8,128)(2,1)} %param.22) | copy-start | bytes 49156
  8.0 204.0 %copy-start.62 = (bf16[16,512]{1,0:T(8,128)(2,1)S(1)}, bf16[16,512]{1,0:T(8,128)(2,1)}, u32[]{:S(2)}) copy-start(bf16[16,512]{1,0:T(8,128)(2,1)} %param.23) | copy-start | bytes 49156
  252.7 48.5 %copy-start.10 = (bf16[512,512]{1,0:T(8,128)(2,1)}, bf16[512,512]{1,0:T(8,128)(2,1)S(1)}, u32[]{:S(2)}) copy-start(bf16[512,512]{1,0:T(8,128)(2,1)S(1)} %get-tuple-element.1126) | copy-start | bytes 1572868 | tf_op jit(solution)/shard_map/while
  252.7 82.8 %all-reduce.25.cloned.1.call-start = ((), (), s32[]{:S(2)}) async-start(), calls=%async_computation.11 | async-start | bytes 1097728 | tf_op jit(solution)/shard_map/while/body/eval_jaxpr/psum | solution.py:101
  254.5 132.9 %copy-start.8 = (f32[512,512]{1,0:T(8,128)}, f32[512,512]{1,0:T(8,128)S(1)}, u32[]{:S(2)}) copy-start(f32[512,512]{1,0:T(8,128)S(1)} %get-tuple-element.988) | copy-start | bytes 3145732 | tf_op jit(solution)/shard_map/while
  259.2 7.7 copy-start.22
  260.8 6.1 copy-start.24
  281.7 7.2 copy-start
  306.0 120.5 %all-reduce.27.cloned.1.call-start = ((), (), s32[]{:S(2)}) async-start(), calls=%async_computation.12 | async-start | bytes 1097728 | tf_op jit(solution)/shard_map/while/body/eval_jaxpr/psum | solution.py:101
  308.6 28.7 %copy-start.16 = (bf16[512,512]{1,0:T(8,128)(2,1)}, bf16[512,512]{1,0:T(8,128)(2,1)S(1)}, u32[]{:S(2)}) copy-start(bf16[512,512]{1,0:T(8,128)(2,1)S(1)} %get-tuple-element.997) | copy-start | bytes 1572868 | tf_op jit(solution)/shard_map/while
  343.7 9.5 copy-start.26
  368.0 7.2 copy-start.1
  393.2 85.6 %all-reduce.29.cloned.1.call-start = ((), (), s32[]{:S(2)}) async-start(), calls=%async_computation.13 | async-start | bytes 2195456 | tf_op jit(solution)/shard_map/while/body/eval_jaxpr/psum | solution.py:119
  395.6 32.6 %copy-start.14 = (bf16[512,512]{1,0:T(8,128)(2,1)S(1)}, bf16[512,512]{1,0:T(8,128)(2,1)}, u32[]{:S(2)}) copy-start(bf16[512,512]{1,0:T(8,128)(2,1)} %get-tuple-element.1004) | copy-start | bytes 1572868 | tf_op jit(solution)/shard_map/while
  441.8 3.4 copy-start.44
  441.8 3.4 copy-start.45
  441.8 3.4 copy-start.65
  441.8 4.8 copy-start.55
  478.7 2.9 copy-start.7
  478.7 2.9 copy-start.38
  478.7 2.9 copy-start.39
  486.4 5.6 copy-start.32
  494.9 34.0 %copy-start.25 = (bf16[532,512]{0,1:T(8,128)(2,1)S(1)}, bf16[532,512]{0,1:T(8,128)(2,1)}, u32[]{:S(2)}) copy-start(bf16[532,512]{0,1:T(8,128)(2,1)} %copy-done.24) | copy-start | bytes 1634308 | tf_op jit(solution)/shard_map/while
  528.9 5.4 copy-start.23
  529.0 5.4 copy-start.73
  534.4 2.9 copy-start.18
  539.2 4.6 copy-start.34
  546.7 33.8 %copy-start.28 = (bf16[532,512]{0,1:T(8,128)(2,1)S(1)}, bf16[532,512]{0,1:T(8,128)(2,1)}, u32[]{:S(2)}) copy-start(bf16[532,512]{0,1:T(8,128)(2,1)} %copy.214) | copy-start | bytes 1634308 | tf_op jit(solution)/shard_map/while
  580.4 4.6 copy-start.27
  580.5 4.6 copy-start.74
  602.4 48.5 %copy-start.10 = (bf16[512,512]{1,0:T(8,128)(2,1)}, bf16[512,512]{1,0:T(8,128)(2,1)S(1)}, u32[]{:S(2)}) copy-start(bf16[512,512]{1,0:T(8,128)(2,1)S(1)} %get-tuple-element.1126) | copy-start | bytes 1572868 | tf_op jit(solution)/shard_map/while
  602.4 87.0 %all-reduce.25.cloned.1.call-start = ((), (), s32[]{:S(2)}) async-start(), calls=%async_computation.11 | async-start | bytes 1097728 | tf_op jit(solution)/shard_map/while/body/eval_jaxpr/psum | solution.py:101
  604.2 137.1 %copy-start.8 = (f32[512,512]{1,0:T(8,128)}, f32[512,512]{1,0:T(8,128)S(1)}, u32[]{:S(2)}) copy-start(f32[512,512]{1,0:T(8,128)S(1)} %get-tuple-element.988) | copy-start | bytes 3145732 | tf_op jit(solution)/shard_map/while
  609.0 7.7 copy-start.22
  610.5 6.1 copy-start.24
  631.4 7.2 copy-start
  655.7 124.7 %all-reduce.27.cloned.1.call-start = ((), (), s32[]{:S(2)}) async-start(), calls=%async_computation.12 | async-start | bytes 1097728 | tf_op jit(solution)/shard_map/while/body/eval_jaxpr/psum | solution.py:101
  658.3 32.9 %copy-start.16 = (bf16[512,512]{1,0:T(8,128)(2,1)}, bf16[512,512]{1,0:T(8,128)(2,1)S(1)}, u32[]{:S(2)}) copy-start(bf16[512,512]{1,0:T(8,128)(2,1)S(1)} %get-tuple-element.997) | copy-start | bytes 1572868 | tf_op jit(solution)/shard_map/while
  697.6 9.5 copy-start.26
  721.9 7.2 copy-start.1
  747.1 85.5 %all-reduce.29.cloned.1.call-start = ((), (), s32[]{:S(2)}) async-start(), calls=%async_computation.13 | async-start | bytes 2195456 | tf_op jit(solution)/shard_map/while/body/eval_jaxpr/psum | solution.py:119
  749.5 32.6 %copy-start.14 = (bf16[512,512]{1,0:T(8,128)(2,1)S(1)}, bf16[512,512]{1,0:T(8,128)(2,1)}, u32[]{:S(2)}) copy-start(bf16[512,512]{1,0:T(8,128)(2,1)} %get-tuple-element.1004) | copy-start | bytes 1572868 | tf_op jit(solution)/shard_map/while
  795.7 3.7 copy-start.44
  795.7 3.7 copy-start.45
  795.7 3.7 copy-start.65
  795.7 5.1 copy-start.55
  832.6 2.9 copy-start.7
  832.6 2.9 copy-start.38
  832.6 2.9 copy-start.39
  840.3 5.6 copy-start.32
  848.8 34.0 %copy-start.25 = (bf16[532,512]{0,1:T(8,128)(2,1)S(1)}, bf16[532,512]{0,1:T(8,128)(2,1)}, u32[]{:S(2)}) copy-start(bf16[532,512]{0,1:T(8,128)(2,1)} %copy-done.24) | copy-start | bytes 1634308 | tf_op jit(solution)/shard_map/while
  882.8 5.4 copy-start.23
  882.8 5.4 copy-start.73
  893.1 4.6 copy-start.34
  900.6 33.8 %copy-start.28 = (bf16[532,512]{0,1:T(8,128)(2,1)S(1)}, bf16[532,512]{0,1:T(8,128)(2,1)}, u32[]{:S(2)}) copy-start(bf16[532,512]{0,1:T(8,128)(2,1)} %copy.214) | copy-start | bytes 1634308 | tf_op jit(solution)/shard_map/while
  934.3 4.6 copy-start.27
  934.3 4.6 copy-start.74
  958.4 162.5 %reduce-scatter.16.cloned.1.call-start = ((), (), s32[]{:S(2)}) async-start(), calls=%async_computation.9 | async-start | bytes 270336
  959.4 161.5 %all-reduce.23.cloned.1.call-start = ((), (), s32[]{:S(2)}) async-start(), calls=%async_computation.10 | async-start | bytes 4194304 | tf_op jit(solution)/shard_map/psum | solution.py:220
  960.2 294.1 %reduce-scatter.14.cloned.1.call-start = ((), (), s32[]{:S(2)}) async-start(), calls=%async_computation.8 | async-start | bytes 1081344 | tf_op jit(solution)/shard_map/reduce_scatter | solution.py:239
  961.7 426.4 %reduce-scatter.12.cloned.1.call-start = ((), (), s32[]{:S(2)}) async-start(), calls=%async_computation.7 | async-start | bytes 1081344 | tf_op jit(solution)/shard_map/reduce_scatter | solution.py:238
  965.4 556.2 %reduce-scatter.8.cloned.1.call-start = ((), (), s32[]{:S(2)}) async-start(), calls=%async_computation.5 | async-start | bytes 1081344 | tf_op jit(solution)/shard_map/reduce_scatter | solution.py:236
  966.2 688.9 %reduce-scatter.10.cloned.1.call-start = ((), (), s32[]{:S(2)}) async-start(), calls=%async_computation.6 | async-start | bytes 1081344 | tf_op jit(solution)/shard_map/reduce_scatter | solution.py:237
  1120.9 536.4 %copy-start.60 = (f32[512,512]{1,0:T(8,128)S(1)}, f32[512,512]{1,0:T(8,128)}, u32[]{:S(2)}) copy-start(f32[512,512]{1,0:T(8,128)} %get-tuple-element.1148) | copy-start | bytes 3145732
  (98 other events, 158.3 us)
Sparse Core Ops, SparseCore 0:
  306.1 29.3 all-reduce.24
  393.3 33.2 all-reduce.26
  441.9 36.7 all-reduce.28
  655.9 33.4 all-reduce.24
  747.2 33.2 all-reduce.26
  795.8 36.7 all-reduce.28
  964.9 104.5 all-reduce.22
Sparse Core Ops, SparseCore 1:
  961.7 159.1 reduce-scatter.15
  1123.7 130.5 reduce-scatter.13
  1257.5 130.5 reduce-scatter.11
  1391.0 130.5 reduce-scatter.7
  1524.5 130.5 reduce-scatter.9
where the time goes:
time: 1670 us
  waiting for transfers between devices  802 us (48%)
  blocking collectives  301 us (18%)
  other arithmetic  231 us (14%)
  matrix products  162 us (10%)
  local copies, waits for them, and re-layouts  147 us (9%)
    sub x4, other arithmetic, span_pass(): grad_attend - jnp.sum(grad_attend * attend, axis=-1, keepdims=True)  136 us
    reduce_scatter x1, waiting for transfers between devices, shards(): lax.psum_scatter(full[2] * fraction, ('dp', 'mp'), scatter_dimension=0, t...  134 us
    reduce_scatter x1, waiting for transfers between devices, shards(): lax.psum_scatter(full[0] * fraction, ('dp', 'mp'), scatter_dimension=0, t...  134 us
    reduce_scatter x1, waiting for transfers between devices, shards(): lax.psum_scatter(full[1] * fraction, ('dp', 'mp'), scatter_dimension=0, t...  133 us
    reduce_scatter x1, waiting for transfers between devices, shards(): lax.psum_scatter(full[3] * fraction, ('dp', 'mp'), scatter_dimension=0, t...  133 us
    psum x4, waiting for transfers between devices, span_pass(): lax.psum(partial_out.astype(jnp.bfloat16), 'mp').astype(jnp.float32)  120 us
    unnamed x7, waiting for transfers between devices  89.8 us
    unnamed x2, blocking collectives  84.2 us
  transfers between devices with their start and end apart: 12, of which 11 were waited for; matrix products, arithmetic and copies ran while one was open for 2% of the time, Pallas kernels for 0%

commit v1 on v0

v1 whole, which is shorter than its diff:
```python
import functools

import jax
import jax.numpy as jnp
from jax import lax
from jax.experimental import pallas as pl
from jax.experimental.pallas import tpu as pltpu
from jax.sharding import PartitionSpec as P

D = 512
HEADS = 8
HEAD = 64
MEM = 20
PAD = 32
SPAN = 512
SPANS = 2
EXTRA = 128
WIDE = 4 * D + EXTRA
EPS = 1e-05
GELU_A = 0.7978845608028654
GELU_B = 0.044715
LOW = jnp.bfloat16
F32 = jnp.float32
SCALE = HEAD ** (-0.5)
ALL = ("dp", "mp")

VMEM = pl.BlockSpec(memory_space=pltpu.VMEM)
SMEM = pl.BlockSpec(memory_space=pltpu.SMEM)
ANY = pl.BlockSpec(memory_space=pl.ANY)


def dg(a, b, ca, cb):
    return lax.dot_general(a, b, (((ca,), (cb,)), ((), ())), preferred_element_type=F32)


def iota(shape, dim):
    return lax.broadcasted_iota(jnp.int32, shape, dim)


def head_mask():
    return (iota((HEADS * PAD, D), 0) >> 5) == (iota((HEADS * PAD, D), 1) >> 6)


def block_diagonal(rows):
    tall = jnp.concatenate([rows] * HEADS, axis=0)
    return jnp.where(head_mask(), tall, 0.0).astype(LOW)


def diagonal_sum(tall):
    kept = jnp.where(head_mask(), tall, 0.0)
    total = kept[:PAD]
    for h in range(1, HEADS):
        total = total + kept[h * PAD : (h + 1) * PAD]
    return total


def normalize(values):
    mean = jnp.mean(values, axis=1, keepdims=True)
    center = values - mean
    spread = jnp.mean(center * center, axis=1, keepdims=True)
    inv = lax.rsqrt(spread + EPS)
    return center * inv, inv


def gelu_parts(a):
    sq = a * a
    t = jnp.tanh(a * (GELU_A + (GELU_A * GELU_B) * sq))
    half = 0.5 * (1.0 + t)
    return half, t, sq


def gelu(a):
    half, _, _ = gelu_parts(a)
    return a * half


def call(kernel, out_shape, in_specs, out_specs, scratch=(), flops=0, bytes_=0):
    return pl.pallas_call(
        kernel,
        out_shape=out_shape,
        in_specs=in_specs,
        out_specs=out_specs,
        scratch_shapes=list(scratch),
        compiler_params=pltpu.CompilerParams(vmem_limit_bytes=56 * 2**20),
        cost_estimate=pl.CostEstimate(flops=flops, bytes_accessed=bytes_, transcendentals=0),
    )


def sds(shape, dtype):
    return jax.ShapeDtypeStruct(shape, dtype)


def pack_kernel(q_ref, k_ref, v_ref, o_ref, mem_ref, g1_ref, b1_ref, ob_ref, g2_ref, b2_ref, out_ref, tall):
    rows = q_ref.shape[0]
    for i, ref in enumerate((q_ref, k_ref, v_ref, o_ref)):
        out_ref[:, i * D : (i + 1) * D] = ref[...]
    tall[...] = jnp.zeros(tall.shape, F32)
    tall[:MEM, :rows] = mem_ref[...].astype(F32)
    for i, ref in enumerate((g1_ref, b1_ref, ob_ref, g2_ref, b2_ref)):
        tall[MEM + i : MEM + i + 1, :rows] = ref[...].astype(F32)
    out_ref[:, 4 * D :] = tall[...].T[:rows].astype(LOW)


def attend_kernel(bits, at_ref, *refs):
    n = len(bits)
    pieces = refs[:n]
    x_ref, x1_ref, w_ref, small_ref, nm_ref, qkv_ref, p_hbm, o_ref, m_ref, l_ref, wext, p_ref, sems = refs[n:]
    me = at_ref[0]
    for piece, offsets in zip(pieces, bits, strict=True):
        if offsets is None:
            wext[...] = piece[...]
            continue
        size = piece.shape[0] // len(offsets)
        for j, offset in enumerate(offsets):
            start = pl.multiple_of((me ^ offset) * size, size)
            wext[pl.ds(start, size), :] = piece[j * size : (j + 1) * size, :]
    w_ref[...] = wext[:, : 4 * D]
    small = wext[:, 4 * D :].T.astype(F32)[:PAD]
    small_ref[...] = small
    x_t = x_ref[...].T
    qkv_ref[:D] = (dg(wext[:, :D], x_t, 0, 0).astype(LOW).astype(F32) * SCALE).astype(LOW)
    qkv_ref[D : 3 * D] = dg(wext[:, D : 3 * D], x_t, 0, 0).astype(LOW)

    def scores(h):
        at = h * HEAD
        return dg(qkv_ref[D + at : D + at + HEAD], qkv_ref[at : at + HEAD], 0, 0)

    s_next = scores(0)
    copies = []
    for h in range(HEADS):
        s = s_next
        if h + 1 < HEADS:
            s_next = scores(h + 1)
        at = h * HEAD
        m = jnp.max(s, axis=0, keepdims=True)
        p = jnp.exp(s - m)
        m_ref[h : h + 1] = m
        l_ref[h : h + 1] = jnp.sum(p, axis=0, keepdims=True)
        p_ref[h] = p.astype(LOW)
        copy = pltpu.make_async_copy(p_ref.at[h], p_hbm.at[h], sems.at[h])
        copy.start()
        copies.append(copy)
        o_ref[at : at + HEAD] = dg(qkv_ref[2 * D + at : 2 * D + at + HEAD], p_ref[h], 1, 0)

    mem = jnp.where(iota((PAD, D), 0) < MEM, small, 0.0)
    packed = dg(mem.astype(LOW), wext[:, : 3 * D], 1, 0).astype(LOW)
    q_tall = block_diagonal(packed[:, :D].astype(F32) * SCALE)
    s_mem = dg(q_tall, packed[:, D : 2 * D], 1, 1)
    s_mem = jnp.where(iota(s_mem.shape, 1) < MEM, s_mem, -1e30)
    kv = dg(x1_ref[...], wext[:, D : 3 * D], 1, 0).astype(LOW)
    s = dg(q_tall, kv[:, :D], 1, 1)
    m = jnp.maximum(jnp.max(s, axis=1, keepdims=True), jnp.max(s_mem, axis=1, keepdims=True))
    p = jnp.exp(s - m)
    p_mem = jnp.exp(s_mem - m)
    total = jnp.sum(p, axis=1, keepdims=True) + jnp.sum(p_mem, axis=1, keepdims=True)
    o = dg(p.astype(LOW), kv[:, D:], 1, 0) + dg(p_mem.astype(LOW), packed[:, 2 * D :], 1, 0)
    mixed = diagonal_sum(o / total).astype(LOW)
    xhat, _ = normalize(mem + dg(mixed, wext[:, 3 * D : 4 * D], 1, 0))
    nm_ref[...] = xhat * small[20:21] + small[21:22]
    for copy in copies:
        copy.wait()


def forward_kernel(
    at_ref, nm_ref, small_ref, x_ref, w_ref, qkv_ref, o_ref, m_ref, l_ref,
    wi0, wi1, wi2, wi3, wo0, wo1, wo2, wo3, bi_ref, cot_ref,
    out_ref, keep_ref, send_ref, slope_ref, nl_ref, gl_ref, gs_ref, xhat_ref, inv_ref,
    mixed_ref, mem_ref, pm_ref, c_ref, cm_ref, vec_ref, hid,
):
    wis, wos = (wi0, wi1, wi2, wi3), (wo0, wo1, wo2, wo3)
    small = small_ref[...]
    gain1, bias1, outer_b, gain2, bias2 = (small[MEM + i : MEM + i + 1] for i in range(5))
    later, first = at_ref[2], at_ref[5]
    nm = nm_ref[...]
    nm_low = nm.astype(LOW)
    value = nm + outer_b
    for k in range(4):
        inner = dg(nm_low, wis[k][...], 1, 0) + bi_ref[k : k + 1]
        value = value + dg(gelu(inner).astype(LOW), wos[k][...], 1, 0)
    carried, _ = normalize(value)
    carried = carried * gain2 + bias2
    mem = jnp.where(later == 1, carried, small)
    mem = jnp.where(iota((PAD, D), 0) < MEM, mem, 0.0)
    mem_ref[...] = mem
    kv_mem = dg(mem.astype(LOW), w_ref[:, D : 3 * D], 1, 0).astype(LOW).astype(F32)
    k_tall = block_diagonal(kv_mem[:, :D])
    v_tall = block_diagonal(kv_mem[:, D:])
    s_all = dg(k_tall, qkv_ref[:D], 1, 0)
    s_all = jnp.where((iota(s_all.shape, 0) & (PAD - 1)) < MEM, s_all, -1e30)
    alphas, invs = [], []
    for h in range(HEADS):
        s = s_all[h * PAD : (h + 1) * PAD]
        m_old = m_ref[h : h + 1]
        m = jnp.maximum(m_old, jnp.max(s, axis=0, keepdims=True))
        alpha = jnp.exp(m_old - m)
        p = jnp.exp(s - m)
        inv = 1.0 / (l_ref[h : h + 1] * alpha + jnp.sum(p, axis=0, keepdims=True))
        pm_ref[h * PAD : (h + 1) * PAD] = p.astype(LOW)
        c_ref[h : h + 1] = alpha * inv
        cm_ref[h : h + 1] = inv
        alphas.append(alpha * inv)
        invs.append(inv)
    o_mem = dg(v_tall, pm_ref[...], 0, 0)
    for h in range(HEADS):
        at = h * HEAD
        mixed_ref[at : at + HEAD] = (
            o_ref[at : at + HEAD] * alphas[h] + o_mem[at : at + HEAD] * invs[h]
        ).astype(LOW)
    xhat1, inv1 = normalize(
        x_ref[...].astype(F32) + dg(mixed_ref[...], w_ref[:, 3 * D : 4 * D], 0, 0)
    )
    xhat_ref[...] = xhat1
    inv_ref[...] = inv1
    normed = xhat1 * gain1 + bias1
    normed_low = normed.astype(LOW)
    nl_ref[...] = normed_low
    total = normed + outer_b
    for k in range(4):
        a = dg(normed_low, wis[k][...], 1, 0) + bi_ref[k : k + 1]
        half, t, sq = gelu_parts(a)
        hid[k] = (a * half).astype(LOW)
        slope = half + (0.5 * a) * (1.0 - t * t) * (GELU_A + (3.0 * GELU_A * GELU_B) * sq)
        slope_ref[k] = slope.astype(LOW)
        total = total + dg(hid[k], wos[k][...], 1, 0)
    xhat2, inv2 = normalize(total)
    out_ref[...] = (xhat2 * gain2 + bias2).astype(LOW)
    cot = cot_ref[...].astype(F32)
    pull = cot * gain2
    grad_sum = inv2 * (
        pull
        - jnp.mean(pull, axis=1, keepdims=True)
        - xhat2 * jnp.mean(pull * xhat2, axis=1, keepdims=True)
    )
    vec_ref[2:3] = jnp.sum(grad_sum, axis=0, keepdims=True)
    vec_ref[3:4] = jnp.sum(cot * xhat2, axis=0, keepdims=True)
    vec_ref[4:5] = jnp.sum(cot, axis=0, keepdims=True)
    gs_ref[...] = grad_sum
    grad_low = grad_sum.astype(LOW)
    gl_ref[...] = grad_low
    for k in (1, 3, 0, 2):
        give(send_ref if k % 2 else keep_ref, k // 2, dg(hid[k], grad_low, 0, 0), first)


def give(ref, k, rows, first):
    size = rows.shape[0] // 4
    for i in range(4):
        ref[k, first ^ i] = rows[i * size : (i + 1) * size].astype(LOW)


def middle_kernel(
    at_ref, small_ref, w_ref, wi0, wi1, wi2, wi3, wo0, wo1, wo2, wo3, slope_ref, nl_ref, gl_ref, gs_ref, xhat_ref, inv_ref,
    mixed_ref, keep_ref, send_ref, resid_ref, dwo_ref, gmix_ref, vec_ref,
):
    wis, wos = (wi0, wi1, wi2, wi3), (wo0, wo1, wo2, wo3)
    first = at_ref[5]
    back = gs_ref[...]
    grad_low = gl_ref[...]
    extra = jnp.zeros((PAD - 8, D), F32)
    for k in (1, 3, 0, 2):
        gi = slope_ref[k].astype(F32) * dg(grad_low, wos[k][...], 1, 1)
        gi_low = gi.astype(LOW)
        bias = jnp.sum(gi_low.astype(F32), axis=0, keepdims=True)
        bias = jnp.where(iota((8, D), 0) == 0, bias, 0.0)
        rows = jnp.concatenate([dg(nl_ref[...], gi_low, 0, 0), bias, extra], axis=0)
        give(send_ref if k % 2 else keep_ref, k // 2, rows, first)
        back = back + dg(gi_low, wis[k][...], 1, 1)
    xhat1 = xhat_ref[...]
    vec_ref[0:1] = jnp.sum(back * xhat1, axis=0, keepdims=True)
    vec_ref[1:2] = jnp.sum(back, axis=0, keepdims=True)
    pull = back * small_ref[MEM : MEM + 1]
    resid = inv_ref[...] * (
        pull
        - jnp.mean(pull, axis=1, keepdims=True)
        - xhat1 * jnp.mean(pull * xhat1, axis=1, keepdims=True)
    )
    resid_ref[...] = resid
    resid_low = resid.astype(LOW)
    dwo_ref[...] = dg(mixed_ref[...], resid_low, 1, 0).astype(LOW)
    gmix_ref[...] = dg(w_ref[:, 3 * D : 4 * D], resid_low, 1, 1).astype(LOW)


def backward_kernel(
    bits, at_ref, x_ref, w_ref, qkv_ref, p_hbm, pm_ref, mixed_ref, c_ref, cm_ref, gmix_ref, mem_ref, resid_ref,
    dwo_ref, vec_ref, vec1_ref, *rest,
):
    g_refs, (tok_ref, p_ref, sems, gp, do_m, ds_m, wext) = rest[: len(bits)], rest[len(bits) :]
    me = at_ref[0]
    copies = [pltpu.make_async_copy(p_hbm.at[h], p_ref.at[h], sems.at[h]) for h in range(HEADS)]
    for copy in copies:
        copy.start()
    mem_low = mem_ref[...].astype(LOW)
    kv_mem = dg(mem_low, w_ref[:, D : 3 * D], 1, 0).astype(LOW).astype(F32)
    k_tall = block_diagonal(kv_mem[:, :D])
    v_tall = block_diagonal(kv_mem[:, D:])
    deltas = []
    for h in range(HEADS):
        at = h * HEAD
        do = gmix_ref[at : at + HEAD].astype(F32)
        deltas.append(
            jnp.sum(do * mixed_ref[at : at + HEAD].astype(F32), axis=0, keepdims=True)
        )
        do_m[at : at + HEAD] = (do * cm_ref[h : h + 1]).astype(LOW)
    da_m = dg(v_tall, do_m[...], 1, 0)
    for h in range(HEADS):
        rows = slice(h * PAD, (h + 1) * PAD)
        ds_m[rows] = (
            pm_ref[rows].astype(F32) * (da_m[rows] - deltas[h] * cm_ref[h : h + 1])
        ).astype(LOW)
    dv_mem = diagonal_sum(dg(pm_ref[...], do_m[...], 1, 1))
    dk_mem = diagonal_sum(dg(ds_m[...], qkv_ref[:D], 1, 1))
    dq_mem = dg(k_tall, ds_m[...], 0, 0)
    for h in range(HEADS):
        at = h * HEAD
        c = c_ref[h : h + 1]
        do = (gmix_ref[at : at + HEAD].astype(F32) * c).astype(LOW)
        copies[h].wait()
        p = p_ref[h]
        da = dg(qkv_ref[2 * D + at : 2 * D + at + HEAD], do, 0, 0)
        ds = (p.astype(F32) * (da - deltas[h] * c)).astype(LOW)
        gp[2 * D + at : 2 * D + at + HEAD] = dg(do, p, 1, 1).astype(LOW)
        gp[D + at : D + at + HEAD] = dg(qkv_ref[at : at + HEAD], ds, 1, 1).astype(LOW)
        gp[at : at + HEAD] = (
            SCALE * (dg(qkv_ref[D + at : D + at + HEAD], ds, 1, 0) + dq_mem[at : at + HEAD])
        ).astype(LOW)
    gp_mem = jnp.concatenate([dk_mem, dv_mem], axis=1).astype(LOW)
    x_t = x_ref[...].T
    wext[:, :D] = dg(x_t, gp[:D], 1, 1).astype(LOW)
    wext[:, D : 3 * D] = (dg(x_t, gp[D:], 1, 1) + dg(mem_low, gp_mem, 0, 0)).astype(LOW)
    wext[:, 3 * D : 4 * D] = dwo_ref[...]
    g_mem = dg(gp_mem, w_ref[:, D : 3 * D], 1, 1)
    g_mem = jnp.where(at_ref[2] == 0, g_mem, 0.0)
    row = iota((EXTRA, D), 0)
    tall = jnp.concatenate([g_mem, jnp.zeros((EXTRA - PAD, D), F32)], axis=0)
    tall = jnp.where(row < MEM, tall, 0.0)
    for i in range(5):
        tall = jnp.where(row == MEM + i, (vec1_ref if i < 2 else vec_ref)[i : i + 1], tall)
    wext[:, 4 * D :] = tall.T.astype(LOW)
    for g_ref, offsets in zip(g_refs, bits, strict=True):
        if offsets is None:
            g_ref[...] = wext[...]
            continue
        size = g_ref.shape[0] // len(offsets)
        for j, offset in enumerate(offsets):
            start = pl.multiple_of((me ^ offset) * size, size)
            g_ref[j * size : (j + 1) * size] = wext[pl.ds(start, size), :]
    tok_ref[...] = (dg(w_ref[:, : 3 * D], gp[...], 1, 0).T + resid_ref[...]).astype(LOW)


def place_kernel(at_ref, r0, r1, r2, r3, out_ref, held, ins, outs):
    me = at_ref[3]
    refs = (r0, r1, r2, r3)
    ins = [pltpu.make_async_copy(refs[k], held.at[k], ins.at[k]) for k in range(4)]
    outs = [pltpu.make_async_copy(held.at[k], out_ref.at[me ^ k], outs.at[k]) for k in range(4)]
    for copy in ins:
        copy.start()
    for k in range(4):
        ins[k].wait()
        outs[k].start()
    for copy in outs:
        copy.wait()


def place(at, pieces):
    rows = call(
        place_kernel,
        sds((4,) + pieces[0].shape, pieces[0].dtype),
        [SMEM] + [ANY] * 4,
        ANY,
        [
            pltpu.VMEM((4,) + pieces[0].shape, pieces[0].dtype),
            pltpu.SemaphoreType.DMA((4,)),
            pltpu.SemaphoreType.DMA((4,)),
        ],
    )(at, *pieces)
    return rows.reshape(-1, D)


def finish_kernel(at_ref, own_ref, other_ref, out_ref, bias_ref, held):
    first = at_ref[5]
    size = own_ref.shape[1]
    for i, ref in enumerate((own_ref, other_ref)):
        for j in range(2):
            start = pl.multiple_of((first ^ (2 * i + j)) * size, size)
            held[pl.ds(start, size), :] = ref[j].astype(F32)
    out_ref[...] = held[:D]
    bias_ref[...] = held[held.shape[0] - PAD : held.shape[0] - PAD + 1]


def swap(value, axis, bit):
    n = lax.axis_size(axis)
    return lax.ppermute(value, axis, [(i, i ^ bit) for i in range(n)])


def add_low(*terms):
    return functools.reduce(jnp.add, [t.astype(F32) for t in terms]).astype(LOW)


def sum_over_dp(at, own, theirs):
    n_dp = lax.axis_size("dp")
    got = swap(theirs, "mp", 2)
    if n_dp != 8:
        total = lax.psum(own.astype(F32) + got.astype(F32), "dp").reshape(-1, D)
        return total[:D], total[-PAD]
    mine, give_x = add_low(own[:2], got[:2]), add_low(own[2:], got[2:])
    got = swap(give_x, "dp", 1)
    mine, give_z = add_low(mine[0], got[0]), add_low(mine[1], got[1])
    mine = add_low(mine, swap(give_z, "dp", 2))
    mine = add_low(mine, swap(mine, "dp", 4))
    pair = jnp.stack([mine, swap(mine, "dp", 2)])
    rows = 4 * own.shape[1]
    grad, bias = call(
        finish_kernel,
        [sds((D, D), F32), sds((1, D), F32)],
        [SMEM] + [VMEM] * 2,
        [VMEM] * 2,
        [pltpu.VMEM((rows, D), F32)],
        bytes_=2 * 2**20,
    )(at, pair, swap(pair, "dp", 1))
    return grad, bias[0]


def shards(
    tokens, cotangent, memory_init, query_weight, key_weight, value_weight, output_weight, first_gain,
    first_bias, inner_weight, inner_bias, outer_weight, outer_bias, second_gain, second_bias,
):
    n_dp, n_mp = lax.axis_size("dp"), lax.axis_size("mp")
    rows_each = query_weight.shape[0]
    by_bits = n_dp == 8 and n_mp == 4 and rows_each % 16 == 0
    me_mp, me_dp = lax.axis_index("mp"), lax.axis_index("dp")
    me = me_dp * n_mp + me_mp
    later = me_mp % SPANS
    first = ((me_dp & 1) * 2 + ((me_dp >> 1) & 1)) if by_bits else 0
    at = jnp.stack([me, me_mp // SPANS, later, me_mp, me_dp, first]).astype(jnp.int32)

    vectors = (first_gain, first_bias, outer_bias, second_gain, second_bias)
    local = call(
        pack_kernel,
        sds((rows_each, WIDE), LOW),
        [VMEM] * 10,
        VMEM,
        [pltpu.VMEM((EXTRA, EXTRA), F32)],
    )(query_weight, key_weight, value_weight, output_weight, memory_init, *[v.reshape(1, -1) for v in vectors])
    if by_bits:
        line = jnp.concatenate([local] + [swap(local, ALL, 8 * j) for j in range(1, 4)], axis=0)
        plane = [line] + [swap(line, ALL, 2 * b) for b in range(1, 4)]
        pieces = plane + [swap(piece, ALL, 1) for piece in plane]
        bits = [[2 * b + c + 8 * j for j in range(4)] for c in range(2) for b in range(4)]
    else:
        pieces = [lax.all_gather(local, ALL, axis=0, tiled=True)]
        bits = [None]

    wis, wos = [inner_weight], [outer_weight]
    bis = [inner_bias.reshape(1, -1)]
    for group in (wis, wos, bis):
        group += [swap(group[0], "mp", k) for k in range(1, 3)]
        group.append(swap(group[2], "mp", 1))
    inner_shift = jnp.concatenate(bis, axis=0).astype(F32)

    blocks = tokens.reshape(-1, SPAN, D)
    pick = lambda v, i: lax.dynamic_index_in_dim(v, i, 0, keepdims=False)
    own = pick(blocks, me_mp)
    start = pick(blocks, me_mp - later)
    cot = pick(cotangent.reshape(-1, SPAN, D), me_mp)

    w, small, nm, qkv, p, o, m, l = call(
        functools.partial(attend_kernel, bits),
        [
            sds((D, 4 * D), LOW),
            sds((PAD, D), F32),
            sds((PAD, D), F32),
            sds((3 * D, SPAN), LOW),
            sds((HEADS, SPAN, SPAN), LOW),
            sds((D, SPAN), F32),
            sds((HEADS, SPAN), F32),
            sds((HEADS, SPAN), F32),
        ],
        [SMEM] + [VMEM] * (len(pieces) + 2),
        [VMEM, VMEM, VMEM, VMEM, ANY, VMEM, VMEM, VMEM],
        [
            pltpu.VMEM((D, WIDE), LOW),
            pltpu.VMEM((HEADS, SPAN, SPAN), LOW),
            pltpu.SemaphoreType.DMA((HEADS,)),
        ],
        flops=10 * 10**9,
        bytes_=10 * 2**20,
    )(at, *pieces, own, start)

    outer_shape = sds((2, 4, D // 4, D), LOW)
    inner_shape = sds((2, 4, (D + PAD) // 4, D), LOW)
    square, square_low = sds((SPAN, D), F32), sds((SPAN, D), LOW)
    (out, outer_keep, outer_send, slope, normed, grad_low, grad_sum, xhat, inv, mixed, mem, p_mem, c, c_mem, vecs) = call(
        forward_kernel,
        [
            square_low,
            outer_shape,
            outer_shape,
            sds((4, SPAN, D), LOW),
            square_low,
            square_low,
            square,
            square,
            sds((SPAN, 1), F32),
            sds((D, SPAN), LOW),
            sds((PAD, D), F32),
            sds((HEADS * PAD, SPAN), LOW),
            sds((HEADS, SPAN), F32),
            sds((HEADS, SPAN), F32),
            sds((8, D), F32),
        ],
        [SMEM] + [VMEM] * 18,
        [VMEM] * 15,
        [pltpu.VMEM((4, SPAN, D), LOW)],
        flops=10 * 10**9,
        bytes_=14 * 2**20,
    )(at, nm, small, own, w, qkv, o, m, l, *wis, *wos, inner_shift, cot)

    theirs = swap(outer_send, "mp", 1)
    grad_outer, _ = sum_over_dp(at, add_low(outer_keep[0], theirs[0]), add_low(outer_keep[1], theirs[1]))

    across = swap(out, "mp", 2)
    layer_out = place(at, [out, swap(out, "mp", 1), across, swap(across, "mp", 1)])

    inner_keep, inner_send, resid, d_mix, g_mixed, vecs1 = call(
        middle_kernel,
        [
            inner_shape,
            inner_shape,
            square,
            sds((D, D), LOW),
            sds((D, SPAN), LOW),
            sds((8, D), F32),
        ],
        [SMEM] + [VMEM] * 17,
        [VMEM] * 6,
        flops=8 * 10**9,
        bytes_=14 * 2**20,
    )(at, small, w, *wis, *wos, slope, normed, grad_low, grad_sum, xhat, inv, mixed)
    theirs = swap(inner_send, "mp", 1)
    grad_inner, grad_inner_bias = sum_over_dp(
        at, add_low(inner_keep[0], theirs[0]), add_low(inner_keep[1], theirs[1])
    )

    if by_bits:
        out_bits = [[2 * b + c + 8 * j for b in range(4) for j in range(4)] for c in range(2)]
    else:
        out_bits = [None]
    *grads, grad_rows = call(
        functools.partial(backward_kernel, out_bits),
        [sds((D // len(out_bits), WIDE), LOW) for _ in out_bits] + [sds((SPAN, D), LOW)],
        [SMEM, VMEM, VMEM, VMEM, ANY] + [VMEM] * 10,
        [VMEM] * (len(out_bits) + 1),
        [
            pltpu.VMEM((HEADS, SPAN, SPAN), LOW),
            pltpu.SemaphoreType.DMA((HEADS,)),
            pltpu.VMEM((3 * D, SPAN), LOW),
            pltpu.VMEM((D, SPAN), LOW),
            pltpu.VMEM((HEADS * PAD, SPAN), LOW),
            pltpu.VMEM((D, WIDE), LOW),
        ],
        flops=12 * 10**9,
        bytes_=12 * 2**20,
    )(at, own, w, qkv, p, p_mem, mixed, c, c_mem, g_mixed, mem, resid, d_mix, vecs, vecs1)

    across = swap(grad_rows, "mp", 2)
    grad_tokens = place(at, [grad_rows, swap(grad_rows, "mp", 1), across, swap(across, "mp", 1)])

    if by_bits:
        chip = add_low(grads[0], swap(grads[1], ALL, 1)).reshape(4, 4 * rows_each, WIDE)
        line = add_low(chip[0], *[swap(chip[b], ALL, 2 * b) for b in range(1, 4)])
        line = line.reshape(4, rows_each, WIDE)
        terms = [line[0]] + [swap(line[j], ALL, 8 * j) for j in range(1, 4)]
        reduced = functools.reduce(jnp.add, [t.astype(F32) for t in terms])
    else:
        reduced = lax.psum_scatter(grads[0], ALL, scatter_dimension=0, tiled=True).astype(F32)
    vector = lambda i: reduced[:, 4 * D + MEM + i]
    return (
        layer_out,
        grad_tokens,
        reduced[:, 4 * D : 4 * D + MEM].T,
        reduced[:, :D],
        reduced[:, D : 2 * D],
        reduced[:, 2 * D : 3 * D],
        reduced[:, 3 * D : 4 * D],
        vector(0),
        vector(1),
        grad_inner,
        grad_inner_bias,
        grad_outer,
        vector(2),
        vector(3),
        vector(4),
    )


def solution(mesh):
    both = ("dp", "mp")
    in_specs = (
        P("dp", None),
        P("dp", None),
        P(None, both),
        P(both, None),
        P(both, None),
        P(both, None),
        P(both, None),
        P(both),
        P(both),
        P(None, "mp"),
        P("mp"),
        P("mp", None),
        P(both),
        P(both),
        P(both),
    )
    out_specs = (
        P("dp", None),
        P("dp", None),
        P(None, both),
        P(both, None),
        P(both, None),
        P(both, None),
        P(both, None),
        P(both),
        P(both),
        P(None, "mp"),
        P("mp"),
        P("mp", None),
        P(both),
        P(both),
        P(both),
    )
    return jax.shard_map(shards, mesh=mesh, in_specs=in_specs, out_specs=out_specs, check_vma=False)
```

time: 1670 us -> 209 us (0.13)
  waiting for transfers between devices: 802 us -> 91.5 us
  blocking collectives: 301 us -> 0 us
  other arithmetic: 231 us -> 5.46 us
  matrix products: 162 us -> 0 us
  local copies, waits for them, and re-layouts: 147 us -> 11.3 us
  Pallas kernels: 0 us -> 60.4 us
  starting transfers between devices: 1.63 us -> 39.1 us
    reduce_scatter x4 -> x0, waiting for transfers between devices: 534 us -> none  [the longest x1 134 us: shards(): lax.psum_scatter(full[2] * fraction, ('dp', 'mp'), scatter_dimension=0, t...]
    all_gather x5 -> x0, blocking collectives: 196 us -> none  [the longest x1 40.8 us: shards(): lax.all_gather(memory_init, ('dp', 'mp'), axis=1, tiled=True)]
    psum x7 -> x0, waiting for transfers between devices: 178 us -> none  [the longest x4 120 us: span_pass(): lax.psum(partial_out.astype(jnp.bfloat16), 'mp').astype(jnp.float32)]
    dot_general x72 -> x0, matrix products: 162 us -> none  [the longest x4 26.4 us: span_pass(): jnp.einsum('qhd,khd->hqk', queries, key_rows, preferred_element_type=jnp....]
    sub x4 -> x0, other arithmetic: 136 us -> none  [span_pass(): grad_attend - jnp.sum(grad_attend * attend, axis=-1, keepdims=True)]
    ppermute x0 -> x46, waiting for transfers between devices: none -> 91.5 us  [swap(): return lax.ppermute(value, axis, [(i, i ^ bit) for i in range(n)])]
    unnamed x7 -> x0, waiting for transfers between devices: 89.8 us -> none
    unnamed x2 -> x0, blocking collectives: 84.2 us -> none
  transfers between devices with their start and end apart: 12 -> 46, of which waited for: 11 -> 22; matrix products, arithmetic and copies ran while one was open for 2% -> 5% of each run, Pallas kernels for 0% -> 9%
where the time goes in v1:
time: 209 us
  waiting for transfers between devices  91.5 us (44%)
  Pallas kernels  60.4 us (29%)
  starting transfers between devices  39.1 us (19%)
  local copies, waits for them, and re-layouts  11.3 us (5%)
  other arithmetic  5.46 us (3%)
    ppermute x46, waiting for transfers between devices, swap(): return lax.ppermute(value, axis, [(i, i ^ bit) for i in range(n)])  91.5 us
    ppermute x46, starting transfers between devices, swap(): return lax.ppermute(value, axis, [(i, i ^ bit) for i in range(n)])  39.1 us
    pallas_call x1, Pallas kernels, shards(): call(forward_kernel, [square_low, outer_shape, outer_shape, sds((4, SPAN,...  14.5 us
    pallas_call x1, Pallas kernels, shards(): call(functools.partial(backward_kernel, out_bits), [sds((D // len(out_bit...  13.1 us
    pallas_call x1, Pallas kernels, shards(): call(functools.partial(attend_kernel, bits), [sds((D, 4 * D), LOW), sds((...  10.8 us
    pallas_call x1, Pallas kernels, shards(): call(middle_kernel, [inner_shape, inner_shape, square, sds((D, D), LOW),...  10 us
    pallas_call x2, Pallas kernels, place(): call(place_kernel, sds((4,) + pieces[0].shape, pieces[0].dtype), [SMEM] +...  6.17 us
    unnamed x41, local copies, waits for them, and re-layouts  4.84 us
  transfers between devices with their start and end apart: 46, of which 22 were waited for; matrix products, arithmetic and copies ran while one was open for 5% of the time, Pallas kernels for 9%

profile of v1, /device:TPU:0, one launch (start us, length us, event | category | flops | bytes accessed | tf_op | source)
XLA Modules:
  0.0 208.8 jit_solution(14802829935922526433)
XLA Ops:
  0.7 1.5 copy.31.mem_ref
  2.2 1.5 shard_map.262
  3.7 3.0 %collective-permute-start = (bf16[16,2176]{1,0:T(8,128)(2,1)}, bf16[16,2176]{1,0:T(8,128)(2,1)S(1)}, u32[]{:S(2)}, u32[]{:S(2)}) collective-permute-start(bf16[16,2176]{1,0:T(8,128)(2,1)} %shard_map.262), channel_id=1, source_target_pairs={{0,8},{1,9},{2,10},{3,11},{4,12},{5,13},{6,14},{7,15},{8,0},{9,1},... | collective-permute-start | bytes 208904 | tf_op jit(solution)/shard_map/ppermute | solution.py:391
  6.7 2.6 %collective-permute-start.1 = (bf16[16,2176]{1,0:T(8,128)(2,1)}, bf16[16,2176]{1,0:T(8,128)(2,1)S(1)}, u32[]{:S(2)}, u32[]{:S(2)}) collective-permute-start(bf16[16,2176]{1,0:T(8,128)(2,1)} %shard_map.262), channel_id=1, source_target_pairs={{0,16},{1,17},{2,18},{3,19},{4,20},{5,21},{6,22},{7,23},{8,24},{9,... | collective-permute-start | bytes 208904 | tf_op jit(solution)/shard_map/ppermute | solution.py:391
  9.3 5.2 %collective-permute-done.1 = bf16[16,2176]{1,0:T(8,128)(2,1)S(1)} collective-permute-done((bf16[16,2176]{1,0:T(8,128)(2,1)}, bf16[16,2176]{1,0:T(8,128)(2,1)S(1)}, u32[]{:S(2)}, u32[]{:S(2)}) %collective-permute-start.1) | collective-permute-done | bytes 69664 | tf_op jit(solution)/shard_map/ppermute | solution.py:391
  14.5 1.3 collective-permute-done.2
  15.7 0.9 pad_maximum_fusion.refs_0_
  16.7 1.6 collective-permute-start.3
  18.2 1.5 collective-permute-start.4
  20.2 0.7 reshape.132
  20.9 1.5 collective-permute-start.17
  22.4 3.1 %collective-permute-done.17 = bf16[1,512]{1,0:T(2,128)(2,1)S(1)} collective-permute-done((bf16[1,512]{1,0:T(2,128)(2,1)S(1)}, bf16[1,512]{1,0:T(2,128)(2,1)S(1)}, u32[]{:S(2)}, u32[]{:S(2)}) %collective-permute-start.17) | collective-permute-done | bytes 1056 | tf_op jit(solution)/shard_map/ppermute | solution.py:391
  25.6 1.2 collective-permute-done.16
  26.9 1.0 collective-permute-done.18
  27.9 1.5 collective-permute-start.11
  29.9 0.6 collective-permute-done.5.refs_3_
  31.3 0.8 dynamic-slice_bitcast_fusion.cot_ref
  32.7 2.2 %dynamic-slice_bitcast_fusion.1 = (bf16[512,512]{1,0:T(8,128)(2,1)}, bf16[512,512]{1,0:T(8,128)(2,1)}) fusion(bf16[4,512,512]{2,1,0:T(8,128)(2,1)} %bitcast.71, s32[]{:T(128)S(6)} %select_n.22, s32[]{:T(128)S(6)} %select_n.21), kind=kLoop, calls=%fused_computation.17 | loop fusion | bytes 2097160 | tf_op jit(solution)/shard_map/jit(dynamic_index_in_dim)/squeeze | solution.py:460
  35.0 0.6 maximum_convert_fusion.bi_ref
  35.6 7.4 %collective-permute-done.11.wi2 = bf16[512,512]{1,0:T(8,128)(2,1)} collective-permute-done((bf16[512,512]{1,0:T(8,128)(2,1)}, bf16[512,512]{1,0:T(8,128)(2,1)}, u32[]{:S(2)}, u32[]{:S(2)}) %collective-permute-start.11) | collective-permute-done | bytes 524320 | tf_op jit(solution)/shard_map/ppermute | solution.py:391
  43.0 10.5 %collective-permute-done.14.wo2 = bf16[512,512]{1,0:T(8,128)(2,1)} collective-permute-done((bf16[512,512]{1,0:T(8,128)(2,1)}, bf16[512,512]{1,0:T(8,128)(2,1)}, u32[]{:S(2)}, u32[]{:S(2)}) %collective-permute-start.14) | collective-permute-done | bytes 524320 | tf_op jit(solution)/shard_map/ppermute | solution.py:391
  54.0 10.8 %shard_map.263 = (bf16[512,2048]{1,0:T(8,128)(2,1)}, f32[32,512]{1,0:T(8,128)}, f32[32,512]{1,0:T(8,128)}, bf16[1536,512]{1,0:T(8,128)(2,1)}, bf16[8,512,512]{2,...) custom-call(s32[6]{0:T(128)} %stack.45.at_ref, bf16[64,2176]{1,0:T(8,128)(2,1)} %copy-done.11, ...), custom_call_target="tpu_custom_call" | custom-call | flops 10000000000 | bytes 10485760 | tf_op jit(solution)/shard_map/pallas_call | solution.py:465
  64.9 0.8 copy-done.15
  66.2 14.5 %shard_map.264 = (bf16[512,512]{1,0:T(8,128)(2,1)}, bf16[2,4,128,512]{3,2,1,0:T(8,128)(2,1)}, bf16[2,4,128,512]{3,2,1,0:T(8,128)(2,1)}, bf16[4,512,512]{2,1,0:T(...) custom-call(s32[6]{0:T(128)} %stack.45.at_ref, ...), custom_call_target="tpu_custom_call" | custom-call | flops 10000000000 | bytes 14680064 | tf_op jit(solution)/shard_map/pallas_call | solution.py:491
  80.6 10.0 %shard_map.266 = (bf16[2,4,136,512]{3,2,1,0:T(8,128)(2,1)}, bf16[2,4,136,512]{3,2,1,0:T(8,128)(2,1)}, f32[512,512]{1,0:T(8,128)}, bf16[512,512]{1,0:T(8,128)(2,1...) custom-call(s32[6]{0:T(128)} %stack.45.at_ref, f32[32,512]{1,0:T(8,128)} %get-tuple-element.51.small_ref, ...), custom_call_target="tpu_custom_call" | custom-call | flops 8000000000 | bytes 14680064 | tf_op jit(solution)/shard_map/pallas_call | solution.py:523
  90.6 13.1 %shard_map.267 = (bf16[256,2176]{1,0:T(8,128)(2,1)}, bf16[256,2176]{1,0:T(8,128)(2,1)}, bf16[512,512]{1,0:T(8,128)(2,1)}) custom-call(s32[6]{0:T(128)} %stack.45.at_ref, bf16[512,512]{1,0:T(8,128)(2,1)} %get-tuple-element.95.refs_8_.x_ref, bf16[512,2048]{1,0:T(8,128)(2,1)} %get-tuple-element.52.w_ref, bf16[1536,512]{1,0:T(8,128)(2,1)} %get-tuple-element.53.qkv_ref, ...), custom_call_target="tpu_custom_call" | custom-call | flops 12000000000 | bytes 12582912 | tf_op jit(solution)/shard_map/pallas_call | solution.py:547
  104.3 1.5 collective-permute-start.23
  106.9 1.5 collective-permute-start.20
  108.4 1.5 add_convert_fusion
  110.0 9.3 %collective-permute-done.23.r2 = bf16[512,512]{1,0:T(8,128)(2,1)S(1)} collective-permute-done((bf16[512,512]{1,0:T(8,128)(2,1)}, bf16[512,512]{1,0:T(8,128)(2,1)S(1)}, u32[]{:S(2)}, u32[]{:S(2)}) %collective-permute-start.23) | collective-permute-done | bytes 524320 | tf_op jit(solution)/shard_map/ppermute | solution.py:391
  119.8 9.9 %collective-permute-done.20.r2 = bf16[512,512]{1,0:T(8,128)(2,1)} collective-permute-done((bf16[512,512]{1,0:T(8,128)(2,1)S(1)}, bf16[512,512]{1,0:T(8,128)(2,1)}, u32[]{:S(2)}, u32[]{:S(2)}) %collective-permute-start.20) | collective-permute-done | bytes 524320 | tf_op jit(solution)/shard_map/ppermute | solution.py:391
  129.8 1.6 collective-permute-start.26
  131.4 1.5 collective-permute-start.27
  134.1 3.1 %shard_map.268 = bf16[4,512,512]{2,1,0:T(8,128)(2,1)} custom-call(s32[6]{0:T(128)} %stack.45.at_ref, bf16[512,512]{1,0:T(8,128)(2,1)} %get-tuple-element.75.r0, bf16[512,512]{1,0:T(8,128)(2,1)} %copy-done.7, bf16[512,512]{1,0:T(8,128)(2,1)} %copy-done.6, bf16[512,512]{1,0:T(8,128)(2,1)} %copy-done.9), custom_call_target="tpu_custom_call" | custom-call | tf_op jit(solution)/shard_map/pallas_call | solution.py:364
  137.2 1.3 collective-permute-start.40
  138.5 3.1 %shard_map.265 = bf16[4,512,512]{2,1,0:T(8,128)(2,1)} custom-call(s32[6]{0:T(128)} %stack.45.at_ref, bf16[512,512]{1,0:T(8,128)(2,1)} %get-tuple-element.57.r0, bf16[512,512]{1,0:T(8,128)(2,1)} %copy-done.8, bf16[512,512]{1,0:T(8,128)(2,1)} %collective-permute-done.20.r2, bf16[512,512]{1,0:T(8,128)(2,1)} %collective-permute-done.21.r3), custom_call_target="tpu_custom_call" | custom-call | tf_op jit(solution)/shard_map/pallas_call | solution.py:364
  141.9 0.9 collective-permute-start.33
  142.8 3.6 %collective-permute-done.28 = bf16[64,2176]{1,0:T(8,128)(2,1)} collective-permute-done((bf16[64,2176]{1,0:T(8,128)(2,1)S(1)}, bf16[64,2176]{1,0:T(8,128)(2,1)}, u32[]{:S(2)}, u32[]{:S(2)}) %collective-permute-start.28) | collective-permute-done | bytes 278560 | tf_op jit(solution)/shard_map/ppermute | solution.py:391
  146.4 1.2 add_convert_fusion.5
  147.6 0.9 collective-permute-start.29
  148.4 2.5 %collective-permute-start.30 = (bf16[16,2176]{1,0:T(8,128)(2,1)S(1)}, bf16[16,2176]{1,0:T(8,128)(2,1)S(1)}, u32[]{:S(2)}, u32[]{:S(2)}) collective-permute-start(bf16[16,2176]{1,0:T(8,128)(2,1)S(1)} %get-tuple-element.105), channel_id=1, source_target_pairs={{0,16},{1,17},{2,18},{3,19},{4,20},{5,21},{6,22},{7,23},{8,24},{9,... | collective-permute-start | bytes 208904 | tf_op jit(solution)/shard_map/ppermute | solution.py:391
  151.0 1.1 collective-permute-start.31
  152.0 5.3 %collective-permute-done.40 = bf16[4,128,512]{2,1,0:T(8,128)(2,1)S(1)} collective-permute-done((bf16[4,128,512]{2,1,0:T(8,128)(2,1)S(1)}, bf16[4,128,512]{2,1,0:T(8,128)(2,1)S(1)}, u32[]{:S(2)}, u32[]{:S(2)}) %collective-permute-start.40) | collective-permute-done | bytes 524320 | tf_op jit(solution)/shard_map/ppermute | solution.py:391
  157.5 1.4 collective-permute-start.41
  158.9 9.9 %collective-permute-done.33 = bf16[4,136,512]{2,1,0:T(8,128)(2,1)S(1)} collective-permute-done((bf16[4,136,512]{2,1,0:T(8,128)(2,1)S(1)}, bf16[4,136,512]{2,1,0:T(8,128)(2,1)S(1)}, u32[]{:S(2)}, u32[]{:S(2)}) %collective-permute-start.33) | collective-permute-done | bytes 557088 | tf_op jit(solution)/shard_map/ppermute | solution.py:391
  168.9 1.1 collective-permute-start.34
  170.2 0.9 collective-permute-start.42
  171.0 6.1 %collective-permute-done.34 = bf16[2,136,512]{2,1,0:T(8,128)(2,1)S(1)} collective-permute-done((bf16[2,136,512]{2,1,0:T(8,128)(2,1)S(1)}, bf16[2,136,512]{2,1,0:T(8,128)(2,1)S(1)}, u32[]{:S(2)}, u32[]{:S(2)}) %collective-permute-start.34) | collective-permute-done | bytes 278560 | tf_op jit(solution)/shard_map/ppermute | solution.py:391
  177.2 0.9 collective-permute-start.35
  178.1 2.6 %collective-permute-start.43 = (bf16[128,512]{1,0:T(8,128)(2,1)S(1)}, bf16[128,512]{1,0:T(8,128)(2,1)S(1)}, u32[]{:S(2)}, u32[]{:S(2)}) collective-permute-start(bf16[128,512]{1,0:T(8,128)(2,1)S(1)} %fusion.7), channel_id=1, source_target_pairs={{0,16},{4,20},{8,24},{12,28},{16,0},{20,4},{24,8},{28,12},{1,17},{... | collective-permute-start | bytes 393224 | tf_op jit(solution)/shard_map/ppermute | solution.py:391
  180.7 2.6 %collective-permute-done.35 = bf16[136,512]{1,0:T(8,128)(2,1)S(1)} collective-permute-done((bf16[136,512]{1,0:T(8,128)(2,1)S(1)}, bf16[136,512]{1,0:T(8,128)(2,1)S(1)}, u32[]{:S(2)}, u32[]{:S(2)}) %collective-permute-start.35) | collective-permute-done | bytes 139296 | tf_op jit(solution)/shard_map/ppermute | solution.py:391
  183.4 2.3 %collective-permute-start.36 = (bf16[136,512]{1,0:T(8,128)(2,1)S(1)}, bf16[136,512]{1,0:T(8,128)(2,1)S(1)}, u32[]{:S(2)}, u32[]{:S(2)}) collective-permute-start(bf16[136,512]{1,0:T(8,128)(2,1)S(1)} %fusion.6), channel_id=1, source_target_pairs={{0,16},{4,20},{8,24},{12,28},{16,0},{20,4},{24,8},{28,12},{1,17},{... | collective-permute-start | bytes 417800 | tf_op jit(solution)/shard_map/ppermute | solution.py:391
  185.7 2.6 %collective-permute-done.43 = bf16[128,512]{1,0:T(8,128)(2,1)S(1)} collective-permute-done((bf16[128,512]{1,0:T(8,128)(2,1)S(1)}, bf16[128,512]{1,0:T(8,128)(2,1)S(1)}, u32[]{:S(2)}, u32[]{:S(2)}) %collective-permute-start.43) | collective-permute-done | bytes 131104 | tf_op jit(solution)/shard_map/ppermute | solution.py:391
  188.5 3.4 %collective-permute-done.36 = bf16[136,512]{1,0:T(8,128)(2,1)S(1)} collective-permute-done((bf16[136,512]{1,0:T(8,128)(2,1)S(1)}, bf16[136,512]{1,0:T(8,128)(2,1)S(1)}, u32[]{:S(2)}, u32[]{:S(2)}) %collective-permute-start.36) | collective-permute-done | bytes 139296 | tf_op jit(solution)/shard_map/ppermute | solution.py:391
  192.6 0.9 collective-permute-done.44
  194.0 3.0 %collective-permute-done.37 = bf16[136,512]{1,0:T(8,128)(2,1)S(1)} collective-permute-done((bf16[136,512]{1,0:T(8,128)(2,1)S(1)}, bf16[136,512]{1,0:T(8,128)(2,1)S(1)}, u32[]{:S(2)}, u32[]{:S(2)}) %collective-permute-start.37) | collective-permute-done | bytes 139296 | tf_op jit(solution)/shard_map/ppermute | solution.py:391
  197.5 0.8 slice_reduce_fusion
  198.3 0.7 fusion.14
  199.0 3.4 %collective-permute-done.45.other_ref = bf16[2,128,512]{2,1,0:T(8,128)(2,1)S(1)} collective-permute-done((bf16[2,128,512]{2,1,0:T(8,128)(2,1)S(1)}, bf16[2,128,512]{2,1,0:T(8,128)(2,1)S(1)}, u32[]{:S(2)}, u32[]{:S(2)}) %collective-permute-start.45) | collective-permute-done | bytes 262176 | tf_op jit(solution)/shard_map/ppermute | solution.py:391
  202.4 0.7 copy-done.12
  203.1 2.1 %shard_map.270 = (f32[512,512]{1,0:T(8,128)}, f32[1,512]{1,0:T(1,128)}) custom-call(s32[6]{0:T(128)} %stack.45.at_ref, bf16[2,128,512]{2,1,0:T(8,128)(2,1)} %copy-done.4, bf16[2,128,512]{2,1,0:T(8,128)(2,1)} %copy-done.12), custom_call_target="tpu_custom_call" | custom-call | bytes 2097152 | tf_op jit(solution)/shard_map/pallas_call | solution.py:411
  205.2 0.7 collective-permute-done.38.other_ref
  206.0 0.7 copy-done.10
  206.7 2.2 %shard_map.269 = (f32[512,512]{1,0:T(8,128)}, f32[1,512]{1,0:T(1,128)}) custom-call(s32[6]{0:T(128)} %stack.45.at_ref, bf16[2,136,512]{2,1,0:T(8,128)(2,1)} %copy-done.1, bf16[2,136,512]{2,1,0:T(8,128)(2,1)} %copy-done.10), custom_call_target="tpu_custom_call" | custom-call | bytes 2097152 | tf_op jit(solution)/shard_map/pallas_call | solution.py:411
  (104 shorter events, 9.7 us)
Async XLA Ops:
  0.6 30.4 %copy-start = (bf16[2048,512]{1,0:T(8,128)(2,1)S(1)}, bf16[2048,512]{1,0:T(8,128)(2,1)}, u32[]{:S(2)}) copy-start(bf16[2048,512]{1,0:T(8,128)(2,1)} %param.16) | copy-start | bytes 6291460
  3.7 5.6 %collective-permute-start = (bf16[16,2176]{1,0:T(8,128)(2,1)}, bf16[16,2176]{1,0:T(8,128)(2,1)S(1)}, u32[]{:S(2)}, u32[]{:S(2)}) collective-permute-start(bf16[16,2176]{1,0:T(8,128)(2,1)} %shard_map.262), channel_id=1, source_target_pairs={{0,8},{1,9},{2,10},{3,11},{4,12},{5,13},{6,14},{7,15},{8,0},{9,1},... | collective-permute-start | bytes 208904 | tf_op jit(solution)/shard_map/ppermute | solution.py:391
  6.7 7.8 %collective-permute-start.1 = (bf16[16,2176]{1,0:T(8,128)(2,1)}, bf16[16,2176]{1,0:T(8,128)(2,1)S(1)}, u32[]{:S(2)}, u32[]{:S(2)}) collective-permute-start(bf16[16,2176]{1,0:T(8,128)(2,1)} %shard_map.262), channel_id=1, source_target_pairs={{0,16},{1,17},{2,18},{3,19},{4,20},{5,21},{6,22},{7,23},{8,24},{9,... | collective-permute-start | bytes 208904 | tf_op jit(solution)/shard_map/ppermute | solution.py:391
  9.3 6.4 %collective-permute-start.2 = (bf16[16,2176]{1,0:T(8,128)(2,1)}, bf16[16,2176]{1,0:T(8,128)(2,1)S(1)}, u32[]{:S(2)}, u32[]{:S(2)}) collective-permute-start(bf16[16,2176]{1,0:T(8,128)(2,1)} %shard_map.262), channel_id=1, source_target_pairs={{0,24},{1,25},{2,26},{3,27},{4,28},{5,29},{6,30},{7,31},{8,16},{9,... | collective-permute-start | bytes 208904 | tf_op jit(solution)/shard_map/ppermute | solution.py:391
  16.6 18.3 %copy-start.11 = (bf16[64,2176]{1,0:T(8,128)(2,1)}, bf16[64,2176]{1,0:T(8,128)(2,1)S(1)}, u32[]{:S(2)}) copy-start(bf16[64,2176]{1,0:T(8,128)(2,1)S(1)} %pad_maximum_fusion.refs_0_) | copy-start | bytes 835588
  16.7 12.7 %collective-permute-start.3 = (bf16[64,2176]{1,0:T(8,128)(2,1)S(1)}, bf16[64,2176]{1,0:T(8,128)(2,1)}, u32[]{:S(2)}, u32[]{:S(2)}) collective-permute-start(bf16[64,2176]{1,0:T(8,128)(2,1)S(1)} %pad_maximum_fusion.refs_0_), channel_id=1, source_target_pairs={{0,2},{1,3},{2,0},{3,1},{4,6},{5,7},{6,4},{7,5},{8,10},{9,11},{10,... | collective-permute-start | bytes 835592 | tf_op jit(solution)/shard_map/ppermute | solution.py:391
  18.2 11.7 %collective-permute-start.4 = (bf16[64,2176]{1,0:T(8,128)(2,1)S(1)}, bf16[64,2176]{1,0:T(8,128)(2,1)}, u32[]{:S(2)}, u32[]{:S(2)}) collective-permute-start(bf16[64,2176]{1,0:T(8,128)(2,1)S(1)} %pad_maximum_fusion.refs_0_), channel_id=1, source_target_pairs={{0,4},{1,5},{2,6},{3,7},{4,0},{5,1},{6,2},{7,3},{8,12},{9,13},{10,... | collective-permute-start | bytes 835592 | tf_op jit(solution)/shard_map/ppermute | solution.py:391
  19.7 10.8 %collective-permute-start.5 = (bf16[64,2176]{1,0:T(8,128)(2,1)S(1)}, bf16[64,2176]{1,0:T(8,128)(2,1)}, u32[]{:S(2)}, u32[]{:S(2)}) collective-permute-start(bf16[64,2176]{1,0:T(8,128)(2,1)S(1)} %pad_maximum_fusion.refs_0_), channel_id=1, source_target_pairs={{0,6},{1,7},{2,4},{3,5},{4,2},{5,3},{6,0},{7,1},{8,14},{9,15},{10,... | collective-permute-start | bytes 835592 | tf_op jit(solution)/shard_map/ppermute | solution.py:391
  20.2 10.4 %collective-permute-start.6 = (bf16[64,2176]{1,0:T(8,128)(2,1)S(1)}, bf16[64,2176]{1,0:T(8,128)(2,1)S(1)}, u32[]{:S(2)}, u32[]{:S(2)}) collective-permute-start(bf16[64,2176]{1,0:T(8,128)(2,1)S(1)} %pad_maximum_fusion.refs_0_), channel_id=1, source_target_pairs={{0,1},{1,0},{2,3},{3,2},{4,5},{5,4},{6,7},{7,6},{8,9},{9,8},{10,11... | collective-permute-start | bytes 835592 | tf_op jit(solution)/shard_map/ppermute | solution.py:391
  20.9 4.7 %collective-permute-start.17 = (bf16[1,512]{1,0:T(2,128)(2,1)S(1)}, bf16[1,512]{1,0:T(2,128)(2,1)S(1)}, u32[]{:S(2)}, u32[]{:S(2)}) collective-permute-start(bf16[1,512]{1,0:T(2,128)(2,1)S(1)} %reshape.132), channel_id=1, source_target_pairs={{0,2},{1,3},{2,0},{3,1},{4,6},{5,7},{6,4},{7,5},{8,10},{9,11},{10,... | collective-permute-start | bytes 3080 | tf_op jit(solution)/shard_map/ppermute | solution.py:391
  25.6 1.2 collective-permute-start.16
  26.7 1.2 collective-permute-start.18
  27.9 15.1 %collective-permute-start.11 = (bf16[512,512]{1,0:T(8,128)(2,1)}, bf16[512,512]{1,0:T(8,128)(2,1)}, u32[]{:S(2)}, u32[]{:S(2)}) collective-permute-start(bf16[512,512]{1,0:T(8,128)(2,1)} %wi0.3), channel_id=1, source_target_pairs={{0,2},{1,3},{2,0},{3,1},{4,6},{5,7},{6,4},{7,5},{8,10},{9,11},{10,... | collective-permute-start | bytes 1572872 | tf_op jit(solution)/shard_map/ppermute | solution.py:391
  29.4 24.0 %collective-permute-start.14 = (bf16[512,512]{1,0:T(8,128)(2,1)}, bf16[512,512]{1,0:T(8,128)(2,1)}, u32[]{:S(2)}, u32[]{:S(2)}) collective-permute-start(bf16[512,512]{1,0:T(8,128)(2,1)} %wo0.3), channel_id=1, source_target_pairs={{0,2},{1,3},{2,0},{3,1},{4,6},{5,7},{6,4},{7,5},{8,10},{9,11},{10,... | collective-permute-start | bytes 1572872 | tf_op jit(solution)/shard_map/ppermute | solution.py:391
  29.9 23.5 %collective-permute-start.7 = (bf16[64,2176]{1,0:T(8,128)(2,1)}, bf16[64,2176]{1,0:T(8,128)(2,1)}, u32[]{:S(2)}, u32[]{:S(2)}) collective-permute-start(bf16[64,2176]{1,0:T(8,128)(2,1)} %collective-permute-done.3.refs_1_), channel_id=1, source_target_pairs={{0,1},{1,0},{2,3},{3,2},{4,5},{5,4},{6,7},{7,6},{8,9},{9,8},{10,11... | collective-permute-start | bytes 835592 | tf_op jit(solution)/shard_map/ppermute | solution.py:391
  30.6 23.4 %collective-permute-start.8 = (bf16[64,2176]{1,0:T(8,128)(2,1)}, bf16[64,2176]{1,0:T(8,128)(2,1)}, u32[]{:S(2)}, u32[]{:S(2)}) collective-permute-start(bf16[64,2176]{1,0:T(8,128)(2,1)} %collective-permute-done.4.refs_2_), channel_id=1, source_target_pairs={{0,1},{1,0},{2,3},{3,2},{4,5},{5,4},{6,7},{7,6},{8,9},{9,8},{10,11... | collective-permute-start | bytes 835592 | tf_op jit(solution)/shard_map/ppermute | solution.py:391
  30.6 0.8 copy-start.19
  30.6 23.5 %collective-permute-start.9 = (bf16[64,2176]{1,0:T(8,128)(2,1)}, bf16[64,2176]{1,0:T(8,128)(2,1)}, u32[]{:S(2)}, u32[]{:S(2)}) collective-permute-start(bf16[64,2176]{1,0:T(8,128)(2,1)} %collective-permute-done.5.refs_3_), channel_id=1, source_target_pairs={{0,1},{1,0},{2,3},{3,2},{4,5},{5,4},{6,7},{7,6},{8,9},{9,8},{10,11... | collective-permute-start | bytes 835592 | tf_op jit(solution)/shard_map/ppermute | solution.py:391
  32.2 10.8 %copy-start.13 = (bf16[512,512]{1,0:T(8,128)(2,1)S(1)}, bf16[512,512]{1,0:T(8,128)(2,1)}, u32[]{:S(2)}) copy-start(bf16[512,512]{1,0:T(8,128)(2,1)} %wi0.3) | copy-start | bytes 1572868
  32.2 21.3 %copy-start.14 = (bf16[512,512]{1,0:T(8,128)(2,1)S(1)}, bf16[512,512]{1,0:T(8,128)(2,1)}, u32[]{:S(2)}) copy-start(bf16[512,512]{1,0:T(8,128)(2,1)} %wo0.3) | copy-start | bytes 1572868
  43.0 21.9 %collective-permute-start.10 = (bf16[512,512]{1,0:T(8,128)(2,1)S(1)}, bf16[512,512]{1,0:T(8,128)(2,1)S(1)}, u32[]{:S(2)}, u32[]{:S(2)}) collective-permute-start(bf16[512,512]{1,0:T(8,128)(2,1)S(1)} %copy-done.13), channel_id=1, source_target_pairs={{0,1},{1,0},{2,3},{3,2},{4,5},{5,4},{6,7},{7,6},{8,9},{9,8},{10,11... | collective-permute-start | bytes 1572872 | tf_op jit(solution)/shard_map/ppermute | solution.py:391
  53.4 11.4 %collective-permute-start.13 = (bf16[512,512]{1,0:T(8,128)(2,1)S(1)}, bf16[512,512]{1,0:T(8,128)(2,1)S(1)}, u32[]{:S(2)}, u32[]{:S(2)}) collective-permute-start(bf16[512,512]{1,0:T(8,128)(2,1)S(1)} %copy-done.14), channel_id=1, source_target_pairs={{0,1},{1,0},{2,3},{3,2},{4,5},{5,4},{6,7},{7,6},{8,9},{9,8},{10,11... | collective-permute-start | bytes 1572872 | tf_op jit(solution)/shard_map/ppermute | solution.py:391
  53.4 11.4 %collective-permute-start.12 = (bf16[512,512]{1,0:T(8,128)(2,1)}, bf16[512,512]{1,0:T(8,128)(2,1)S(1)}, u32[]{:S(2)}, u32[]{:S(2)}) collective-permute-start(bf16[512,512]{1,0:T(8,128)(2,1)} %collective-permute-done.11.wi2), channel_id=1, source_target_pairs={{0,1},{1,0},{2,3},{3,2},{4,5},{5,4},{6,7},{7,6},{8,9},{9,8},{10,11... | collective-permute-start | bytes 1572872 | tf_op jit(solution)/shard_map/ppermute | solution.py:391
  53.9 10.9 %collective-permute-start.15 = (bf16[512,512]{1,0:T(8,128)(2,1)}, bf16[512,512]{1,0:T(8,128)(2,1)S(1)}, u32[]{:S(2)}, u32[]{:S(2)}) collective-permute-start(bf16[512,512]{1,0:T(8,128)(2,1)} %collective-permute-done.14.wo2), channel_id=1, source_target_pairs={{0,1},{1,0},{2,3},{3,2},{4,5},{5,4},{6,7},{7,6},{8,9},{9,8},{10,11... | collective-permute-start | bytes 1572872 | tf_op jit(solution)/shard_map/ppermute | solution.py:391
  64.8 0.8 copy-start.15
  64.9 1.0 copy-start.16
  64.9 1.1 copy-start.17
  64.9 1.3 copy-start.18
  90.6 16.3 %copy-start.5 = (bf16[512,512]{1,0:T(8,128)(2,1)S(1)}, bf16[512,512]{1,0:T(8,128)(2,1)}, u32[]{:S(2)}) copy-start(bf16[512,512]{1,0:T(8,128)(2,1)} %get-tuple-element.57.r0) | copy-start | bytes 1572868
  103.8 3.1 %collective-permute-start.25 = (bf16[256,2176]{1,0:T(8,128)(2,1)}, bf16[256,2176]{1,0:T(8,128)(2,1)S(1)}, u32[]{:S(2)}, u32[]{:S(2)}) collective-permute-start(bf16[256,2176]{1,0:T(8,128)(2,1)} %get-tuple-element.77), channel_id=1, source_target_pairs={{0,1},{1,0},{2,3},{3,2},{4,5},{5,4},{6,7},{7,6},{8,9},{9,8},{10,11... | collective-permute-start | bytes 3342344 | tf_op jit(solution)/shard_map/ppermute | solution.py:391
  104.3 15.0 %collective-permute-start.23 = (bf16[512,512]{1,0:T(8,128)(2,1)}, bf16[512,512]{1,0:T(8,128)(2,1)S(1)}, u32[]{:S(2)}, u32[]{:S(2)}) collective-permute-start(bf16[512,512]{1,0:T(8,128)(2,1)} %get-tuple-element.75.r0), channel_id=1, source_target_pairs={{0,2},{1,3},{2,0},{3,1},{4,6},{5,7},{6,4},{7,5},{8,10},{9,11},{10,... | collective-permute-start | bytes 1572872 | tf_op jit(solution)/shard_map/ppermute | solution.py:391
  105.8 13.5 %collective-permute-start.22 = (bf16[512,512]{1,0:T(8,128)(2,1)}, bf16[512,512]{1,0:T(8,128)(2,1)S(1)}, u32[]{:S(2)}, u32[]{:S(2)}) collective-permute-start(bf16[512,512]{1,0:T(8,128)(2,1)} %get-tuple-element.75.r0), channel_id=1, source_target_pairs={{0,1},{1,0},{2,3},{3,2},{4,5},{5,4},{6,7},{7,6},{8,9},{9,8},{10,11... | collective-permute-start | bytes 1572872 | tf_op jit(solution)/shard_map/ppermute | solution.py:391
  105.8 25.6 %collective-permute-start.39 = (bf16[2,4,128,512]{3,2,1,0:T(8,128)(2,1)}, bf16[2,4,128,512]{3,2,1,0:T(8,128)(2,1)S(1)}, u32[]{:S(2)}, u32[]{:S(2)}) collective-permute-start(bf16[2,4,128,512]{3,2,1,0:T(8,128)(2,1)} %get-tuple-element.83), channel_id=1, source_target_pairs={{0,1},{1,0},{2,3},{3,2},{4,5},{5,4},{6,7},{7,6},{8,9},{9,8},{10,11... | collective-permute-start | bytes 3145736 | tf_op jit(solution)/shard_map/ppermute | solution.py:391
  106.3 35.2 %collective-permute-start.32 = (bf16[2,4,136,512]{3,2,1,0:T(8,128)(2,1)}, bf16[2,4,136,512]{3,2,1,0:T(8,128)(2,1)S(1)}, u32[]{:S(2)}, u32[]{:S(2)}) collective-permute-start(bf16[2,4,136,512]{3,2,1,0:T(8,128)(2,1)} %get-tuple-element.79), channel_id=1, source_target_pairs={{0,1},{1,0},{2,3},{3,2},{4,5},{5,4},{6,7},{7,6},{8,9},{9,8},{10,11... | collective-permute-start | bytes 3342344 | tf_op jit(solution)/shard_map/ppermute | solution.py:391
  106.9 22.9 %collective-permute-start.20 = (bf16[512,512]{1,0:T(8,128)(2,1)S(1)}, bf16[512,512]{1,0:T(8,128)(2,1)}, u32[]{:S(2)}, u32[]{:S(2)}) collective-permute-start(bf16[512,512]{1,0:T(8,128)(2,1)S(1)} %copy-done.5), channel_id=1, source_target_pairs={{0,2},{1,3},{2,0},{3,1},{4,6},{5,7},{6,4},{7,5},{8,10},{9,11},{10,... | collective-permute-start | bytes 1572872 | tf_op jit(solution)/shard_map/ppermute | solution.py:391
  109.9 23.8 %copy-start.3 = (bf16[2,4,128,512]{3,2,1,0:T(8,128)(2,1)S(1)}, bf16[2,4,128,512]{3,2,1,0:T(8,128)(2,1)}, u32[]{:S(2)}) copy-start(bf16[2,4,128,512]{3,2,1,0:T(8,128)(2,1)} %get-tuple-element.82) | copy-start | bytes 3145732
  119.3 14.8 %copy-start.6 = (bf16[512,512]{1,0:T(8,128)(2,1)}, bf16[512,512]{1,0:T(8,128)(2,1)S(1)}, u32[]{:S(2)}) copy-start(bf16[512,512]{1,0:T(8,128)(2,1)S(1)} %collective-permute-done.23.r2) | copy-start | bytes 1572868
  119.3 10.5 %collective-permute-start.19 = (bf16[512,512]{1,0:T(8,128)(2,1)S(1)}, bf16[512,512]{1,0:T(8,128)(2,1)S(1)}, u32[]{:S(2)}, u32[]{:S(2)}) collective-permute-start(bf16[512,512]{1,0:T(8,128)(2,1)S(1)} %copy-done.5), channel_id=1, source_target_pairs={{0,1},{1,0},{2,3},{3,2},{4,5},{5,4},{6,7},{7,6},{8,9},{9,8},{10,11... | collective-permute-start | bytes 1572872 | tf_op jit(solution)/shard_map/ppermute | solution.py:391
  119.3 14.1 %copy-start.7 = (bf16[512,512]{1,0:T(8,128)(2,1)}, bf16[512,512]{1,0:T(8,128)(2,1)S(1)}, u32[]{:S(2)}) copy-start(bf16[512,512]{1,0:T(8,128)(2,1)S(1)} %collective-permute-done.22.r1) | copy-start | bytes 1572868
  119.3 13.6 %collective-permute-start.24 = (bf16[512,512]{1,0:T(8,128)(2,1)S(1)}, bf16[512,512]{1,0:T(8,128)(2,1)S(1)}, u32[]{:S(2)}, u32[]{:S(2)}) collective-permute-start(bf16[512,512]{1,0:T(8,128)(2,1)S(1)} %collective-permute-done.23.r2), channel_id=1, source_target_pairs={{0,1},{1,0},{2,3},{3,2},{4,5},{5,4},{6,7},{7,6},{8,9},{9,8},{10,11... | collective-permute-start | bytes 1572872 | tf_op jit(solution)/shard_map/ppermute | solution.py:391
  129.8 7.4 %collective-permute-start.21 = (bf16[512,512]{1,0:T(8,128)(2,1)}, bf16[512,512]{1,0:T(8,128)(2,1)}, u32[]{:S(2)}, u32[]{:S(2)}) collective-permute-start(bf16[512,512]{1,0:T(8,128)(2,1)} %collective-permute-done.20.r2), channel_id=1, source_target_pairs={{0,1},{1,0},{2,3},{3,2},{4,5},{5,4},{6,7},{7,6},{8,9},{9,8},{10,11... | collective-permute-start | bytes 1572872 | tf_op jit(solution)/shard_map/ppermute | solution.py:391
  129.8 4.2 %copy-start.8 = (bf16[512,512]{1,0:T(8,128)(2,1)}, bf16[512,512]{1,0:T(8,128)(2,1)S(1)}, u32[]{:S(2)}) copy-start(bf16[512,512]{1,0:T(8,128)(2,1)S(1)} %collective-permute-done.19.r1) | copy-start | bytes 1572868
  129.8 12.9 %collective-permute-start.26 = (bf16[64,2176]{1,0:T(8,128)(2,1)S(1)}, bf16[64,2176]{1,0:T(8,128)(2,1)S(1)}, u32[]{:S(2)}, u32[]{:S(2)}) collective-permute-start(bf16[64,2176]{1,0:T(8,128)(2,1)S(1)} %get-tuple-element.98), channel_id=1, source_target_pairs={{0,2},{1,3},{2,0},{3,1},{4,6},{5,7},{6,4},{7,5},{8,10},{9,11},{10,... | collective-permute-start | bytes 835592 | tf_op jit(solution)/shard_map/ppermute | solution.py:391
  131.4 11.4 %collective-permute-start.27 = (bf16[64,2176]{1,0:T(8,128)(2,1)S(1)}, bf16[64,2176]{1,0:T(8,128)(2,1)}, u32[]{:S(2)}, u32[]{:S(2)}) collective-permute-start(bf16[64,2176]{1,0:T(8,128)(2,1)S(1)} %get-tuple-element.100), channel_id=1, source_target_pairs={{0,4},{1,5},{2,6},{3,7},{4,0},{5,1},{6,2},{7,3},{8,12},{9,13},{10,... | collective-permute-start | bytes 835592 | tf_op jit(solution)/shard_map/ppermute | solution.py:391
  132.9 0.8 copy-start.9
  132.9 13.4 %collective-permute-start.28 = (bf16[64,2176]{1,0:T(8,128)(2,1)S(1)}, bf16[64,2176]{1,0:T(8,128)(2,1)}, u32[]{:S(2)}, u32[]{:S(2)}) collective-permute-start(bf16[64,2176]{1,0:T(8,128)(2,1)S(1)} %get-tuple-element.99), channel_id=1, source_target_pairs={{0,6},{1,7},{2,4},{3,5},{4,2},{5,3},{6,0},{7,1},{8,14},{9,15},{10,... | collective-permute-start | bytes 835592 | tf_op jit(solution)/shard_map/ppermute | solution.py:391
  137.2 4.4 %copy-start.2 = (bf16[2,4,136,512]{3,2,1,0:T(8,128)(2,1)S(1)}, bf16[2,4,136,512]{3,2,1,0:T(8,128)(2,1)}, u32[]{:S(2)}) copy-start(bf16[2,4,136,512]{3,2,1,0:T(8,128)(2,1)} %get-tuple-element.78) | copy-start | bytes 3342340
  137.2 20.1 %collective-permute-start.40 = (bf16[4,128,512]{2,1,0:T(8,128)(2,1)S(1)}, bf16[4,128,512]{2,1,0:T(8,128)(2,1)S(1)}, u32[]{:S(2)}, u32[]{:S(2)}) collective-permute-start(bf16[4,128,512]{2,1,0:T(8,128)(2,1)S(1)} %get-tuple-element.93), channel_id=1, source_target_pairs={{0,2},{1,3},{2,0},{3,1},{4,6},{5,7},{6,4},{7,5},{8,10},{9,11},{10,... | collective-permute-start | bytes 1572872 | tf_op jit(solution)/shard_map/ppermute | solution.py:391
  141.9 26.9 %collective-permute-start.33 = (bf16[4,136,512]{2,1,0:T(8,128)(2,1)S(1)}, bf16[4,136,512]{2,1,0:T(8,128)(2,1)S(1)}, u32[]{:S(2)}, u32[]{:S(2)}) collective-permute-start(bf16[4,136,512]{2,1,0:T(8,128)(2,1)S(1)} %get-tuple-element.91), channel_id=1, source_target_pairs={{0,2},{1,3},{2,0},{3,1},{4,6},{5,7},{6,4},{7,5},{8,10},{9,11},{10,... | collective-permute-start | bytes 1671176 | tf_op jit(solution)/shard_map/ppermute | solution.py:391
  147.6 22.5 %collective-permute-start.29 = (bf16[16,2176]{1,0:T(8,128)(2,1)S(1)}, bf16[16,2176]{1,0:T(8,128)(2,1)S(1)}, u32[]{:S(2)}, u32[]{:S(2)}) collective-permute-start(bf16[16,2176]{1,0:T(8,128)(2,1)S(1)} %get-tuple-element.103), channel_id=1, source_target_pairs={{0,8},{1,9},{2,10},{3,11},{4,12},{5,13},{6,14},{7,15},{8,0},{9,1},... | collective-permute-start | bytes 208904 | tf_op jit(solution)/shard_map/ppermute | solution.py:391
  148.4 21.6 %collective-permute-start.30 = (bf16[16,2176]{1,0:T(8,128)(2,1)S(1)}, bf16[16,2176]{1,0:T(8,128)(2,1)S(1)}, u32[]{:S(2)}, u32[]{:S(2)}) collective-permute-start(bf16[16,2176]{1,0:T(8,128)(2,1)S(1)} %get-tuple-element.105), channel_id=1, source_target_pairs={{0,16},{1,17},{2,18},{3,19},{4,20},{5,21},{6,22},{7,23},{8,24},{9,... | collective-permute-start | bytes 208904 | tf_op jit(solution)/shard_map/ppermute | solution.py:391
  151.0 19.1 %collective-permute-start.31 = (bf16[16,2176]{1,0:T(8,128)(2,1)S(1)}, bf16[16,2176]{1,0:T(8,128)(2,1)S(1)}, u32[]{:S(2)}, u32[]{:S(2)}) collective-permute-start(bf16[16,2176]{1,0:T(8,128)(2,1)S(1)} %get-tuple-element.104), channel_id=1, source_target_pairs={{0,24},{1,25},{2,26},{3,27},{4,28},{5,29},{6,30},{7,31},{8,16},{9,... | collective-permute-start | bytes 208904 | tf_op jit(solution)/shard_map/ppermute | solution.py:391
  157.5 12.6 %collective-permute-start.41 = (bf16[2,128,512]{2,1,0:T(8,128)(2,1)S(1)}, bf16[2,128,512]{2,1,0:T(8,128)(2,1)S(1)}, u32[]{:S(2)}, u32[]{:S(2)}) collective-permute-start(bf16[2,128,512]{2,1,0:T(8,128)(2,1)S(1)} %get-tuple-element.102), channel_id=1, source_target_pairs={{0,4},{4,0},{8,12},{12,8},{16,20},{20,16},{24,28},{28,24},{1,5},{5... | collective-permute-start | bytes 786440 | tf_op jit(solution)/shard_map/ppermute | solution.py:391
  168.9 8.2 %collective-permute-start.34 = (bf16[2,136,512]{2,1,0:T(8,128)(2,1)S(1)}, bf16[2,136,512]{2,1,0:T(8,128)(2,1)S(1)}, u32[]{:S(2)}, u32[]{:S(2)}) collective-permute-start(bf16[2,136,512]{2,1,0:T(8,128)(2,1)S(1)} %get-tuple-element.97), channel_id=1, source_target_pairs={{0,4},{4,0},{8,12},{12,8},{16,20},{20,16},{24,28},{28,24},{1,5},{5... | collective-permute-start | bytes 835592 | tf_op jit(solution)/shard_map/ppermute | solution.py:391
  170.2 7.9 %collective-permute-start.42 = (bf16[128,512]{1,0:T(8,128)(2,1)S(1)}, bf16[128,512]{1,0:T(8,128)(2,1)S(1)}, u32[]{:S(2)}, u32[]{:S(2)}) collective-permute-start(bf16[128,512]{1,0:T(8,128)(2,1)S(1)} %fusion.11), channel_id=1, source_target_pairs={{0,8},{4,12},{8,0},{12,4},{16,24},{20,28},{24,16},{28,20},{1,9},{5... | collective-permute-start | bytes 393224 | tf_op jit(solution)/shard_map/ppermute | solution.py:391
  177.2 6.1 %collective-permute-start.35 = (bf16[136,512]{1,0:T(8,128)(2,1)S(1)}, bf16[136,512]{1,0:T(8,128)(2,1)S(1)}, u32[]{:S(2)}, u32[]{:S(2)}) collective-permute-start(bf16[136,512]{1,0:T(8,128)(2,1)S(1)} %fusion.9), channel_id=1, source_target_pairs={{0,8},{4,12},{8,0},{12,4},{16,24},{20,28},{24,16},{28,20},{1,9},{5... | collective-permute-start | bytes 417800 | tf_op jit(solution)/shard_map/ppermute | solution.py:391
  178.1 10.2 %collective-permute-start.43 = (bf16[128,512]{1,0:T(8,128)(2,1)S(1)}, bf16[128,512]{1,0:T(8,128)(2,1)S(1)}, u32[]{:S(2)}, u32[]{:S(2)}) collective-permute-start(bf16[128,512]{1,0:T(8,128)(2,1)S(1)} %fusion.7), channel_id=1, source_target_pairs={{0,16},{4,20},{8,24},{12,28},{16,0},{20,4},{24,8},{28,12},{1,17},{... | collective-permute-start | bytes 393224 | tf_op jit(solution)/shard_map/ppermute | solution.py:391
  183.4 8.5 %collective-permute-start.36 = (bf16[136,512]{1,0:T(8,128)(2,1)S(1)}, bf16[136,512]{1,0:T(8,128)(2,1)S(1)}, u32[]{:S(2)}, u32[]{:S(2)}) collective-permute-start(bf16[136,512]{1,0:T(8,128)(2,1)S(1)} %fusion.6), channel_id=1, source_target_pairs={{0,16},{4,20},{8,24},{12,28},{16,0},{20,4},{24,8},{28,12},{1,17},{... | collective-permute-start | bytes 417800 | tf_op jit(solution)/shard_map/ppermute | solution.py:391
  188.4 5.0 %collective-permute-start.44 = (bf16[128,512]{1,0:T(8,128)(2,1)S(1)}, bf16[128,512]{1,0:T(8,128)(2,1)S(1)}, u32[]{:S(2)}, u32[]{:S(2)}) collective-permute-start(bf16[128,512]{1,0:T(8,128)(2,1)S(1)} %add_convert_fusion.9), channel_id=1, source_target_pairs={{0,8},{4,12},{8,0},{12,4},{16,24},{20,28},{24,16},{28,20},{1,9},{5... | collective-permute-start | bytes 393224 | tf_op jit(solution)/shard_map/ppermute | solution.py:391
  191.9 5.1 %collective-permute-start.37 = (bf16[136,512]{1,0:T(8,128)(2,1)S(1)}, bf16[136,512]{1,0:T(8,128)(2,1)S(1)}, u32[]{:S(2)}, u32[]{:S(2)}) collective-permute-start(bf16[136,512]{1,0:T(8,128)(2,1)S(1)} %add_convert_fusion.6), channel_id=1, source_target_pairs={{0,8},{4,12},{8,0},{12,4},{16,24},{20,28},{24,16},{28,20},{1,9},{5... | collective-permute-start | bytes 417800 | tf_op jit(solution)/shard_map/ppermute | solution.py:391
  193.5 8.9 %copy-start.4 = (bf16[2,128,512]{2,1,0:T(8,128)(2,1)}, bf16[2,128,512]{2,1,0:T(8,128)(2,1)S(1)}, u32[]{:S(2)}) copy-start(bf16[2,128,512]{2,1,0:T(8,128)(2,1)S(1)} %pad_maximum_fusion.2.own_ref) | copy-start | bytes 786436
  193.5 8.9 %collective-permute-start.45 = (bf16[2,128,512]{2,1,0:T(8,128)(2,1)S(1)}, bf16[2,128,512]{2,1,0:T(8,128)(2,1)S(1)}, u32[]{:S(2)}, u32[]{:S(2)}) collective-permute-start(bf16[2,128,512]{2,1,0:T(8,128)(2,1)S(1)} %pad_maximum_fusion.2.own_ref), channel_id=1, source_target_pairs={{0,4},{4,0},{8,12},{12,8},{16,20},{20,16},{24,28},{28,24},{1,5},{5... | collective-permute-start | bytes 786440 | tf_op jit(solution)/shard_map/ppermute | solution.py:391
  197.0 8.9 %copy-start.1 = (bf16[2,136,512]{2,1,0:T(8,128)(2,1)}, bf16[2,136,512]{2,1,0:T(8,128)(2,1)S(1)}, u32[]{:S(2)}) copy-start(bf16[2,136,512]{2,1,0:T(8,128)(2,1)S(1)} %pad_maximum_fusion.1.own_ref) | copy-start | bytes 835588
  197.0 8.9 %collective-permute-start.38 = (bf16[2,136,512]{2,1,0:T(8,128)(2,1)S(1)}, bf16[2,136,512]{2,1,0:T(8,128)(2,1)S(1)}, u32[]{:S(2)}, u32[]{:S(2)}) collective-permute-start(bf16[2,136,512]{2,1,0:T(8,128)(2,1)S(1)} %pad_maximum_fusion.1.own_ref), channel_id=1, source_target_pairs={{0,4},{4,0},{8,12},{12,8},{16,20},{20,16},{24,28},{28,24},{1,5},{5... | collective-permute-start | bytes 835592 | tf_op jit(solution)/shard_map/ppermute | solution.py:391
  (2 other events, 1.4 us)

commit v2 on v1

v2 whole, which is shorter than its diff:
```python
import functools

import jax
import jax.numpy as jnp
from jax import lax
from jax.experimental import pallas as pl
from jax.experimental.pallas import tpu as pltpu
from jax.sharding import PartitionSpec as P

D = 512
HEADS = 8
HEAD = 64
MEM = 20
PAD = 32
SPAN = 512
SPANS = 2
EXTRA = 128
WIDE = 4 * D + EXTRA
EPS = 1e-05
GELU_A = 0.7978845608028654
GELU_B = 0.044715
LOW = jnp.bfloat16
F32 = jnp.float32
SCALE = HEAD ** (-0.5)
ALL = ("dp", "mp")

VMEM = pl.BlockSpec(memory_space=pltpu.VMEM)
SMEM = pl.BlockSpec(memory_space=pltpu.SMEM)
ANY = pl.BlockSpec(memory_space=pl.ANY)


def dg(a, b, ca, cb):
    return lax.dot_general(a, b, (((ca,), (cb,)), ((), ())), preferred_element_type=F32)


def iota(shape, dim):
    return lax.broadcasted_iota(jnp.int32, shape, dim)


def head_mask(heads):
    shape = (heads * PAD, heads * HEAD)
    return (iota(shape, 0) >> 5) == (iota(shape, 1) >> 6)


def block_diagonal(rows):
    heads = rows.shape[1] // HEAD
    tall = jnp.concatenate([rows] * heads, axis=0)
    return jnp.where(head_mask(heads), tall, 0.0).astype(LOW)


def diagonal_sum(tall):
    heads = tall.shape[1] // HEAD
    kept = jnp.where(head_mask(heads), tall, 0.0)
    total = kept[:PAD]
    for h in range(1, heads):
        total = total + kept[h * PAD : (h + 1) * PAD]
    return total


def normalize(values):
    mean = jnp.mean(values, axis=1, keepdims=True)
    center = values - mean
    spread = jnp.mean(center * center, axis=1, keepdims=True)
    inv = lax.rsqrt(spread + EPS)
    return center * inv, inv


def gelu_parts(a):
    sq = a * a
    t = jnp.tanh(a * (GELU_A + (GELU_A * GELU_B) * sq))
    half = 0.5 * (1.0 + t)
    return half, t, sq


def gelu(a):
    half, _, _ = gelu_parts(a)
    return a * half


def call(kernel, out_shape, in_specs, out_specs, scratch=(), flops=1, bytes_=1, mib=32):
    return pl.pallas_call(
        kernel,
        out_shape=out_shape,
        in_specs=in_specs,
        out_specs=out_specs,
        scratch_shapes=list(scratch),
        compiler_params=pltpu.CompilerParams(vmem_limit_bytes=mib * 2**20),
        cost_estimate=pl.CostEstimate(flops=flops, bytes_accessed=bytes_, transcendentals=0),
    )


def sds(shape, dtype):
    return jax.ShapeDtypeStruct(shape, dtype)


def pack_kernel(q_ref, k_ref, v_ref, o_ref, mem_ref, g1_ref, b1_ref, ob_ref, g2_ref, b2_ref, out_ref, tall):
    rows = q_ref.shape[0]
    for i, ref in enumerate((q_ref, k_ref, v_ref, o_ref)):
        out_ref[:, i * D : (i + 1) * D] = ref[...]
    tall[...] = jnp.zeros(tall.shape, F32)
    for i, ref in enumerate((g1_ref, b1_ref, ob_ref, g2_ref, b2_ref)):
        tall[MEM + i : MEM + i + 1, :rows] = ref[...].astype(F32)
    out_ref[:, 4 * D :] = tall[...].T[:rows].astype(LOW)
    out_ref[:, 4 * D : 4 * D + MEM] = mem_ref[...]


def assemble(me, pieces, bits, out_ref):
    for piece, offsets in zip(pieces, bits, strict=True):
        if offsets is None:
            out_ref[...] = piece[...]
            continue
        size = piece.shape[0] // len(offsets)
        for j, offset in enumerate(offsets):
            start = pl.multiple_of((me ^ offset) * size, size)
            out_ref[pl.ds(start, size), :] = piece[j * size : (j + 1) * size, :]


def project_kernel(bits, at_ref, *refs):
    n = len(bits)
    x_ref, w_ref, qkv_ref = refs[n:]
    assemble(at_ref[0], refs[:n], bits, w_ref)
    x_t = x_ref[...].T
    qkv_ref[:D] = (dg(w_ref[:, :D], x_t, 0, 0).astype(LOW).astype(F32) * SCALE).astype(LOW)
    qkv_ref[D : 3 * D] = dg(w_ref[:, D : 3 * D], x_t, 0, 0).astype(LOW)


def attend_kernel(qkv_ref, p_ref, o_ref, m_ref, l_ref):
    def scores(h):
        at = h * HEAD
        return dg(qkv_ref[D + at : D + at + HEAD], qkv_ref[at : at + HEAD], 0, 0)

    s_next = scores(0)
    for h in range(HEADS):
        s = s_next
        if h + 1 < HEADS:
            s_next = scores(h + 1)
        at = h * HEAD
        m = jnp.max(s, axis=0, keepdims=True)
        p = jnp.exp(s - m)
        m_ref[h : h + 1] = m
        l_ref[h : h + 1] = jnp.sum(p, axis=0, keepdims=True)
        p_ref[h] = p.astype(LOW)
        o_ref[at : at + HEAD] = dg(qkv_ref[2 * D + at : 2 * D + at + HEAD], p_ref[h], 1, 0)


def memory_kernel(x1_ref, w_ref, nm_ref, small_ref):
    small = w_ref[:, 4 * D :].T.astype(F32)[:PAD]
    small_ref[...] = small
    mem = jnp.where(iota((PAD, D), 0) < MEM, small, 0.0)
    packed = dg(mem.astype(LOW), w_ref[:, : 3 * D], 1, 0).astype(LOW)
    q_tall = block_diagonal(packed[:, :D].astype(F32) * SCALE)
    s_mem = dg(q_tall, packed[:, D : 2 * D], 1, 1)
    s_mem = jnp.where(iota(s_mem.shape, 1) < MEM, s_mem, -1e30)
    kv = dg(x1_ref[...], w_ref[:, D : 3 * D], 1, 0).astype(LOW)
    s = dg(q_tall, kv[:, :D], 1, 1)
    m = jnp.maximum(jnp.max(s, axis=1, keepdims=True), jnp.max(s_mem, axis=1, keepdims=True))
    p = jnp.exp(s - m)
    p_mem = jnp.exp(s_mem - m)
    total = jnp.sum(p, axis=1, keepdims=True) + jnp.sum(p_mem, axis=1, keepdims=True)
    o = dg(p.astype(LOW), kv[:, D:], 1, 0) + dg(p_mem.astype(LOW), packed[:, 2 * D :], 1, 0)
    mixed = diagonal_sum(o / total).astype(LOW)
    xhat, _ = normalize(mem + dg(mixed, w_ref[:, 3 * D : 4 * D], 1, 0))
    nm_ref[...] = xhat * small[MEM : MEM + 1] + small[MEM + 1 : MEM + 2]


def forward_kernel(
    at_ref, nm_ref, small_ref, x_ref, w_ref, qkv_ref, o_ref, m_ref, l_ref,
    wi0, wi1, wi2, wi3, wo0, wo1, wo2, wo3, cot_ref,
    out_ref, keep_ref, send_ref, slope_ref, nl_ref, gl_ref, gs_ref, xhat_ref, inv_ref,
    mixed_ref, mem_ref, kv_ref, pm_ref, c_ref, cm_ref, vec_ref, hid,
):
    wis, wos = (wi0, wi1, wi2, wi3), (wo0, wo1, wo2, wo3)
    shifts = [ref[D : D + 1].astype(F32) for ref in wos]
    small = small_ref[...]
    gain1, bias1, outer_b, gain2, bias2 = (small[MEM + i : MEM + i + 1] for i in range(5))
    later, first = at_ref[2], at_ref[5]
    nm = nm_ref[...]
    nm_low = nm.astype(LOW)
    value = nm + outer_b
    for k in range(4):
        inner = dg(nm_low, wis[k][...], 1, 0) + shifts[k]
        value = value + dg(gelu(inner).astype(LOW), wos[k][:D], 1, 0)
    carried, _ = normalize(value)
    carried = carried * gain2 + bias2
    mem = jnp.where(later == 1, carried, small)
    mem = jnp.where(iota((PAD, D), 0) < MEM, mem, 0.0)
    mem_ref[...] = mem
    kv_mem = dg(mem.astype(LOW), w_ref[:, D : 3 * D], 1, 0).astype(LOW)
    kv_ref[...] = kv_mem
    k_tall = block_diagonal(kv_mem[:, :D].astype(F32))
    v_tall = block_diagonal(kv_mem[:, D:].astype(F32))
    s_all = dg(k_tall, qkv_ref[:D], 1, 0)
    s_all = jnp.where((iota(s_all.shape, 0) & (PAD - 1)) < MEM, s_all, -1e30)
    alphas, invs = [], []
    for h in range(HEADS):
        s = s_all[h * PAD : (h + 1) * PAD]
        m_old = m_ref[h : h + 1]
        m = jnp.maximum(m_old, jnp.max(s, axis=0, keepdims=True))
        alpha = jnp.exp(m_old - m)
        p = jnp.exp(s - m)
        inv = 1.0 / (l_ref[h : h + 1] * alpha + jnp.sum(p, axis=0, keepdims=True))
        pm_ref[h * PAD : (h + 1) * PAD] = p.astype(LOW)
        c_ref[h : h + 1] = alpha * inv
        cm_ref[h : h + 1] = inv
        alphas.append(alpha * inv)
        invs.append(inv)
    o_mem = dg(v_tall, pm_ref[...], 0, 0)
    for h in range(HEADS):
        at = h * HEAD
        mixed_ref[at : at + HEAD] = (
            o_ref[at : at + HEAD] * alphas[h] + o_mem[at : at + HEAD] * invs[h]
        ).astype(LOW)
    xhat1, inv1 = normalize(
        x_ref[...].astype(F32) + dg(mixed_ref[...], w_ref[:, 3 * D : 4 * D], 0, 0)
    )
    xhat_ref[...] = xhat1
    inv_ref[...] = inv1
    normed = xhat1 * gain1 + bias1
    normed_low = normed.astype(LOW)
    nl_ref[...] = normed_low
    total = normed + outer_b
    for k in range(4):
        a = dg(normed_low, wis[k][...], 1, 0) + shifts[k]
        half, t, sq = gelu_parts(a)
        hid[k] = (a * half).astype(LOW)
        slope = half + (0.5 * a) * (1.0 - t * t) * (GELU_A + (3.0 * GELU_A * GELU_B) * sq)
        slope_ref[k] = slope.astype(LOW)
        total = total + dg(hid[k], wos[k][:D], 1, 0)
    xhat2, inv2 = normalize(total)
    out_ref[...] = (xhat2 * gain2 + bias2).astype(LOW)
    cot = cot_ref[...].astype(F32)
    pull = cot * gain2
    grad_sum = inv2 * (
        pull
        - jnp.mean(pull, axis=1, keepdims=True)
        - xhat2 * jnp.mean(pull * xhat2, axis=1, keepdims=True)
    )
    vec_ref[2:3] = jnp.sum(grad_sum, axis=0, keepdims=True)
    vec_ref[3:4] = jnp.sum(cot * xhat2, axis=0, keepdims=True)
    vec_ref[4:5] = jnp.sum(cot, axis=0, keepdims=True)
    gs_ref[...] = grad_sum
    grad_low = grad_sum.astype(LOW)
    gl_ref[...] = grad_low
    for k in (1, 3, 0, 2):
        give(send_ref if k % 2 else keep_ref, k // 2, dg(hid[k], grad_low, 0, 0), first)


def give(ref, k, rows, first):
    size = rows.shape[0] // 4
    for i in range(4):
        ref[k, first ^ i] = rows[i * size : (i + 1) * size].astype(LOW)


def inner_terms(k, wi_ref, wo_ref, slope_ref, normed_low, grad_low, ref, first):
    gi = slope_ref[k].astype(F32) * dg(grad_low, wo_ref[:D], 1, 1)
    gi_low = gi.astype(LOW)
    bias = jnp.sum(gi_low.astype(F32), axis=0, keepdims=True)
    bias = jnp.where(iota((PAD, D), 0) == 0, bias, 0.0)
    rows = jnp.concatenate([dg(normed_low, gi_low, 0, 0), bias], axis=0)
    give(ref, k // 2, rows, first)
    return dg(gi_low, wi_ref[...], 1, 1)


def send_kernel(at_ref, wi1, wi3, wo1, wo3, slope_ref, nl_ref, gl_ref, gs_ref, send_ref, back_ref):
    first = at_ref[5]
    back = gs_ref[...]
    for k, wi_ref, wo_ref in ((1, wi1, wo1), (3, wi3, wo3)):
        back = back + inner_terms(k, wi_ref, wo_ref, slope_ref, nl_ref[...], gl_ref[...], send_ref, first)
    back_ref[...] = back


def keep_kernel(
    at_ref, after_ref, small_ref, w_ref, wi0, wi2, wo0, wo2, slope_ref, nl_ref, gl_ref, back_ref, xhat_ref, inv_ref, mixed_ref,
    keep_ref, resid_ref, dwo_ref, gmix_ref, vec_ref,
):
    first = at_ref[5]
    back = back_ref[...]
    for k, wi_ref, wo_ref in ((0, wi0, wo0), (2, wi2, wo2)):
        back = back + inner_terms(k, wi_ref, wo_ref, slope_ref, nl_ref[...], gl_ref[...], keep_ref, first)
    xhat1 = xhat_ref[...]
    vec_ref[0:1] = jnp.sum(back * xhat1, axis=0, keepdims=True)
    vec_ref[1:2] = jnp.sum(back, axis=0, keepdims=True)
    pull = back * small_ref[MEM : MEM + 1]
    resid = inv_ref[...] * (
        pull
        - jnp.mean(pull, axis=1, keepdims=True)
        - xhat1 * jnp.mean(pull * xhat1, axis=1, keepdims=True)
    )
    resid_ref[...] = resid
    resid_low = resid.astype(LOW)
    dwo_ref[...] = dg(mixed_ref[...], resid_low, 1, 0).astype(LOW)
    gmix_ref[...] = dg(w_ref[:, 3 * D : 4 * D], resid_low, 1, 1).astype(LOW)


def heads_kernel(
    low_h, high_h, after_ref, qkv_ref, p_ref, pm_ref, mixed_ref, c_ref, cm_ref, gmix_ref, kv_ref, gp_ref, gm_ref,
    do_m, ds_m,
):
    heads = range(low_h, high_h)
    f0, f1 = low_h * HEAD, high_h * HEAD
    m0, m1 = low_h * PAD, high_h * PAD
    k_tall = block_diagonal(kv_ref[:, f0:f1].astype(F32))
    v_tall = block_diagonal(kv_ref[:, D + f0 : D + f1].astype(F32))
    deltas = []
    for i, h in enumerate(heads):
        at = h * HEAD
        do = gmix_ref[at : at + HEAD].astype(F32)
        deltas.append(
            jnp.sum(do * mixed_ref[at : at + HEAD].astype(F32), axis=0, keepdims=True)
        )
        do_m[i * HEAD : (i + 1) * HEAD] = (do * cm_ref[h : h + 1]).astype(LOW)
    da_m = dg(v_tall, do_m[...], 1, 0)
    for i, h in enumerate(heads):
        rows = slice(i * PAD, (i + 1) * PAD)
        p = pm_ref[h * PAD : (h + 1) * PAD].astype(F32)
        ds_m[rows] = (p * (da_m[rows] - deltas[i] * cm_ref[h : h + 1])).astype(LOW)
    gm_ref[0] = diagonal_sum(dg(ds_m[...], qkv_ref[f0:f1], 1, 1))
    gm_ref[1] = diagonal_sum(dg(pm_ref[m0:m1], do_m[...], 1, 1))
    dq_mem = dg(k_tall, ds_m[...], 0, 0)
    for i, h in enumerate(heads):
        at = h * HEAD
        rows = slice(i * HEAD, (i + 1) * HEAD)
        c = c_ref[h : h + 1]
        do = (gmix_ref[at : at + HEAD].astype(F32) * c).astype(LOW)
        p = p_ref[h]
        da = dg(qkv_ref[2 * D + at : 2 * D + at + HEAD], do, 0, 0)
        ds = (p.astype(F32) * (da - deltas[i] * c)).astype(LOW)
        gp_ref[2, rows] = dg(do, p, 1, 1).astype(LOW)
        gp_ref[1, rows] = dg(qkv_ref[at : at + HEAD], ds, 1, 1).astype(LOW)
        gp_ref[0, rows] = (
            SCALE * (dg(qkv_ref[D + at : D + at + HEAD], ds, 1, 0) + dq_mem[rows])
        ).astype(LOW)


def weights_kernel(
    bits, after_ref, at_ref, x_ref, w_ref, mem_ref, gp0_ref, gp1_ref, gm0_ref, gm1_ref, dwo_ref, vec_ref, vec1_ref, *rest
):
    g_refs, wext = rest[: len(bits)], rest[len(bits)]
    me = at_ref[0]
    mem_low = mem_ref[...].astype(LOW)
    x_t = x_ref[...].T
    width = gp0_ref.shape[1]
    for part, (gp_ref, gm_ref) in enumerate(((gp0_ref, gm0_ref), (gp1_ref, gm1_ref))):
        for i in range(3):
            grad = dg(x_t, gp_ref[i], 1, 1)
            if i > 0:
                grad = grad + dg(mem_low, gm_ref[i - 1].astype(LOW), 0, 0)
            at = i * D + part * width
            wext[:, at : at + width] = grad.astype(LOW)
    wext[:, 3 * D : 4 * D] = dwo_ref[...]
    gp_mem = jnp.concatenate([gm0_ref[0], gm1_ref[0], gm0_ref[1], gm1_ref[1]], axis=1).astype(LOW)
    g_mem = dg(gp_mem, w_ref[:, D : 3 * D], 1, 1)
    g_mem = jnp.where(at_ref[2] == 0, g_mem, 0.0)
    row = iota((EXTRA, D), 0)
    tall = jnp.concatenate([g_mem, jnp.zeros((EXTRA - PAD, D), F32)], axis=0)
    tall = jnp.where(row < MEM, tall, 0.0)
    for i in range(5):
        tall = jnp.where(row == MEM + i, (vec1_ref if i < 2 else vec_ref)[i : i + 1], tall)
    wext[:, 4 * D :] = tall.T.astype(LOW)
    for g_ref, offsets in zip(g_refs, bits, strict=True):
        if offsets is None:
            g_ref[...] = wext[...]
            continue
        size = g_ref.shape[0] // len(offsets)
        for j, offset in enumerate(offsets):
            start = pl.multiple_of((me ^ offset) * size, size)
            g_ref[j * size : (j + 1) * size] = wext[pl.ds(start, size), :]


def tokens_kernel(after_ref, w_ref, gp0_ref, gp1_ref, resid_ref, tok_ref):
    width = gp0_ref.shape[1]
    total = jnp.zeros((D, SPAN), F32)
    for part, gp_ref in enumerate((gp0_ref, gp1_ref)):
        for i in range(3):
            at = i * D + part * width
            total = total + dg(w_ref[:, at : at + width], gp_ref[i], 1, 0)
    tok_ref[...] = (total.T + resid_ref[...]).astype(LOW)


def place_kernel(at_ref, r0, r1, r2, r3, out_ref, sems):
    me = at_ref[3]
    copies = [pltpu.make_async_copy(ref, out_ref.at[me ^ k], sems.at[k]) for k, ref in enumerate((r0, r1, r2, r3))]
    for copy in copies:
        copy.start()
    for copy in copies:
        copy.wait()


def place(at, pieces):
    rows = call(
        place_kernel,
        sds((4,) + pieces[0].shape, pieces[0].dtype),
        [SMEM] + [VMEM] * 4,
        ANY,
        [pltpu.SemaphoreType.DMA((4,))],
        mib=8,
    )(at, *pieces)
    return rows.reshape(-1, D)


def finish_kernel(at_ref, own_ref, other_ref, out_ref, bias_ref, held):
    first = at_ref[5]
    size = own_ref.shape[1]
    for i, ref in enumerate((own_ref, other_ref)):
        for j in range(2):
            start = pl.multiple_of((first ^ (2 * i + j)) * size, size)
            held[pl.ds(start, size), :] = ref[j].astype(F32)
    out_ref[...] = held[:D]
    bias_ref[...] = held[held.shape[0] - PAD : held.shape[0] - PAD + 1]


def swap(value, axis, bit):
    n = lax.axis_size(axis)
    return lax.ppermute(value, axis, [(i, i ^ bit) for i in range(n)])


def tie(*values):
    return lax.optimization_barrier(values)


def add_low(*terms):
    return functools.reduce(jnp.add, [t.astype(F32) for t in terms]).astype(LOW)


def finish(at, pair, other):
    grad, bias = call(
        finish_kernel,
        [sds((D, D), F32), sds((1, D), F32)],
        [SMEM] + [VMEM] * 2,
        [VMEM] * 2,
        [pltpu.VMEM((4 * pair.shape[1], D), F32)],
        bytes_=2 * 2**20,
    )(at, pair, other)
    return grad, bias[0]


def shards(
    tokens, cotangent, memory_init, query_weight, key_weight, value_weight, output_weight, first_gain,
    first_bias, inner_weight, inner_bias, outer_weight, outer_bias, second_gain, second_bias,
):
    n_dp, n_mp = lax.axis_size("dp"), lax.axis_size("mp")
    rows_each = query_weight.shape[0]
    by_bits = n_dp == 8 and n_mp == 4 and rows_each % 16 == 0
    me_mp, me_dp = lax.axis_index("mp"), lax.axis_index("dp")
    me = me_dp * n_mp + me_mp
    later = me_mp % SPANS
    x = (me_dp & 1) if by_bits else 0
    first = (x * 2 + ((me_dp >> 1) & 1)) if by_bits else 0
    at = jnp.stack([me, me_mp // SPANS, later, me_mp, me_dp, first, x]).astype(jnp.int32)

    vectors = (first_gain, first_bias, outer_bias, second_gain, second_bias)
    local = call(
        pack_kernel,
        sds((rows_each, WIDE), LOW),
        [VMEM] * 10,
        VMEM,
        [pltpu.VMEM((EXTRA, EXTRA), F32)],
        mib=56,
    )(query_weight, key_weight, value_weight, output_weight, memory_init.T, *[v.reshape(1, -1) for v in vectors])

    pick = lambda v, i: lax.dynamic_index_in_dim(v, i, 0, keepdims=False)
    outer_rows = jnp.concatenate([outer_weight, inner_bias.reshape(1, -1), jnp.zeros((15, D), LOW)], axis=0)
    wi2 = swap(inner_weight, "mp", 2)
    if by_bits:
        line = [local] + [swap(local, ALL, 8 * j) for j in range(1, 4)]
        *line, wi2 = tie(*line, wi2)
        line = jnp.concatenate(line, axis=0)
        plane = [line] + [swap(line, ALL, 2 * b) for b in range(1, 4)]
        *plane, outer_rows = tie(*plane, outer_rows)
        pieces = plane + [swap(piece, ALL, 1) for piece in plane]
        bits = [[2 * b + c + 8 * j for j in range(4)] for c in range(2) for b in range(4)]
    else:
        pieces = [lax.all_gather(local, ALL, axis=0, tiled=True)]
        bits = [None]
    wo2 = swap(outer_rows, "mp", 2)
    wi1, wo1, wi3 = swap(inner_weight, "mp", 1), swap(outer_rows, "mp", 1), swap(wi2, "mp", 1)
    blocks = tokens.reshape(-1, SPAN, D)
    own = pick(blocks, me_mp)
    start = pick(blocks, me_mp - later)
    cot = pick(cotangent.reshape(-1, SPAN, D), me_mp)

    w, qkv = call(
        functools.partial(project_kernel, bits),
        [sds((D, WIDE), LOW), sds((3 * D, SPAN), LOW)],
        [SMEM] + [VMEM] * (len(pieces) + 1),
        [VMEM] * 2,
        flops=2 * 10**9,
        bytes_=5 * 2**20,
    )(at, *pieces, own)
    p, o, m, l = call(
        attend_kernel,
        [
            sds((HEADS, SPAN, SPAN), LOW),
            sds((D, SPAN), F32),
            sds((HEADS, SPAN), F32),
            sds((HEADS, SPAN), F32),
        ],
        [VMEM],
        [VMEM] * 4,
        flops=5 * 10**9,
        bytes_=7 * 2**20,
    )(qkv)

    nm, small = call(
        memory_kernel,
        [sds((PAD, D), F32), sds((PAD, D), F32)],
        [VMEM] * 2,
        [VMEM] * 2,
        flops=3 * 10**9,
        bytes_=4 * 2**20,
        mib=16,
    )(start, w)
    nm, m, wo2 = tie(nm, m, wo2)
    wo3 = swap(wo2, "mp", 1)

    outer_shape = sds((2, 4, D // 4, D), LOW)
    inner_shape = sds((2, 4, (D + PAD) // 4, D), LOW)
    square, square_low = sds((SPAN, D), F32), sds((SPAN, D), LOW)
    (
        out, outer_keep, outer_send, slope, normed, grad_low, grad_sum, xhat, inv, mixed, mem, kv_mem, p_mem, c, c_mem, vecs,
    ) = call(
        forward_kernel,
        [
            square_low,
            outer_shape,
            outer_shape,
            sds((4, SPAN, D), LOW),
            square_low,
            square_low,
            square,
            square,
            sds((SPAN, 1), F32),
            sds((D, SPAN), LOW),
            sds((PAD, D), F32),
            sds((PAD, 2 * D), LOW),
            sds((HEADS * PAD, SPAN), LOW),
            sds((HEADS, SPAN), F32),
            sds((HEADS, SPAN), F32),
            sds((8, D), F32),
        ],
        [SMEM] + [VMEM] * 17,
        [VMEM] * 16,
        [pltpu.VMEM((4, SPAN, D), LOW)],
        flops=10 * 10**9,
        bytes_=14 * 2**20,
    )(
        at, nm, small, own, w, qkv, o, m, l, inner_weight, wi1, wi2, wi3, outer_rows, wo1, wo2, wo3, cot,
    )
    wis, wos = (inner_weight, wi1, wi2, wi3), (outer_rows, wo1, wo2, wo3)

    outer_got = swap(outer_send, "mp", 1)

    inner_send, back = call(
        send_kernel,
        [inner_shape, square],
        [SMEM] + [VMEM] * 8,
        [VMEM] * 2,
    )(at, wis[1], wis[3], wos[1], wos[3], slope, normed, grad_low, grad_sum)
    inner_got = swap(inner_send, "mp", 1)

    outer_mine, outer_give = add_low(outer_keep[0], outer_got[0]), add_low(outer_keep[1], outer_got[1])
    outer_y = swap(outer_give, "mp", 2)

    inner_keep, resid, d_mix, g_mixed, vecs1 = call(
        keep_kernel,
        [
            inner_shape,
            square,
            sds((D, D), LOW),
            sds((D, SPAN), LOW),
            sds((8, D), F32),
        ],
        [SMEM, ANY] + [VMEM] * 13,
        [VMEM] * 5,
    )(at, outer_give, small, w, wis[0], wis[2], wos[0], wos[2], slope, normed, grad_low, back, xhat, inv, mixed)

    half = HEADS // 2
    some = half * HEAD

    def heads_backward(low_h, gate):
        return call(
            functools.partial(heads_kernel, low_h, low_h + half),
            [sds((3, some, SPAN), LOW), sds((2, PAD, some), F32)],
            [ANY] + [VMEM] * 8,
            [VMEM] * 2,
            [
                pltpu.VMEM((some, SPAN), LOW),
                pltpu.VMEM((half * PAD, SPAN), LOW),
            ],
        )(gate, qkv, p, p_mem, mixed, c, c_mem, g_mixed, kv_mem)

    if by_bits:
        inner_give = add_low(inner_keep[:, 2:], inner_got[:, 2:])
        inner_mine = add_low(inner_keep[:, :2], inner_got[:, :2])
        inner_x = swap(inner_give, "dp", 1)
    else:
        inner_give = inner_got
    gp0, gm0 = heads_backward(0, inner_give)
    gp1, gm1 = heads_backward(half, inner_give)

    if by_bits:
        out_bits = [[2 * b + c + 8 * j for b in range(4) for j in (0, 2, 1, 3)] for c in range(2)]
    else:
        out_bits = [None]

    def weights_backward(gate):
        return call(
            functools.partial(weights_kernel, out_bits),
            [sds((D // len(out_bits), WIDE), LOW) for _ in out_bits],
            [ANY, SMEM] + [VMEM] * 10,
            [VMEM] * len(out_bits),
            [pltpu.VMEM((D, WIDE), LOW)],
        )(gate, at, own, w, mem, gp0, gp1, gm0, gm1, d_mix, vecs, vecs1)

    def tokens_backward(gate):
        return call(tokens_kernel, sds((SPAN, D), LOW), [ANY] + [VMEM] * 4, VMEM)(gate, w, gp0, gp1, resid)

    if by_bits:
        halves_of = lambda v: (v[: v.shape[0] // 2], v[v.shape[0] // 2 :])
        both = lambda mine, got: [add_low(u, v) for u, v in zip(halves_of(mine), halves_of(got), strict=True)]

        a_mine, a_give = [g.reshape(16, rows_each, WIDE) for g in weights_backward(inner_give)]
        a_got = swap(a_give, ALL, 1)
        grad_rows = tokens_backward(inner_give)

        rows_got = swap(grad_rows, "mp", 1)
        out_got, out_across = swap(out, "mp", 1), swap(out, "mp", 2)

        outer_y, out_across, grad_rows = tie(outer_y, out_across, grad_rows)
        q_mine, q_give = both(outer_mine, outer_y)
        q_got = swap(q_give, "dp", 1)

        inner_x, q_mine = tie(inner_x, q_mine)
        p_mine, p_give = add_low(inner_mine[0], inner_x[0]), add_low(inner_mine[1], inner_x[1])
        p_got = swap(p_give, "mp", 2)

        out_across, p_mine = tie(out_across, p_mine)
        out_last = swap(out_across, "mp", 1)
        layer_out = place(at, [out, out_got, out_across, out_last])

        q_got, layer_out = tie(q_got, layer_out)
        q_mine, q_give = [v[0] for v in both(q_mine, q_got)]
        q_got = swap(q_give, "dp", 2)

        p_got, q_mine = tie(p_got, q_mine)
        p_mine, p_give = [v[0] for v in both(p_mine, p_got)]
        p_got = swap(p_give, "dp", 2)

        a_got, p_mine = tie(a_got, p_mine)
        a_mine, a_give = both(a_mine, a_got)
        a_got = swap(a_give, ALL, 4)

        grad_rows, a_mine = tie(grad_rows, a_mine)
        rows_across = swap(grad_rows, "mp", 2)

        q_got, a_mine = tie(q_got, a_mine)
        q_mine = add_low(q_mine, q_got)
        q_got = swap(q_mine, "dp", 4)

        p_got, q_mine = tie(p_got, q_mine)
        p_mine = add_low(p_mine, p_got)
        p_got = swap(p_mine, "dp", 4)

        q_got, p_mine = tie(q_got, p_mine)
        q_mine = add_low(q_mine, q_got)
        q_got = swap(q_mine, "dp", 2)

        a_got, q_mine = tie(a_got, q_mine)
        a_mine, a_give = both(a_mine, a_got)
        a_got = swap(a_give, ALL, 2)

        p_got, a_mine = tie(p_got, a_mine)
        p_mine = add_low(p_mine, p_got)
        p_got = swap(p_mine, "dp", 2)

        rows_across, p_mine = tie(rows_across, p_mine)
        rows_last = swap(rows_across, "mp", 1)

        q_got, rows_across = tie(q_got, rows_across)
        q_pair = jnp.stack([q_mine, q_got])
        q_got = swap(q_pair, "dp", 1)

        a_got, q_pair = tie(a_got, q_pair)
        a_mine, a_give = both(a_mine, a_got)
        a_got = swap(a_give, ALL, 8)

        p_got, a_mine = tie(p_got, a_mine)
        p_pair = jnp.stack([p_mine, p_got])
        p_got = swap(p_pair, "dp", 1)

        rows_last, p_pair = tie(rows_last, p_pair)
        grad_tokens = place(at, [grad_rows, rows_got, rows_across, rows_last])

        a_got, grad_tokens = tie(a_got, grad_tokens)
        a_mine, a_give = both(a_mine, a_got)
        a_got = swap(a_give, ALL, 16)

        q_got, a_mine = tie(q_got, a_mine)
        grad_outer, _ = finish(at, q_pair, q_got)

        a_got, grad_outer = tie(a_got, grad_outer)
        reduced = a_mine.astype(F32) + a_got.astype(F32)

        p_got, reduced = tie(p_got, reduced)
        grad_inner, grad_inner_bias = finish(at, p_pair, p_got)
    else:
        grad_outer = lax.psum(outer_mine.astype(F32) + outer_y.astype(F32), "dp").reshape(-1, D)
        grad_rows = tokens_backward(inner_give)
        grads = weights_backward(inner_give)
        inner = add_low(inner_keep, inner_got)
        layer_out = lax.all_gather(out, "mp", axis=0, tiled=True)
        grad_tokens = lax.all_gather(grad_rows, "mp", axis=0, tiled=True)
        inner = lax.psum(inner[0].astype(F32) + swap(inner[1], "mp", 2).astype(F32), "dp").reshape(-1, D)
        grad_inner, grad_inner_bias = inner[:D], inner[D]
        reduced = lax.psum_scatter(grads[0], ALL, scatter_dimension=0, tiled=True).astype(F32)
    reduced = reduced.reshape(rows_each, WIDE)
    vector = lambda i: reduced[:, 4 * D + MEM + i]
    return (
        layer_out,
        grad_tokens,
        reduced[:, 4 * D : 4 * D + MEM].T,
        reduced[:, :D],
        reduced[:, D : 2 * D],
        reduced[:, 2 * D : 3 * D],
        reduced[:, 3 * D : 4 * D],
        vector(0),
        vector(1),
        grad_inner,
        grad_inner_bias,
        grad_outer,
        vector(2),
        vector(3),
        vector(4),
    )


def solution(mesh):
    both = ("dp", "mp")
    in_specs = (
        P("dp", None),
        P("dp", None),
        P(None, both),
        P(both, None),
        P(both, None),
        P(both, None),
        P(both, None),
        P(both),
        P(both),
        P(None, "mp"),
        P("mp"),
        P("mp", None),
        P(both),
        P(both),
        P(both),
    )
    out_specs = (
        P("dp", None),
        P("dp", None),
        P(None, both),
        P(both, None),
        P(both, None),
        P(both, None),
        P(both, None),
        P(both),
        P(both),
        P(None, "mp"),
        P("mp"),
        P("mp", None),
        P(both),
        P(both),
        P(both),
    )
    return jax.shard_map(shards, mesh=mesh, in_specs=in_specs, out_specs=out_specs, check_vma=False)
```

time: 209 us -> 146 us (0.70)
  waiting for transfers between devices: 91.5 us -> 56.8 us
  Pallas kernels: 60.4 us -> 40.9 us
  local copies, waits for them, and re-layouts: 11.3 us -> 5.19 us
  other arithmetic: 5.46 us -> 3.04 us
    ppermute x46 -> x41, waiting for transfers between devices: 91.5 us -> 56.8 us  [swap(): return lax.ppermute(value, axis, [(i, i ^ bit) for i in range(n)])]
    pallas_call x5 -> x11, Pallas kernels: 38.3 us -> 26.1 us  [the longest x2 4.48 us: heads_backward(): call(functools.partial(heads_kernel, low_h, low_h + half), [sds((3, some,...]
    pallas_call x1, Pallas kernels: 14.5 us -> 9.52 us  [shards(): call(forward_kernel, [square_low, outer_shape, outer_shape, sds((4, SPAN,...]
    unnamed x41 -> x7, local copies, waits for them, and re-layouts: 4.84 us -> 0.93 us
    pallas_call x2, Pallas kernels: 6.17 us -> 3.78 us  [place(): call(place_kernel, sds((4,) + pieces[0].shape, pieces[0].dtype), [SMEM] +...]
    convert_element_type x12, other arithmetic: 3.86 us -> 1.61 us  [add_low(): return functools.reduce(jnp.add, [t.astype(F32) for t in terms]).astype(LOW)]
    ppermute x46 -> x41, starting transfers between devices: 39.1 us -> 38.6 us  [swap(): return lax.ppermute(value, axis, [(i, i ^ bit) for i in range(n)])]
  transfers between devices with their start and end apart: 46 -> 41, of which waited for: 22 -> 22; matrix products, arithmetic and copies ran while one was open for 5% -> 4% of each run, Pallas kernels for 9% -> 20%
where the time goes in v2:
time: 146 us
  waiting for transfers between devices  56.8 us (39%)
  Pallas kernels  40.9 us (28%)
  starting transfers between devices  38.6 us (26%)
  local copies, waits for them, and re-layouts  5.19 us (4%)
  other arithmetic  3.04 us (2%)
    ppermute x41, waiting for transfers between devices, swap(): return lax.ppermute(value, axis, [(i, i ^ bit) for i in range(n)])  56.8 us
    ppermute x41, starting transfers between devices, swap(): return lax.ppermute(value, axis, [(i, i ^ bit) for i in range(n)])  38.6 us
    pallas_call x1, Pallas kernels, shards(): call(forward_kernel, [square_low, outer_shape, outer_shape, sds((4, SPAN,...  9.52 us
    pallas_call x2, Pallas kernels, heads_backward(): call(functools.partial(heads_kernel, low_h, low_h + half), [sds((3, some,...  4.48 us
    pallas_call x2, Pallas kernels, place(): call(place_kernel, sds((4,) + pieces[0].shape, pieces[0].dtype), [SMEM] +...  3.78 us
    pallas_call x1, Pallas kernels, shards(): call(attend_kernel, [sds((HEADS, SPAN, SPAN), LOW), sds((D, SPAN), F32),...  3.56 us
    pallas_call x1, Pallas kernels, shards(): call(keep_kernel, [inner_shape, square, sds((D, D), LOW), sds((D, SPAN),...  3.53 us
    pallas_call x2, Pallas kernels, finish(): call(finish_kernel, [sds((D, D), F32), sds((1, D), F32)], [SMEM] + [VMEM]...  3.31 us
  transfers between devices with their start and end apart: 41, of which 22 were waited for; matrix products, arithmetic and copies ran while one was open for 4% of the time, Pallas kernels for 20%

profile of v2, /device:TPU:0, one launch (start us, length us, event | category | flops | bytes accessed | tf_op | source)
XLA Modules:
  0.0 145.5 jit_solution(12906833242286040434)
XLA Ops:
  0.7 3.0 %collective-permute-start.3 = (bf16[512,512]{1,0:T(8,128)(2,1)}, bf16[512,512]{1,0:T(8,128)(2,1)S(1)}, u32[]{:S(2)}, u32[]{:S(2)}) collective-permute-start(bf16[512,512]{1,0:T(8,128)(2,1)} %wi0.3), channel_id=1, source_target_pairs={{0,2},{1,3},{2,0},{3,1},{4,6},{5,7},{6,4},{7,5},{8,10},{9,11},{10,... | collective-permute-start | bytes 1572872 | tf_op jit(solution)/shard_map/ppermute | solution.py:414
  3.7 1.5 %shard_map.262 = bf16[16,2176]{1,0:T(8,128)(2,1)} custom-call(bf16[16,512]{1,0:T(8,128)(2,1)} %q_ref.1, bf16[16,512]{1,0:T(8,128)(2,1)} %k_ref.1, bf16[16,512]{1,0:T(8,128)(2,1)} %v_ref.1, bf16[16,512]{1,0:T(8,128)(2,1)} %o_ref.1, bf16[16,20]{1,0:T(8,128)(2,1)} %bitcast.74, bf16[1,16]{1,0:T(2,128)(2,1)} %bitcast.75, bf16[1,16]{1,0:T(2,128)(2,1)} %bitcast.76, ...), custom_call_target="tpu_custom_call" | custom-call | flops 1 | bytes 1 | tf_op jit(solution)/shard_map/pallas_call | solution.py:452
  5.2 1.6 %collective-permute-start = (bf16[16,2176]{1,0:T(8,128)(2,1)}, bf16[16,2176]{1,0:T(8,128)(2,1)S(1)}, u32[]{:S(2)}, u32[]{:S(2)}) collective-permute-start(bf16[16,2176]{1,0:T(8,128)(2,1)} %shard_map.262), channel_id=1, source_target_pairs={{0,8},{1,9},{2,10},{3,11},{4,12},{5,13},{6,14},{7,15},{8,0},{9,1},... | collective-permute-start | bytes 208904 | tf_op jit(solution)/shard_map/ppermute | solution.py:414
  6.8 2.6 %collective-permute-start.1 = (bf16[16,2176]{1,0:T(8,128)(2,1)}, bf16[16,2176]{1,0:T(8,128)(2,1)S(1)}, u32[]{:S(2)}, u32[]{:S(2)}) collective-permute-start(bf16[16,2176]{1,0:T(8,128)(2,1)} %shard_map.262), channel_id=1, source_target_pairs={{0,16},{1,17},{2,18},{3,19},{4,20},{5,21},{6,22},{7,23},{8,24},{9,... | collective-permute-start | bytes 208904 | tf_op jit(solution)/shard_map/ppermute | solution.py:414
  9.7 4.5 %collective-permute-done.1 = bf16[16,2176]{1,0:T(8,128)(2,1)S(1)} collective-permute-done((bf16[16,2176]{1,0:T(8,128)(2,1)}, bf16[16,2176]{1,0:T(8,128)(2,1)S(1)}, u32[]{:S(2)}, u32[]{:S(2)}) %collective-permute-start.1) | collective-permute-done | bytes 69664 | tf_op jit(solution)/shard_map/ppermute | solution.py:414
  14.3 1.5 %collective-permute-done.2 = bf16[16,2176]{1,0:T(8,128)(2,1)S(1)} collective-permute-done((bf16[16,2176]{1,0:T(8,128)(2,1)}, bf16[16,2176]{1,0:T(8,128)(2,1)S(1)}, u32[]{:S(2)}, u32[]{:S(2)}) %collective-permute-start.2) | collective-permute-done | bytes 69664 | tf_op jit(solution)/shard_map/ppermute | solution.py:414
  15.8 0.9 constant_dynamic-update-slice_fusion.3
  16.8 1.8 %collective-permute-start.4 = (bf16[64,2176]{1,0:T(8,128)(2,1)S(1)}, bf16[64,2176]{1,0:T(8,128)(2,1)}, u32[]{:S(2)}, u32[]{:S(2)}) collective-permute-start(bf16[64,2176]{1,0:T(8,128)(2,1)S(1)} %constant_dynamic-update-slice_fusion.refs_0_), channel_id=1, source_target_pairs={{0,2},{1,3},{2,0},{3,1},{4,6},{5,7},{6,4},{7,5},{8,10},{9,11},{10,... | collective-permute-start | bytes 835592 | tf_op jit(solution)/shard_map/ppermute | solution.py:414
  18.6 1.5 %collective-permute-start.5 = (bf16[64,2176]{1,0:T(8,128)(2,1)S(1)}, bf16[64,2176]{1,0:T(8,128)(2,1)}, u32[]{:S(2)}, u32[]{:S(2)}) collective-permute-start(bf16[64,2176]{1,0:T(8,128)(2,1)S(1)} %constant_dynamic-update-slice_fusion.refs_0_), channel_id=1, source_target_pairs={{0,4},{1,5},{2,6},{3,7},{4,0},{5,1},{6,2},{7,3},{8,12},{9,13},{10,... | collective-permute-start | bytes 835592 | tf_op jit(solution)/shard_map/ppermute | solution.py:414
  20.3 0.7 reshape.101
  21.1 1.2 maximum_maximum_fusion.wo0
  22.3 3.3 %collective-permute-done.4.refs_1_ = bf16[64,2176]{1,0:T(8,128)(2,1)} collective-permute-done((bf16[64,2176]{1,0:T(8,128)(2,1)S(1)}, bf16[64,2176]{1,0:T(8,128)(2,1)}, u32[]{:S(2)}, u32[]{:S(2)}) %collective-permute-start.4) | collective-permute-done | bytes 278560 | tf_op jit(solution)/shard_map/ppermute | solution.py:414
  25.6 2.6 %collective-permute-done.5.refs_2_ = bf16[64,2176]{1,0:T(8,128)(2,1)} collective-permute-done((bf16[64,2176]{1,0:T(8,128)(2,1)S(1)}, bf16[64,2176]{1,0:T(8,128)(2,1)}, u32[]{:S(2)}, u32[]{:S(2)}) %collective-permute-start.5) | collective-permute-done | bytes 278560 | tf_op jit(solution)/shard_map/ppermute | solution.py:414
  28.3 3.7 %collective-permute-done.6.refs_3_ = bf16[64,2176]{1,0:T(8,128)(2,1)} collective-permute-done((bf16[64,2176]{1,0:T(8,128)(2,1)S(1)}, bf16[64,2176]{1,0:T(8,128)(2,1)}, u32[]{:S(2)}, u32[]{:S(2)}) %collective-permute-start.6) | collective-permute-done | bytes 278560 | tf_op jit(solution)/shard_map/ppermute | solution.py:414
  33.0 1.3 dynamic-slice_bitcast_fusion.1
  34.3 1.5 %collective-permute-start.11 = (bf16[528,512]{1,0:T(8,128)(2,1)S(1)}, bf16[528,512]{1,0:T(8,128)(2,1)S(1)}, u32[]{:S(2)}, u32[]{:S(2)}) collective-permute-start(bf16[528,512]{1,0:T(8,128)(2,1)S(1)} %maximum_maximum_fusion.wo0), channel_id=1, source_target_pairs={{0,2},{1,3},{2,0},{3,1},{4,6},{5,7},{6,4},{7,5},{8,10},{9,11},{10,... | collective-permute-start | bytes 1622024 | tf_op jit(solution)/shard_map/ppermute | solution.py:414
  35.8 2.6 %shard_map.263 = (bf16[512,2176]{1,0:T(8,128)(2,1)S(1)}, bf16[1536,512]{1,0:T(8,128)(2,1)S(1)}) custom-call(s32[7]{0:T(128)S(1)} %stack.49.at_ref, bf16[64,2176]{1,0:T(8,128)(2,1)S(1)} %constant_dynamic-update-slice_fusion.refs_0_, bf16[64,2176]{1,0:T(8,128)(2,1)} %collective-permute-done.4.refs_1_, bf16[64,2176]{1,0:T(8,128)(2,1)} %collective-permute-done.5.refs_2_, ...), custom_call_target="tpu_custom_call" | custom-call | flops 2000000000 | bytes 5242880 | tf_op jit(solution)/shard_map/pallas_call | solution.py:482
  38.5 2.3 %shard_map.264 = (f32[32,512]{1,0:T(8,128)S(1)}, f32[32,512]{1,0:T(8,128)S(1)}) custom-call(bf16[512,512]{1,0:T(8,128)(2,1)S(1)} %get-tuple-element.217.x1_ref, bf16[512,2176]{1,0:T(8,128)(2,1)S(1)} %get-tuple-element.119.w_ref), custom_call_target="tpu_custom_call" | custom-call | flops 3000000000 | bytes 4194304 | tf_op jit(solution)/shard_map/pallas_call | solution.py:504
  40.8 3.6 %shard_map.265 = (bf16[8,512,512]{2,1,0:T(8,128)(2,1)S(1)}, f32[512,512]{1,0:T(8,128)S(1)}, f32[8,512]{1,0:T(8,128)S(1)}, f32[8,512]{1,0:T(8,128)S(1)}) custom-call(bf16[1536,512]{1,0:T(8,128)(2,1)S(1)} %get-tuple-element.121.qkv_ref), custom_call_target="tpu_custom_call" | custom-call | flops 5000000000 | bytes 7340032 | tf_op jit(solution)/shard_map/pallas_call | solution.py:490
  44.4 4.2 %collective-permute-done.11.wo2 = bf16[528,512]{1,0:T(8,128)(2,1)S(1)} collective-permute-done((bf16[528,512]{1,0:T(8,128)(2,1)S(1)}, bf16[528,512]{1,0:T(8,128)(2,1)S(1)}, u32[]{:S(2)}, u32[]{:S(2)}) %collective-permute-start.11) | collective-permute-done | bytes 540704 | tf_op jit(solution)/shard_map/ppermute | solution.py:414
  49.1 2.1 %collective-permute-done.12.wi1 = bf16[512,512]{1,0:T(8,128)(2,1)S(1)} collective-permute-done((bf16[512,512]{1,0:T(8,128)(2,1)S(1)}, bf16[512,512]{1,0:T(8,128)(2,1)S(1)}, u32[]{:S(2)}, u32[]{:S(2)}) %collective-permute-start.12) | collective-permute-done | bytes 524320 | tf_op jit(solution)/shard_map/ppermute | solution.py:414
  51.2 0.7 collective-permute-done.13.wi3
  52.0 9.5 %shard_map.266 = (bf16[512,512]{1,0:T(8,128)(2,1)S(1)}, bf16[2,4,128,512]{3,2,1,0:T(8,128)(2,1)S(1)}, bf16[2,4,128,512]{3,2,1,0:T(8,128)(2,1)S(1)}, bf16[4,512,5...) custom-call(s32[7]{0:T(128)S(1)} %stack.49.at_ref, ...), custom_call_target="tpu_custom_call" | custom-call | flops 10000000000 | bytes 14680064 | tf_op jit(solution)/shard_map/pallas_call | solution.py:521
  61.7 2.5 %shard_map.267 = (bf16[2,4,136,512]{3,2,1,0:T(8,128)(2,1)S(1)}, f32[512,512]{1,0:T(8,128)S(1)}) custom-call(s32[7]{0:T(128)S(1)} %stack.49.at_ref, bf16[512,512]{1,0:T(8,128)(2,1)S(1)} %collective-permute-done.12.wi1, bf16[512,512]{1,0:T(8,128)(2,1)S(1)} %collective-permute-done.13.wi3, bf16[528,512]{1,0:T(8,128)(2,1)S(1)} %collective-permute-done.14.wo1, ...), custom_call_target="tpu_custom_call" | custom-call | flops 1 | bytes 1 | tf_op jit(solution)/shard_map/pallas_call | solution.py:553
  64.7 1.4 collective-permute-start.18
  66.5 0.7 collective-permute-start.17
  67.1 3.5 %shard_map.268 = (bf16[2,4,136,512]{3,2,1,0:T(8,128)(2,1)S(1)}, f32[512,512]{1,0:T(8,128)S(1)}, bf16[512,512]{1,0:T(8,128)(2,1)S(1)}, bf16[512,512]{1,0:T(8,128)(2,1)S(1)}, f32[8,512]{1,0:T(8,128)S(1)}) custom-call(s32[7]{0:T(128)S(1)} %stack.49.at_ref, bf16[4,128,512]{2,1,0:T(8,128)(2,1)S(1)} %get-tuple-element.214.after_ref, ...), custom_call_target="tpu_custom_call" | custom-call | flops 1 | bytes 1 | tf_op jit(solution)/shard_map/pallas_call | solution.py:564
  71.0 1.5 %collective-permute-start.22 = (bf16[2,2,136,512]{3,2,1,0:T(8,128)(2,1)S(1)}, bf16[2,2,136,512]{3,2,1,0:T(8,128)(2,1)S(1)}, u32[]{:S(2)}, u32[]{:S(2)}) collective-permute-start(bf16[2,2,136,512]{3,2,1,0:T(8,128)(2,1)S(1)} %get-tuple-element.213.after_ref), channel_id=1, source_target_pairs={{0,4},{4,0},{8,12},{12,8},{16,20},{20,16},{24,28},{28,24},{1,5},{5... | collective-permute-start | bytes 1671176 | tf_op jit(solution)/shard_map/ppermute | solution.py:414
  72.5 2.2 %shard_map.270 = (bf16[3,256,512]{2,1,0:T(8,128)(2,1)S(1)}, f32[2,32,256]{2,1,0:T(8,128)S(1)}) custom-call(bf16[2,2,136,512]{3,2,1,0:T(8,128)(2,1)S(1)} %get-tuple-element.213.after_ref, bf16[1536,512]{1,0:T(8,128)(2,1)S(1)} %get-tuple-element.121.qkv_ref, bf16[8,512,512]{2,1,0:T(8,128)(2,1)S(1)} %get-tuple-element.144.p_ref, ...), custom_call_target="tpu_custom_call" | custom-call | flops 1 | bytes 1 | tf_op jit(solution)/shard_map/pallas_call | solution.py:581
  74.7 2.2 %shard_map.269 = (bf16[3,256,512]{2,1,0:T(8,128)(2,1)S(1)}, f32[2,32,256]{2,1,0:T(8,128)S(1)}) custom-call(bf16[2,2,136,512]{3,2,1,0:T(8,128)(2,1)S(1)} %get-tuple-element.213.after_ref, bf16[1536,512]{1,0:T(8,128)(2,1)S(1)} %get-tuple-element.121.qkv_ref, bf16[8,512,512]{2,1,0:T(8,128)(2,1)S(1)} %get-tuple-element.144.p_ref, ...), custom_call_target="tpu_custom_call" | custom-call | flops 1 | bytes 1 | tf_op jit(solution)/shard_map/pallas_call | solution.py:581
  77.0 1.2 shard_map.271.r0
  78.2 2.6 %shard_map.273 = (bf16[256,2176]{1,0:T(8,128)(2,1)S(1)}, bf16[256,2176]{1,0:T(8,128)(2,1)S(1)}) custom-call(bf16[2,2,136,512]{3,2,1,0:T(8,128)(2,1)S(1)} %get-tuple-element.213.after_ref, s32[7]{0:T(128)S(1)} %stack.49.at_ref, bf16[512,512]{1,0:T(8,128)(2,1)S(1)} %get-tuple-element.216.refs_8_.x_ref, bf16[512,2176]{1,0:T(8,128)(2,1)S(1)} %get-tuple-element.119.w_ref, ...), custom_call_target="tpu_custom_call" | custom-call | flops 1 | bytes 1 | tf_op jit(solution)/shard_map/pallas_call | solution.py:607
  80.8 0.6 collective-permute-start.24
  81.3 8.6 %collective-permute-done.17 = bf16[4,128,512]{2,1,0:T(8,128)(2,1)S(1)} collective-permute-done((bf16[4,128,512]{2,1,0:T(8,128)(2,1)S(1)}, bf16[4,128,512]{2,1,0:T(8,128)(2,1)S(1)}, u32[]{:S(2)}, u32[]{:S(2)}) %collective-permute-start.17) | collective-permute-done | bytes 524320 | tf_op jit(solution)/shard_map/ppermute | solution.py:414
  90.0 1.5 collective-permute-start.20
  91.7 1.6 %collective-permute-start.25 = (bf16[2,136,512]{2,1,0:T(8,128)(2,1)S(1)}, bf16[2,136,512]{2,1,0:T(8,128)(2,1)S(1)}, u32[]{:S(2)}, u32[]{:S(2)}) collective-permute-start(bf16[2,136,512]{2,1,0:T(8,128)(2,1)S(1)} %get-tuple-element.224), channel_id=1, source_target_pairs={{0,2},{1,3},{2,0},{3,1},{4,6},{5,7},{6,4},{7,5},{8,10},{9,11},{10,... | collective-permute-start | bytes 835592 | tf_op jit(solution)/shard_map/ppermute | solution.py:414
  93.6 1.9 %shard_map.272 = bf16[4,512,512]{2,1,0:T(8,128)(2,1)} custom-call(s32[7]{0:T(128)S(1)} %stack.49.at_ref, bf16[512,512]{1,0:T(8,128)(2,1)S(1)} %get-tuple-element.133.r0, bf16[512,512]{1,0:T(8,128)(2,1)S(1)} %collective-permute-done.21.r1, bf16[512,512]{1,0:T(8,128)(2,1)S(1)} %collective-permute-done.18.r2, bf16[512,512]{1,0:T(8,128)(2,1)S(1)} %collective-permute-done.23.r3), custom_call_target="tpu_custom_call" | custom-call | flops 1 | bytes 1 | tf_op jit(solution)/shard_map/pallas_call | solution.py:390
  95.5 2.1 %collective-permute-done.20 = bf16[2,128,512]{2,1,0:T(8,128)(2,1)S(1)} collective-permute-done((bf16[2,128,512]{2,1,0:T(8,128)(2,1)S(1)}, bf16[2,128,512]{2,1,0:T(8,128)(2,1)S(1)}, u32[]{:S(2)}, u32[]{:S(2)}) %collective-permute-start.20) | collective-permute-done | bytes 262176 | tf_op jit(solution)/shard_map/ppermute | solution.py:414
  97.7 3.1 %collective-permute-done.25 = bf16[2,136,512]{2,1,0:T(8,128)(2,1)S(1)} collective-permute-done((bf16[2,136,512]{2,1,0:T(8,128)(2,1)S(1)}, bf16[2,136,512]{2,1,0:T(8,128)(2,1)S(1)}, u32[]{:S(2)}, u32[]{:S(2)}) %collective-permute-start.25) | collective-permute-done | bytes 278560 | tf_op jit(solution)/shard_map/ppermute | solution.py:414
  100.8 1.6 %collective-permute-start.27 = (bf16[128,512]{1,0:T(8,128)(2,1)S(1)}, bf16[128,512]{1,0:T(8,128)(2,1)S(1)}, u32[]{:S(2)}, u32[]{:S(2)}) collective-permute-start(bf16[128,512]{1,0:T(8,128)(2,1)S(1)} %get-tuple-element.232), channel_id=1, source_target_pairs={{0,8},{4,12},{8,0},{12,4},{16,24},{20,28},{24,16},{28,20},{1,9},{5... | collective-permute-start | bytes 393224 | tf_op jit(solution)/shard_map/ppermute | solution.py:414
  102.5 0.5 collective-permute-start.26
  103.2 0.7 collective-permute-start.29
  103.9 1.4 collective-permute-start.33
  105.4 1.9 %collective-permute-done.27 = bf16[128,512]{1,0:T(8,128)(2,1)S(1)} collective-permute-done((bf16[128,512]{1,0:T(8,128)(2,1)S(1)}, bf16[128,512]{1,0:T(8,128)(2,1)S(1)}, u32[]{:S(2)}, u32[]{:S(2)}) %collective-permute-start.27) | collective-permute-done | bytes 131104 | tf_op jit(solution)/shard_map/ppermute | solution.py:414
  107.3 2.7 %collective-permute-start.30 = (bf16[128,512]{1,0:T(8,128)(2,1)S(1)}, bf16[128,512]{1,0:T(8,128)(2,1)S(1)}, u32[]{:S(2)}, u32[]{:S(2)}) collective-permute-start(bf16[128,512]{1,0:T(8,128)(2,1)S(1)} %add_convert_fusion.15), channel_id=1, source_target_pairs={{0,16},{4,20},{8,24},{12,28},{16,0},{20,4},{24,8},{28,12},{1,17},{... | collective-permute-start | bytes 393224 | tf_op jit(solution)/shard_map/ppermute | solution.py:414
  110.3 2.6 %collective-permute-start.28 = (bf16[136,512]{1,0:T(8,128)(2,1)S(1)}, bf16[136,512]{1,0:T(8,128)(2,1)S(1)}, u32[]{:S(2)}, u32[]{:S(2)}) collective-permute-start(bf16[136,512]{1,0:T(8,128)(2,1)S(1)} %add_convert_fusion.11), channel_id=1, source_target_pairs={{0,16},{4,20},{8,24},{12,28},{16,0},{20,4},{24,8},{28,12},{1,17},{... | collective-permute-start | bytes 417800 | tf_op jit(solution)/shard_map/ppermute | solution.py:414
  112.9 6.2 %collective-permute-done.30 = bf16[128,512]{1,0:T(8,128)(2,1)S(1)} collective-permute-done((bf16[128,512]{1,0:T(8,128)(2,1)S(1)}, bf16[128,512]{1,0:T(8,128)(2,1)S(1)}, u32[]{:S(2)}, u32[]{:S(2)}) %collective-permute-start.30) | collective-permute-done | bytes 131104 | tf_op jit(solution)/shard_map/ppermute | solution.py:414
  119.4 1.2 collective-permute-done.28
  120.6 1.5 %collective-permute-start.31 = (bf16[4,16,2176]{2,1,0:T(8,128)(2,1)S(1)}, bf16[4,16,2176]{2,1,0:T(8,128)(2,1)S(1)}, u32[]{:S(2)}, u32[]{:S(2)}) collective-permute-start(bf16[4,16,2176]{2,1,0:T(8,128)(2,1)S(1)} %get-tuple-element.219), channel_id=1, source_target_pairs={{0,2},{1,3},{2,0},{3,1},{4,6},{5,7},{6,4},{7,5},{8,10},{9,11},{10,... | collective-permute-start | bytes 835592 | tf_op jit(solution)/shard_map/ppermute | solution.py:414
  122.1 0.9 collective-permute-start.37
  123.1 2.3 %collective-permute-done.32 = bf16[128,512]{1,0:T(8,128)(2,1)S(1)} collective-permute-done((bf16[128,512]{1,0:T(8,128)(2,1)S(1)}, bf16[128,512]{1,0:T(8,128)(2,1)S(1)}, u32[]{:S(2)}, u32[]{:S(2)}) %collective-permute-start.32) | collective-permute-done | bytes 131104 | tf_op jit(solution)/shard_map/ppermute | solution.py:414
  125.4 2.2 %collective-permute-done.31 = bf16[4,16,2176]{2,1,0:T(8,128)(2,1)S(1)} collective-permute-done((bf16[4,16,2176]{2,1,0:T(8,128)(2,1)S(1)}, bf16[4,16,2176]{2,1,0:T(8,128)(2,1)S(1)}, u32[]{:S(2)}, u32[]{:S(2)}) %collective-permute-start.31) | collective-permute-done | bytes 278560 | tf_op jit(solution)/shard_map/ppermute | solution.py:414
  128.1 0.6 collective-permute-start.39
  128.8 1.9 %shard_map.274 = bf16[4,512,512]{2,1,0:T(8,128)(2,1)} custom-call(s32[7]{0:T(128)S(1)} %stack.49.at_ref, bf16[512,512]{1,0:T(8,128)(2,1)S(1)} %shard_map.271.r0, bf16[512,512]{1,0:T(8,128)(2,1)S(1)} %collective-permute-done.35.r1, bf16[512,512]{1,0:T(8,128)(2,1)S(1)} %collective-permute-done.33.r2, bf16[512,512]{1,0:T(8,128)(2,1)S(1)} %collective-permute-done.36.r3), custom_call_target="tpu_custom_call" | custom-call | flops 1 | bytes 1 | tf_op jit(solution)/shard_map/pallas_call | solution.py:390
  130.7 2.1 %collective-permute-done.34 = bf16[2,16,2176]{2,1,0:T(8,128)(2,1)S(1)} collective-permute-done((bf16[2,16,2176]{2,1,0:T(8,128)(2,1)S(1)}, bf16[2,16,2176]{2,1,0:T(8,128)(2,1)S(1)}, u32[]{:S(2)}, u32[]{:S(2)}) %collective-permute-start.34) | collective-permute-done | bytes 139296 | tf_op jit(solution)/shard_map/ppermute | solution.py:414
  132.8 2.5 %collective-permute-start.40 = (bf16[1,16,2176]{2,1,0:T(8,128)(2,1)S(1)}, bf16[1,16,2176]{2,1,0:T(8,128)(2,1)S(1)}, u32[]{:S(2)}, u32[]{:S(2)}) collective-permute-start(bf16[1,16,2176]{2,1,0:T(8,128)(2,1)S(1)} %get-tuple-element.235), channel_id=1, source_target_pairs={{0,16},{1,17},{2,18},{3,19},{4,20},{5,21},{6,22},{7,23},{8,24},{9,... | collective-permute-start | bytes 208904 | tf_op jit(solution)/shard_map/ppermute | solution.py:414
  135.3 0.9 collective-permute-start.38
  136.2 1.7 %shard_map.275 = (f32[512,512]{1,0:T(8,128)}, f32[1,512]{1,0:T(1,128)}) custom-call(s32[7]{0:T(128)S(1)} %stack.49.at_ref, bf16[2,128,512]{2,1,0:T(8,128)(2,1)S(1)} %pad_maximum_fusion.1.own_ref, bf16[2,128,512]{2,1,0:T(8,128)(2,1)S(1)} %collective-permute-done.39.other_ref), custom_call_target="tpu_custom_call" | custom-call | flops 1 | bytes 2097152 | tf_op jit(solution)/shard_map/pallas_call | solution.py:426
  137.9 1.0 collective-permute-done.40
  138.9 3.0 %collective-permute-done.38.other_ref = bf16[2,136,512]{2,1,0:T(8,128)(2,1)S(1)} collective-permute-done((bf16[2,136,512]{2,1,0:T(8,128)(2,1)S(1)}, bf16[2,136,512]{2,1,0:T(8,128)(2,1)S(1)}, u32[]{:S(2)}, u32[]{:S(2)}) %collective-permute-start.38) | collective-permute-done | bytes 278560 | tf_op jit(solution)/shard_map/ppermute | solution.py:414
  141.8 0.7 fusion.12
  142.5 0.6 slice_bitcast_fusion.2
  143.1 0.8 slice_reduce_fusion
  143.8 1.7 %shard_map.276 = (f32[512,512]{1,0:T(8,128)}, f32[1,512]{1,0:T(1,128)}) custom-call(s32[7]{0:T(128)S(1)} %stack.49.at_ref, bf16[2,136,512]{2,1,0:T(8,128)(2,1)S(1)} %pad_maximum_fusion.own_ref, bf16[2,136,512]{2,1,0:T(8,128)(2,1)S(1)} %collective-permute-done.38.other_ref), custom_call_target="tpu_custom_call" | custom-call | flops 1 | bytes 2097152 | tf_op jit(solution)/shard_map/pallas_call | solution.py:426
  (69 shorter events, 6.3 us)
Async XLA Ops:
  0.6 48.4 %copy-start = (bf16[2048,512]{1,0:T(8,128)(2,1)S(1)}, bf16[2048,512]{1,0:T(8,128)(2,1)}, u32[]{:S(2)}) copy-start(bf16[2048,512]{1,0:T(8,128)(2,1)} %param.16) | copy-start | bytes 6291460
  0.7 15.2 %collective-permute-start.3 = (bf16[512,512]{1,0:T(8,128)(2,1)}, bf16[512,512]{1,0:T(8,128)(2,1)S(1)}, u32[]{:S(2)}, u32[]{:S(2)}) collective-permute-start(bf16[512,512]{1,0:T(8,128)(2,1)} %wi0.3), channel_id=1, source_target_pairs={{0,2},{1,3},{2,0},{3,1},{4,6},{5,7},{6,4},{7,5},{8,10},{9,11},{10,... | collective-permute-start | bytes 1572872 | tf_op jit(solution)/shard_map/ppermute | solution.py:414
  5.2 4.5 %collective-permute-start = (bf16[16,2176]{1,0:T(8,128)(2,1)}, bf16[16,2176]{1,0:T(8,128)(2,1)S(1)}, u32[]{:S(2)}, u32[]{:S(2)}) collective-permute-start(bf16[16,2176]{1,0:T(8,128)(2,1)} %shard_map.262), channel_id=1, source_target_pairs={{0,8},{1,9},{2,10},{3,11},{4,12},{5,13},{6,14},{7,15},{8,0},{9,1},... | collective-permute-start | bytes 208904 | tf_op jit(solution)/shard_map/ppermute | solution.py:414
  6.8 7.5 %collective-permute-start.1 = (bf16[16,2176]{1,0:T(8,128)(2,1)}, bf16[16,2176]{1,0:T(8,128)(2,1)S(1)}, u32[]{:S(2)}, u32[]{:S(2)}) collective-permute-start(bf16[16,2176]{1,0:T(8,128)(2,1)} %shard_map.262), channel_id=1, source_target_pairs={{0,16},{1,17},{2,18},{3,19},{4,20},{5,21},{6,22},{7,23},{8,24},{9,... | collective-permute-start | bytes 208904 | tf_op jit(solution)/shard_map/ppermute | solution.py:414
  9.4 6.4 %collective-permute-start.2 = (bf16[16,2176]{1,0:T(8,128)(2,1)}, bf16[16,2176]{1,0:T(8,128)(2,1)S(1)}, u32[]{:S(2)}, u32[]{:S(2)}) collective-permute-start(bf16[16,2176]{1,0:T(8,128)(2,1)} %shard_map.262), channel_id=1, source_target_pairs={{0,24},{1,25},{2,26},{3,27},{4,28},{5,29},{6,30},{7,31},{8,16},{9,... | collective-permute-start | bytes 208904 | tf_op jit(solution)/shard_map/ppermute | solution.py:414
  16.8 8.9 %collective-permute-start.4 = (bf16[64,2176]{1,0:T(8,128)(2,1)S(1)}, bf16[64,2176]{1,0:T(8,128)(2,1)}, u32[]{:S(2)}, u32[]{:S(2)}) collective-permute-start(bf16[64,2176]{1,0:T(8,128)(2,1)S(1)} %constant_dynamic-update-slice_fusion.refs_0_), channel_id=1, source_target_pairs={{0,2},{1,3},{2,0},{3,1},{4,6},{5,7},{6,4},{7,5},{8,10},{9,11},{10,... | collective-permute-start | bytes 835592 | tf_op jit(solution)/shard_map/ppermute | solution.py:414
  18.6 9.7 %collective-permute-start.5 = (bf16[64,2176]{1,0:T(8,128)(2,1)S(1)}, bf16[64,2176]{1,0:T(8,128)(2,1)}, u32[]{:S(2)}, u32[]{:S(2)}) collective-permute-start(bf16[64,2176]{1,0:T(8,128)(2,1)S(1)} %constant_dynamic-update-slice_fusion.refs_0_), channel_id=1, source_target_pairs={{0,4},{1,5},{2,6},{3,7},{4,0},{5,1},{6,2},{7,3},{8,12},{9,13},{10,... | collective-permute-start | bytes 835592 | tf_op jit(solution)/shard_map/ppermute | solution.py:414
  20.1 11.9 %collective-permute-start.6 = (bf16[64,2176]{1,0:T(8,128)(2,1)S(1)}, bf16[64,2176]{1,0:T(8,128)(2,1)}, u32[]{:S(2)}, u32[]{:S(2)}) collective-permute-start(bf16[64,2176]{1,0:T(8,128)(2,1)S(1)} %constant_dynamic-update-slice_fusion.refs_0_), channel_id=1, source_target_pairs={{0,6},{1,7},{2,4},{3,5},{4,2},{5,3},{6,0},{7,1},{8,14},{9,15},{10,... | collective-permute-start | bytes 835592 | tf_op jit(solution)/shard_map/ppermute | solution.py:414
  31.9 3.9 %collective-permute-start.10 = (bf16[64,2176]{1,0:T(8,128)(2,1)}, bf16[64,2176]{1,0:T(8,128)(2,1)}, u32[]{:S(2)}, u32[]{:S(2)}) collective-permute-start(bf16[64,2176]{1,0:T(8,128)(2,1)} %collective-permute-done.6.refs_3_), channel_id=1, source_target_pairs={{0,1},{1,0},{2,3},{3,2},{4,5},{5,4},{6,7},{7,6},{8,9},{9,8},{10,11... | collective-permute-start | bytes 835592 | tf_op jit(solution)/shard_map/ppermute | solution.py:414
  31.9 3.9 %collective-permute-start.7 = (bf16[64,2176]{1,0:T(8,128)(2,1)S(1)}, bf16[64,2176]{1,0:T(8,128)(2,1)}, u32[]{:S(2)}, u32[]{:S(2)}) collective-permute-start(bf16[64,2176]{1,0:T(8,128)(2,1)S(1)} %constant_dynamic-update-slice_fusion.refs_0_), channel_id=1, source_target_pairs={{0,1},{1,0},{2,3},{3,2},{4,5},{5,4},{6,7},{7,6},{8,9},{9,8},{10,11... | collective-permute-start | bytes 835592 | tf_op jit(solution)/shard_map/ppermute | solution.py:414
  32.4 3.4 %collective-permute-start.8 = (bf16[64,2176]{1,0:T(8,128)(2,1)}, bf16[64,2176]{1,0:T(8,128)(2,1)}, u32[]{:S(2)}, u32[]{:S(2)}) collective-permute-start(bf16[64,2176]{1,0:T(8,128)(2,1)} %collective-permute-done.4.refs_1_), channel_id=1, source_target_pairs={{0,1},{1,0},{2,3},{3,2},{4,5},{5,4},{6,7},{7,6},{8,9},{9,8},{10,11... | collective-permute-start | bytes 835592 | tf_op jit(solution)/shard_map/ppermute | solution.py:414
  32.4 3.4 %collective-permute-start.9 = (bf16[64,2176]{1,0:T(8,128)(2,1)}, bf16[64,2176]{1,0:T(8,128)(2,1)}, u32[]{:S(2)}, u32[]{:S(2)}) collective-permute-start(bf16[64,2176]{1,0:T(8,128)(2,1)} %collective-permute-done.5.refs_2_), channel_id=1, source_target_pairs={{0,1},{1,0},{2,3},{3,2},{4,5},{5,4},{6,7},{7,6},{8,9},{9,8},{10,11... | collective-permute-start | bytes 835592 | tf_op jit(solution)/shard_map/ppermute | solution.py:414
  34.3 14.2 %collective-permute-start.11 = (bf16[528,512]{1,0:T(8,128)(2,1)S(1)}, bf16[528,512]{1,0:T(8,128)(2,1)S(1)}, u32[]{:S(2)}, u32[]{:S(2)}) collective-permute-start(bf16[528,512]{1,0:T(8,128)(2,1)S(1)} %maximum_maximum_fusion.wo0), channel_id=1, source_target_pairs={{0,2},{1,3},{2,0},{3,1},{4,6},{5,7},{6,4},{7,5},{8,10},{9,11},{10,... | collective-permute-start | bytes 1622024 | tf_op jit(solution)/shard_map/ppermute | solution.py:414
  35.8 16.2 %collective-permute-start.14 = (bf16[528,512]{1,0:T(8,128)(2,1)S(1)}, bf16[528,512]{1,0:T(8,128)(2,1)S(1)}, u32[]{:S(2)}, u32[]{:S(2)}) collective-permute-start(bf16[528,512]{1,0:T(8,128)(2,1)S(1)} %maximum_maximum_fusion.wo0), channel_id=1, source_target_pairs={{0,1},{1,0},{2,3},{3,2},{4,5},{5,4},{6,7},{7,6},{8,9},{9,8},{10,11... | collective-permute-start | bytes 1622024 | tf_op jit(solution)/shard_map/ppermute | solution.py:414
  40.8 7.8 %copy-start.1 = (bf16[512,512]{1,0:T(8,128)(2,1)S(1)}, bf16[512,512]{1,0:T(8,128)(2,1)}, u32[]{:S(2)}) copy-start(bf16[512,512]{1,0:T(8,128)(2,1)} %wi0.3) | copy-start | bytes 1572868
  48.6 3.4 %collective-permute-start.15 = (bf16[528,512]{1,0:T(8,128)(2,1)S(1)}, bf16[528,512]{1,0:T(8,128)(2,1)S(1)}, u32[]{:S(2)}, u32[]{:S(2)}) collective-permute-start(bf16[528,512]{1,0:T(8,128)(2,1)S(1)} %collective-permute-done.11.wo2), channel_id=1, source_target_pairs={{0,1},{1,0},{2,3},{3,2},{4,5},{5,4},{6,7},{7,6},{8,9},{9,8},{10,11... | collective-permute-start | bytes 1622024 | tf_op jit(solution)/shard_map/ppermute | solution.py:414
  48.6 2.7 %collective-permute-start.12 = (bf16[512,512]{1,0:T(8,128)(2,1)S(1)}, bf16[512,512]{1,0:T(8,128)(2,1)S(1)}, u32[]{:S(2)}, u32[]{:S(2)}) collective-permute-start(bf16[512,512]{1,0:T(8,128)(2,1)S(1)} %copy-done.1), channel_id=1, source_target_pairs={{0,1},{1,0},{2,3},{3,2},{4,5},{5,4},{6,7},{7,6},{8,9},{9,8},{10,11... | collective-permute-start | bytes 1572872 | tf_op jit(solution)/shard_map/ppermute | solution.py:414
  49.1 2.9 %collective-permute-start.13 = (bf16[512,512]{1,0:T(8,128)(2,1)S(1)}, bf16[512,512]{1,0:T(8,128)(2,1)S(1)}, u32[]{:S(2)}, u32[]{:S(2)}) collective-permute-start(bf16[512,512]{1,0:T(8,128)(2,1)S(1)} %collective-permute-done.3.wi2), channel_id=1, source_target_pairs={{0,1},{1,0},{2,3},{3,2},{4,5},{5,4},{6,7},{7,6},{8,9},{9,8},{10,11... | collective-permute-start | bytes 1572872 | tf_op jit(solution)/shard_map/ppermute | solution.py:414
  61.5 4.6 %collective-permute-start.16 = (bf16[2,4,128,512]{3,2,1,0:T(8,128)(2,1)S(1)}, bf16[2,4,128,512]{3,2,1,0:T(8,128)(2,1)S(1)}, u32[]{:S(2)}, u32[]{:S(2)}) collective-permute-start(bf16[2,4,128,512]{3,2,1,0:T(8,128)(2,1)S(1)} %get-tuple-element.132), channel_id=1, source_target_pairs={{0,1},{1,0},{2,3},{3,2},{4,5},{5,4},{6,7},{7,6},{8,9},{9,8},{10,11... | collective-permute-start | bytes 3145736 | tf_op jit(solution)/shard_map/ppermute | solution.py:414
  64.3 6.4 %collective-permute-start.19 = (bf16[2,4,136,512]{3,2,1,0:T(8,128)(2,1)S(1)}, bf16[2,4,136,512]{3,2,1,0:T(8,128)(2,1)S(1)}, u32[]{:S(2)}, u32[]{:S(2)}) collective-permute-start(bf16[2,4,136,512]{3,2,1,0:T(8,128)(2,1)S(1)} %get-tuple-element.143), channel_id=1, source_target_pairs={{0,1},{1,0},{2,3},{3,2},{4,5},{5,4},{6,7},{7,6},{8,9},{9,8},{10,11... | collective-permute-start | bytes 3342344 | tf_op jit(solution)/shard_map/ppermute | solution.py:414
  64.7 16.6 %collective-permute-start.18 = (bf16[512,512]{1,0:T(8,128)(2,1)S(1)}, bf16[512,512]{1,0:T(8,128)(2,1)S(1)}, u32[]{:S(2)}, u32[]{:S(2)}) collective-permute-start(bf16[512,512]{1,0:T(8,128)(2,1)S(1)} %get-tuple-element.133.r0), channel_id=1, source_target_pairs={{0,2},{1,3},{2,0},{3,1},{4,6},{5,7},{6,4},{7,5},{8,10},{9,11},{10,... | collective-permute-start | bytes 1572872 | tf_op jit(solution)/shard_map/ppermute | solution.py:414
  66.5 23.4 %collective-permute-start.17 = (bf16[4,128,512]{2,1,0:T(8,128)(2,1)S(1)}, bf16[4,128,512]{2,1,0:T(8,128)(2,1)S(1)}, u32[]{:S(2)}, u32[]{:S(2)}) collective-permute-start(bf16[4,128,512]{2,1,0:T(8,128)(2,1)S(1)} %get-tuple-element.214.after_ref), channel_id=1, source_target_pairs={{0,2},{1,3},{2,0},{3,1},{4,6},{5,7},{6,4},{7,5},{8,10},{9,11},{10,... | collective-permute-start | bytes 1572872 | tf_op jit(solution)/shard_map/ppermute | solution.py:414
  71.0 20.5 %collective-permute-start.22 = (bf16[2,2,136,512]{3,2,1,0:T(8,128)(2,1)S(1)}, bf16[2,2,136,512]{3,2,1,0:T(8,128)(2,1)S(1)}, u32[]{:S(2)}, u32[]{:S(2)}) collective-permute-start(bf16[2,2,136,512]{3,2,1,0:T(8,128)(2,1)S(1)} %get-tuple-element.213.after_ref), channel_id=1, source_target_pairs={{0,4},{4,0},{8,12},{12,8},{16,20},{20,16},{24,28},{28,24},{1,5},{5... | collective-permute-start | bytes 1671176 | tf_op jit(solution)/shard_map/ppermute | solution.py:414
  72.5 20.9 %collective-permute-start.21 = (bf16[512,512]{1,0:T(8,128)(2,1)S(1)}, bf16[512,512]{1,0:T(8,128)(2,1)S(1)}, u32[]{:S(2)}, u32[]{:S(2)}) collective-permute-start(bf16[512,512]{1,0:T(8,128)(2,1)S(1)} %get-tuple-element.133.r0), channel_id=1, source_target_pairs={{0,1},{1,0},{2,3},{3,2},{4,5},{5,4},{6,7},{7,6},{8,9},{9,8},{10,11... | collective-permute-start | bytes 1572872 | tf_op jit(solution)/shard_map/ppermute | solution.py:414
  80.8 22.2 %collective-permute-start.24 = (bf16[16,16,2176]{2,1,0:T(8,128)(2,1)S(1)}, bf16[16,16,2176]{2,1,0:T(8,128)(2,1)S(1)}, u32[]{:S(2)}, u32[]{:S(2)}) collective-permute-start(bf16[16,16,2176]{2,1,0:T(8,128)(2,1)S(1)} %bitcast.61), channel_id=1, source_target_pairs={{0,1},{1,0},{2,3},{3,2},{4,5},{5,4},{6,7},{7,6},{8,9},{9,8},{10,11... | collective-permute-start | bytes 3342344 | tf_op jit(solution)/shard_map/ppermute | solution.py:414
  90.0 7.6 %collective-permute-start.20 = (bf16[2,128,512]{2,1,0:T(8,128)(2,1)S(1)}, bf16[2,128,512]{2,1,0:T(8,128)(2,1)S(1)}, u32[]{:S(2)}, u32[]{:S(2)}) collective-permute-start(bf16[2,128,512]{2,1,0:T(8,128)(2,1)S(1)} %get-tuple-element.227), channel_id=1, source_target_pairs={{0,4},{4,0},{8,12},{12,8},{16,20},{20,16},{24,28},{28,24},{1,5},{5... | collective-permute-start | bytes 786440 | tf_op jit(solution)/shard_map/ppermute | solution.py:414
  91.7 2.0 %collective-permute-start.23 = (bf16[512,512]{1,0:T(8,128)(2,1)S(1)}, bf16[512,512]{1,0:T(8,128)(2,1)S(1)}, u32[]{:S(2)}, u32[]{:S(2)}) collective-permute-start(bf16[512,512]{1,0:T(8,128)(2,1)S(1)} %collective-permute-done.18.r2), channel_id=1, source_target_pairs={{0,1},{1,0},{2,3},{3,2},{4,5},{5,4},{6,7},{7,6},{8,9},{9,8},{10,11... | collective-permute-start | bytes 1572872 | tf_op jit(solution)/shard_map/ppermute | solution.py:414
  91.7 9.1 %collective-permute-start.25 = (bf16[2,136,512]{2,1,0:T(8,128)(2,1)S(1)}, bf16[2,136,512]{2,1,0:T(8,128)(2,1)S(1)}, u32[]{:S(2)}, u32[]{:S(2)}) collective-permute-start(bf16[2,136,512]{2,1,0:T(8,128)(2,1)S(1)} %get-tuple-element.224), channel_id=1, source_target_pairs={{0,2},{1,3},{2,0},{3,1},{4,6},{5,7},{6,4},{7,5},{8,10},{9,11},{10,... | collective-permute-start | bytes 835592 | tf_op jit(solution)/shard_map/ppermute | solution.py:414
  93.4 35.4 %collective-permute-start.35 = (bf16[512,512]{1,0:T(8,128)(2,1)S(1)}, bf16[512,512]{1,0:T(8,128)(2,1)S(1)}, u32[]{:S(2)}, u32[]{:S(2)}) collective-permute-start(bf16[512,512]{1,0:T(8,128)(2,1)S(1)} %shard_map.271.r0), channel_id=1, source_target_pairs={{0,1},{1,0},{2,3},{3,2},{4,5},{5,4},{6,7},{7,6},{8,9},{9,8},{10,11... | collective-permute-start | bytes 1572872 | tf_op jit(solution)/shard_map/ppermute | solution.py:414
  100.8 6.4 %collective-permute-start.27 = (bf16[128,512]{1,0:T(8,128)(2,1)S(1)}, bf16[128,512]{1,0:T(8,128)(2,1)S(1)}, u32[]{:S(2)}, u32[]{:S(2)}) collective-permute-start(bf16[128,512]{1,0:T(8,128)(2,1)S(1)} %get-tuple-element.232), channel_id=1, source_target_pairs={{0,8},{4,12},{8,0},{12,4},{16,24},{20,28},{24,16},{28,20},{1,9},{5... | collective-permute-start | bytes 393224 | tf_op jit(solution)/shard_map/ppermute | solution.py:414
  102.5 7.8 %collective-permute-start.26 = (bf16[136,512]{1,0:T(8,128)(2,1)S(1)}, bf16[136,512]{1,0:T(8,128)(2,1)S(1)}, u32[]{:S(2)}, u32[]{:S(2)}) collective-permute-start(bf16[136,512]{1,0:T(8,128)(2,1)S(1)} %get-tuple-element.230), channel_id=1, source_target_pairs={{0,8},{4,12},{8,0},{12,4},{16,24},{20,28},{24,16},{28,20},{1,9},{5... | collective-permute-start | bytes 417800 | tf_op jit(solution)/shard_map/ppermute | solution.py:414
  103.2 16.0 %collective-permute-start.29 = (bf16[8,16,2176]{2,1,0:T(8,128)(2,1)S(1)}, bf16[8,16,2176]{2,1,0:T(8,128)(2,1)S(1)}, u32[]{:S(2)}, u32[]{:S(2)}) collective-permute-start(bf16[8,16,2176]{2,1,0:T(8,128)(2,1)S(1)} %get-tuple-element.221), channel_id=1, source_target_pairs={{0,4},{1,5},{2,6},{3,7},{4,0},{5,1},{6,2},{7,3},{8,12},{9,13},{10,... | collective-permute-start | bytes 1671176 | tf_op jit(solution)/shard_map/ppermute | solution.py:414
  103.9 19.1 %collective-permute-start.33 = (bf16[512,512]{1,0:T(8,128)(2,1)S(1)}, bf16[512,512]{1,0:T(8,128)(2,1)S(1)}, u32[]{:S(2)}, u32[]{:S(2)}) collective-permute-start(bf16[512,512]{1,0:T(8,128)(2,1)S(1)} %shard_map.271.r0), channel_id=1, source_target_pairs={{0,2},{1,3},{2,0},{3,1},{4,6},{5,7},{6,4},{7,5},{8,10},{9,11},{10,... | collective-permute-start | bytes 1572872 | tf_op jit(solution)/shard_map/ppermute | solution.py:414
  107.3 11.8 %collective-permute-start.30 = (bf16[128,512]{1,0:T(8,128)(2,1)S(1)}, bf16[128,512]{1,0:T(8,128)(2,1)S(1)}, u32[]{:S(2)}, u32[]{:S(2)}) collective-permute-start(bf16[128,512]{1,0:T(8,128)(2,1)S(1)} %add_convert_fusion.15), channel_id=1, source_target_pairs={{0,16},{4,20},{8,24},{12,28},{16,0},{20,4},{24,8},{28,12},{1,17},{... | collective-permute-start | bytes 393224 | tf_op jit(solution)/shard_map/ppermute | solution.py:414
  110.3 10.3 %collective-permute-start.28 = (bf16[136,512]{1,0:T(8,128)(2,1)S(1)}, bf16[136,512]{1,0:T(8,128)(2,1)S(1)}, u32[]{:S(2)}, u32[]{:S(2)}) collective-permute-start(bf16[136,512]{1,0:T(8,128)(2,1)S(1)} %add_convert_fusion.11), channel_id=1, source_target_pairs={{0,16},{4,20},{8,24},{12,28},{16,0},{20,4},{24,8},{28,12},{1,17},{... | collective-permute-start | bytes 417800 | tf_op jit(solution)/shard_map/ppermute | solution.py:414
  119.1 6.2 %collective-permute-start.32 = (bf16[128,512]{1,0:T(8,128)(2,1)S(1)}, bf16[128,512]{1,0:T(8,128)(2,1)S(1)}, u32[]{:S(2)}, u32[]{:S(2)}) collective-permute-start(bf16[128,512]{1,0:T(8,128)(2,1)S(1)} %add_convert_fusion.14), channel_id=1, source_target_pairs={{0,8},{4,12},{8,0},{12,4},{16,24},{20,28},{24,16},{28,20},{1,9},{5... | collective-permute-start | bytes 393224 | tf_op jit(solution)/shard_map/ppermute | solution.py:414
  120.6 7.0 %collective-permute-start.31 = (bf16[4,16,2176]{2,1,0:T(8,128)(2,1)S(1)}, bf16[4,16,2176]{2,1,0:T(8,128)(2,1)S(1)}, u32[]{:S(2)}, u32[]{:S(2)}) collective-permute-start(bf16[4,16,2176]{2,1,0:T(8,128)(2,1)S(1)} %get-tuple-element.219), channel_id=1, source_target_pairs={{0,2},{1,3},{2,0},{3,1},{4,6},{5,7},{6,4},{7,5},{8,10},{9,11},{10,... | collective-permute-start | bytes 835592 | tf_op jit(solution)/shard_map/ppermute | solution.py:414
  122.1 6.6 %collective-permute-start.37 = (bf16[136,512]{1,0:T(8,128)(2,1)S(1)}, bf16[136,512]{1,0:T(8,128)(2,1)S(1)}, u32[]{:S(2)}, u32[]{:S(2)}) collective-permute-start(bf16[136,512]{1,0:T(8,128)(2,1)S(1)} %add_convert_fusion.10), channel_id=1, source_target_pairs={{0,8},{4,12},{8,0},{12,4},{16,24},{20,28},{24,16},{28,20},{1,9},{5... | collective-permute-start | bytes 417800 | tf_op jit(solution)/shard_map/ppermute | solution.py:414
  123.1 5.7 %collective-permute-start.36 = (bf16[512,512]{1,0:T(8,128)(2,1)S(1)}, bf16[512,512]{1,0:T(8,128)(2,1)S(1)}, u32[]{:S(2)}, u32[]{:S(2)}) collective-permute-start(bf16[512,512]{1,0:T(8,128)(2,1)S(1)} %collective-permute-done.33.r2), channel_id=1, source_target_pairs={{0,1},{1,0},{2,3},{3,2},{4,5},{5,4},{6,7},{7,6},{8,9},{9,8},{10,11... | collective-permute-start | bytes 1572872 | tf_op jit(solution)/shard_map/ppermute | solution.py:414
  127.6 5.1 %collective-permute-start.34 = (bf16[2,16,2176]{2,1,0:T(8,128)(2,1)S(1)}, bf16[2,16,2176]{2,1,0:T(8,128)(2,1)S(1)}, u32[]{:S(2)}, u32[]{:S(2)}) collective-permute-start(bf16[2,16,2176]{2,1,0:T(8,128)(2,1)S(1)} %get-tuple-element.229), channel_id=1, source_target_pairs={{0,8},{1,9},{2,10},{3,11},{4,12},{5,13},{6,14},{7,15},{8,0},{9,1},... | collective-permute-start | bytes 417800 | tf_op jit(solution)/shard_map/ppermute | solution.py:414
  128.1 8.1 %collective-permute-start.39 = (bf16[2,128,512]{2,1,0:T(8,128)(2,1)S(1)}, bf16[2,128,512]{2,1,0:T(8,128)(2,1)S(1)}, u32[]{:S(2)}, u32[]{:S(2)}) collective-permute-start(bf16[2,128,512]{2,1,0:T(8,128)(2,1)S(1)} %pad_maximum_fusion.1.own_ref), channel_id=1, source_target_pairs={{0,4},{4,0},{8,12},{12,8},{16,20},{20,16},{24,28},{28,24},{1,5},{5... | collective-permute-start | bytes 786440 | tf_op jit(solution)/shard_map/ppermute | solution.py:414
  132.8 6.0 %collective-permute-start.40 = (bf16[1,16,2176]{2,1,0:T(8,128)(2,1)S(1)}, bf16[1,16,2176]{2,1,0:T(8,128)(2,1)S(1)}, u32[]{:S(2)}, u32[]{:S(2)}) collective-permute-start(bf16[1,16,2176]{2,1,0:T(8,128)(2,1)S(1)} %get-tuple-element.235), channel_id=1, source_target_pairs={{0,16},{1,17},{2,18},{3,19},{4,20},{5,21},{6,22},{7,23},{8,24},{9,... | collective-permute-start | bytes 208904 | tf_op jit(solution)/shard_map/ppermute | solution.py:414
  135.3 6.5 %collective-permute-start.38 = (bf16[2,136,512]{2,1,0:T(8,128)(2,1)S(1)}, bf16[2,136,512]{2,1,0:T(8,128)(2,1)S(1)}, u32[]{:S(2)}, u32[]{:S(2)}) collective-permute-start(bf16[2,136,512]{2,1,0:T(8,128)(2,1)S(1)} %pad_maximum_fusion.own_ref), channel_id=1, source_target_pairs={{0,4},{4,0},{8,12},{12,8},{16,20},{20,16},{24,28},{28,24},{1,5},{5... | collective-permute-start | bytes 835592 | tf_op jit(solution)/shard_map/ppermute | solution.py:414

commit v3 on v2

--- a/solution.py
+++ b/solution.py
@@ -409,6 +409,47 @@
     bias_ref[...] = held[held.shape[0] - PAD : held.shape[0] - PAD + 1]
 
 
+def closing_kernel(at_ref, r0, r1, r2, r3, own_ref, other_ref, mine_ref, got_ref, rows_ref, out_ref, *rest):
+    memory_ref, *square_refs, held, sems = rest
+    squares, vectors = square_refs[:4], square_refs[4:]
+    me, first = at_ref[3], at_ref[5]
+    copies = [pltpu.make_async_copy(ref, rows_ref.at[me ^ k], sems.at[k]) for k, ref in enumerate((r0, r1, r2, r3))]
+    for copy in copies:
+        copy.start()
+    size = own_ref.shape[1]
+    for i, ref in enumerate((own_ref, other_ref)):
+        for j in range(2):
+            start = pl.multiple_of((first ^ (2 * i + j)) * size, size)
+            out_ref[pl.ds(start, size), :] = ref[j].astype(F32)
+    total = mine_ref[0].astype(F32) + got_ref[0].astype(F32)
+    for i, ref in enumerate(squares):
+        ref[...] = total[:, i * D : (i + 1) * D]
+    memory_ref[...] = total[:, 4 * D : 4 * D + MEM]
+    held[...] = jnp.zeros(held.shape, F32)
+    held[: total.shape[0]] = total[:, 4 * D :]
+    tall = held[...].T
+    for i, ref in enumerate(vectors):
+        ref[...] = tall[MEM + i : MEM + i + 1, : total.shape[0]]
+    for copy in copies:
+        copy.wait()
+
+
+def closing(at, rows, pair, other, mine, got):
+    n = mine.shape[1]
+    shapes = [sds((4,) + rows[0].shape, LOW), sds((D, D), F32), sds((n, MEM), F32)]
+    shapes += [sds((n, D), F32)] * 4 + [sds((1, n), F32)] * 5
+    grad_tokens, grad_outer, grad_memory, *others = call(
+        closing_kernel,
+        shapes,
+        [SMEM] + [VMEM] * 8,
+        [ANY] + [VMEM] * (len(shapes) - 1),
+        [pltpu.VMEM((EXTRA, EXTRA), F32), pltpu.SemaphoreType.DMA((4,))],
+        mib=16,
+    )(at, *rows, pair, other, mine, got)
+    vectors = [v.reshape(-1) for v in others[4:]]
+    return grad_tokens.reshape(-1, D), grad_outer, [grad_memory.T, *others[:4], *vectors]
+
+
 def swap(value, axis, bit):
     n = lax.axis_size(axis)
     return lax.ppermute(value, axis, [(i, i ^ bit) for i in range(n)])
@@ -432,6 +473,13 @@
         bytes_=2 * 2**20,
     )(at, pair, other)
     return grad, bias[0]
+
+
+def split(reduced):
+    reduced = reduced.reshape(-1, WIDE)
+    squares = [reduced[:, i * D : (i + 1) * D] for i in range(4)]
+    vectors = [reduced[:, 4 * D + MEM + i] for i in range(5)]
+    return [reduced[:, 4 * D : 4 * D + MEM].T, *squares, *vectors]
 
 
 def shards(
@@ -448,6 +496,16 @@
     first = (x * 2 + ((me_dp >> 1) & 1)) if by_bits else 0
     at = jnp.stack([me, me_mp // SPANS, later, me_mp, me_dp, first, x]).astype(jnp.int32)
 
+    pick = lambda v, i: lax.dynamic_index_in_dim(v, i, 0, keepdims=False)
+    blocks = tokens.reshape(-1, SPAN, D)
+    own = pick(blocks, me_mp)
+    start = pick(blocks, me_mp - later)
+    cot = pick(cotangent.reshape(-1, SPAN, D), me_mp)
+
+    wi_halves = inner_weight.reshape(2, D // 2, D)
+    wi_near = swap(pick(wi_halves, x), "mp", 2)
+    outer_rows = jnp.concatenate([outer_weight, inner_bias.reshape(1, -1), jnp.zeros((15, D), LOW)], axis=0)
+
     vectors = (first_gain, first_bias, outer_bias, second_gain, second_bias)
     local = call(
         pack_kernel,
@@ -457,27 +515,23 @@
         [pltpu.VMEM((EXTRA, EXTRA), F32)],
         mib=56,
     )(query_weight, key_weight, value_weight, output_weight, memory_init.T, *[v.reshape(1, -1) for v in vectors])
-
-    pick = lambda v, i: lax.dynamic_index_in_dim(v, i, 0, keepdims=False)
-    outer_rows = jnp.concatenate([outer_weight, inner_bias.reshape(1, -1), jnp.zeros((15, D), LOW)], axis=0)
-    wi2 = swap(inner_weight, "mp", 2)
+    wo2 = swap(outer_rows, "mp", 2)
     if by_bits:
         line = [local] + [swap(local, ALL, 8 * j) for j in range(1, 4)]
-        *line, wi2 = tie(*line, wi2)
+        *line, wi_near = tie(*line, wi_near)
+        wi_far = swap(wi_near, "dp", 1)
         line = jnp.concatenate(line, axis=0)
         plane = [line] + [swap(line, ALL, 2 * b) for b in range(1, 4)]
-        *plane, outer_rows = tie(*plane, outer_rows)
+        wi2 = jnp.where(x == 0, jnp.concatenate([wi_near, wi_far]), jnp.concatenate([wi_far, wi_near]))
+        plane[1], own, start, cot = tie(plane[1], own, start, cot)
+        *plane, wo2, wi2 = tie(*plane, wo2, wi2)
         pieces = plane + [swap(piece, ALL, 1) for piece in plane]
         bits = [[2 * b + c + 8 * j for j in range(4)] for c in range(2) for b in range(4)]
     else:
         pieces = [lax.all_gather(local, ALL, axis=0, tiled=True)]
         bits = [None]
-    wo2 = swap(outer_rows, "mp", 2)
-    wi1, wo1, wi3 = swap(inner_weight, "mp", 1), swap(outer_rows, "mp", 1), swap(wi2, "mp", 1)
-    blocks = tokens.reshape(-1, SPAN, D)
-    own = pick(blocks, me_mp)
-    start = pick(blocks, me_mp - later)
-    cot = pick(cotangent.reshape(-1, SPAN, D), me_mp)
+        wi2 = jnp.concatenate([wi_near, swap(wi_halves[1], "mp", 2)])
+    wi1, wo1, wi3, wo3 = [swap(v, "mp", 1) for v in (inner_weight, outer_rows, wi2, wo2)]
 
     w, qkv = call(
         functools.partial(project_kernel, bits),
@@ -510,8 +564,7 @@
         bytes_=4 * 2**20,
         mib=16,
     )(start, w)
-    nm, m, wo2 = tie(nm, m, wo2)
-    wo3 = swap(wo2, "mp", 1)
+    nm, m, wi1, wi3, wo1, wo3 = tie(nm, m, wi1, wi3, wo1, wo3)
 
     outer_shape = sds((2, 4, D // 4, D), LOW)
     inner_shape = sds((2, 4, (D + PAD) // 4, D), LOW)
@@ -599,14 +652,15 @@
     gp1, gm1 = heads_backward(half, inner_give)
 
     if by_bits:
-        out_bits = [[2 * b + c + 8 * j for b in range(4) for j in (0, 2, 1, 3)] for c in range(2)]
+        out_bits = [[[2 * b + c + 8 * j for j in (0, 2, 1, 3)] for b in range(4)] for c in range(2)]
+        out_bits = [sum(out_bits[0], []), *out_bits[1]]
     else:
         out_bits = [None]
 
     def weights_backward(gate):
         return call(
             functools.partial(weights_kernel, out_bits),
-            [sds((D // len(out_bits), WIDE), LOW) for _ in out_bits],
+            [sds((len(o) * rows_each if o else D, WIDE), LOW) for o in out_bits],
             [ANY, SMEM] + [VMEM] * 10,
             [VMEM] * len(out_bits),
             [pltpu.VMEM((D, WIDE), LOW)],
@@ -619,14 +673,13 @@
         halves_of = lambda v: (v[: v.shape[0] // 2], v[v.shape[0] // 2 :])
         both = lambda mine, got: [add_low(u, v) for u, v in zip(halves_of(mine), halves_of(got), strict=True)]
 
-        a_mine, a_give = [g.reshape(16, rows_each, WIDE) for g in weights_backward(inner_give)]
-        a_got = swap(a_give, ALL, 1)
+        a_mine, *a_give = [g.reshape(-1, rows_each, WIDE) for g in weights_backward(inner_give)]
+        a_got = [swap(g, ALL, 1) for g in a_give]
+
         grad_rows = tokens_backward(inner_give)
-
         rows_got = swap(grad_rows, "mp", 1)
-        out_got, out_across = swap(out, "mp", 1), swap(out, "mp", 2)
-
-        outer_y, out_across, grad_rows = tie(outer_y, out_across, grad_rows)
+
+        outer_y, grad_rows, a_mine = tie(outer_y, grad_rows, a_mine)
         q_mine, q_give = both(outer_mine, outer_y)
         q_got = swap(q_give, "dp", 1)
 
@@ -634,74 +687,74 @@
         p_mine, p_give = add_low(inner_mine[0], inner_x[0]), add_low(inner_mine[1], inner_x[1])
         p_got = swap(p_give, "mp", 2)
 
-        out_across, p_mine = tie(out_across, p_mine)
-        out_last = swap(out_across, "mp", 1)
-        layer_out = place(at, [out, out_got, out_across, out_last])
-
-        q_got, layer_out = tie(q_got, layer_out)
+        *a_got, p_mine = tie(*a_got, p_mine)
+        a_mine, a_give = both(a_mine, jnp.concatenate(a_got))
+        a_got = swap(a_give, ALL, 4)
+
+        q_got, a_mine = tie(q_got, a_mine)
         q_mine, q_give = [v[0] for v in both(q_mine, q_got)]
         q_got = swap(q_give, "dp", 2)
 
-        p_got, q_mine = tie(p_got, q_mine)
+        grad_rows, q_mine = tie(grad_rows, q_mine)
+        rows_across = swap(grad_rows, "mp", 2)
+
+        p_got, grad_rows = tie(p_got, grad_rows)
         p_mine, p_give = [v[0] for v in both(p_mine, p_got)]
         p_got = swap(p_give, "dp", 2)
 
+        q_got, p_mine = tie(q_got, p_mine)
+        q_mine = add_low(q_mine, q_got)
+        q_got = swap(q_mine, "dp", 4)
+
+        out, q_mine = tie(out, q_mine)
+        out_got, out_across = swap(out, "mp", 1), swap(out, "mp", 2)
+
+        p_got, out = tie(p_got, out)
+        p_mine = add_low(p_mine, p_got)
+        p_got = swap(p_mine, "dp", 4)
+
         a_got, p_mine = tie(a_got, p_mine)
         a_mine, a_give = both(a_mine, a_got)
-        a_got = swap(a_give, ALL, 4)
-
-        grad_rows, a_mine = tie(grad_rows, a_mine)
-        rows_across = swap(grad_rows, "mp", 2)
+        a_got = swap(a_give, ALL, 2)
 
         q_got, a_mine = tie(q_got, a_mine)
         q_mine = add_low(q_mine, q_got)
-        q_got = swap(q_mine, "dp", 4)
-
-        p_got, q_mine = tie(p_got, q_mine)
-        p_mine = add_low(p_mine, p_got)
-        p_got = swap(p_mine, "dp", 4)
-
-        q_got, p_mine = tie(q_got, p_mine)
-        q_mine = add_low(q_mine, q_got)
         q_got = swap(q_mine, "dp", 2)
 
-        a_got, q_mine = tie(a_got, q_mine)
+        rows_across, q_mine = tie(rows_across, q_mine)
+        rows_last = swap(rows_across, "mp", 1)
+
+        a_got, rows_across = tie(a_got, rows_across)
         a_mine, a_give = both(a_mine, a_got)
-        a_got = swap(a_give, ALL, 2)
+        a_got = swap(a_give, ALL, 8)
 
         p_got, a_mine = tie(p_got, a_mine)
         p_mine = add_low(p_mine, p_got)
         p_got = swap(p_mine, "dp", 2)
 
-        rows_across, p_mine = tie(rows_across, p_mine)
-        rows_last = swap(rows_across, "mp", 1)
-
-        q_got, rows_across = tie(q_got, rows_across)
+        q_got, p_mine = tie(q_got, p_mine)
         q_pair = jnp.stack([q_mine, q_got])
         q_got = swap(q_pair, "dp", 1)
 
-        a_got, q_pair = tie(a_got, q_pair)
-        a_mine, a_give = both(a_mine, a_got)
-        a_got = swap(a_give, ALL, 8)
-
-        p_got, a_mine = tie(p_got, a_mine)
+        out_across, q_pair = tie(out_across, q_pair)
+        out_last = swap(out_across, "mp", 1)
+
+        p_got, out_across = tie(p_got, out_across)
         p_pair = jnp.stack([p_mine, p_got])
         p_got = swap(p_pair, "dp", 1)
 
-        rows_last, p_pair = tie(rows_last, p_pair)
-        grad_tokens = place(at, [grad_rows, rows_got, rows_across, rows_last])
-
-        a_got, grad_tokens = tie(a_got, grad_tokens)
+        a_got, p_pair = tie(a_got, p_pair)
         a_mine, a_give = both(a_mine, a_got)
         a_got = swap(a_give, ALL, 16)
 
-        q_got, a_mine = tie(q_got, a_mine)
-        grad_outer, _ = finish(at, q_pair, q_got)
-
-        a_got, grad_outer = tie(a_got, grad_outer)
-        reduced = a_mine.astype(F32) + a_got.astype(F32)
-
-        p_got, reduced = tie(p_got, reduced)
+        out_last, a_mine = tie(out_last, a_mine)
+        layer_out = place(at, [out, out_got, out_across, out_last])
+
+        rows_last, q_got, a_got, layer_out = tie(rows_last, q_got, a_got, layer_out)
+        rows = [grad_rows, rows_got, rows_across, rows_last]
+        grad_tokens, grad_outer, outputs = closing(at, rows, q_pair, q_got, a_mine, a_got)
+
+        p_got, grad_outer = tie(p_got, grad_outer)
         grad_inner, grad_inner_bias = finish(at, p_pair, p_got)
     else:
         grad_outer = lax.psum(outer_mine.astype(F32) + outer_y.astype(F32), "dp").reshape(-1, D)
@@ -712,25 +765,22 @@
         grad_tokens = lax.all_gather(grad_rows, "mp", axis=0, tiled=True)
         inner = lax.psum(inner[0].astype(F32) + swap(inner[1], "mp", 2).astype(F32), "dp").reshape(-1, D)
         grad_inner, grad_inner_bias = inner[:D], inner[D]
-        reduced = lax.psum_scatter(grads[0], ALL, scatter_dimension=0, tiled=True).astype(F32)
-    reduced = reduced.reshape(rows_each, WIDE)
-    vector = lambda i: reduced[:, 4 * D + MEM + i]
+        outputs = split(lax.psum_scatter(grads[0], ALL, scatter_dimension=0, tiled=True).astype(F32))
+    grad_memory, grad_query, grad_key, grad_value, grad_output, *grad_vectors = outputs
     return (
         layer_out,
         grad_tokens,
-        reduced[:, 4 * D : 4 * D + MEM].T,
-        reduced[:, :D],
-        reduced[:, D : 2 * D],
-        reduced[:, 2 * D : 3 * D],
-        reduced[:, 3 * D : 4 * D],
-        vector(0),
-        vector(1),
+        grad_memory,
+        grad_query,
+        grad_key,
+        grad_value,
+        grad_output,
+        grad_vectors[0],
+        grad_vectors[1],
         grad_inner,
         grad_inner_bias,
         grad_outer,
-        vector(2),
-        vector(3),
-        vector(4),
+        *grad_vectors[2:],
     )
 
 

time: 146 us -> 136 us (0.932)
  waiting for transfers between devices: 56.8 us -> 47.9 us
    ppermute x41 -> x45, waiting for transfers between devices: 56.8 us -> 47.9 us  [swap(): return lax.ppermute(value, axis, [(i, i ^ bit) for i in range(n)])]
    pallas_call x1 -> x2, Pallas kernels: 2.57 us -> 5.5 us  [the longest x1 2.92 us: closing(): call(closing_kernel, shapes, [SMEM] + [VMEM] * 8, [ANY] + [VMEM] * (len(s...]
    squeeze x2, local copies, waits for them, and re-layouts: 1.31 us -> 3.45 us  [shards(): pick = lambda v, i: lax.dynamic_index_in_dim(v, i, 0, keepdims=False)]
    pallas_call x2 -> x1, Pallas kernels: 3.78 us -> 1.89 us  [place(): call(place_kernel, sds((4,) + pieces[0].shape, pieces[0].dtype), [SMEM] +...]
    pallas_call x2 -> x1, Pallas kernels: 3.31 us -> 1.66 us  [finish(): call(finish_kernel, [sds((D, D), F32), sds((1, D), F32)], [SMEM] + [VMEM]...]
    slice x3 -> x0, local copies, waits for them, and re-layouts: 1.5 us -> none  [the longest x1 0.77 us: shards(): vector = lambda i: reduced[:, 4 * D + MEM + i]]
    ppermute x41 -> x45, starting transfers between devices: 38.6 us -> 37.8 us  [swap(): return lax.ppermute(value, axis, [(i, i ^ bit) for i in range(n)])]
  transfers between devices with their start and end apart: 41 -> 45, of which waited for: 22 -> 21; matrix products, arithmetic and copies ran while one was open for 4% -> 6% of each run, Pallas kernels for 20% -> 21%
where the time goes in v3:
time: 136 us; the launch traced here: 135 us
  waiting for transfers between devices  47.9 us (35%)
  Pallas kernels  40.3 us (30%)
  starting transfers between devices  37.8 us (28%)
  local copies, waits for them, and re-layouts  4.36 us (3%)
  other arithmetic  4.19 us (3%)
    ppermute x45, waiting for transfers between devices, swap(): return lax.ppermute(value, axis, [(i, i ^ bit) for i in range(n)])  47.9 us
    ppermute x45, starting transfers between devices, swap(): return lax.ppermute(value, axis, [(i, i ^ bit) for i in range(n)])  37.8 us
    pallas_call x1, Pallas kernels, shards(): call(forward_kernel, [square_low, outer_shape, outer_shape, sds((4, SPAN,...  9.46 us
    pallas_call x2, Pallas kernels, heads_backward(): call(functools.partial(heads_kernel, low_h, low_h + half), [sds((3, some,...  4.48 us
    pallas_call x1, Pallas kernels, shards(): call(attend_kernel, [sds((HEADS, SPAN, SPAN), LOW), sds((D, SPAN), F32),...  3.56 us
    pallas_call x1, Pallas kernels, shards(): call(keep_kernel, [inner_shape, square, sds((D, D), LOW), sds((D, SPAN),...  3.5 us
    squeeze x2, local copies, waits for them, and re-layouts, shards(): pick = lambda v, i: lax.dynamic_index_in_dim(v, i, 0, keepdims=False)  3.45 us
    pallas_call x1, Pallas kernels, closing(): call(closing_kernel, shapes, [SMEM] + [VMEM] * 8, [ANY] + [VMEM] * (len(s...  2.92 us
  transfers between devices with their start and end apart: 45, of which 21 were waited for; matrix products, arithmetic and copies ran while one was open for 6% of the time, Pallas kernels for 21%

profile of v3, /device:TPU:0, one launch (start us, length us, event | category | flops | bytes accessed | tf_op | source)
XLA Modules:
  0.0 135.5 jit_solution(12642092423230948324)
XLA Ops:
  0.7 1.0 dynamic-slice_bitcast_fusion.3
  1.6 3.0 %collective-permute-start.3 = (bf16[256,512]{1,0:T(8,128)(2,1)S(1)}, bf16[256,512]{1,0:T(8,128)(2,1)S(1)}, u32[]{:S(2)}, u32[]{:S(2)}) collective-permute-start(bf16[256,512]{1,0:T(8,128)(2,1)S(1)} %dynamic-slice_bitcast_fusion.3), channel_id=1, source_target_pairs={{0,2},{1,3},{2,0},{3,1},{4,6},{5,7},{6,4},{7,5},{8,10},{9,11},{10,... | collective-permute-start | bytes 786440 | tf_op jit(solution)/shard_map/ppermute | solution.py:455
  4.7 1.5 %shard_map.262 = bf16[16,2176]{1,0:T(8,128)(2,1)} custom-call(bf16[16,512]{1,0:T(8,128)(2,1)} %q_ref.1, bf16[16,512]{1,0:T(8,128)(2,1)} %k_ref.1, bf16[16,512]{1,0:T(8,128)(2,1)} %v_ref.1, bf16[16,512]{1,0:T(8,128)(2,1)} %o_ref.1, bf16[16,20]{1,0:T(8,128)(2,1)} %bitcast.79, bf16[1,16]{1,0:T(2,128)(2,1)} %bitcast.80, bf16[1,16]{1,0:T(2,128)(2,1)} %bitcast.81, ...), custom_call_target="tpu_custom_call" | custom-call | flops 1 | bytes 1 | tf_op jit(solution)/shard_map/pallas_call | solution.py:510
  6.2 1.6 %collective-permute-start = (bf16[16,2176]{1,0:T(8,128)(2,1)}, bf16[16,2176]{1,0:T(8,128)(2,1)S(1)}, u32[]{:S(2)}, u32[]{:S(2)}) collective-permute-start(bf16[16,2176]{1,0:T(8,128)(2,1)} %shard_map.262), channel_id=1, source_target_pairs={{0,8},{1,9},{2,10},{3,11},{4,12},{5,13},{6,14},{7,15},{8,0},{9,1},... | collective-permute-start | bytes 208904 | tf_op jit(solution)/shard_map/ppermute | solution.py:455
  7.8 2.6 %collective-permute-start.1 = (bf16[16,2176]{1,0:T(8,128)(2,1)}, bf16[16,2176]{1,0:T(8,128)(2,1)S(1)}, u32[]{:S(2)}, u32[]{:S(2)}) collective-permute-start(bf16[16,2176]{1,0:T(8,128)(2,1)} %shard_map.262), channel_id=1, source_target_pairs={{0,16},{1,17},{2,18},{3,19},{4,20},{5,21},{6,22},{7,23},{8,24},{9,... | collective-permute-start | bytes 208904 | tf_op jit(solution)/shard_map/ppermute | solution.py:455
  10.6 0.7 reshape.123
  11.3 1.2 maximum_maximum_fusion.wo0
  12.9 2.3 %collective-permute-done.1 = bf16[16,2176]{1,0:T(8,128)(2,1)S(1)} collective-permute-done((bf16[16,2176]{1,0:T(8,128)(2,1)}, bf16[16,2176]{1,0:T(8,128)(2,1)S(1)}, u32[]{:S(2)}, u32[]{:S(2)}) %collective-permute-start.1) | collective-permute-done | bytes 69664 | tf_op jit(solution)/shard_map/ppermute | solution.py:455
  15.2 1.5 %collective-permute-done.2 = bf16[16,2176]{1,0:T(8,128)(2,1)S(1)} collective-permute-done((bf16[16,2176]{1,0:T(8,128)(2,1)}, bf16[16,2176]{1,0:T(8,128)(2,1)S(1)}, u32[]{:S(2)}, u32[]{:S(2)}) %collective-permute-start.2) | collective-permute-done | bytes 69664 | tf_op jit(solution)/shard_map/ppermute | solution.py:455
  16.7 1.6 %collective-permute-start.8 = (bf16[256,512]{1,0:T(8,128)(2,1)S(1)}, bf16[256,512]{1,0:T(8,128)(2,1)}, u32[]{:S(2)}, u32[]{:S(2)}) collective-permute-start(bf16[256,512]{1,0:T(8,128)(2,1)S(1)} %collective-permute-done.3), channel_id=1, source_target_pairs={{0,4},{4,0},{8,12},{12,8},{16,20},{20,16},{24,28},{28,24},{1,5},{5... | collective-permute-start | bytes 786440 | tf_op jit(solution)/shard_map/ppermute | solution.py:455
  18.3 0.6 collective-permute-start.4
  18.9 0.5 collective-permute-start.5
  19.4 2.4 %collective-permute-start.6 = (bf16[64,2176]{1,0:T(8,128)(2,1)S(1)}, bf16[64,2176]{1,0:T(8,128)(2,1)}, u32[]{:S(2)}, u32[]{:S(2)}) collective-permute-start(bf16[64,2176]{1,0:T(8,128)(2,1)S(1)} %constant_dynamic-update-slice_fusion.refs_0_), channel_id=1, source_target_pairs={{0,6},{1,7},{2,4},{3,5},{4,2},{5,3},{6,0},{7,1},{8,14},{9,15},{10,... | collective-permute-start | bytes 835592 | tf_op jit(solution)/shard_map/ppermute | solution.py:455
  21.9 2.5 %dynamic-slice_bitcast_fusion.1 = (bf16[512,512]{1,0:T(8,128)(2,1)}, bf16[512,512]{1,0:T(8,128)(2,1)S(1)}, bf16[512,512]{1,0:T(8,128)(2,1)}) fusion(bf16[4,512,512]{2,1,0:T(8,128)(2,1)} %bitcast.74, s32[]{:T(128)S(6)} %select_n.35, s32[]{:T(128)S(6)} %select_n.34, bf16[4,512,512]{2,1,0:T(8,128)(2,1)} %bitcast.77), kind=kLoop, calls=%fused_computation.18 | loop fusion | bytes 3145736 | tf_op jit(solution)/shard_map/jit(dynamic_index_in_dim)/squeeze | solution.py:499
  24.4 1.8 %collective-permute-done.8 = bf16[256,512]{1,0:T(8,128)(2,1)} collective-permute-done((bf16[256,512]{1,0:T(8,128)(2,1)S(1)}, bf16[256,512]{1,0:T(8,128)(2,1)}, u32[]{:S(2)}, u32[]{:S(2)}) %collective-permute-start.8) | collective-permute-done | bytes 262176 | tf_op jit(solution)/shard_map/ppermute | solution.py:455
  26.1 1.2 maximum_select_fusion.wi2
  27.3 10.3 %collective-permute-done.4.refs_1_ = bf16[64,2176]{1,0:T(8,128)(2,1)} collective-permute-done((bf16[64,2176]{1,0:T(8,128)(2,1)S(1)}, bf16[64,2176]{1,0:T(8,128)(2,1)}, u32[]{:S(2)}, u32[]{:S(2)}) %collective-permute-start.4) | collective-permute-done | bytes 278560 | tf_op jit(solution)/shard_map/ppermute | solution.py:455
  37.7 0.5 collective-permute-start.10
  38.9 0.5 collective-permute-done.9.refs_4_
  39.5 0.5 collective-permute-done.10.refs_5_
  40.5 0.7 collective-permute-done.12.refs_7_
  41.2 2.7 %shard_map.263 = (bf16[512,2176]{1,0:T(8,128)(2,1)S(1)}, bf16[1536,512]{1,0:T(8,128)(2,1)S(1)}) custom-call(s32[7]{0:T(128)S(1)} %stack.49.at_ref, bf16[64,2176]{1,0:T(8,128)(2,1)S(1)} %constant_dynamic-update-slice_fusion.refs_0_, bf16[64,2176]{1,0:T(8,128)(2,1)} %collective-permute-done.4.refs_1_, bf16[64,2176]{1,0:T(8,128)(2,1)} %collective-permute-done.5.refs_2_, ...), custom_call_target="tpu_custom_call" | custom-call | flops 2000000000 | bytes 5242880 | tf_op jit(solution)/shard_map/pallas_call | solution.py:536
  43.9 2.3 %shard_map.264 = (f32[32,512]{1,0:T(8,128)S(1)}, f32[32,512]{1,0:T(8,128)S(1)}) custom-call(bf16[512,512]{1,0:T(8,128)(2,1)S(1)} %copy-done.2, bf16[512,2176]{1,0:T(8,128)(2,1)S(1)} %get-tuple-element.150.w_ref), custom_call_target="tpu_custom_call" | custom-call | flops 3000000000 | bytes 4194304 | tf_op jit(solution)/shard_map/pallas_call | solution.py:558
  46.2 3.6 %shard_map.265 = (bf16[8,512,512]{2,1,0:T(8,128)(2,1)S(1)}, f32[512,512]{1,0:T(8,128)S(1)}, f32[8,512]{1,0:T(8,128)S(1)}, f32[8,512]{1,0:T(8,128)S(1)}) custom-call(bf16[1536,512]{1,0:T(8,128)(2,1)S(1)} %get-tuple-element.152.qkv_ref), custom_call_target="tpu_custom_call" | custom-call | flops 5000000000 | bytes 7340032 | tf_op jit(solution)/shard_map/pallas_call | solution.py:544
  49.8 9.5 %shard_map.266 = (bf16[512,512]{1,0:T(8,128)(2,1)S(1)}, bf16[2,4,128,512]{3,2,1,0:T(8,128)(2,1)S(1)}, bf16[2,4,128,512]{3,2,1,0:T(8,128)(2,1)S(1)}, bf16[4,512,5...) custom-call(s32[7]{0:T(128)S(1)} %stack.49.at_ref, ...), custom_call_target="tpu_custom_call" | custom-call | flops 10000000000 | bytes 14680064 | tf_op jit(solution)/shard_map/pallas_call | solution.py:574
  59.5 2.5 %shard_map.267 = (bf16[2,4,136,512]{3,2,1,0:T(8,128)(2,1)S(1)}, f32[512,512]{1,0:T(8,128)S(1)}) custom-call(s32[7]{0:T(128)S(1)} %stack.49.at_ref, bf16[512,512]{1,0:T(8,128)(2,1)S(1)} %collective-permute-done.13.wi1, bf16[512,512]{1,0:T(8,128)(2,1)S(1)} %collective-permute-done.14.wi3, bf16[528,512]{1,0:T(8,128)(2,1)S(1)} %collective-permute-done.15.wo1, ...), custom_call_target="tpu_custom_call" | custom-call | flops 1 | bytes 1 | tf_op jit(solution)/shard_map/pallas_call | solution.py:606
  62.0 0.4 collective-permute-start.19
  62.8 0.6 collective-permute-start.18
  63.4 3.5 %shard_map.268 = (bf16[2,4,136,512]{3,2,1,0:T(8,128)(2,1)S(1)}, f32[512,512]{1,0:T(8,128)S(1)}, bf16[512,512]{1,0:T(8,128)(2,1)S(1)}, bf16[512,512]{1,0:T(8,128)(2,1)S(1)}, f32[8,512]{1,0:T(8,128)S(1)}) custom-call(s32[7]{0:T(128)S(1)} %stack.49.at_ref, bf16[4,128,512]{2,1,0:T(8,128)(2,1)S(1)} %get-tuple-element.264.after_ref, ...), custom_call_target="tpu_custom_call" | custom-call | flops 1 | bytes 1 | tf_op jit(solution)/shard_map/pallas_call | solution.py:617
  67.2 1.6 %collective-permute-start.20 = (bf16[2,2,136,512]{3,2,1,0:T(8,128)(2,1)S(1)}, bf16[2,2,136,512]{3,2,1,0:T(8,128)(2,1)S(1)}, u32[]{:S(2)}, u32[]{:S(2)}) collective-permute-start(bf16[2,2,136,512]{3,2,1,0:T(8,128)(2,1)S(1)} %get-tuple-element.262.after_ref), channel_id=1, source_target_pairs={{0,4},{4,0},{8,12},{12,8},{16,20},{20,16},{24,28},{28,24},{1,5},{5... | collective-permute-start | bytes 1671176 | tf_op jit(solution)/shard_map/ppermute | solution.py:455
  68.8 2.2 %shard_map.269 = (bf16[3,256,512]{2,1,0:T(8,128)(2,1)S(1)}, f32[2,32,256]{2,1,0:T(8,128)S(1)}) custom-call(bf16[2,2,136,512]{3,2,1,0:T(8,128)(2,1)S(1)} %get-tuple-element.262.after_ref, bf16[1536,512]{1,0:T(8,128)(2,1)S(1)} %get-tuple-element.152.qkv_ref, bf16[8,512,512]{2,1,0:T(8,128)(2,1)S(1)} %get-tuple-element.178.p_ref, ...), custom_call_target="tpu_custom_call" | custom-call | flops 1 | bytes 1 | tf_op jit(solution)/shard_map/pallas_call | solution.py:634
  71.0 2.2 %shard_map.270 = (bf16[3,256,512]{2,1,0:T(8,128)(2,1)S(1)}, f32[2,32,256]{2,1,0:T(8,128)S(1)}) custom-call(bf16[2,2,136,512]{3,2,1,0:T(8,128)(2,1)S(1)} %get-tuple-element.262.after_ref, bf16[1536,512]{1,0:T(8,128)(2,1)S(1)} %get-tuple-element.152.qkv_ref, bf16[8,512,512]{2,1,0:T(8,128)(2,1)S(1)} %get-tuple-element.178.p_ref, ...), custom_call_target="tpu_custom_call" | custom-call | flops 1 | bytes 1 | tf_op jit(solution)/shard_map/pallas_call | solution.py:634
  73.3 1.2 shard_map.271.r0
  74.5 2.6 %shard_map.272 = (bf16[256,2176]{1,0:T(8,128)(2,1)S(1)}, bf16[64,2176]{1,0:T(8,128)(2,1)S(1)}, bf16[64,2176]{1,0:T(8,128)(2,1)S(1)}, bf16[64,2176]{1,0:T(8,128)(2,1)S(1)}, bf16[64,2176]{1,0:T(8,128)(2,1)S(1)}) custom-call(bf16[2,2,136,512]{3,2,1,0:T(8,128)(2,1)S(1)} %get-tuple-element.262.after_ref, s32[7]{0:T(128)S(1)} %stack.49.at_ref, ...), custom_call_target="tpu_custom_call" | custom-call | flops 1 | bytes 1 | tf_op jit(solution)/shard_map/pallas_call | solution.py:661
  77.2 0.5 collective-permute-start.23
  78.3 3.4 %collective-permute-done.20 = bf16[2,2,136,512]{3,2,1,0:T(8,128)(2,1)S(1)} collective-permute-done((bf16[2,2,136,512]{3,2,1,0:T(8,128)(2,1)S(1)}, bf16[2,2,136,512]{3,2,1,0:T(8,128)(2,1)S(1)}, u32[]{:S(2)}, u32[]{:S(2)}) %collective-permute-start.20) | collective-permute-done | bytes 557088 | tf_op jit(solution)/shard_map/ppermute | solution.py:455
  81.7 1.5 %collective-permute-start.21 = (bf16[2,128,512]{2,1,0:T(8,128)(2,1)S(1)}, bf16[2,128,512]{2,1,0:T(8,128)(2,1)S(1)}, u32[]{:S(2)}, u32[]{:S(2)}) collective-permute-start(bf16[2,128,512]{2,1,0:T(8,128)(2,1)S(1)} %get-tuple-element.274), channel_id=1, source_target_pairs={{0,4},{4,0},{8,12},{12,8},{16,20},{20,16},{24,28},{28,24},{1,5},{5... | collective-permute-start | bytes 786440 | tf_op jit(solution)/shard_map/ppermute | solution.py:455
  83.4 1.6 %collective-permute-start.28 = (bf16[2,136,512]{2,1,0:T(8,128)(2,1)S(1)}, bf16[2,136,512]{2,1,0:T(8,128)(2,1)S(1)}, u32[]{:S(2)}, u32[]{:S(2)}) collective-permute-start(bf16[2,136,512]{2,1,0:T(8,128)(2,1)S(1)} %get-tuple-element.271), channel_id=1, source_target_pairs={{0,2},{1,3},{2,0},{3,1},{4,6},{5,7},{6,4},{7,5},{8,10},{9,11},{10,... | collective-permute-start | bytes 835592 | tf_op jit(solution)/shard_map/ppermute | solution.py:455
  85.2 0.6 collective-permute-start.30
  85.8 5.1 %collective-permute-done.21 = bf16[2,128,512]{2,1,0:T(8,128)(2,1)S(1)} collective-permute-done((bf16[2,128,512]{2,1,0:T(8,128)(2,1)S(1)}, bf16[2,128,512]{2,1,0:T(8,128)(2,1)S(1)}, u32[]{:S(2)}, u32[]{:S(2)}) %collective-permute-start.21) | collective-permute-done | bytes 262176 | tf_op jit(solution)/shard_map/ppermute | solution.py:455
  91.0 1.6 %collective-permute-start.26 = (bf16[512,512]{1,0:T(8,128)(2,1)S(1)}, bf16[512,512]{1,0:T(8,128)(2,1)S(1)}, u32[]{:S(2)}, u32[]{:S(2)}) collective-permute-start(bf16[512,512]{1,0:T(8,128)(2,1)S(1)} %shard_map.271.r0), channel_id=1, source_target_pairs={{0,2},{1,3},{2,0},{3,1},{4,6},{5,7},{6,4},{7,5},{8,10},{9,11},{10,... | collective-permute-start | bytes 1572872 | tf_op jit(solution)/shard_map/ppermute | solution.py:455
  92.6 0.6 collective-permute-start.27
  93.3 1.5 %collective-permute-start.31 = (bf16[136,512]{1,0:T(8,128)(2,1)S(1)}, bf16[136,512]{1,0:T(8,128)(2,1)S(1)}, u32[]{:S(2)}, u32[]{:S(2)}) collective-permute-start(bf16[136,512]{1,0:T(8,128)(2,1)S(1)} %get-tuple-element.277), channel_id=1, source_target_pairs={{0,8},{4,12},{8,0},{12,4},{16,24},{20,28},{24,16},{28,20},{1,9},{5... | collective-permute-start | bytes 417800 | tf_op jit(solution)/shard_map/ppermute | solution.py:455
  94.7 4.1 %collective-permute-done.27 = bf16[128,512]{1,0:T(8,128)(2,1)S(1)} collective-permute-done((bf16[128,512]{1,0:T(8,128)(2,1)S(1)}, bf16[128,512]{1,0:T(8,128)(2,1)S(1)}, u32[]{:S(2)}, u32[]{:S(2)}) %collective-permute-start.27) | collective-permute-done | bytes 131104 | tf_op jit(solution)/shard_map/ppermute | solution.py:455
  98.8 1.7 %collective-permute-start.29 = (bf16[128,512]{1,0:T(8,128)(2,1)S(1)}, bf16[128,512]{1,0:T(8,128)(2,1)S(1)}, u32[]{:S(2)}, u32[]{:S(2)}) collective-permute-start(bf16[128,512]{1,0:T(8,128)(2,1)S(1)} %add_convert_fusion.17), channel_id=1, source_target_pairs={{0,16},{4,20},{8,24},{12,28},{16,0},{20,4},{24,8},{28,12},{1,17},{... | collective-permute-start | bytes 393224 | tf_op jit(solution)/shard_map/ppermute | solution.py:455
  100.9 1.6 %collective-permute-start.35 = (bf16[4,16,2176]{2,1,0:T(8,128)(2,1)S(1)}, bf16[4,16,2176]{2,1,0:T(8,128)(2,1)S(1)}, u32[]{:S(2)}, u32[]{:S(2)}) collective-permute-start(bf16[4,16,2176]{2,1,0:T(8,128)(2,1)S(1)} %get-tuple-element.267), channel_id=1, source_target_pairs={{0,2},{1,3},{2,0},{3,1},{4,6},{5,7},{6,4},{7,5},{8,10},{9,11},{10,... | collective-permute-start | bytes 835592 | tf_op jit(solution)/shard_map/ppermute | solution.py:455
  102.5 0.5 collective-permute-start.39
  103.0 3.2 %collective-permute-done.29 = bf16[128,512]{1,0:T(8,128)(2,1)S(1)} collective-permute-done((bf16[128,512]{1,0:T(8,128)(2,1)S(1)}, bf16[128,512]{1,0:T(8,128)(2,1)S(1)}, u32[]{:S(2)}, u32[]{:S(2)}) %collective-permute-start.29) | collective-permute-done | bytes 131104 | tf_op jit(solution)/shard_map/ppermute | solution.py:455
  106.5 2.9 %collective-permute-start.33 = (bf16[128,512]{1,0:T(8,128)(2,1)S(1)}, bf16[128,512]{1,0:T(8,128)(2,1)S(1)}, u32[]{:S(2)}, u32[]{:S(2)}) collective-permute-start(bf16[128,512]{1,0:T(8,128)(2,1)S(1)} %add_convert_fusion.16), channel_id=1, source_target_pairs={{0,8},{4,12},{8,0},{12,4},{16,24},{20,28},{24,16},{28,20},{1,9},{5... | collective-permute-start | bytes 393224 | tf_op jit(solution)/shard_map/ppermute | solution.py:455
  109.4 1.2 collective-permute-done.35
  110.7 2.9 %collective-permute-done.34 = bf16[136,512]{1,0:T(8,128)(2,1)S(1)} collective-permute-done((bf16[136,512]{1,0:T(8,128)(2,1)S(1)}, bf16[136,512]{1,0:T(8,128)(2,1)S(1)}, u32[]{:S(2)}, u32[]{:S(2)}) %collective-permute-start.34) | collective-permute-done | bytes 139296 | tf_op jit(solution)/shard_map/ppermute | solution.py:455
  114.0 0.5 collective-permute-done.33
  114.5 1.2 collective-permute-start.37
  115.7 3.4 %collective-permute-done.39.r2 = bf16[512,512]{1,0:T(8,128)(2,1)S(1)} collective-permute-done((bf16[512,512]{1,0:T(8,128)(2,1)S(1)}, bf16[512,512]{1,0:T(8,128)(2,1)S(1)}, u32[]{:S(2)}, u32[]{:S(2)}) %collective-permute-start.39) | collective-permute-done | bytes 524320 | tf_op jit(solution)/shard_map/ppermute | solution.py:455
  119.1 1.0 collective-permute-done.38
  120.1 1.5 %collective-permute-start.36 = (bf16[2,128,512]{2,1,0:T(8,128)(2,1)S(1)}, bf16[2,128,512]{2,1,0:T(8,128)(2,1)S(1)}, u32[]{:S(2)}, u32[]{:S(2)}) collective-permute-start(bf16[2,128,512]{2,1,0:T(8,128)(2,1)S(1)} %pad_maximum_fusion.1.own_ref), channel_id=1, source_target_pairs={{0,4},{4,0},{8,12},{12,8},{16,20},{20,16},{24,28},{28,24},{1,5},{5... | collective-permute-start | bytes 786440 | tf_op jit(solution)/shard_map/ppermute | solution.py:455
  121.7 1.4 %collective-permute-start.44 = (bf16[2,136,512]{2,1,0:T(8,128)(2,1)S(1)}, bf16[2,136,512]{2,1,0:T(8,128)(2,1)S(1)}, u32[]{:S(2)}, u32[]{:S(2)}) collective-permute-start(bf16[2,136,512]{2,1,0:T(8,128)(2,1)S(1)} %pad_maximum_fusion.own_ref), channel_id=1, source_target_pairs={{0,4},{4,0},{8,12},{12,8},{16,20},{20,16},{24,28},{28,24},{1,5},{5... | collective-permute-start | bytes 835592 | tf_op jit(solution)/shard_map/ppermute | solution.py:455
  123.1 0.5 collective-permute-done.42.r3
  123.6 0.7 collective-permute-start.40
  124.3 1.9 %shard_map.273 = bf16[4,512,512]{2,1,0:T(8,128)(2,1)} custom-call(s32[7]{0:T(128)S(1)} %stack.49.at_ref, bf16[512,512]{1,0:T(8,128)(2,1)S(1)} %get-tuple-element.233.r0, bf16[512,512]{1,0:T(8,128)(2,1)S(1)} %collective-permute-done.41.r1, bf16[512,512]{1,0:T(8,128)(2,1)S(1)} %collective-permute-done.39.r2, bf16[512,512]{1,0:T(8,128)(2,1)S(1)} %collective-permute-done.42.r3), custom_call_target="tpu_custom_call" | custom-call | flops 1 | bytes 1 | tf_op jit(solution)/shard_map/pallas_call | solution.py:390
  126.2 3.9 %collective-permute-done.40.got_ref = bf16[1,16,2176]{2,1,0:T(8,128)(2,1)S(1)} collective-permute-done((bf16[1,16,2176]{2,1,0:T(8,128)(2,1)S(1)}, bf16[1,16,2176]{2,1,0:T(8,128)(2,1)S(1)}, u32[]{:S(2)}, u32[]{:S(2)}) %collective-permute-start.40) | collective-permute-done | bytes 69664 | tf_op jit(solution)/shard_map/ppermute | solution.py:455
  130.1 2.9 %shard_map.274 = (bf16[4,512,512]{2,1,0:T(8,128)(2,1)}, f32[512,512]{1,0:T(8,128)}, f32[16,20]{1,0:T(8,128)}, f32[16,512]{1,0:T(8,128)}, f32[16,512]{1,0:T(8,128...) custom-call(s32[7]{0:T(128)S(1)} %stack.49.at_ref, ...), custom_call_target="tpu_custom_call" | custom-call | flops 1 | bytes 1 | tf_op jit(solution)/shard_map/pallas_call | solution.py:441
  133.0 0.8 collective-permute-done.44.other_ref
  133.8 1.7 %shard_map.275 = (f32[512,512]{1,0:T(8,128)}, f32[1,512]{1,0:T(1,128)}) custom-call(s32[7]{0:T(128)S(1)} %stack.49.at_ref, bf16[2,136,512]{2,1,0:T(8,128)(2,1)S(1)} %pad_maximum_fusion.own_ref, bf16[2,136,512]{2,1,0:T(8,128)(2,1)S(1)} %collective-permute-done.44.other_ref), custom_call_target="tpu_custom_call" | custom-call | flops 1 | bytes 2097152 | tf_op jit(solution)/shard_map/pallas_call | solution.py:467
  (76 shorter events, 5.7 us)
Async XLA Ops:
  1.6 15.1 %collective-permute-start.3 = (bf16[256,512]{1,0:T(8,128)(2,1)S(1)}, bf16[256,512]{1,0:T(8,128)(2,1)S(1)}, u32[]{:S(2)}, u32[]{:S(2)}) collective-permute-start(bf16[256,512]{1,0:T(8,128)(2,1)S(1)} %dynamic-slice_bitcast_fusion.3), channel_id=1, source_target_pairs={{0,2},{1,3},{2,0},{3,1},{4,6},{5,7},{6,4},{7,5},{8,10},{9,11},{10,... | collective-permute-start | bytes 786440 | tf_op jit(solution)/shard_map/ppermute | solution.py:455
  6.2 10.5 %copy-start.3 = (bf16[16,2176]{1,0:T(8,128)(2,1)S(1)}, bf16[16,2176]{1,0:T(8,128)(2,1)}, u32[]{:S(2)}) copy-start(bf16[16,2176]{1,0:T(8,128)(2,1)} %shard_map.262) | copy-start | bytes 208900
  6.2 6.7 %collective-permute-start = (bf16[16,2176]{1,0:T(8,128)(2,1)}, bf16[16,2176]{1,0:T(8,128)(2,1)S(1)}, u32[]{:S(2)}, u32[]{:S(2)}) collective-permute-start(bf16[16,2176]{1,0:T(8,128)(2,1)} %shard_map.262), channel_id=1, source_target_pairs={{0,8},{1,9},{2,10},{3,11},{4,12},{5,13},{6,14},{7,15},{8,0},{9,1},... | collective-permute-start | bytes 208904 | tf_op jit(solution)/shard_map/ppermute | solution.py:455
  7.8 7.5 %collective-permute-start.1 = (bf16[16,2176]{1,0:T(8,128)(2,1)}, bf16[16,2176]{1,0:T(8,128)(2,1)S(1)}, u32[]{:S(2)}, u32[]{:S(2)}) collective-permute-start(bf16[16,2176]{1,0:T(8,128)(2,1)} %shard_map.262), channel_id=1, source_target_pairs={{0,16},{1,17},{2,18},{3,19},{4,20},{5,21},{6,22},{7,23},{8,24},{9,... | collective-permute-start | bytes 208904 | tf_op jit(solution)/shard_map/ppermute | solution.py:455
  10.3 6.4 %collective-permute-start.2 = (bf16[16,2176]{1,0:T(8,128)(2,1)}, bf16[16,2176]{1,0:T(8,128)(2,1)S(1)}, u32[]{:S(2)}, u32[]{:S(2)}) collective-permute-start(bf16[16,2176]{1,0:T(8,128)(2,1)} %shard_map.262), channel_id=1, source_target_pairs={{0,24},{1,25},{2,26},{3,27},{4,28},{5,29},{6,30},{7,31},{8,16},{9,... | collective-permute-start | bytes 208904 | tf_op jit(solution)/shard_map/ppermute | solution.py:455
  12.6 25.1 %collective-permute-start.7 = (bf16[528,512]{1,0:T(8,128)(2,1)S(1)}, bf16[528,512]{1,0:T(8,128)(2,1)S(1)}, u32[]{:S(2)}, u32[]{:S(2)}) collective-permute-start(bf16[528,512]{1,0:T(8,128)(2,1)S(1)} %maximum_maximum_fusion.wo0), channel_id=1, source_target_pairs={{0,2},{1,3},{2,0},{3,1},{4,6},{5,7},{6,4},{7,5},{8,10},{9,11},{10,... | collective-permute-start | bytes 1622024 | tf_op jit(solution)/shard_map/ppermute | solution.py:455
  16.7 9.4 %collective-permute-start.8 = (bf16[256,512]{1,0:T(8,128)(2,1)S(1)}, bf16[256,512]{1,0:T(8,128)(2,1)}, u32[]{:S(2)}, u32[]{:S(2)}) collective-permute-start(bf16[256,512]{1,0:T(8,128)(2,1)S(1)} %collective-permute-done.3), channel_id=1, source_target_pairs={{0,4},{4,0},{8,12},{12,8},{16,20},{20,16},{24,28},{28,24},{1,5},{5... | collective-permute-start | bytes 786440 | tf_op jit(solution)/shard_map/ppermute | solution.py:455
  18.3 19.3 %collective-permute-start.4 = (bf16[64,2176]{1,0:T(8,128)(2,1)S(1)}, bf16[64,2176]{1,0:T(8,128)(2,1)}, u32[]{:S(2)}, u32[]{:S(2)}) collective-permute-start(bf16[64,2176]{1,0:T(8,128)(2,1)S(1)} %constant_dynamic-update-slice_fusion.refs_0_), channel_id=1, source_target_pairs={{0,2},{1,3},{2,0},{3,1},{4,6},{5,7},{6,4},{7,5},{8,10},{9,11},{10,... | collective-permute-start | bytes 835592 | tf_op jit(solution)/shard_map/ppermute | solution.py:455
  18.9 18.7 %collective-permute-start.5 = (bf16[64,2176]{1,0:T(8,128)(2,1)S(1)}, bf16[64,2176]{1,0:T(8,128)(2,1)}, u32[]{:S(2)}, u32[]{:S(2)}) collective-permute-start(bf16[64,2176]{1,0:T(8,128)(2,1)S(1)} %constant_dynamic-update-slice_fusion.refs_0_), channel_id=1, source_target_pairs={{0,4},{1,5},{2,6},{3,7},{4,0},{5,1},{6,2},{7,3},{8,12},{9,13},{10,... | collective-permute-start | bytes 835592 | tf_op jit(solution)/shard_map/ppermute | solution.py:455
  19.4 18.2 %collective-permute-start.6 = (bf16[64,2176]{1,0:T(8,128)(2,1)S(1)}, bf16[64,2176]{1,0:T(8,128)(2,1)}, u32[]{:S(2)}, u32[]{:S(2)}) collective-permute-start(bf16[64,2176]{1,0:T(8,128)(2,1)S(1)} %constant_dynamic-update-slice_fusion.refs_0_), channel_id=1, source_target_pairs={{0,6},{1,7},{2,4},{3,5},{4,2},{5,3},{6,0},{7,1},{8,14},{9,15},{10,... | collective-permute-start | bytes 835592 | tf_op jit(solution)/shard_map/ppermute | solution.py:455
  21.9 16.8 %copy-start = (bf16[512,512]{1,0:T(8,128)(2,1)S(1)}, bf16[512,512]{1,0:T(8,128)(2,1)}, u32[]{:S(2)}) copy-start(bf16[512,512]{1,0:T(8,128)(2,1)} %wi0.3) | copy-start | bytes 1572868
  37.6 1.8 %collective-permute-start.9 = (bf16[64,2176]{1,0:T(8,128)(2,1)S(1)}, bf16[64,2176]{1,0:T(8,128)(2,1)}, u32[]{:S(2)}, u32[]{:S(2)}) collective-permute-start(bf16[64,2176]{1,0:T(8,128)(2,1)S(1)} %constant_dynamic-update-slice_fusion.refs_0_), channel_id=1, source_target_pairs={{0,1},{1,0},{2,3},{3,2},{4,5},{5,4},{6,7},{7,6},{8,9},{9,8},{10,11... | collective-permute-start | bytes 835592 | tf_op jit(solution)/shard_map/ppermute | solution.py:455
  37.7 2.3 %collective-permute-start.10 = (bf16[64,2176]{1,0:T(8,128)(2,1)}, bf16[64,2176]{1,0:T(8,128)(2,1)}, u32[]{:S(2)}, u32[]{:S(2)}) collective-permute-start(bf16[64,2176]{1,0:T(8,128)(2,1)} %collective-permute-done.4.refs_1_), channel_id=1, source_target_pairs={{0,1},{1,0},{2,3},{3,2},{4,5},{5,4},{6,7},{7,6},{8,9},{9,8},{10,11... | collective-permute-start | bytes 835592 | tf_op jit(solution)/shard_map/ppermute | solution.py:455
  38.2 2.2 %collective-permute-start.11 = (bf16[64,2176]{1,0:T(8,128)(2,1)}, bf16[64,2176]{1,0:T(8,128)(2,1)}, u32[]{:S(2)}, u32[]{:S(2)}) collective-permute-start(bf16[64,2176]{1,0:T(8,128)(2,1)} %collective-permute-done.5.refs_2_), channel_id=1, source_target_pairs={{0,1},{1,0},{2,3},{3,2},{4,5},{5,4},{6,7},{7,6},{8,9},{9,8},{10,11... | collective-permute-start | bytes 835592 | tf_op jit(solution)/shard_map/ppermute | solution.py:455
  38.3 2.9 %collective-permute-start.12 = (bf16[64,2176]{1,0:T(8,128)(2,1)}, bf16[64,2176]{1,0:T(8,128)(2,1)}, u32[]{:S(2)}, u32[]{:S(2)}) collective-permute-start(bf16[64,2176]{1,0:T(8,128)(2,1)} %collective-permute-done.6.refs_3_), channel_id=1, source_target_pairs={{0,1},{1,0},{2,3},{3,2},{4,5},{5,4},{6,7},{7,6},{8,9},{9,8},{10,11... | collective-permute-start | bytes 835592 | tf_op jit(solution)/shard_map/ppermute | solution.py:455
  38.7 11.0 %collective-permute-start.13 = (bf16[512,512]{1,0:T(8,128)(2,1)S(1)}, bf16[512,512]{1,0:T(8,128)(2,1)S(1)}, u32[]{:S(2)}, u32[]{:S(2)}) collective-permute-start(bf16[512,512]{1,0:T(8,128)(2,1)S(1)} %copy-done), channel_id=1, source_target_pairs={{0,1},{1,0},{2,3},{3,2},{4,5},{5,4},{6,7},{7,6},{8,9},{9,8},{10,11... | collective-permute-start | bytes 1572872 | tf_op jit(solution)/shard_map/ppermute | solution.py:455
  38.9 5.0 %copy-start.2 = (bf16[512,512]{1,0:T(8,128)(2,1)S(1)}, bf16[512,512]{1,0:T(8,128)(2,1)}, u32[]{:S(2)}) copy-start(bf16[512,512]{1,0:T(8,128)(2,1)} %get-tuple-element.142.x1_ref) | copy-start | bytes 1572868
  39.4 10.4 %collective-permute-start.15 = (bf16[528,512]{1,0:T(8,128)(2,1)S(1)}, bf16[528,512]{1,0:T(8,128)(2,1)S(1)}, u32[]{:S(2)}, u32[]{:S(2)}) collective-permute-start(bf16[528,512]{1,0:T(8,128)(2,1)S(1)} %maximum_maximum_fusion.wo0), channel_id=1, source_target_pairs={{0,1},{1,0},{2,3},{3,2},{4,5},{5,4},{6,7},{7,6},{8,9},{9,8},{10,11... | collective-permute-start | bytes 1622024 | tf_op jit(solution)/shard_map/ppermute | solution.py:455
  40.0 9.8 %collective-permute-start.14 = (bf16[512,512]{1,0:T(8,128)(2,1)S(1)}, bf16[512,512]{1,0:T(8,128)(2,1)S(1)}, u32[]{:S(2)}, u32[]{:S(2)}) collective-permute-start(bf16[512,512]{1,0:T(8,128)(2,1)S(1)} %maximum_select_fusion.wi2), channel_id=1, source_target_pairs={{0,1},{1,0},{2,3},{3,2},{4,5},{5,4},{6,7},{7,6},{8,9},{9,8},{10,11... | collective-permute-start | bytes 1572872 | tf_op jit(solution)/shard_map/ppermute | solution.py:455
  40.4 9.4 %collective-permute-start.16 = (bf16[528,512]{1,0:T(8,128)(2,1)S(1)}, bf16[528,512]{1,0:T(8,128)(2,1)S(1)}, u32[]{:S(2)}, u32[]{:S(2)}) collective-permute-start(bf16[528,512]{1,0:T(8,128)(2,1)S(1)} %collective-permute-done.7.wo2), channel_id=1, source_target_pairs={{0,1},{1,0},{2,3},{3,2},{4,5},{5,4},{6,7},{7,6},{8,9},{9,8},{10,11... | collective-permute-start | bytes 1622024 | tf_op jit(solution)/shard_map/ppermute | solution.py:455
  46.2 3.6 %copy-start.1 = (bf16[512,512]{1,0:T(8,128)(2,1)S(1)}, bf16[512,512]{1,0:T(8,128)(2,1)}, u32[]{:S(2)}) copy-start(bf16[512,512]{1,0:T(8,128)(2,1)} %get-tuple-element.165.cot_ref) | copy-start | bytes 1572868
  59.3 3.2 %collective-permute-start.17 = (bf16[2,4,128,512]{3,2,1,0:T(8,128)(2,1)S(1)}, bf16[2,4,128,512]{3,2,1,0:T(8,128)(2,1)S(1)}, u32[]{:S(2)}, u32[]{:S(2)}) collective-permute-start(bf16[2,4,128,512]{3,2,1,0:T(8,128)(2,1)S(1)} %get-tuple-element.167), channel_id=1, source_target_pairs={{0,1},{1,0},{2,3},{3,2},{4,5},{5,4},{6,7},{7,6},{8,9},{9,8},{10,11... | collective-permute-start | bytes 3145736 | tf_op jit(solution)/shard_map/ppermute | solution.py:455
  62.0 4.9 %collective-permute-start.19 = (bf16[2,4,136,512]{3,2,1,0:T(8,128)(2,1)S(1)}, bf16[2,4,136,512]{3,2,1,0:T(8,128)(2,1)S(1)}, u32[]{:S(2)}, u32[]{:S(2)}) collective-permute-start(bf16[2,4,136,512]{3,2,1,0:T(8,128)(2,1)S(1)} %get-tuple-element.177), channel_id=1, source_target_pairs={{0,1},{1,0},{2,3},{3,2},{4,5},{5,4},{6,7},{7,6},{8,9},{9,8},{10,11... | collective-permute-start | bytes 3342344 | tf_op jit(solution)/shard_map/ppermute | solution.py:455
  62.8 14.9 %collective-permute-start.18 = (bf16[4,128,512]{2,1,0:T(8,128)(2,1)S(1)}, bf16[4,128,512]{2,1,0:T(8,128)(2,1)S(1)}, u32[]{:S(2)}, u32[]{:S(2)}) collective-permute-start(bf16[4,128,512]{2,1,0:T(8,128)(2,1)S(1)} %get-tuple-element.264.after_ref), channel_id=1, source_target_pairs={{0,2},{1,3},{2,0},{3,1},{4,6},{5,7},{6,4},{7,5},{8,10},{9,11},{10,... | collective-permute-start | bytes 1572872 | tf_op jit(solution)/shard_map/ppermute | solution.py:455
  67.2 14.4 %collective-permute-start.20 = (bf16[2,2,136,512]{3,2,1,0:T(8,128)(2,1)S(1)}, bf16[2,2,136,512]{3,2,1,0:T(8,128)(2,1)S(1)}, u32[]{:S(2)}, u32[]{:S(2)}) collective-permute-start(bf16[2,2,136,512]{3,2,1,0:T(8,128)(2,1)S(1)} %get-tuple-element.262.after_ref), channel_id=1, source_target_pairs={{0,4},{4,0},{8,12},{12,8},{16,20},{20,16},{24,28},{28,24},{1,5},{5... | collective-permute-start | bytes 1671176 | tf_op jit(solution)/shard_map/ppermute | solution.py:455
  77.1 6.2 %collective-permute-start.22 = (bf16[4,16,2176]{2,1,0:T(8,128)(2,1)S(1)}, bf16[4,16,2176]{2,1,0:T(8,128)(2,1)S(1)}, u32[]{:S(2)}, u32[]{:S(2)}) collective-permute-start(bf16[4,16,2176]{2,1,0:T(8,128)(2,1)S(1)} %bitcast.71), channel_id=1, source_target_pairs={{0,1},{1,0},{2,3},{3,2},{4,5},{5,4},{6,7},{7,6},{8,9},{9,8},{10,11... | collective-permute-start | bytes 835592 | tf_op jit(solution)/shard_map/ppermute | solution.py:455
  77.2 6.2 %collective-permute-start.23 = (bf16[4,16,2176]{2,1,0:T(8,128)(2,1)S(1)}, bf16[4,16,2176]{2,1,0:T(8,128)(2,1)S(1)}, u32[]{:S(2)}, u32[]{:S(2)}) collective-permute-start(bf16[4,16,2176]{2,1,0:T(8,128)(2,1)S(1)} %bitcast.70), channel_id=1, source_target_pairs={{0,1},{1,0},{2,3},{3,2},{4,5},{5,4},{6,7},{7,6},{8,9},{9,8},{10,11... | collective-permute-start | bytes 835592 | tf_op jit(solution)/shard_map/ppermute | solution.py:455
  77.7 5.7 %collective-permute-start.24 = (bf16[4,16,2176]{2,1,0:T(8,128)(2,1)S(1)}, bf16[4,16,2176]{2,1,0:T(8,128)(2,1)S(1)}, u32[]{:S(2)}, u32[]{:S(2)}) collective-permute-start(bf16[4,16,2176]{2,1,0:T(8,128)(2,1)S(1)} %bitcast.69), channel_id=1, source_target_pairs={{0,1},{1,0},{2,3},{3,2},{4,5},{5,4},{6,7},{7,6},{8,9},{9,8},{10,11... | collective-permute-start | bytes 835592 | tf_op jit(solution)/shard_map/ppermute | solution.py:455
  77.7 5.6 %collective-permute-start.25 = (bf16[4,16,2176]{2,1,0:T(8,128)(2,1)S(1)}, bf16[4,16,2176]{2,1,0:T(8,128)(2,1)S(1)}, u32[]{:S(2)}, u32[]{:S(2)}) collective-permute-start(bf16[4,16,2176]{2,1,0:T(8,128)(2,1)S(1)} %bitcast.68), channel_id=1, source_target_pairs={{0,1},{1,0},{2,3},{3,2},{4,5},{5,4},{6,7},{7,6},{8,9},{9,8},{10,11... | collective-permute-start | bytes 835592 | tf_op jit(solution)/shard_map/ppermute | solution.py:455
  81.7 9.2 %collective-permute-start.21 = (bf16[2,128,512]{2,1,0:T(8,128)(2,1)S(1)}, bf16[2,128,512]{2,1,0:T(8,128)(2,1)S(1)}, u32[]{:S(2)}, u32[]{:S(2)}) collective-permute-start(bf16[2,128,512]{2,1,0:T(8,128)(2,1)S(1)} %get-tuple-element.274), channel_id=1, source_target_pairs={{0,4},{4,0},{8,12},{12,8},{16,20},{20,16},{24,28},{28,24},{1,5},{5... | collective-permute-start | bytes 786440 | tf_op jit(solution)/shard_map/ppermute | solution.py:455
  83.4 9.8 %collective-permute-start.28 = (bf16[2,136,512]{2,1,0:T(8,128)(2,1)S(1)}, bf16[2,136,512]{2,1,0:T(8,128)(2,1)S(1)}, u32[]{:S(2)}, u32[]{:S(2)}) collective-permute-start(bf16[2,136,512]{2,1,0:T(8,128)(2,1)S(1)} %get-tuple-element.271), channel_id=1, source_target_pairs={{0,2},{1,3},{2,0},{3,1},{4,6},{5,7},{6,4},{7,5},{8,10},{9,11},{10,... | collective-permute-start | bytes 835592 | tf_op jit(solution)/shard_map/ppermute | solution.py:455
  85.2 15.5 %collective-permute-start.30 = (bf16[8,16,2176]{2,1,0:T(8,128)(2,1)S(1)}, bf16[8,16,2176]{2,1,0:T(8,128)(2,1)S(1)}, u32[]{:S(2)}, u32[]{:S(2)}) collective-permute-start(bf16[8,16,2176]{2,1,0:T(8,128)(2,1)S(1)} %get-tuple-element.269), channel_id=1, source_target_pairs={{0,4},{1,5},{2,6},{3,7},{4,0},{5,1},{6,2},{7,3},{8,12},{9,13},{10,... | collective-permute-start | bytes 1671176 | tf_op jit(solution)/shard_map/ppermute | solution.py:455
  91.0 15.5 %collective-permute-start.26 = (bf16[512,512]{1,0:T(8,128)(2,1)S(1)}, bf16[512,512]{1,0:T(8,128)(2,1)S(1)}, u32[]{:S(2)}, u32[]{:S(2)}) collective-permute-start(bf16[512,512]{1,0:T(8,128)(2,1)S(1)} %shard_map.271.r0), channel_id=1, source_target_pairs={{0,2},{1,3},{2,0},{3,1},{4,6},{5,7},{6,4},{7,5},{8,10},{9,11},{10,... | collective-permute-start | bytes 1572872 | tf_op jit(solution)/shard_map/ppermute | solution.py:455
  92.6 6.2 %collective-permute-start.27 = (bf16[128,512]{1,0:T(8,128)(2,1)S(1)}, bf16[128,512]{1,0:T(8,128)(2,1)S(1)}, u32[]{:S(2)}, u32[]{:S(2)}) collective-permute-start(bf16[128,512]{1,0:T(8,128)(2,1)S(1)} %get-tuple-element.279), channel_id=1, source_target_pairs={{0,8},{4,12},{8,0},{12,4},{16,24},{20,28},{24,16},{28,20},{1,9},{5... | collective-permute-start | bytes 393224 | tf_op jit(solution)/shard_map/ppermute | solution.py:455
  93.3 7.3 %collective-permute-start.31 = (bf16[136,512]{1,0:T(8,128)(2,1)S(1)}, bf16[136,512]{1,0:T(8,128)(2,1)S(1)}, u32[]{:S(2)}, u32[]{:S(2)}) collective-permute-start(bf16[136,512]{1,0:T(8,128)(2,1)S(1)} %get-tuple-element.277), channel_id=1, source_target_pairs={{0,8},{4,12},{8,0},{12,4},{16,24},{20,28},{24,16},{28,20},{1,9},{5... | collective-permute-start | bytes 417800 | tf_op jit(solution)/shard_map/ppermute | solution.py:455
  98.8 7.3 %collective-permute-start.29 = (bf16[128,512]{1,0:T(8,128)(2,1)S(1)}, bf16[128,512]{1,0:T(8,128)(2,1)S(1)}, u32[]{:S(2)}, u32[]{:S(2)}) collective-permute-start(bf16[128,512]{1,0:T(8,128)(2,1)S(1)} %add_convert_fusion.17), channel_id=1, source_target_pairs={{0,16},{4,20},{8,24},{12,28},{16,0},{20,4},{24,8},{28,12},{1,17},{... | collective-permute-start | bytes 393224 | tf_op jit(solution)/shard_map/ppermute | solution.py:455
  100.9 9.7 %collective-permute-start.35 = (bf16[4,16,2176]{2,1,0:T(8,128)(2,1)S(1)}, bf16[4,16,2176]{2,1,0:T(8,128)(2,1)S(1)}, u32[]{:S(2)}, u32[]{:S(2)}) collective-permute-start(bf16[4,16,2176]{2,1,0:T(8,128)(2,1)S(1)} %get-tuple-element.267), channel_id=1, source_target_pairs={{0,2},{1,3},{2,0},{3,1},{4,6},{5,7},{6,4},{7,5},{8,10},{9,11},{10,... | collective-permute-start | bytes 835592 | tf_op jit(solution)/shard_map/ppermute | solution.py:455
  102.5 16.6 %collective-permute-start.39 = (bf16[512,512]{1,0:T(8,128)(2,1)S(1)}, bf16[512,512]{1,0:T(8,128)(2,1)S(1)}, u32[]{:S(2)}, u32[]{:S(2)}) collective-permute-start(bf16[512,512]{1,0:T(8,128)(2,1)S(1)} %get-tuple-element.233.r0), channel_id=1, source_target_pairs={{0,2},{1,3},{2,0},{3,1},{4,6},{5,7},{6,4},{7,5},{8,10},{9,11},{10,... | collective-permute-start | bytes 1572872 | tf_op jit(solution)/shard_map/ppermute | solution.py:455
  103.0 18.7 %collective-permute-start.41 = (bf16[512,512]{1,0:T(8,128)(2,1)S(1)}, bf16[512,512]{1,0:T(8,128)(2,1)S(1)}, u32[]{:S(2)}, u32[]{:S(2)}) collective-permute-start(bf16[512,512]{1,0:T(8,128)(2,1)S(1)} %get-tuple-element.233.r0), channel_id=1, source_target_pairs={{0,1},{1,0},{2,3},{3,2},{4,5},{5,4},{6,7},{7,6},{8,9},{9,8},{10,11... | collective-permute-start | bytes 1572872 | tf_op jit(solution)/shard_map/ppermute | solution.py:455
  106.2 7.3 %collective-permute-start.34 = (bf16[136,512]{1,0:T(8,128)(2,1)S(1)}, bf16[136,512]{1,0:T(8,128)(2,1)S(1)}, u32[]{:S(2)}, u32[]{:S(2)}) collective-permute-start(bf16[136,512]{1,0:T(8,128)(2,1)S(1)} %add_convert_fusion.13), channel_id=1, source_target_pairs={{0,16},{4,20},{8,24},{12,28},{16,0},{20,4},{24,8},{28,12},{1,17},{... | collective-permute-start | bytes 417800 | tf_op jit(solution)/shard_map/ppermute | solution.py:455
  106.5 8.0 %collective-permute-start.33 = (bf16[128,512]{1,0:T(8,128)(2,1)S(1)}, bf16[128,512]{1,0:T(8,128)(2,1)S(1)}, u32[]{:S(2)}, u32[]{:S(2)}) collective-permute-start(bf16[128,512]{1,0:T(8,128)(2,1)S(1)} %add_convert_fusion.16), channel_id=1, source_target_pairs={{0,8},{4,12},{8,0},{12,4},{16,24},{20,28},{24,16},{28,20},{1,9},{5... | collective-permute-start | bytes 393224 | tf_op jit(solution)/shard_map/ppermute | solution.py:455
  113.6 6.5 %collective-permute-start.38 = (bf16[136,512]{1,0:T(8,128)(2,1)S(1)}, bf16[136,512]{1,0:T(8,128)(2,1)S(1)}, u32[]{:S(2)}, u32[]{:S(2)}) collective-permute-start(bf16[136,512]{1,0:T(8,128)(2,1)S(1)} %add_convert_fusion.11), channel_id=1, source_target_pairs={{0,8},{4,12},{8,0},{12,4},{16,24},{20,28},{24,16},{28,20},{1,9},{5... | collective-permute-start | bytes 417800 | tf_op jit(solution)/shard_map/ppermute | solution.py:455
  114.0 16.1 %collective-permute-start.43 = (bf16[512,512]{1,0:T(8,128)(2,1)S(1)}, bf16[512,512]{1,0:T(8,128)(2,1)S(1)}, u32[]{:S(2)}, u32[]{:S(2)}) collective-permute-start(bf16[512,512]{1,0:T(8,128)(2,1)S(1)} %shard_map.271.r0), channel_id=1, source_target_pairs={{0,1},{1,0},{2,3},{3,2},{4,5},{5,4},{6,7},{7,6},{8,9},{9,8},{10,11... | collective-permute-start | bytes 1572872 | tf_op jit(solution)/shard_map/ppermute | solution.py:455
  114.5 7.1 %collective-permute-start.37 = (bf16[2,16,2176]{2,1,0:T(8,128)(2,1)S(1)}, bf16[2,16,2176]{2,1,0:T(8,128)(2,1)S(1)}, u32[]{:S(2)}, u32[]{:S(2)}) collective-permute-start(bf16[2,16,2176]{2,1,0:T(8,128)(2,1)S(1)} %get-tuple-element.275), channel_id=1, source_target_pairs={{0,8},{1,9},{2,10},{3,11},{4,12},{5,13},{6,14},{7,15},{8,0},{9,1},... | collective-permute-start | bytes 417800 | tf_op jit(solution)/shard_map/ppermute | solution.py:455
  119.1 10.9 %collective-permute-start.32 = (bf16[512,512]{1,0:T(8,128)(2,1)S(1)}, bf16[512,512]{1,0:T(8,128)(2,1)S(1)}, u32[]{:S(2)}, u32[]{:S(2)}) collective-permute-start(bf16[512,512]{1,0:T(8,128)(2,1)S(1)} %collective-permute-done.26.r2), channel_id=1, source_target_pairs={{0,1},{1,0},{2,3},{3,2},{4,5},{5,4},{6,7},{7,6},{8,9},{9,8},{10,11... | collective-permute-start | bytes 1572872 | tf_op jit(solution)/shard_map/ppermute | solution.py:455
  120.1 10.0 %collective-permute-start.36 = (bf16[2,128,512]{2,1,0:T(8,128)(2,1)S(1)}, bf16[2,128,512]{2,1,0:T(8,128)(2,1)S(1)}, u32[]{:S(2)}, u32[]{:S(2)}) collective-permute-start(bf16[2,128,512]{2,1,0:T(8,128)(2,1)S(1)} %pad_maximum_fusion.1.own_ref), channel_id=1, source_target_pairs={{0,4},{4,0},{8,12},{12,8},{16,20},{20,16},{24,28},{28,24},{1,5},{5... | collective-permute-start | bytes 786440 | tf_op jit(solution)/shard_map/ppermute | solution.py:455
  121.6 2.0 %collective-permute-start.42 = (bf16[512,512]{1,0:T(8,128)(2,1)S(1)}, bf16[512,512]{1,0:T(8,128)(2,1)S(1)}, u32[]{:S(2)}, u32[]{:S(2)}) collective-permute-start(bf16[512,512]{1,0:T(8,128)(2,1)S(1)} %collective-permute-done.39.r2), channel_id=1, source_target_pairs={{0,1},{1,0},{2,3},{3,2},{4,5},{5,4},{6,7},{7,6},{8,9},{9,8},{10,11... | collective-permute-start | bytes 1572872 | tf_op jit(solution)/shard_map/ppermute | solution.py:455
  121.7 12.1 %collective-permute-start.44 = (bf16[2,136,512]{2,1,0:T(8,128)(2,1)S(1)}, bf16[2,136,512]{2,1,0:T(8,128)(2,1)S(1)}, u32[]{:S(2)}, u32[]{:S(2)}) collective-permute-start(bf16[2,136,512]{2,1,0:T(8,128)(2,1)S(1)} %pad_maximum_fusion.own_ref), channel_id=1, source_target_pairs={{0,4},{4,0},{8,12},{12,8},{16,20},{20,16},{24,28},{28,24},{1,5},{5... | collective-permute-start | bytes 835592 | tf_op jit(solution)/shard_map/ppermute | solution.py:455
  123.6 6.5 %collective-permute-start.40 = (bf16[1,16,2176]{2,1,0:T(8,128)(2,1)S(1)}, bf16[1,16,2176]{2,1,0:T(8,128)(2,1)S(1)}, u32[]{:S(2)}, u32[]{:S(2)}) collective-permute-start(bf16[1,16,2176]{2,1,0:T(8,128)(2,1)S(1)} %get-tuple-element.282), channel_id=1, source_target_pairs={{0,16},{1,17},{2,18},{3,19},{4,20},{5,21},{6,22},{7,23},{8,24},{9,... | collective-permute-start | bytes 208904 | tf_op jit(solution)/shard_map/ppermute | solution.py:455

commit v4 on v3

--- a/solution.py
+++ b/solution.py
@@ -503,7 +503,8 @@
     cot = pick(cotangent.reshape(-1, SPAN, D), me_mp)
 
     wi_halves = inner_weight.reshape(2, D // 2, D)
-    wi_near = swap(pick(wi_halves, x), "mp", 2)
+    z = ((me_dp >> 1) & 1) if by_bits else 0
+    wi_near = swap(pick(wi_halves, z), "mp", 2)
     outer_rows = jnp.concatenate([outer_weight, inner_bias.reshape(1, -1), jnp.zeros((15, D), LOW)], axis=0)
 
     vectors = (first_gain, first_bias, outer_bias, second_gain, second_bias)
@@ -515,14 +516,19 @@
         [pltpu.VMEM((EXTRA, EXTRA), F32)],
         mib=56,
     )(query_weight, key_weight, value_weight, output_weight, memory_init.T, *[v.reshape(1, -1) for v in vectors])
-    wo2 = swap(outer_rows, "mp", 2)
+    z = ((me_dp >> 1) & 1) if by_bits else 0
+    wo_halves = outer_weight.reshape(2, D // 2, D)
+    wo_near = swap(jnp.concatenate([pick(wo_halves, z), outer_rows[D:]]), "mp", 2)
     if by_bits:
         line = [local] + [swap(local, ALL, 8 * j) for j in range(1, 4)]
         *line, wi_near = tie(*line, wi_near)
-        wi_far = swap(wi_near, "dp", 1)
+        wi_far = swap(wi_near, "dp", 2)
         line = jnp.concatenate(line, axis=0)
         plane = [line] + [swap(line, ALL, 2 * b) for b in range(1, 4)]
-        wi2 = jnp.where(x == 0, jnp.concatenate([wi_near, wi_far]), jnp.concatenate([wi_far, wi_near]))
+        wi2 = jnp.where(z == 0, jnp.concatenate([wi_near, wi_far]), jnp.concatenate([wi_far, wi_near]))
+        wo_far = swap(wo_near, "dp", 2)
+        top, bottom, biases = wo_near[: D // 2], wo_far[: D // 2], wo_near[D // 2 :]
+        wo2 = jnp.where(z == 0, jnp.concatenate([top, bottom, biases]), jnp.concatenate([bottom, top, biases]))
         plane[1], own, start, cot = tie(plane[1], own, start, cot)
         *plane, wo2, wi2 = tie(*plane, wo2, wi2)
         pieces = plane + [swap(piece, ALL, 1) for piece in plane]
@@ -531,6 +537,7 @@
         pieces = [lax.all_gather(local, ALL, axis=0, tiled=True)]
         bits = [None]
         wi2 = jnp.concatenate([wi_near, swap(wi_halves[1], "mp", 2)])
+        wo2 = jnp.concatenate([wo_near[: D // 2], swap(wo_halves[1], "mp", 2), wo_near[D // 2 :]])
     wi1, wo1, wi3, wo3 = [swap(v, "mp", 1) for v in (inner_weight, outer_rows, wi2, wo2)]
 
     w, qkv = call(

time: 136 us -> 131 us (0.963)
  waiting for transfers between devices: 47.9 us -> 41.8 us
  starting transfers between devices: 37.8 us -> 39.5 us
    ppermute x45 -> x46, waiting for transfers between devices: 47.9 us -> 41.8 us  [swap(): return lax.ppermute(value, axis, [(i, i ^ bit) for i in range(n)])]
    ppermute x45 -> x46, starting transfers between devices: 37.8 us -> 39.5 us  [swap(): return lax.ppermute(value, axis, [(i, i ^ bit) for i in range(n)])]
    squeeze x2 -> x3, local copies, waits for them, and re-layouts: 3.45 us -> 4.19 us  [shards(): pick = lambda v, i: lax.dynamic_index_in_dim(v, i, 0, keepdims=False)]
  transfers between devices with their start and end apart: 45 -> 46, of which waited for: 21 -> 22; matrix products, arithmetic and copies ran while one was open for 6% -> 6% of each run, Pallas kernels for 21% -> 22%
where the time goes in v4:
time: 131 us
  waiting for transfers between devices  41.8 us (32%)
  Pallas kernels  40.1 us (31%)
  starting transfers between devices  39.5 us (30%)
  local copies, waits for them, and re-layouts  5.14 us (4%)
  other arithmetic  3.34 us (3%)
    ppermute x46, waiting for transfers between devices, swap(): return lax.ppermute(value, axis, [(i, i ^ bit) for i in range(n)])  41.8 us
    ppermute x46, starting transfers between devices, swap(): return lax.ppermute(value, axis, [(i, i ^ bit) for i in range(n)])  39.5 us
    pallas_call x1, Pallas kernels, shards(): call(forward_kernel, [square_low, outer_shape, outer_shape, sds((4, SPAN,...  9.5 us
    pallas_call x2, Pallas kernels, heads_backward(): call(functools.partial(heads_kernel, low_h, low_h + half), [sds((3, some,...  4.45 us
    squeeze x3, local copies, waits for them, and re-layouts, shards(): pick = lambda v, i: lax.dynamic_index_in_dim(v, i, 0, keepdims=False)  4.19 us
    pallas_call x1, Pallas kernels, shards(): call(attend_kernel, [sds((HEADS, SPAN, SPAN), LOW), sds((D, SPAN), F32),...  3.46 us
    pallas_call x1, Pallas kernels, shards(): call(keep_kernel, [inner_shape, square, sds((D, D), LOW), sds((D, SPAN),...  3.45 us
    pallas_call x1, Pallas kernels, closing(): call(closing_kernel, shapes, [SMEM] + [VMEM] * 8, [ANY] + [VMEM] * (len(s...  2.92 us
  transfers between devices with their start and end apart: 46, of which 22 were waited for; matrix products, arithmetic and copies ran while one was open for 6% of the time, Pallas kernels for 22%

profile of v4, /device:TPU:0, one launch (start us, length us, event | category | flops | bytes accessed | tf_op | source)
XLA Modules:
  0.0 131.0 jit_solution(15865970247448040408)
XLA Ops:
  0.7 1.0 dynamic-slice_bitcast_fusion.4
  1.6 3.0 %collective-permute-start.3 = (bf16[256,512]{1,0:T(8,128)(2,1)S(1)}, bf16[256,512]{1,0:T(8,128)(2,1)S(1)}, u32[]{:S(2)}, u32[]{:S(2)}) collective-permute-start(bf16[256,512]{1,0:T(8,128)(2,1)S(1)} %dynamic-slice_bitcast_fusion.4), channel_id=1, source_target_pairs={{0,2},{1,3},{2,0},{3,1},{4,6},{5,7},{6,4},{7,5},{8,10},{9,11},{10,... | collective-permute-start | bytes 786440 | tf_op jit(solution)/shard_map/ppermute | solution.py:455
  4.7 1.5 %shard_map.262 = bf16[16,2176]{1,0:T(8,128)(2,1)} custom-call(bf16[16,512]{1,0:T(8,128)(2,1)} %q_ref.1, bf16[16,512]{1,0:T(8,128)(2,1)} %k_ref.1, bf16[16,512]{1,0:T(8,128)(2,1)} %v_ref.1, bf16[16,512]{1,0:T(8,128)(2,1)} %o_ref.1, bf16[16,20]{1,0:T(8,128)(2,1)} %bitcast.83, bf16[1,16]{1,0:T(2,128)(2,1)} %bitcast.84, bf16[1,16]{1,0:T(2,128)(2,1)} %bitcast.85, ...), custom_call_target="tpu_custom_call" | custom-call | flops 1 | bytes 1 | tf_op jit(solution)/shard_map/pallas_call | solution.py:511
  6.2 1.6 %collective-permute-start = (bf16[16,2176]{1,0:T(8,128)(2,1)}, bf16[16,2176]{1,0:T(8,128)(2,1)S(1)}, u32[]{:S(2)}, u32[]{:S(2)}) collective-permute-start(bf16[16,2176]{1,0:T(8,128)(2,1)} %shard_map.262), channel_id=1, source_target_pairs={{0,8},{1,9},{2,10},{3,11},{4,12},{5,13},{6,14},{7,15},{8,0},{9,1},... | collective-permute-start | bytes 208904 | tf_op jit(solution)/shard_map/ppermute | solution.py:455
  7.8 2.6 %collective-permute-start.1 = (bf16[16,2176]{1,0:T(8,128)(2,1)}, bf16[16,2176]{1,0:T(8,128)(2,1)S(1)}, u32[]{:S(2)}, u32[]{:S(2)}) collective-permute-start(bf16[16,2176]{1,0:T(8,128)(2,1)} %shard_map.262), channel_id=1, source_target_pairs={{0,16},{1,17},{2,18},{3,19},{4,20},{5,21},{6,22},{7,23},{8,24},{9,... | collective-permute-start | bytes 208904 | tf_op jit(solution)/shard_map/ppermute | solution.py:455
  10.6 0.7 reshape.127
  11.2 1.0 dynamic-slice_bitcast_fusion.3
  12.6 2.6 %collective-permute-done.1 = bf16[16,2176]{1,0:T(8,128)(2,1)S(1)} collective-permute-done((bf16[16,2176]{1,0:T(8,128)(2,1)}, bf16[16,2176]{1,0:T(8,128)(2,1)S(1)}, u32[]{:S(2)}, u32[]{:S(2)}) %collective-permute-start.1) | collective-permute-done | bytes 69664 | tf_op jit(solution)/shard_map/ppermute | solution.py:455
  15.2 1.5 %collective-permute-done.2 = bf16[16,2176]{1,0:T(8,128)(2,1)S(1)} collective-permute-done((bf16[16,2176]{1,0:T(8,128)(2,1)}, bf16[16,2176]{1,0:T(8,128)(2,1)S(1)}, u32[]{:S(2)}, u32[]{:S(2)}) %collective-permute-start.2) | collective-permute-done | bytes 69664 | tf_op jit(solution)/shard_map/ppermute | solution.py:455
  16.9 0.6 collective-permute-start.4
  17.4 3.9 %collective-permute-done.7 = bf16[272,512]{1,0:T(8,128)(2,1)S(1)} collective-permute-done((bf16[272,512]{1,0:T(8,128)(2,1)S(1)}, bf16[272,512]{1,0:T(8,128)(2,1)S(1)}, u32[]{:S(2)}, u32[]{:S(2)}) %collective-permute-start.7) | collective-permute-done | bytes 278560 | tf_op jit(solution)/shard_map/ppermute | solution.py:455
  21.4 1.5 %collective-permute-start.5 = (bf16[64,2176]{1,0:T(8,128)(2,1)S(1)}, bf16[64,2176]{1,0:T(8,128)(2,1)}, u32[]{:S(2)}, u32[]{:S(2)}) collective-permute-start(bf16[64,2176]{1,0:T(8,128)(2,1)S(1)} %constant_dynamic-update-slice_fusion.refs_0_), channel_id=1, source_target_pairs={{0,4},{1,5},{2,6},{3,7},{4,0},{5,1},{6,2},{7,3},{8,12},{9,13},{10,... | collective-permute-start | bytes 835592 | tf_op jit(solution)/shard_map/ppermute | solution.py:455
  22.9 0.5 collective-permute-start.6
  23.4 2.3 %dynamic-slice_bitcast_fusion.1 = (bf16[512,512]{1,0:T(8,128)(2,1)}, bf16[512,512]{1,0:T(8,128)(2,1)S(1)}, bf16[512,512]{1,0:T(8,128)(2,1)S(1)}) fusion(bf16[4,512,512]{2,1,0:T(8,128)(2,1)} %bitcast.78, s32[]{:T(128)S(6)} %select_n.44, s32[]{:T(128)S(6)} %select_n.43, bf16[4,512,512]{2,1,0:T(8,128)(2,1)} %bitcast.81), kind=kLoop, calls=%fused_computation.21 | loop fusion | bytes 3145736 | tf_op jit(solution)/shard_map/jit(dynamic_index_in_dim)/squeeze | solution.py:499
  26.1 2.6 %collective-permute-done.4.refs_1_ = bf16[64,2176]{1,0:T(8,128)(2,1)} collective-permute-done((bf16[64,2176]{1,0:T(8,128)(2,1)S(1)}, bf16[64,2176]{1,0:T(8,128)(2,1)}, u32[]{:S(2)}, u32[]{:S(2)}) %collective-permute-start.4) | collective-permute-done | bytes 278560 | tf_op jit(solution)/shard_map/ppermute | solution.py:455
  29.1 0.4 collective-permute-done.5.refs_2_
  29.5 2.9 %collective-permute-done.6.refs_3_ = bf16[64,2176]{1,0:T(8,128)(2,1)} collective-permute-done((bf16[64,2176]{1,0:T(8,128)(2,1)S(1)}, bf16[64,2176]{1,0:T(8,128)(2,1)}, u32[]{:S(2)}, u32[]{:S(2)}) %collective-permute-start.6) | collective-permute-done | bytes 278560 | tf_op jit(solution)/shard_map/ppermute | solution.py:455
  32.4 0.5 collective-permute-start.11
  32.9 0.5 collective-permute-start.13
  33.6 1.2 maximum_maximum_fusion.wo0
  34.8 0.6 collective-permute-start.16
  35.5 0.4 collective-permute-start.17
  35.9 2.6 %shard_map.263 = (bf16[512,2176]{1,0:T(8,128)(2,1)S(1)}, bf16[1536,512]{1,0:T(8,128)(2,1)S(1)}) custom-call(s32[7]{0:T(128)S(1)} %stack.49.at_ref, bf16[64,2176]{1,0:T(8,128)(2,1)S(1)} %constant_dynamic-update-slice_fusion.refs_0_, bf16[64,2176]{1,0:T(8,128)(2,1)} %collective-permute-done.4.refs_1_, bf16[64,2176]{1,0:T(8,128)(2,1)} %collective-permute-done.5.refs_2_, ...), custom_call_target="tpu_custom_call" | custom-call | flops 2000000000 | bytes 5242880 | tf_op jit(solution)/shard_map/pallas_call | solution.py:543
  38.6 2.3 %shard_map.264 = (f32[32,512]{1,0:T(8,128)S(1)}, f32[32,512]{1,0:T(8,128)S(1)}) custom-call(bf16[512,512]{1,0:T(8,128)(2,1)S(1)} %copy-done.1, bf16[512,2176]{1,0:T(8,128)(2,1)S(1)} %get-tuple-element.150.w_ref), custom_call_target="tpu_custom_call" | custom-call | flops 3000000000 | bytes 4194304 | tf_op jit(solution)/shard_map/pallas_call | solution.py:565
  40.9 3.5 %shard_map.265 = (bf16[8,512,512]{2,1,0:T(8,128)(2,1)S(1)}, f32[512,512]{1,0:T(8,128)S(1)}, f32[8,512]{1,0:T(8,128)S(1)}, f32[8,512]{1,0:T(8,128)S(1)}) custom-call(bf16[1536,512]{1,0:T(8,128)(2,1)S(1)} %get-tuple-element.152.qkv_ref), custom_call_target="tpu_custom_call" | custom-call | flops 5000000000 | bytes 7340032 | tf_op jit(solution)/shard_map/pallas_call | solution.py:551
  44.4 9.5 %shard_map.266 = (bf16[512,512]{1,0:T(8,128)(2,1)S(1)}, bf16[2,4,128,512]{3,2,1,0:T(8,128)(2,1)S(1)}, bf16[2,4,128,512]{3,2,1,0:T(8,128)(2,1)S(1)}, bf16[4,512,5...) custom-call(s32[7]{0:T(128)S(1)} %stack.49.at_ref, ...), custom_call_target="tpu_custom_call" | custom-call | flops 10000000000 | bytes 14680064 | tf_op jit(solution)/shard_map/pallas_call | solution.py:581
  54.1 2.5 %shard_map.267 = (bf16[2,4,136,512]{3,2,1,0:T(8,128)(2,1)S(1)}, f32[512,512]{1,0:T(8,128)S(1)}) custom-call(s32[7]{0:T(128)S(1)} %stack.49.at_ref, bf16[512,512]{1,0:T(8,128)(2,1)S(1)} %collective-permute-done.14.wi1, bf16[512,512]{1,0:T(8,128)(2,1)S(1)} %collective-permute-done.15.wi3, bf16[528,512]{1,0:T(8,128)(2,1)S(1)} %collective-permute-done.16.wo1, ...), custom_call_target="tpu_custom_call" | custom-call | flops 1 | bytes 1 | tf_op jit(solution)/shard_map/pallas_call | solution.py:613
  56.6 0.5 collective-permute-start.20
  57.4 1.6 %collective-permute-start.19 = (bf16[4,128,512]{2,1,0:T(8,128)(2,1)S(1)}, bf16[4,128,512]{2,1,0:T(8,128)(2,1)S(1)}, u32[]{:S(2)}, u32[]{:S(2)}) collective-permute-start(bf16[4,128,512]{2,1,0:T(8,128)(2,1)S(1)} %get-tuple-element.264.after_ref), channel_id=1, source_target_pairs={{0,2},{1,3},{2,0},{3,1},{4,6},{5,7},{6,4},{7,5},{8,10},{9,11},{10,... | collective-permute-start | bytes 1572872 | tf_op jit(solution)/shard_map/ppermute | solution.py:455
  59.0 3.5 %shard_map.268 = (bf16[2,4,136,512]{3,2,1,0:T(8,128)(2,1)S(1)}, f32[512,512]{1,0:T(8,128)S(1)}, bf16[512,512]{1,0:T(8,128)(2,1)S(1)}, bf16[512,512]{1,0:T(8,128)(2,1)S(1)}, f32[8,512]{1,0:T(8,128)S(1)}) custom-call(s32[7]{0:T(128)S(1)} %stack.49.at_ref, bf16[4,128,512]{2,1,0:T(8,128)(2,1)S(1)} %get-tuple-element.264.after_ref, ...), custom_call_target="tpu_custom_call" | custom-call | flops 1 | bytes 1 | tf_op jit(solution)/shard_map/pallas_call | solution.py:624
  62.8 1.5 %collective-permute-start.21 = (bf16[2,2,136,512]{3,2,1,0:T(8,128)(2,1)S(1)}, bf16[2,2,136,512]{3,2,1,0:T(8,128)(2,1)S(1)}, u32[]{:S(2)}, u32[]{:S(2)}) collective-permute-start(bf16[2,2,136,512]{3,2,1,0:T(8,128)(2,1)S(1)} %get-tuple-element.262.after_ref), channel_id=1, source_target_pairs={{0,4},{4,0},{8,12},{12,8},{16,20},{20,16},{24,28},{28,24},{1,5},{5... | collective-permute-start | bytes 1671176 | tf_op jit(solution)/shard_map/ppermute | solution.py:455
  64.3 2.2 %shard_map.269 = (bf16[3,256,512]{2,1,0:T(8,128)(2,1)S(1)}, f32[2,32,256]{2,1,0:T(8,128)S(1)}) custom-call(bf16[2,2,136,512]{3,2,1,0:T(8,128)(2,1)S(1)} %get-tuple-element.262.after_ref, bf16[1536,512]{1,0:T(8,128)(2,1)S(1)} %get-tuple-element.152.qkv_ref, bf16[8,512,512]{2,1,0:T(8,128)(2,1)S(1)} %get-tuple-element.178.p_ref, ...), custom_call_target="tpu_custom_call" | custom-call | flops 1 | bytes 1 | tf_op jit(solution)/shard_map/pallas_call | solution.py:641
  66.6 2.2 %shard_map.270 = (bf16[3,256,512]{2,1,0:T(8,128)(2,1)S(1)}, f32[2,32,256]{2,1,0:T(8,128)S(1)}) custom-call(bf16[2,2,136,512]{3,2,1,0:T(8,128)(2,1)S(1)} %get-tuple-element.262.after_ref, bf16[1536,512]{1,0:T(8,128)(2,1)S(1)} %get-tuple-element.152.qkv_ref, bf16[8,512,512]{2,1,0:T(8,128)(2,1)S(1)} %get-tuple-element.178.p_ref, ...), custom_call_target="tpu_custom_call" | custom-call | flops 1 | bytes 1 | tf_op jit(solution)/shard_map/pallas_call | solution.py:641
  68.8 1.2 shard_map.271.r0
  70.0 2.6 %shard_map.272 = (bf16[256,2176]{1,0:T(8,128)(2,1)S(1)}, bf16[64,2176]{1,0:T(8,128)(2,1)S(1)}, bf16[64,2176]{1,0:T(8,128)(2,1)S(1)}, bf16[64,2176]{1,0:T(8,128)(2,1)S(1)}, bf16[64,2176]{1,0:T(8,128)(2,1)S(1)}) custom-call(bf16[2,2,136,512]{3,2,1,0:T(8,128)(2,1)S(1)} %get-tuple-element.262.after_ref, s32[7]{0:T(128)S(1)} %stack.49.at_ref, ...), custom_call_target="tpu_custom_call" | custom-call | flops 1 | bytes 1 | tf_op jit(solution)/shard_map/pallas_call | solution.py:668
  72.7 0.5 collective-permute-start.24
  73.2 0.4 collective-permute-start.26
  73.8 3.4 %collective-permute-done.21 = bf16[2,2,136,512]{3,2,1,0:T(8,128)(2,1)S(1)} collective-permute-done((bf16[2,2,136,512]{3,2,1,0:T(8,128)(2,1)S(1)}, bf16[2,2,136,512]{3,2,1,0:T(8,128)(2,1)S(1)}, u32[]{:S(2)}, u32[]{:S(2)}) %collective-permute-start.21) | collective-permute-done | bytes 557088 | tf_op jit(solution)/shard_map/ppermute | solution.py:455
  77.2 1.5 %collective-permute-start.22 = (bf16[2,128,512]{2,1,0:T(8,128)(2,1)S(1)}, bf16[2,128,512]{2,1,0:T(8,128)(2,1)S(1)}, u32[]{:S(2)}, u32[]{:S(2)}) collective-permute-start(bf16[2,128,512]{2,1,0:T(8,128)(2,1)S(1)} %get-tuple-element.274), channel_id=1, source_target_pairs={{0,4},{4,0},{8,12},{12,8},{16,20},{20,16},{24,28},{28,24},{1,5},{5... | collective-permute-start | bytes 786440 | tf_op jit(solution)/shard_map/ppermute | solution.py:455
  78.9 0.6 collective-permute-start.29
  79.7 0.6 collective-permute-start.31
  80.3 6.1 %collective-permute-done.22 = bf16[2,128,512]{2,1,0:T(8,128)(2,1)S(1)} collective-permute-done((bf16[2,128,512]{2,1,0:T(8,128)(2,1)S(1)}, bf16[2,128,512]{2,1,0:T(8,128)(2,1)S(1)}, u32[]{:S(2)}, u32[]{:S(2)}) %collective-permute-start.22) | collective-permute-done | bytes 262176 | tf_op jit(solution)/shard_map/ppermute | solution.py:455
  86.5 0.6 collective-permute-start.27
  87.1 1.7 %collective-permute-start.28 = (bf16[128,512]{1,0:T(8,128)(2,1)S(1)}, bf16[128,512]{1,0:T(8,128)(2,1)S(1)}, u32[]{:S(2)}, u32[]{:S(2)}) collective-permute-start(bf16[128,512]{1,0:T(8,128)(2,1)S(1)} %get-tuple-element.279), channel_id=1, source_target_pairs={{0,8},{4,12},{8,0},{12,4},{16,24},{20,28},{24,16},{28,20},{1,9},{5... | collective-permute-start | bytes 393224 | tf_op jit(solution)/shard_map/ppermute | solution.py:455
  89.2 3.2 %collective-permute-done.28 = bf16[128,512]{1,0:T(8,128)(2,1)S(1)} collective-permute-done((bf16[128,512]{1,0:T(8,128)(2,1)S(1)}, bf16[128,512]{1,0:T(8,128)(2,1)S(1)}, u32[]{:S(2)}, u32[]{:S(2)}) %collective-permute-start.28) | collective-permute-done | bytes 131104 | tf_op jit(solution)/shard_map/ppermute | solution.py:455
  92.5 3.2 %collective-permute-start.30 = (bf16[128,512]{1,0:T(8,128)(2,1)S(1)}, bf16[128,512]{1,0:T(8,128)(2,1)S(1)}, u32[]{:S(2)}, u32[]{:S(2)}) collective-permute-start(bf16[128,512]{1,0:T(8,128)(2,1)S(1)} %add_convert_fusion.17), channel_id=1, source_target_pairs={{0,16},{4,20},{8,24},{12,28},{16,0},{20,4},{24,8},{28,12},{1,17},{... | collective-permute-start | bytes 393224 | tf_op jit(solution)/shard_map/ppermute | solution.py:455
  95.7 0.6 collective-permute-done.31
  96.4 1.0 collective-permute-start.36
  97.4 1.1 collective-permute-start.40
  98.6 3.3 %collective-permute-start.35 = (bf16[136,512]{1,0:T(8,128)(2,1)S(1)}, bf16[136,512]{1,0:T(8,128)(2,1)S(1)}, u32[]{:S(2)}, u32[]{:S(2)}) collective-permute-start(bf16[136,512]{1,0:T(8,128)(2,1)S(1)} %add_convert_fusion.13), channel_id=1, source_target_pairs={{0,16},{4,20},{8,24},{12,28},{16,0},{20,4},{24,8},{28,12},{1,17},{... | collective-permute-start | bytes 417800 | tf_op jit(solution)/shard_map/ppermute | solution.py:455
  102.0 2.5 %collective-permute-start.34 = (bf16[128,512]{1,0:T(8,128)(2,1)S(1)}, bf16[128,512]{1,0:T(8,128)(2,1)S(1)}, u32[]{:S(2)}, u32[]{:S(2)}) collective-permute-start(bf16[128,512]{1,0:T(8,128)(2,1)S(1)} %add_convert_fusion.16), channel_id=1, source_target_pairs={{0,8},{4,12},{8,0},{12,4},{16,24},{20,28},{24,16},{28,20},{1,9},{5... | collective-permute-start | bytes 393224 | tf_op jit(solution)/shard_map/ppermute | solution.py:455
  104.5 1.6 %collective-permute-done.36 = bf16[4,16,2176]{2,1,0:T(8,128)(2,1)S(1)} collective-permute-done((bf16[4,16,2176]{2,1,0:T(8,128)(2,1)S(1)}, bf16[4,16,2176]{2,1,0:T(8,128)(2,1)S(1)}, u32[]{:S(2)}, u32[]{:S(2)}) %collective-permute-start.36) | collective-permute-done | bytes 278560 | tf_op jit(solution)/shard_map/ppermute | solution.py:455
  106.1 3.2 %collective-permute-done.35 = bf16[136,512]{1,0:T(8,128)(2,1)S(1)} collective-permute-done((bf16[136,512]{1,0:T(8,128)(2,1)S(1)}, bf16[136,512]{1,0:T(8,128)(2,1)S(1)}, u32[]{:S(2)}, u32[]{:S(2)}) %collective-permute-start.35) | collective-permute-done | bytes 139296 | tf_op jit(solution)/shard_map/ppermute | solution.py:455
  109.6 0.9 collective-permute-done.34
  110.4 1.1 collective-permute-start.38
  111.5 3.1 %collective-permute-done.40.r2 = bf16[512,512]{1,0:T(8,128)(2,1)S(1)} collective-permute-done((bf16[512,512]{1,0:T(8,128)(2,1)S(1)}, bf16[512,512]{1,0:T(8,128)(2,1)S(1)}, u32[]{:S(2)}, u32[]{:S(2)}) %collective-permute-start.40) | collective-permute-done | bytes 524320 | tf_op jit(solution)/shard_map/ppermute | solution.py:455
  114.6 1.4 %collective-permute-done.39 = bf16[136,512]{1,0:T(8,128)(2,1)S(1)} collective-permute-done((bf16[136,512]{1,0:T(8,128)(2,1)S(1)}, bf16[136,512]{1,0:T(8,128)(2,1)S(1)}, u32[]{:S(2)}, u32[]{:S(2)}) %collective-permute-start.39) | collective-permute-done | bytes 139296 | tf_op jit(solution)/shard_map/ppermute | solution.py:455
  116.0 1.5 %collective-permute-start.37 = (bf16[2,128,512]{2,1,0:T(8,128)(2,1)S(1)}, bf16[2,128,512]{2,1,0:T(8,128)(2,1)S(1)}, u32[]{:S(2)}, u32[]{:S(2)}) collective-permute-start(bf16[2,128,512]{2,1,0:T(8,128)(2,1)S(1)} %pad_maximum_fusion.1.own_ref), channel_id=1, source_target_pairs={{0,4},{4,0},{8,12},{12,8},{16,20},{20,16},{24,28},{28,24},{1,5},{5... | collective-permute-start | bytes 786440 | tf_op jit(solution)/shard_map/ppermute | solution.py:455
  117.9 1.5 %collective-permute-start.45 = (bf16[2,136,512]{2,1,0:T(8,128)(2,1)S(1)}, bf16[2,136,512]{2,1,0:T(8,128)(2,1)S(1)}, u32[]{:S(2)}, u32[]{:S(2)}) collective-permute-start(bf16[2,136,512]{2,1,0:T(8,128)(2,1)S(1)} %pad_maximum_fusion.own_ref), channel_id=1, source_target_pairs={{0,4},{4,0},{8,12},{12,8},{16,20},{20,16},{24,28},{28,24},{1,5},{5... | collective-permute-start | bytes 835592 | tf_op jit(solution)/shard_map/ppermute | solution.py:455
  119.8 1.4 %collective-permute-start.41 = (bf16[1,16,2176]{2,1,0:T(8,128)(2,1)S(1)}, bf16[1,16,2176]{2,1,0:T(8,128)(2,1)S(1)}, u32[]{:S(2)}, u32[]{:S(2)}) collective-permute-start(bf16[1,16,2176]{2,1,0:T(8,128)(2,1)S(1)} %get-tuple-element.282), channel_id=1, source_target_pairs={{0,16},{1,17},{2,18},{3,19},{4,20},{5,21},{6,22},{7,23},{8,24},{9,... | collective-permute-start | bytes 208904 | tf_op jit(solution)/shard_map/ppermute | solution.py:455
  121.3 1.9 %shard_map.273 = bf16[4,512,512]{2,1,0:T(8,128)(2,1)} custom-call(s32[7]{0:T(128)S(1)} %stack.49.at_ref, bf16[512,512]{1,0:T(8,128)(2,1)S(1)} %get-tuple-element.233.r0, bf16[512,512]{1,0:T(8,128)(2,1)S(1)} %collective-permute-done.42.r1, bf16[512,512]{1,0:T(8,128)(2,1)S(1)} %collective-permute-done.40.r2, bf16[512,512]{1,0:T(8,128)(2,1)S(1)} %collective-permute-done.43.r3), custom_call_target="tpu_custom_call" | custom-call | flops 1 | bytes 1 | tf_op jit(solution)/shard_map/pallas_call | solution.py:390
  123.2 3.0 %collective-permute-done.41.got_ref = bf16[1,16,2176]{2,1,0:T(8,128)(2,1)S(1)} collective-permute-done((bf16[1,16,2176]{2,1,0:T(8,128)(2,1)S(1)}, bf16[1,16,2176]{2,1,0:T(8,128)(2,1)S(1)}, u32[]{:S(2)}, u32[]{:S(2)}) %collective-permute-start.41) | collective-permute-done | bytes 69664 | tf_op jit(solution)/shard_map/ppermute | solution.py:455
  126.2 2.9 %shard_map.274 = (bf16[4,512,512]{2,1,0:T(8,128)(2,1)}, f32[512,512]{1,0:T(8,128)}, f32[16,20]{1,0:T(8,128)}, f32[16,512]{1,0:T(8,128)}, f32[16,512]{1,0:T(8,128...) custom-call(s32[7]{0:T(128)S(1)} %stack.49.at_ref, ...), custom_call_target="tpu_custom_call" | custom-call | flops 1 | bytes 1 | tf_op jit(solution)/shard_map/pallas_call | solution.py:441
  129.3 1.7 %shard_map.275 = (f32[512,512]{1,0:T(8,128)}, f32[1,512]{1,0:T(1,128)}) custom-call(s32[7]{0:T(128)S(1)} %stack.49.at_ref, bf16[2,136,512]{2,1,0:T(8,128)(2,1)S(1)} %pad_maximum_fusion.own_ref, bf16[2,136,512]{2,1,0:T(8,128)(2,1)S(1)} %collective-permute-done.45.other_ref), custom_call_target="tpu_custom_call" | custom-call | flops 1 | bytes 2097152 | tf_op jit(solution)/shard_map/pallas_call | solution.py:467
  (82 shorter events, 5.5 us)
Async XLA Ops:
  1.6 15.1 %collective-permute-start.3 = (bf16[256,512]{1,0:T(8,128)(2,1)S(1)}, bf16[256,512]{1,0:T(8,128)(2,1)S(1)}, u32[]{:S(2)}, u32[]{:S(2)}) collective-permute-start(bf16[256,512]{1,0:T(8,128)(2,1)S(1)} %dynamic-slice_bitcast_fusion.4), channel_id=1, source_target_pairs={{0,2},{1,3},{2,0},{3,1},{4,6},{5,7},{6,4},{7,5},{8,10},{9,11},{10,... | collective-permute-start | bytes 786440 | tf_op jit(solution)/shard_map/ppermute | solution.py:455
  6.2 10.5 %copy-start.2 = (bf16[16,2176]{1,0:T(8,128)(2,1)S(1)}, bf16[16,2176]{1,0:T(8,128)(2,1)}, u32[]{:S(2)}) copy-start(bf16[16,2176]{1,0:T(8,128)(2,1)} %shard_map.262) | copy-start | bytes 208900
  6.2 6.4 %collective-permute-start = (bf16[16,2176]{1,0:T(8,128)(2,1)}, bf16[16,2176]{1,0:T(8,128)(2,1)S(1)}, u32[]{:S(2)}, u32[]{:S(2)}) collective-permute-start(bf16[16,2176]{1,0:T(8,128)(2,1)} %shard_map.262), channel_id=1, source_target_pairs={{0,8},{1,9},{2,10},{3,11},{4,12},{5,13},{6,14},{7,15},{8,0},{9,1},... | collective-permute-start | bytes 208904 | tf_op jit(solution)/shard_map/ppermute | solution.py:455
  7.8 7.5 %collective-permute-start.1 = (bf16[16,2176]{1,0:T(8,128)(2,1)}, bf16[16,2176]{1,0:T(8,128)(2,1)S(1)}, u32[]{:S(2)}, u32[]{:S(2)}) collective-permute-start(bf16[16,2176]{1,0:T(8,128)(2,1)} %shard_map.262), channel_id=1, source_target_pairs={{0,16},{1,17},{2,18},{3,19},{4,20},{5,21},{6,22},{7,23},{8,24},{9,... | collective-permute-start | bytes 208904 | tf_op jit(solution)/shard_map/ppermute | solution.py:455
  10.3 6.4 %collective-permute-start.2 = (bf16[16,2176]{1,0:T(8,128)(2,1)}, bf16[16,2176]{1,0:T(8,128)(2,1)S(1)}, u32[]{:S(2)}, u32[]{:S(2)}) collective-permute-start(bf16[16,2176]{1,0:T(8,128)(2,1)} %shard_map.262), channel_id=1, source_target_pairs={{0,24},{1,25},{2,26},{3,27},{4,28},{5,29},{6,30},{7,31},{8,16},{9,... | collective-permute-start | bytes 208904 | tf_op jit(solution)/shard_map/ppermute | solution.py:455
  12.2 9.1 %collective-permute-start.7 = (bf16[272,512]{1,0:T(8,128)(2,1)S(1)}, bf16[272,512]{1,0:T(8,128)(2,1)S(1)}, u32[]{:S(2)}, u32[]{:S(2)}) collective-permute-start(bf16[272,512]{1,0:T(8,128)(2,1)S(1)} %fusion.4), channel_id=1, source_target_pairs={{0,2},{1,3},{2,0},{3,1},{4,6},{5,7},{6,4},{7,5},{8,10},{9,11},{10,... | collective-permute-start | bytes 835592 | tf_op jit(solution)/shard_map/ppermute | solution.py:455
  16.7 9.2 %collective-permute-start.9 = (bf16[256,512]{1,0:T(8,128)(2,1)S(1)}, bf16[256,512]{1,0:T(8,128)(2,1)S(1)}, u32[]{:S(2)}, u32[]{:S(2)}) collective-permute-start(bf16[256,512]{1,0:T(8,128)(2,1)S(1)} %collective-permute-done.3), channel_id=1, source_target_pairs={{0,8},{4,12},{8,0},{12,4},{16,24},{20,28},{24,16},{28,20},{1,9},{5... | collective-permute-start | bytes 786440 | tf_op jit(solution)/shard_map/ppermute | solution.py:455
  16.9 11.8 %collective-permute-start.4 = (bf16[64,2176]{1,0:T(8,128)(2,1)S(1)}, bf16[64,2176]{1,0:T(8,128)(2,1)}, u32[]{:S(2)}, u32[]{:S(2)}) collective-permute-start(bf16[64,2176]{1,0:T(8,128)(2,1)S(1)} %constant_dynamic-update-slice_fusion.refs_0_), channel_id=1, source_target_pairs={{0,2},{1,3},{2,0},{3,1},{4,6},{5,7},{6,4},{7,5},{8,10},{9,11},{10,... | collective-permute-start | bytes 835592 | tf_op jit(solution)/shard_map/ppermute | solution.py:455
  21.4 7.5 %collective-permute-start.8 = (bf16[272,512]{1,0:T(8,128)(2,1)S(1)}, bf16[272,512]{1,0:T(8,128)(2,1)S(1)}, u32[]{:S(2)}, u32[]{:S(2)}) collective-permute-start(bf16[272,512]{1,0:T(8,128)(2,1)S(1)} %collective-permute-done.7), channel_id=1, source_target_pairs={{0,8},{4,12},{8,0},{12,4},{16,24},{20,28},{24,16},{28,20},{1,9},{5... | collective-permute-start | bytes 835592 | tf_op jit(solution)/shard_map/ppermute | solution.py:455
  21.4 8.0 %collective-permute-start.5 = (bf16[64,2176]{1,0:T(8,128)(2,1)S(1)}, bf16[64,2176]{1,0:T(8,128)(2,1)}, u32[]{:S(2)}, u32[]{:S(2)}) collective-permute-start(bf16[64,2176]{1,0:T(8,128)(2,1)S(1)} %constant_dynamic-update-slice_fusion.refs_0_), channel_id=1, source_target_pairs={{0,4},{1,5},{2,6},{3,7},{4,0},{5,1},{6,2},{7,3},{8,12},{9,13},{10,... | collective-permute-start | bytes 835592 | tf_op jit(solution)/shard_map/ppermute | solution.py:455
  22.9 9.5 %collective-permute-start.6 = (bf16[64,2176]{1,0:T(8,128)(2,1)S(1)}, bf16[64,2176]{1,0:T(8,128)(2,1)}, u32[]{:S(2)}, u32[]{:S(2)}) collective-permute-start(bf16[64,2176]{1,0:T(8,128)(2,1)S(1)} %constant_dynamic-update-slice_fusion.refs_0_), channel_id=1, source_target_pairs={{0,6},{1,7},{2,4},{3,5},{4,2},{5,3},{6,0},{7,1},{8,14},{9,15},{10,... | collective-permute-start | bytes 835592 | tf_op jit(solution)/shard_map/ppermute | solution.py:455
  26.1 7.3 %copy-start = (bf16[512,512]{1,0:T(8,128)(2,1)S(1)}, bf16[512,512]{1,0:T(8,128)(2,1)}, u32[]{:S(2)}) copy-start(bf16[512,512]{1,0:T(8,128)(2,1)} %wi0.3) | copy-start | bytes 1572868
  32.4 2.4 %collective-permute-start.10 = (bf16[64,2176]{1,0:T(8,128)(2,1)S(1)}, bf16[64,2176]{1,0:T(8,128)(2,1)}, u32[]{:S(2)}, u32[]{:S(2)}) collective-permute-start(bf16[64,2176]{1,0:T(8,128)(2,1)S(1)} %constant_dynamic-update-slice_fusion.refs_0_), channel_id=1, source_target_pairs={{0,1},{1,0},{2,3},{3,2},{4,5},{5,4},{6,7},{7,6},{8,9},{9,8},{10,11... | collective-permute-start | bytes 835592 | tf_op jit(solution)/shard_map/ppermute | solution.py:455
  32.4 3.0 %collective-permute-start.11 = (bf16[64,2176]{1,0:T(8,128)(2,1)}, bf16[64,2176]{1,0:T(8,128)(2,1)}, u32[]{:S(2)}, u32[]{:S(2)}) collective-permute-start(bf16[64,2176]{1,0:T(8,128)(2,1)} %collective-permute-done.4.refs_1_), channel_id=1, source_target_pairs={{0,1},{1,0},{2,3},{3,2},{4,5},{5,4},{6,7},{7,6},{8,9},{9,8},{10,11... | collective-permute-start | bytes 835592 | tf_op jit(solution)/shard_map/ppermute | solution.py:455
  32.9 2.6 %collective-permute-start.12 = (bf16[64,2176]{1,0:T(8,128)(2,1)}, bf16[64,2176]{1,0:T(8,128)(2,1)}, u32[]{:S(2)}, u32[]{:S(2)}) collective-permute-start(bf16[64,2176]{1,0:T(8,128)(2,1)} %collective-permute-done.5.refs_2_), channel_id=1, source_target_pairs={{0,1},{1,0},{2,3},{3,2},{4,5},{5,4},{6,7},{7,6},{8,9},{9,8},{10,11... | collective-permute-start | bytes 835592 | tf_op jit(solution)/shard_map/ppermute | solution.py:455
  32.9 3.0 %collective-permute-start.13 = (bf16[64,2176]{1,0:T(8,128)(2,1)}, bf16[64,2176]{1,0:T(8,128)(2,1)}, u32[]{:S(2)}, u32[]{:S(2)}) collective-permute-start(bf16[64,2176]{1,0:T(8,128)(2,1)} %collective-permute-done.6.refs_3_), channel_id=1, source_target_pairs={{0,1},{1,0},{2,3},{3,2},{4,5},{5,4},{6,7},{7,6},{8,9},{9,8},{10,11... | collective-permute-start | bytes 835592 | tf_op jit(solution)/shard_map/ppermute | solution.py:455
  33.4 11.0 %collective-permute-start.14 = (bf16[512,512]{1,0:T(8,128)(2,1)S(1)}, bf16[512,512]{1,0:T(8,128)(2,1)S(1)}, u32[]{:S(2)}, u32[]{:S(2)}) collective-permute-start(bf16[512,512]{1,0:T(8,128)(2,1)S(1)} %copy-done), channel_id=1, source_target_pairs={{0,1},{1,0},{2,3},{3,2},{4,5},{5,4},{6,7},{7,6},{8,9},{9,8},{10,11... | collective-permute-start | bytes 1572872 | tf_op jit(solution)/shard_map/ppermute | solution.py:455
  34.8 3.8 %copy-start.1 = (bf16[512,512]{1,0:T(8,128)(2,1)S(1)}, bf16[512,512]{1,0:T(8,128)(2,1)}, u32[]{:S(2)}) copy-start(bf16[512,512]{1,0:T(8,128)(2,1)} %get-tuple-element.142.x1_ref) | copy-start | bytes 1572868
  34.8 9.5 %collective-permute-start.16 = (bf16[528,512]{1,0:T(8,128)(2,1)S(1)}, bf16[528,512]{1,0:T(8,128)(2,1)S(1)}, u32[]{:S(2)}, u32[]{:S(2)}) collective-permute-start(bf16[528,512]{1,0:T(8,128)(2,1)S(1)} %maximum_maximum_fusion.wo0), channel_id=1, source_target_pairs={{0,1},{1,0},{2,3},{3,2},{4,5},{5,4},{6,7},{7,6},{8,9},{9,8},{10,11... | collective-permute-start | bytes 1622024 | tf_op jit(solution)/shard_map/ppermute | solution.py:455
  35.4 9.0 %collective-permute-start.15 = (bf16[512,512]{1,0:T(8,128)(2,1)S(1)}, bf16[512,512]{1,0:T(8,128)(2,1)S(1)}, u32[]{:S(2)}, u32[]{:S(2)}) collective-permute-start(bf16[512,512]{1,0:T(8,128)(2,1)S(1)} %maximum_select_fusion.1.wi2), channel_id=1, source_target_pairs={{0,1},{1,0},{2,3},{3,2},{4,5},{5,4},{6,7},{7,6},{8,9},{9,8},{10,11... | collective-permute-start | bytes 1572872 | tf_op jit(solution)/shard_map/ppermute | solution.py:455
  35.5 8.9 %collective-permute-start.17 = (bf16[528,512]{1,0:T(8,128)(2,1)S(1)}, bf16[528,512]{1,0:T(8,128)(2,1)S(1)}, u32[]{:S(2)}, u32[]{:S(2)}) collective-permute-start(bf16[528,512]{1,0:T(8,128)(2,1)S(1)} %maximum_select_fusion.wo2), channel_id=1, source_target_pairs={{0,1},{1,0},{2,3},{3,2},{4,5},{5,4},{6,7},{7,6},{8,9},{9,8},{10,11... | collective-permute-start | bytes 1622024 | tf_op jit(solution)/shard_map/ppermute | solution.py:455
  53.9 3.2 %collective-permute-start.18 = (bf16[2,4,128,512]{3,2,1,0:T(8,128)(2,1)S(1)}, bf16[2,4,128,512]{3,2,1,0:T(8,128)(2,1)S(1)}, u32[]{:S(2)}, u32[]{:S(2)}) collective-permute-start(bf16[2,4,128,512]{3,2,1,0:T(8,128)(2,1)S(1)} %get-tuple-element.167), channel_id=1, source_target_pairs={{0,1},{1,0},{2,3},{3,2},{4,5},{5,4},{6,7},{7,6},{8,9},{9,8},{10,11... | collective-permute-start | bytes 3145736 | tf_op jit(solution)/shard_map/ppermute | solution.py:455
  56.6 5.9 %collective-permute-start.20 = (bf16[2,4,136,512]{3,2,1,0:T(8,128)(2,1)S(1)}, bf16[2,4,136,512]{3,2,1,0:T(8,128)(2,1)S(1)}, u32[]{:S(2)}, u32[]{:S(2)}) collective-permute-start(bf16[2,4,136,512]{3,2,1,0:T(8,128)(2,1)S(1)} %get-tuple-element.177), channel_id=1, source_target_pairs={{0,1},{1,0},{2,3},{3,2},{4,5},{5,4},{6,7},{7,6},{8,9},{9,8},{10,11... | collective-permute-start | bytes 3342344 | tf_op jit(solution)/shard_map/ppermute | solution.py:455
  57.4 15.8 %collective-permute-start.19 = (bf16[4,128,512]{2,1,0:T(8,128)(2,1)S(1)}, bf16[4,128,512]{2,1,0:T(8,128)(2,1)S(1)}, u32[]{:S(2)}, u32[]{:S(2)}) collective-permute-start(bf16[4,128,512]{2,1,0:T(8,128)(2,1)S(1)} %get-tuple-element.264.after_ref), channel_id=1, source_target_pairs={{0,2},{1,3},{2,0},{3,1},{4,6},{5,7},{6,4},{7,5},{8,10},{9,11},{10,... | collective-permute-start | bytes 1572872 | tf_op jit(solution)/shard_map/ppermute | solution.py:455
  62.8 14.4 %collective-permute-start.21 = (bf16[2,2,136,512]{3,2,1,0:T(8,128)(2,1)S(1)}, bf16[2,2,136,512]{3,2,1,0:T(8,128)(2,1)S(1)}, u32[]{:S(2)}, u32[]{:S(2)}) collective-permute-start(bf16[2,2,136,512]{3,2,1,0:T(8,128)(2,1)S(1)} %get-tuple-element.262.after_ref), channel_id=1, source_target_pairs={{0,4},{4,0},{8,12},{12,8},{16,20},{20,16},{24,28},{28,24},{1,5},{5... | collective-permute-start | bytes 1671176 | tf_op jit(solution)/shard_map/ppermute | solution.py:455
  72.6 6.3 %collective-permute-start.23 = (bf16[4,16,2176]{2,1,0:T(8,128)(2,1)S(1)}, bf16[4,16,2176]{2,1,0:T(8,128)(2,1)S(1)}, u32[]{:S(2)}, u32[]{:S(2)}) collective-permute-start(bf16[4,16,2176]{2,1,0:T(8,128)(2,1)S(1)} %bitcast.74), channel_id=1, source_target_pairs={{0,1},{1,0},{2,3},{3,2},{4,5},{5,4},{6,7},{7,6},{8,9},{9,8},{10,11... | collective-permute-start | bytes 835592 | tf_op jit(solution)/shard_map/ppermute | solution.py:455
  72.7 6.2 %collective-permute-start.24 = (bf16[4,16,2176]{2,1,0:T(8,128)(2,1)S(1)}, bf16[4,16,2176]{2,1,0:T(8,128)(2,1)S(1)}, u32[]{:S(2)}, u32[]{:S(2)}) collective-permute-start(bf16[4,16,2176]{2,1,0:T(8,128)(2,1)S(1)} %bitcast.73), channel_id=1, source_target_pairs={{0,1},{1,0},{2,3},{3,2},{4,5},{5,4},{6,7},{7,6},{8,9},{9,8},{10,11... | collective-permute-start | bytes 835592 | tf_op jit(solution)/shard_map/ppermute | solution.py:455
  73.2 5.7 %collective-permute-start.25 = (bf16[4,16,2176]{2,1,0:T(8,128)(2,1)S(1)}, bf16[4,16,2176]{2,1,0:T(8,128)(2,1)S(1)}, u32[]{:S(2)}, u32[]{:S(2)}) collective-permute-start(bf16[4,16,2176]{2,1,0:T(8,128)(2,1)S(1)} %bitcast.72), channel_id=1, source_target_pairs={{0,1},{1,0},{2,3},{3,2},{4,5},{5,4},{6,7},{7,6},{8,9},{9,8},{10,11... | collective-permute-start | bytes 835592 | tf_op jit(solution)/shard_map/ppermute | solution.py:455
  73.2 5.6 %collective-permute-start.26 = (bf16[4,16,2176]{2,1,0:T(8,128)(2,1)S(1)}, bf16[4,16,2176]{2,1,0:T(8,128)(2,1)S(1)}, u32[]{:S(2)}, u32[]{:S(2)}) collective-permute-start(bf16[4,16,2176]{2,1,0:T(8,128)(2,1)S(1)} %bitcast.71), channel_id=1, source_target_pairs={{0,1},{1,0},{2,3},{3,2},{4,5},{5,4},{6,7},{7,6},{8,9},{9,8},{10,11... | collective-permute-start | bytes 835592 | tf_op jit(solution)/shard_map/ppermute | solution.py:455
  77.2 9.2 %collective-permute-start.22 = (bf16[2,128,512]{2,1,0:T(8,128)(2,1)S(1)}, bf16[2,128,512]{2,1,0:T(8,128)(2,1)S(1)}, u32[]{:S(2)}, u32[]{:S(2)}) collective-permute-start(bf16[2,128,512]{2,1,0:T(8,128)(2,1)S(1)} %get-tuple-element.274), channel_id=1, source_target_pairs={{0,4},{4,0},{8,12},{12,8},{16,20},{20,16},{24,28},{28,24},{1,5},{5... | collective-permute-start | bytes 786440 | tf_op jit(solution)/shard_map/ppermute | solution.py:455
  78.9 9.9 %collective-permute-start.29 = (bf16[2,136,512]{2,1,0:T(8,128)(2,1)S(1)}, bf16[2,136,512]{2,1,0:T(8,128)(2,1)S(1)}, u32[]{:S(2)}, u32[]{:S(2)}) collective-permute-start(bf16[2,136,512]{2,1,0:T(8,128)(2,1)S(1)} %get-tuple-element.271), channel_id=1, source_target_pairs={{0,2},{1,3},{2,0},{3,1},{4,6},{5,7},{6,4},{7,5},{8,10},{9,11},{10,... | collective-permute-start | bytes 835592 | tf_op jit(solution)/shard_map/ppermute | solution.py:455
  79.7 16.5 %collective-permute-start.31 = (bf16[8,16,2176]{2,1,0:T(8,128)(2,1)S(1)}, bf16[8,16,2176]{2,1,0:T(8,128)(2,1)S(1)}, u32[]{:S(2)}, u32[]{:S(2)}) collective-permute-start(bf16[8,16,2176]{2,1,0:T(8,128)(2,1)S(1)} %get-tuple-element.269), channel_id=1, source_target_pairs={{0,4},{1,5},{2,6},{3,7},{4,0},{5,1},{6,2},{7,3},{8,12},{9,13},{10,... | collective-permute-start | bytes 1671176 | tf_op jit(solution)/shard_map/ppermute | solution.py:455
  86.5 15.5 %collective-permute-start.27 = (bf16[512,512]{1,0:T(8,128)(2,1)S(1)}, bf16[512,512]{1,0:T(8,128)(2,1)S(1)}, u32[]{:S(2)}, u32[]{:S(2)}) collective-permute-start(bf16[512,512]{1,0:T(8,128)(2,1)S(1)} %shard_map.271.r0), channel_id=1, source_target_pairs={{0,2},{1,3},{2,0},{3,1},{4,6},{5,7},{6,4},{7,5},{8,10},{9,11},{10,... | collective-permute-start | bytes 1572872 | tf_op jit(solution)/shard_map/ppermute | solution.py:455
  87.1 5.3 %collective-permute-start.28 = (bf16[128,512]{1,0:T(8,128)(2,1)S(1)}, bf16[128,512]{1,0:T(8,128)(2,1)S(1)}, u32[]{:S(2)}, u32[]{:S(2)}) collective-permute-start(bf16[128,512]{1,0:T(8,128)(2,1)S(1)} %get-tuple-element.279), channel_id=1, source_target_pairs={{0,8},{4,12},{8,0},{12,4},{16,24},{20,28},{24,16},{28,20},{1,9},{5... | collective-permute-start | bytes 393224 | tf_op jit(solution)/shard_map/ppermute | solution.py:455
  88.8 6.8 %collective-permute-start.32 = (bf16[136,512]{1,0:T(8,128)(2,1)S(1)}, bf16[136,512]{1,0:T(8,128)(2,1)S(1)}, u32[]{:S(2)}, u32[]{:S(2)}) collective-permute-start(bf16[136,512]{1,0:T(8,128)(2,1)S(1)} %get-tuple-element.277), channel_id=1, source_target_pairs={{0,8},{4,12},{8,0},{12,4},{16,24},{20,28},{24,16},{28,20},{1,9},{5... | collective-permute-start | bytes 417800 | tf_op jit(solution)/shard_map/ppermute | solution.py:455
  92.5 6.1 %collective-permute-start.30 = (bf16[128,512]{1,0:T(8,128)(2,1)S(1)}, bf16[128,512]{1,0:T(8,128)(2,1)S(1)}, u32[]{:S(2)}, u32[]{:S(2)}) collective-permute-start(bf16[128,512]{1,0:T(8,128)(2,1)S(1)} %add_convert_fusion.17), channel_id=1, source_target_pairs={{0,16},{4,20},{8,24},{12,28},{16,0},{20,4},{24,8},{28,12},{1,17},{... | collective-permute-start | bytes 393224 | tf_op jit(solution)/shard_map/ppermute | solution.py:455
  96.4 9.7 %collective-permute-start.36 = (bf16[4,16,2176]{2,1,0:T(8,128)(2,1)S(1)}, bf16[4,16,2176]{2,1,0:T(8,128)(2,1)S(1)}, u32[]{:S(2)}, u32[]{:S(2)}) collective-permute-start(bf16[4,16,2176]{2,1,0:T(8,128)(2,1)S(1)} %get-tuple-element.267), channel_id=1, source_target_pairs={{0,2},{1,3},{2,0},{3,1},{4,6},{5,7},{6,4},{7,5},{8,10},{9,11},{10,... | collective-permute-start | bytes 835592 | tf_op jit(solution)/shard_map/ppermute | solution.py:455
  97.4 17.2 %collective-permute-start.40 = (bf16[512,512]{1,0:T(8,128)(2,1)S(1)}, bf16[512,512]{1,0:T(8,128)(2,1)S(1)}, u32[]{:S(2)}, u32[]{:S(2)}) collective-permute-start(bf16[512,512]{1,0:T(8,128)(2,1)S(1)} %get-tuple-element.233.r0), channel_id=1, source_target_pairs={{0,2},{1,3},{2,0},{3,1},{4,6},{5,7},{6,4},{7,5},{8,10},{9,11},{10,... | collective-permute-start | bytes 1572872 | tf_op jit(solution)/shard_map/ppermute | solution.py:455
  98.5 19.4 %collective-permute-start.42 = (bf16[512,512]{1,0:T(8,128)(2,1)S(1)}, bf16[512,512]{1,0:T(8,128)(2,1)S(1)}, u32[]{:S(2)}, u32[]{:S(2)}) collective-permute-start(bf16[512,512]{1,0:T(8,128)(2,1)S(1)} %get-tuple-element.233.r0), channel_id=1, source_target_pairs={{0,1},{1,0},{2,3},{3,2},{4,5},{5,4},{6,7},{7,6},{8,9},{9,8},{10,11... | collective-permute-start | bytes 1572872 | tf_op jit(solution)/shard_map/ppermute | solution.py:455
  98.6 10.8 %collective-permute-start.35 = (bf16[136,512]{1,0:T(8,128)(2,1)S(1)}, bf16[136,512]{1,0:T(8,128)(2,1)S(1)}, u32[]{:S(2)}, u32[]{:S(2)}) collective-permute-start(bf16[136,512]{1,0:T(8,128)(2,1)S(1)} %add_convert_fusion.13), channel_id=1, source_target_pairs={{0,16},{4,20},{8,24},{12,28},{16,0},{20,4},{24,8},{28,12},{1,17},{... | collective-permute-start | bytes 417800 | tf_op jit(solution)/shard_map/ppermute | solution.py:455
  102.0 8.4 %collective-permute-start.34 = (bf16[128,512]{1,0:T(8,128)(2,1)S(1)}, bf16[128,512]{1,0:T(8,128)(2,1)S(1)}, u32[]{:S(2)}, u32[]{:S(2)}) collective-permute-start(bf16[128,512]{1,0:T(8,128)(2,1)S(1)} %add_convert_fusion.16), channel_id=1, source_target_pairs={{0,8},{4,12},{8,0},{12,4},{16,24},{20,28},{24,16},{28,20},{1,9},{5... | collective-permute-start | bytes 393224 | tf_op jit(solution)/shard_map/ppermute | solution.py:455
  109.4 6.6 %collective-permute-start.39 = (bf16[136,512]{1,0:T(8,128)(2,1)S(1)}, bf16[136,512]{1,0:T(8,128)(2,1)S(1)}, u32[]{:S(2)}, u32[]{:S(2)}) collective-permute-start(bf16[136,512]{1,0:T(8,128)(2,1)S(1)} %add_convert_fusion.11), channel_id=1, source_target_pairs={{0,8},{4,12},{8,0},{12,4},{16,24},{20,28},{24,16},{28,20},{1,9},{5... | collective-permute-start | bytes 417800 | tf_op jit(solution)/shard_map/ppermute | solution.py:455
  109.5 16.7 %collective-permute-start.44 = (bf16[512,512]{1,0:T(8,128)(2,1)S(1)}, bf16[512,512]{1,0:T(8,128)(2,1)S(1)}, u32[]{:S(2)}, u32[]{:S(2)}) collective-permute-start(bf16[512,512]{1,0:T(8,128)(2,1)S(1)} %shard_map.271.r0), channel_id=1, source_target_pairs={{0,1},{1,0},{2,3},{3,2},{4,5},{5,4},{6,7},{7,6},{8,9},{9,8},{10,11... | collective-permute-start | bytes 1572872 | tf_op jit(solution)/shard_map/ppermute | solution.py:455
  110.4 7.5 %collective-permute-start.38 = (bf16[2,16,2176]{2,1,0:T(8,128)(2,1)S(1)}, bf16[2,16,2176]{2,1,0:T(8,128)(2,1)S(1)}, u32[]{:S(2)}, u32[]{:S(2)}) collective-permute-start(bf16[2,16,2176]{2,1,0:T(8,128)(2,1)S(1)} %get-tuple-element.275), channel_id=1, source_target_pairs={{0,8},{1,9},{2,10},{3,11},{4,12},{5,13},{6,14},{7,15},{8,0},{9,1},... | collective-permute-start | bytes 417800 | tf_op jit(solution)/shard_map/ppermute | solution.py:455
  114.6 11.6 %collective-permute-start.33 = (bf16[512,512]{1,0:T(8,128)(2,1)S(1)}, bf16[512,512]{1,0:T(8,128)(2,1)S(1)}, u32[]{:S(2)}, u32[]{:S(2)}) collective-permute-start(bf16[512,512]{1,0:T(8,128)(2,1)S(1)} %collective-permute-done.27.r2), channel_id=1, source_target_pairs={{0,1},{1,0},{2,3},{3,2},{4,5},{5,4},{6,7},{7,6},{8,9},{9,8},{10,11... | collective-permute-start | bytes 1572872 | tf_op jit(solution)/shard_map/ppermute | solution.py:455
  116.0 10.1 %collective-permute-start.37 = (bf16[2,128,512]{2,1,0:T(8,128)(2,1)S(1)}, bf16[2,128,512]{2,1,0:T(8,128)(2,1)S(1)}, u32[]{:S(2)}, u32[]{:S(2)}) collective-permute-start(bf16[2,128,512]{2,1,0:T(8,128)(2,1)S(1)} %pad_maximum_fusion.1.own_ref), channel_id=1, source_target_pairs={{0,4},{4,0},{8,12},{12,8},{16,20},{20,16},{24,28},{28,24},{1,5},{5... | collective-permute-start | bytes 786440 | tf_op jit(solution)/shard_map/ppermute | solution.py:455
  117.9 1.9 %collective-permute-start.43 = (bf16[512,512]{1,0:T(8,128)(2,1)S(1)}, bf16[512,512]{1,0:T(8,128)(2,1)S(1)}, u32[]{:S(2)}, u32[]{:S(2)}) collective-permute-start(bf16[512,512]{1,0:T(8,128)(2,1)S(1)} %collective-permute-done.40.r2), channel_id=1, source_target_pairs={{0,1},{1,0},{2,3},{3,2},{4,5},{5,4},{6,7},{7,6},{8,9},{9,8},{10,11... | collective-permute-start | bytes 1572872 | tf_op jit(solution)/shard_map/ppermute | solution.py:455
  117.9 11.4 %collective-permute-start.45 = (bf16[2,136,512]{2,1,0:T(8,128)(2,1)S(1)}, bf16[2,136,512]{2,1,0:T(8,128)(2,1)S(1)}, u32[]{:S(2)}, u32[]{:S(2)}) collective-permute-start(bf16[2,136,512]{2,1,0:T(8,128)(2,1)S(1)} %pad_maximum_fusion.own_ref), channel_id=1, source_target_pairs={{0,4},{4,0},{8,12},{12,8},{16,20},{20,16},{24,28},{28,24},{1,5},{5... | collective-permute-start | bytes 835592 | tf_op jit(solution)/shard_map/ppermute | solution.py:455
  119.8 6.3 %collective-permute-start.41 = (bf16[1,16,2176]{2,1,0:T(8,128)(2,1)S(1)}, bf16[1,16,2176]{2,1,0:T(8,128)(2,1)S(1)}, u32[]{:S(2)}, u32[]{:S(2)}) collective-permute-start(bf16[1,16,2176]{2,1,0:T(8,128)(2,1)S(1)} %get-tuple-element.282), channel_id=1, source_target_pairs={{0,16},{1,17},{2,18},{3,19},{4,20},{5,21},{6,22},{7,23},{8,24},{9,... | collective-permute-start | bytes 208904 | tf_op jit(solution)/shard_map/ppermute | solution.py:455

commit v5 on v4

--- a/solution.py
+++ b/solution.py
@@ -269,14 +269,16 @@
     back_ref[...] = back
 
 
-def keep_kernel(
-    at_ref, after_ref, small_ref, w_ref, wi0, wi2, wo0, wo2, slope_ref, nl_ref, gl_ref, back_ref, xhat_ref, inv_ref, mixed_ref,
-    keep_ref, resid_ref, dwo_ref, gmix_ref, vec_ref,
-):
+def keep_kernel(at_ref, after_ref, wi0, wi2, wo0, wo2, slope_ref, nl_ref, gl_ref, back_ref, keep_ref, sum_ref):
     first = at_ref[5]
     back = back_ref[...]
     for k, wi_ref, wo_ref in ((0, wi0, wo0), (2, wi2, wo2)):
         back = back + inner_terms(k, wi_ref, wo_ref, slope_ref, nl_ref[...], gl_ref[...], keep_ref, first)
+    sum_ref[...] = back
+
+
+def resid_kernel(back_ref, small_ref, w_ref, xhat_ref, inv_ref, mixed_ref, resid_ref, dwo_ref, gmix_ref, vec_ref):
+    back = back_ref[...]
     xhat1 = xhat_ref[...]
     vec_ref[0:1] = jnp.sum(back * xhat1, axis=0, keepdims=True)
     vec_ref[1:2] = jnp.sum(back, axis=0, keepdims=True)
@@ -529,7 +531,7 @@
         wo_far = swap(wo_near, "dp", 2)
         top, bottom, biases = wo_near[: D // 2], wo_far[: D // 2], wo_near[D // 2 :]
         wo2 = jnp.where(z == 0, jnp.concatenate([top, bottom, biases]), jnp.concatenate([bottom, top, biases]))
-        plane[1], own, start, cot = tie(plane[1], own, start, cot)
+        plane[2], own, start, cot = tie(plane[2], own, start, cot)
         *plane, wo2, wi2 = tie(*plane, wo2, wi2)
         pieces = plane + [swap(piece, ALL, 1) for piece in plane]
         bits = [[2 * b + c + 8 * j for j in range(4)] for c in range(2) for b in range(4)]
@@ -621,18 +623,18 @@
     outer_mine, outer_give = add_low(outer_keep[0], outer_got[0]), add_low(outer_keep[1], outer_got[1])
     outer_y = swap(outer_give, "mp", 2)
 
-    inner_keep, resid, d_mix, g_mixed, vecs1 = call(
+    inner_keep, back = call(
         keep_kernel,
-        [
-            inner_shape,
-            square,
-            sds((D, D), LOW),
-            sds((D, SPAN), LOW),
-            sds((8, D), F32),
-        ],
-        [SMEM, ANY] + [VMEM] * 13,
-        [VMEM] * 5,
-    )(at, outer_give, small, w, wis[0], wis[2], wos[0], wos[2], slope, normed, grad_low, back, xhat, inv, mixed)
+        [inner_shape, square],
+        [SMEM, ANY] + [VMEM] * 8,
+        [VMEM] * 2,
+    )(at, outer_give, wis[0], wis[2], wos[0], wos[2], slope, normed, grad_low, back)
+    resid, d_mix, g_mixed, vecs1 = call(
+        resid_kernel,
+        [square, sds((D, D), LOW), sds((D, SPAN), LOW), sds((8, D), F32)],
+        [VMEM] * 6,
+        [VMEM] * 4,
+    )(back, small, w, xhat, inv, mixed)
 
     half = HEADS // 2
     some = half * HEAD
@@ -680,11 +682,11 @@
         halves_of = lambda v: (v[: v.shape[0] // 2], v[v.shape[0] // 2 :])
         both = lambda mine, got: [add_low(u, v) for u, v in zip(halves_of(mine), halves_of(got), strict=True)]
 
+        grad_rows = tokens_backward(inner_give)
+        rows_got = swap(grad_rows, "mp", 1)
+
         a_mine, *a_give = [g.reshape(-1, rows_each, WIDE) for g in weights_backward(inner_give)]
         a_got = [swap(g, ALL, 1) for g in a_give]
-
-        grad_rows = tokens_backward(inner_give)
-        rows_got = swap(grad_rows, "mp", 1)
 
         outer_y, grad_rows, a_mine = tie(outer_y, grad_rows, a_mine)
         q_mine, q_give = both(outer_mine, outer_y)

time: 131 us -> 130 us (level)
  waiting for transfers between devices: 41.8 us -> 36.5 us
  starting transfers between devices: 39.5 us -> 42.6 us
    ppermute x46, waiting for transfers between devices: 41.8 us -> 36.5 us  [swap(): return lax.ppermute(value, axis, [(i, i ^ bit) for i in range(n)])]
    ppermute x46, starting transfers between devices: 39.5 us -> 42.6 us  [swap(): return lax.ppermute(value, axis, [(i, i ^ bit) for i in range(n)])]
    pallas_call x1 -> x2, Pallas kernels: 3.45 us -> 3.68 us  [the longest x1 2.52 us: shards(): call(keep_kernel, [inner_shape, square], [SMEM, ANY] + [VMEM] * 8, [VMEM]...]
  transfers between devices with their start and end apart: 46 -> 46, of which waited for: 22 -> 19; matrix products, arithmetic and copies ran while one was open for 6% -> 6% of each run, Pallas kernels for 22% -> 23%
where the time goes in v5:
time: 130 us; the launch traced here: 129 us
  starting transfers between devices  42.6 us (33%)
  Pallas kernels  40.5 us (31%)
  waiting for transfers between devices  36.5 us (28%)
  local copies, waits for them, and re-layouts  5.14 us (4%)
  other arithmetic  3.39 us (3%)
    ppermute x46, starting transfers between devices, swap(): return lax.ppermute(value, axis, [(i, i ^ bit) for i in range(n)])  42.6 us
    ppermute x46, waiting for transfers between devices, swap(): return lax.ppermute(value, axis, [(i, i ^ bit) for i in range(n)])  36.5 us
    pallas_call x1, Pallas kernels, shards(): call(forward_kernel, [square_low, outer_shape, outer_shape, sds((4, SPAN,...  9.54 us
    pallas_call x2, Pallas kernels, heads_backward(): call(functools.partial(heads_kernel, low_h, low_h + half), [sds((3, some,...  4.48 us
    squeeze x3, local copies, waits for them, and re-layouts, shards(): pick = lambda v, i: lax.dynamic_index_in_dim(v, i, 0, keepdims=False)  4.19 us
    pallas_call x1, Pallas kernels, shards(): call(attend_kernel, [sds((HEADS, SPAN, SPAN), LOW), sds((D, SPAN), F32),...  3.56 us
    pallas_call x1, Pallas kernels, closing(): call(closing_kernel, shapes, [SMEM] + [VMEM] * 8, [ANY] + [VMEM] * (len(s...  2.92 us
    pallas_call x1, Pallas kernels, shards(): call(functools.partial(project_kernel, bits), [sds((D, WIDE), LOW), sds((...  2.63 us
  transfers between devices with their start and end apart: 46, of which 19 were waited for; matrix products, arithmetic and copies ran while one was open for 6% of the time, Pallas kernels for 23%

profile of v5, /device:TPU:0, one launch (start us, length us, event | category | flops | bytes accessed | tf_op | source)
XLA Modules:
  0.0 129.2 jit_solution(10501150388064718530)
XLA Ops:
  0.7 1.0 dynamic-slice_bitcast_fusion.4
  1.6 3.0 %collective-permute-start.3 = (bf16[256,512]{1,0:T(8,128)(2,1)S(1)}, bf16[256,512]{1,0:T(8,128)(2,1)S(1)}, u32[]{:S(2)}, u32[]{:S(2)}) collective-permute-start(bf16[256,512]{1,0:T(8,128)(2,1)S(1)} %dynamic-slice_bitcast_fusion.4), channel_id=1, source_target_pairs={{0,2},{1,3},{2,0},{3,1},{4,6},{5,7},{6,4},{7,5},{8,10},{9,11},{10,... | collective-permute-start | bytes 786440 | tf_op jit(solution)/shard_map/ppermute | solution.py:457
  4.7 1.5 %shard_map.262 = bf16[16,2176]{1,0:T(8,128)(2,1)} custom-call(bf16[16,512]{1,0:T(8,128)(2,1)} %q_ref.1, bf16[16,512]{1,0:T(8,128)(2,1)} %k_ref.1, bf16[16,512]{1,0:T(8,128)(2,1)} %v_ref.1, bf16[16,512]{1,0:T(8,128)(2,1)} %o_ref.1, bf16[16,20]{1,0:T(8,128)(2,1)} %bitcast.83, bf16[1,16]{1,0:T(2,128)(2,1)} %bitcast.84, bf16[1,16]{1,0:T(2,128)(2,1)} %bitcast.85, ...), custom_call_target="tpu_custom_call" | custom-call | flops 1 | bytes 1 | tf_op jit(solution)/shard_map/pallas_call | solution.py:513
  6.2 1.6 %collective-permute-start = (bf16[16,2176]{1,0:T(8,128)(2,1)}, bf16[16,2176]{1,0:T(8,128)(2,1)S(1)}, u32[]{:S(2)}, u32[]{:S(2)}) collective-permute-start(bf16[16,2176]{1,0:T(8,128)(2,1)} %shard_map.262), channel_id=1, source_target_pairs={{0,8},{1,9},{2,10},{3,11},{4,12},{5,13},{6,14},{7,15},{8,0},{9,1},... | collective-permute-start | bytes 208904 | tf_op jit(solution)/shard_map/ppermute | solution.py:457
  7.8 2.6 %collective-permute-start.1 = (bf16[16,2176]{1,0:T(8,128)(2,1)}, bf16[16,2176]{1,0:T(8,128)(2,1)S(1)}, u32[]{:S(2)}, u32[]{:S(2)}) collective-permute-start(bf16[16,2176]{1,0:T(8,128)(2,1)} %shard_map.262), channel_id=1, source_target_pairs={{0,16},{1,17},{2,18},{3,19},{4,20},{5,21},{6,22},{7,23},{8,24},{9,... | collective-permute-start | bytes 208904 | tf_op jit(solution)/shard_map/ppermute | solution.py:457
  10.6 0.7 reshape.127
  11.2 1.0 dynamic-slice_bitcast_fusion.3
  12.6 2.6 %collective-permute-done.1 = bf16[16,2176]{1,0:T(8,128)(2,1)S(1)} collective-permute-done((bf16[16,2176]{1,0:T(8,128)(2,1)}, bf16[16,2176]{1,0:T(8,128)(2,1)S(1)}, u32[]{:S(2)}, u32[]{:S(2)}) %collective-permute-start.1) | collective-permute-done | bytes 69664 | tf_op jit(solution)/shard_map/ppermute | solution.py:457
  15.2 1.5 %collective-permute-done.2 = bf16[16,2176]{1,0:T(8,128)(2,1)S(1)} collective-permute-done((bf16[16,2176]{1,0:T(8,128)(2,1)}, bf16[16,2176]{1,0:T(8,128)(2,1)S(1)}, u32[]{:S(2)}, u32[]{:S(2)}) %collective-permute-start.2) | collective-permute-done | bytes 69664 | tf_op jit(solution)/shard_map/ppermute | solution.py:457
  16.9 1.6 %collective-permute-start.4 = (bf16[64,2176]{1,0:T(8,128)(2,1)S(1)}, bf16[64,2176]{1,0:T(8,128)(2,1)}, u32[]{:S(2)}, u32[]{:S(2)}) collective-permute-start(bf16[64,2176]{1,0:T(8,128)(2,1)S(1)} %constant_dynamic-update-slice_fusion.refs_0_), channel_id=1, source_target_pairs={{0,4},{1,5},{2,6},{3,7},{4,0},{5,1},{6,2},{7,3},{8,12},{9,13},{10,... | collective-permute-start | bytes 835592 | tf_op jit(solution)/shard_map/ppermute | solution.py:457
  18.4 1.2 collective-permute-done.7
  19.6 0.8 collective-permute-start.8
  20.4 0.5 collective-permute-start.5
  20.9 2.3 %collective-permute-start.6 = (bf16[64,2176]{1,0:T(8,128)(2,1)S(1)}, bf16[64,2176]{1,0:T(8,128)(2,1)}, u32[]{:S(2)}, u32[]{:S(2)}) collective-permute-start(bf16[64,2176]{1,0:T(8,128)(2,1)S(1)} %constant_dynamic-update-slice_fusion.refs_0_), channel_id=1, source_target_pairs={{0,6},{1,7},{2,4},{3,5},{4,2},{5,3},{6,0},{7,1},{8,14},{9,15},{10,... | collective-permute-start | bytes 835592 | tf_op jit(solution)/shard_map/ppermute | solution.py:457
  23.2 2.3 %dynamic-slice_bitcast_fusion.1 = (bf16[512,512]{1,0:T(8,128)(2,1)}, bf16[512,512]{1,0:T(8,128)(2,1)S(1)}, bf16[512,512]{1,0:T(8,128)(2,1)S(1)}) fusion(bf16[4,512,512]{2,1,0:T(8,128)(2,1)} %bitcast.78, s32[]{:T(128)S(6)} %select_n.44, s32[]{:T(128)S(6)} %select_n.43, bf16[4,512,512]{2,1,0:T(8,128)(2,1)} %bitcast.81), kind=kLoop, calls=%fused_computation.21 | loop fusion | bytes 3145736 | tf_op jit(solution)/shard_map/jit(dynamic_index_in_dim)/squeeze | solution.py:501
  26.2 2.7 %collective-permute-done.8 = bf16[272,512]{1,0:T(8,128)(2,1)S(1)} collective-permute-done((bf16[272,512]{1,0:T(8,128)(2,1)S(1)}, bf16[272,512]{1,0:T(8,128)(2,1)S(1)}, u32[]{:S(2)}, u32[]{:S(2)}) %collective-permute-start.8) | collective-permute-done | bytes 278560 | tf_op jit(solution)/shard_map/ppermute | solution.py:457
  29.0 3.4 %collective-permute-done.5.refs_1_ = bf16[64,2176]{1,0:T(8,128)(2,1)} collective-permute-done((bf16[64,2176]{1,0:T(8,128)(2,1)S(1)}, bf16[64,2176]{1,0:T(8,128)(2,1)}, u32[]{:S(2)}, u32[]{:S(2)}) %collective-permute-start.5) | collective-permute-done | bytes 278560 | tf_op jit(solution)/shard_map/ppermute | solution.py:457
  32.4 0.5 collective-permute-start.11
  32.9 0.5 collective-permute-start.13
  33.6 1.2 maximum_maximum_fusion.wo0
  34.9 0.6 collective-permute-start.16
  36.0 2.6 %shard_map.263 = (bf16[512,2176]{1,0:T(8,128)(2,1)S(1)}, bf16[1536,512]{1,0:T(8,128)(2,1)S(1)}) custom-call(s32[7]{0:T(128)S(1)} %stack.49.at_ref, bf16[64,2176]{1,0:T(8,128)(2,1)S(1)} %constant_dynamic-update-slice_fusion.refs_0_, bf16[64,2176]{1,0:T(8,128)(2,1)} %collective-permute-done.5.refs_1_, bf16[64,2176]{1,0:T(8,128)(2,1)} %collective-permute-done.4.refs_2_, ...), custom_call_target="tpu_custom_call" | custom-call | flops 2000000000 | bytes 5242880 | tf_op jit(solution)/shard_map/pallas_call | solution.py:545
  38.6 2.3 %shard_map.264 = (f32[32,512]{1,0:T(8,128)S(1)}, f32[32,512]{1,0:T(8,128)S(1)}) custom-call(bf16[512,512]{1,0:T(8,128)(2,1)S(1)} %copy-done.1, bf16[512,2176]{1,0:T(8,128)(2,1)S(1)} %get-tuple-element.151.w_ref), custom_call_target="tpu_custom_call" | custom-call | flops 3000000000 | bytes 4194304 | tf_op jit(solution)/shard_map/pallas_call | solution.py:567
  40.9 3.6 %shard_map.265 = (bf16[8,512,512]{2,1,0:T(8,128)(2,1)S(1)}, f32[512,512]{1,0:T(8,128)S(1)}, f32[8,512]{1,0:T(8,128)S(1)}, f32[8,512]{1,0:T(8,128)S(1)}) custom-call(bf16[1536,512]{1,0:T(8,128)(2,1)S(1)} %get-tuple-element.153.qkv_ref), custom_call_target="tpu_custom_call" | custom-call | flops 5000000000 | bytes 7340032 | tf_op jit(solution)/shard_map/pallas_call | solution.py:553
  44.5 9.5 %shard_map.266 = (bf16[512,512]{1,0:T(8,128)(2,1)S(1)}, bf16[2,4,128,512]{3,2,1,0:T(8,128)(2,1)S(1)}, bf16[2,4,128,512]{3,2,1,0:T(8,128)(2,1)S(1)}, bf16[4,512,5...) custom-call(s32[7]{0:T(128)S(1)} %stack.49.at_ref, ...), custom_call_target="tpu_custom_call" | custom-call | flops 10000000000 | bytes 14680064 | tf_op jit(solution)/shard_map/pallas_call | solution.py:583
  54.2 2.5 %shard_map.267 = (bf16[2,4,136,512]{3,2,1,0:T(8,128)(2,1)S(1)}, f32[512,512]{1,0:T(8,128)S(1)}) custom-call(s32[7]{0:T(128)S(1)} %stack.49.at_ref, bf16[512,512]{1,0:T(8,128)(2,1)S(1)} %collective-permute-done.14.wi1, bf16[512,512]{1,0:T(8,128)(2,1)S(1)} %collective-permute-done.15.wi3, bf16[528,512]{1,0:T(8,128)(2,1)S(1)} %collective-permute-done.16.wo1, ...), custom_call_target="tpu_custom_call" | custom-call | flops 1 | bytes 1 | tf_op jit(solution)/shard_map/pallas_call | solution.py:615
  56.8 0.5 collective-permute-start.20
  57.6 0.6 collective-permute-start.19
  58.2 2.5 %shard_map.268 = (bf16[2,4,136,512]{3,2,1,0:T(8,128)(2,1)S(1)}, f32[512,512]{1,0:T(8,128)S(1)}) custom-call(s32[7]{0:T(128)S(1)} %stack.49.at_ref, bf16[4,128,512]{2,1,0:T(8,128)(2,1)S(1)} %get-tuple-element.266.after_ref, bf16[512,512]{1,0:T(8,128)(2,1)S(1)} %copy-done, bf16[512,512]{1,0:T(8,128)(2,1)S(1)} %maximum_select_fusion.1.wi2, ...), custom_call_target="tpu_custom_call" | custom-call | flops 1 | bytes 1 | tf_op jit(solution)/shard_map/pallas_call | solution.py:626
  61.1 1.6 %collective-permute-start.21 = (bf16[2,2,136,512]{3,2,1,0:T(8,128)(2,1)S(1)}, bf16[2,2,136,512]{3,2,1,0:T(8,128)(2,1)S(1)}, u32[]{:S(2)}, u32[]{:S(2)}) collective-permute-start(bf16[2,2,136,512]{3,2,1,0:T(8,128)(2,1)S(1)} %get-tuple-element.264.after_ref), channel_id=1, source_target_pairs={{0,4},{4,0},{8,12},{12,8},{16,20},{20,16},{24,28},{28,24},{1,5},{5... | collective-permute-start | bytes 1671176 | tf_op jit(solution)/shard_map/ppermute | solution.py:457
  62.6 1.2 shard_map.269
  63.8 2.2 %shard_map.270 = (bf16[3,256,512]{2,1,0:T(8,128)(2,1)S(1)}, f32[2,32,256]{2,1,0:T(8,128)S(1)}) custom-call(bf16[2,2,136,512]{3,2,1,0:T(8,128)(2,1)S(1)} %get-tuple-element.264.after_ref, bf16[1536,512]{1,0:T(8,128)(2,1)S(1)} %get-tuple-element.153.qkv_ref, bf16[8,512,512]{2,1,0:T(8,128)(2,1)S(1)} %get-tuple-element.176.p_ref, ...), custom_call_target="tpu_custom_call" | custom-call | flops 1 | bytes 1 | tf_op jit(solution)/shard_map/pallas_call | solution.py:643
  66.0 2.2 %shard_map.271 = (bf16[3,256,512]{2,1,0:T(8,128)(2,1)S(1)}, f32[2,32,256]{2,1,0:T(8,128)S(1)}) custom-call(bf16[2,2,136,512]{3,2,1,0:T(8,128)(2,1)S(1)} %get-tuple-element.264.after_ref, bf16[1536,512]{1,0:T(8,128)(2,1)S(1)} %get-tuple-element.153.qkv_ref, bf16[8,512,512]{2,1,0:T(8,128)(2,1)S(1)} %get-tuple-element.176.p_ref, ...), custom_call_target="tpu_custom_call" | custom-call | flops 1 | bytes 1 | tf_op jit(solution)/shard_map/pallas_call | solution.py:643
  68.3 1.2 shard_map.272.r0
  69.5 2.6 %shard_map.273 = (bf16[256,2176]{1,0:T(8,128)(2,1)S(1)}, bf16[64,2176]{1,0:T(8,128)(2,1)S(1)}, bf16[64,2176]{1,0:T(8,128)(2,1)S(1)}, bf16[64,2176]{1,0:T(8,128)(2,1)S(1)}, bf16[64,2176]{1,0:T(8,128)(2,1)S(1)}) custom-call(bf16[2,2,136,512]{3,2,1,0:T(8,128)(2,1)S(1)} %get-tuple-element.264.after_ref, s32[7]{0:T(128)S(1)} %stack.49.at_ref, ...), custom_call_target="tpu_custom_call" | custom-call | flops 1 | bytes 1 | tf_op jit(solution)/shard_map/pallas_call | solution.py:670
  72.1 0.5 collective-permute-start.24
  73.3 2.2 %collective-permute-done.21 = bf16[2,2,136,512]{3,2,1,0:T(8,128)(2,1)S(1)} collective-permute-done((bf16[2,2,136,512]{3,2,1,0:T(8,128)(2,1)S(1)}, bf16[2,2,136,512]{3,2,1,0:T(8,128)(2,1)S(1)}, u32[]{:S(2)}, u32[]{:S(2)}) %collective-permute-start.21) | collective-permute-done | bytes 557088 | tf_op jit(solution)/shard_map/ppermute | solution.py:457
  75.5 1.5 %collective-permute-start.22 = (bf16[2,128,512]{2,1,0:T(8,128)(2,1)S(1)}, bf16[2,128,512]{2,1,0:T(8,128)(2,1)S(1)}, u32[]{:S(2)}, u32[]{:S(2)}) collective-permute-start(bf16[2,128,512]{2,1,0:T(8,128)(2,1)S(1)} %get-tuple-element.276), channel_id=1, source_target_pairs={{0,4},{4,0},{8,12},{12,8},{16,20},{20,16},{24,28},{28,24},{1,5},{5... | collective-permute-start | bytes 786440 | tf_op jit(solution)/shard_map/ppermute | solution.py:457
  77.2 1.6 %collective-permute-start.29 = (bf16[2,136,512]{2,1,0:T(8,128)(2,1)S(1)}, bf16[2,136,512]{2,1,0:T(8,128)(2,1)S(1)}, u32[]{:S(2)}, u32[]{:S(2)}) collective-permute-start(bf16[2,136,512]{2,1,0:T(8,128)(2,1)S(1)} %get-tuple-element.273), channel_id=1, source_target_pairs={{0,2},{1,3},{2,0},{3,1},{4,6},{5,7},{6,4},{7,5},{8,10},{9,11},{10,... | collective-permute-start | bytes 835592 | tf_op jit(solution)/shard_map/ppermute | solution.py:457
  79.0 0.6 collective-permute-start.31
  79.6 5.1 %collective-permute-done.22 = bf16[2,128,512]{2,1,0:T(8,128)(2,1)S(1)} collective-permute-done((bf16[2,128,512]{2,1,0:T(8,128)(2,1)S(1)}, bf16[2,128,512]{2,1,0:T(8,128)(2,1)S(1)}, u32[]{:S(2)}, u32[]{:S(2)}) %collective-permute-start.22) | collective-permute-done | bytes 262176 | tf_op jit(solution)/shard_map/ppermute | solution.py:457
  84.8 1.6 %collective-permute-start.27 = (bf16[512,512]{1,0:T(8,128)(2,1)S(1)}, bf16[512,512]{1,0:T(8,128)(2,1)S(1)}, u32[]{:S(2)}, u32[]{:S(2)}) collective-permute-start(bf16[512,512]{1,0:T(8,128)(2,1)S(1)} %shard_map.272.r0), channel_id=1, source_target_pairs={{0,2},{1,3},{2,0},{3,1},{4,6},{5,7},{6,4},{7,5},{8,10},{9,11},{10,... | collective-permute-start | bytes 1572872 | tf_op jit(solution)/shard_map/ppermute | solution.py:457
  86.4 1.5 %collective-permute-start.28 = (bf16[128,512]{1,0:T(8,128)(2,1)S(1)}, bf16[128,512]{1,0:T(8,128)(2,1)S(1)}, u32[]{:S(2)}, u32[]{:S(2)}) collective-permute-start(bf16[128,512]{1,0:T(8,128)(2,1)S(1)} %get-tuple-element.281), channel_id=1, source_target_pairs={{0,8},{4,12},{8,0},{12,4},{16,24},{20,28},{24,16},{28,20},{1,9},{5... | collective-permute-start | bytes 393224 | tf_op jit(solution)/shard_map/ppermute | solution.py:457
  87.9 0.6 collective-permute-start.32
  88.5 2.9 %collective-permute-done.28 = bf16[128,512]{1,0:T(8,128)(2,1)S(1)} collective-permute-done((bf16[128,512]{1,0:T(8,128)(2,1)S(1)}, bf16[128,512]{1,0:T(8,128)(2,1)S(1)}, u32[]{:S(2)}, u32[]{:S(2)}) %collective-permute-start.28) | collective-permute-done | bytes 131104 | tf_op jit(solution)/shard_map/ppermute | solution.py:457
  91.5 3.4 %collective-permute-start.30 = (bf16[128,512]{1,0:T(8,128)(2,1)S(1)}, bf16[128,512]{1,0:T(8,128)(2,1)S(1)}, u32[]{:S(2)}, u32[]{:S(2)}) collective-permute-start(bf16[128,512]{1,0:T(8,128)(2,1)S(1)} %add_convert_fusion.17), channel_id=1, source_target_pairs={{0,16},{4,20},{8,24},{12,28},{16,0},{20,4},{24,8},{28,12},{1,17},{... | collective-permute-start | bytes 393224 | tf_op jit(solution)/shard_map/ppermute | solution.py:457
  95.1 1.2 collective-permute-start.36
  96.3 0.9 collective-permute-start.40
  97.2 2.1 %collective-permute-done.30 = bf16[128,512]{1,0:T(8,128)(2,1)S(1)} collective-permute-done((bf16[128,512]{1,0:T(8,128)(2,1)S(1)}, bf16[128,512]{1,0:T(8,128)(2,1)S(1)}, u32[]{:S(2)}, u32[]{:S(2)}) %collective-permute-start.30) | collective-permute-done | bytes 131104 | tf_op jit(solution)/shard_map/ppermute | solution.py:457
  99.3 1.6 %collective-permute-start.35 = (bf16[136,512]{1,0:T(8,128)(2,1)S(1)}, bf16[136,512]{1,0:T(8,128)(2,1)S(1)}, u32[]{:S(2)}, u32[]{:S(2)}) collective-permute-start(bf16[136,512]{1,0:T(8,128)(2,1)S(1)} %add_convert_fusion.13), channel_id=1, source_target_pairs={{0,16},{4,20},{8,24},{12,28},{16,0},{20,4},{24,8},{28,12},{1,17},{... | collective-permute-start | bytes 417800 | tf_op jit(solution)/shard_map/ppermute | solution.py:457
  100.9 2.8 %collective-permute-start.34 = (bf16[128,512]{1,0:T(8,128)(2,1)S(1)}, bf16[128,512]{1,0:T(8,128)(2,1)S(1)}, u32[]{:S(2)}, u32[]{:S(2)}) collective-permute-start(bf16[128,512]{1,0:T(8,128)(2,1)S(1)} %add_convert_fusion.16), channel_id=1, source_target_pairs={{0,8},{4,12},{8,0},{12,4},{16,24},{20,28},{24,16},{28,20},{1,9},{5... | collective-permute-start | bytes 393224 | tf_op jit(solution)/shard_map/ppermute | solution.py:457
  103.8 1.0 collective-permute-done.36
  104.9 2.9 %collective-permute-done.35 = bf16[136,512]{1,0:T(8,128)(2,1)S(1)} collective-permute-done((bf16[136,512]{1,0:T(8,128)(2,1)S(1)}, bf16[136,512]{1,0:T(8,128)(2,1)S(1)}, u32[]{:S(2)}, u32[]{:S(2)}) %collective-permute-start.35) | collective-permute-done | bytes 139296 | tf_op jit(solution)/shard_map/ppermute | solution.py:457
  108.4 1.5 %collective-permute-start.38 = (bf16[2,16,2176]{2,1,0:T(8,128)(2,1)S(1)}, bf16[2,16,2176]{2,1,0:T(8,128)(2,1)S(1)}, u32[]{:S(2)}, u32[]{:S(2)}) collective-permute-start(bf16[2,16,2176]{2,1,0:T(8,128)(2,1)S(1)} %get-tuple-element.277), channel_id=1, source_target_pairs={{0,8},{1,9},{2,10},{3,11},{4,12},{5,13},{6,14},{7,15},{8,0},{9,1},... | collective-permute-start | bytes 417800 | tf_op jit(solution)/shard_map/ppermute | solution.py:457
  109.9 3.0 %collective-permute-done.40.r2 = bf16[512,512]{1,0:T(8,128)(2,1)S(1)} collective-permute-done((bf16[512,512]{1,0:T(8,128)(2,1)S(1)}, bf16[512,512]{1,0:T(8,128)(2,1)S(1)}, u32[]{:S(2)}, u32[]{:S(2)}) %collective-permute-start.40) | collective-permute-done | bytes 524320 | tf_op jit(solution)/shard_map/ppermute | solution.py:457
  112.9 1.4 %collective-permute-done.39 = bf16[136,512]{1,0:T(8,128)(2,1)S(1)} collective-permute-done((bf16[136,512]{1,0:T(8,128)(2,1)S(1)}, bf16[136,512]{1,0:T(8,128)(2,1)S(1)}, u32[]{:S(2)}, u32[]{:S(2)}) %collective-permute-start.39) | collective-permute-done | bytes 139296 | tf_op jit(solution)/shard_map/ppermute | solution.py:457
  114.2 1.5 %collective-permute-start.37 = (bf16[2,128,512]{2,1,0:T(8,128)(2,1)S(1)}, bf16[2,128,512]{2,1,0:T(8,128)(2,1)S(1)}, u32[]{:S(2)}, u32[]{:S(2)}) collective-permute-start(bf16[2,128,512]{2,1,0:T(8,128)(2,1)S(1)} %pad_maximum_fusion.1.own_ref), channel_id=1, source_target_pairs={{0,4},{4,0},{8,12},{12,8},{16,20},{20,16},{24,28},{28,24},{1,5},{5... | collective-permute-start | bytes 786440 | tf_op jit(solution)/shard_map/ppermute | solution.py:457
  115.9 1.4 %collective-permute-start.45 = (bf16[2,136,512]{2,1,0:T(8,128)(2,1)S(1)}, bf16[2,136,512]{2,1,0:T(8,128)(2,1)S(1)}, u32[]{:S(2)}, u32[]{:S(2)}) collective-permute-start(bf16[2,136,512]{2,1,0:T(8,128)(2,1)S(1)} %pad_maximum_fusion.own_ref), channel_id=1, source_target_pairs={{0,4},{4,0},{8,12},{12,8},{16,20},{20,16},{24,28},{28,24},{1,5},{5... | collective-permute-start | bytes 835592 | tf_op jit(solution)/shard_map/ppermute | solution.py:457
  117.8 1.8 %collective-permute-start.41 = (bf16[1,16,2176]{2,1,0:T(8,128)(2,1)S(1)}, bf16[1,16,2176]{2,1,0:T(8,128)(2,1)S(1)}, u32[]{:S(2)}, u32[]{:S(2)}) collective-permute-start(bf16[1,16,2176]{2,1,0:T(8,128)(2,1)S(1)} %get-tuple-element.284), channel_id=1, source_target_pairs={{0,16},{1,17},{2,18},{3,19},{4,20},{5,21},{6,22},{7,23},{8,24},{9,... | collective-permute-start | bytes 208904 | tf_op jit(solution)/shard_map/ppermute | solution.py:457
  119.6 1.9 %shard_map.274 = bf16[4,512,512]{2,1,0:T(8,128)(2,1)} custom-call(s32[7]{0:T(128)S(1)} %stack.49.at_ref, bf16[512,512]{1,0:T(8,128)(2,1)S(1)} %get-tuple-element.235.r0, bf16[512,512]{1,0:T(8,128)(2,1)S(1)} %collective-permute-done.42.r1, bf16[512,512]{1,0:T(8,128)(2,1)S(1)} %collective-permute-done.40.r2, bf16[512,512]{1,0:T(8,128)(2,1)S(1)} %collective-permute-done.43.r3), custom_call_target="tpu_custom_call" | custom-call | flops 1 | bytes 1 | tf_op jit(solution)/shard_map/pallas_call | solution.py:392
  121.5 2.5 %collective-permute-done.41.got_ref = bf16[1,16,2176]{2,1,0:T(8,128)(2,1)S(1)} collective-permute-done((bf16[1,16,2176]{2,1,0:T(8,128)(2,1)S(1)}, bf16[1,16,2176]{2,1,0:T(8,128)(2,1)S(1)}, u32[]{:S(2)}, u32[]{:S(2)}) %collective-permute-start.41) | collective-permute-done | bytes 69664 | tf_op jit(solution)/shard_map/ppermute | solution.py:457
  124.0 2.9 %shard_map.275 = (bf16[4,512,512]{2,1,0:T(8,128)(2,1)}, f32[512,512]{1,0:T(8,128)}, f32[16,20]{1,0:T(8,128)}, f32[16,512]{1,0:T(8,128)}, f32[16,512]{1,0:T(8,128...) custom-call(s32[7]{0:T(128)S(1)} %stack.49.at_ref, ...), custom_call_target="tpu_custom_call" | custom-call | flops 1 | bytes 1 | tf_op jit(solution)/shard_map/pallas_call | solution.py:443
  126.9 0.7 collective-permute-done.45.other_ref
  127.6 1.7 %shard_map.276 = (f32[512,512]{1,0:T(8,128)}, f32[1,512]{1,0:T(1,128)}) custom-call(s32[7]{0:T(128)S(1)} %stack.49.at_ref, bf16[2,136,512]{2,1,0:T(8,128)(2,1)S(1)} %pad_maximum_fusion.own_ref, bf16[2,136,512]{2,1,0:T(8,128)(2,1)S(1)} %collective-permute-done.45.other_ref), custom_call_target="tpu_custom_call" | custom-call | flops 1 | bytes 2097152 | tf_op jit(solution)/shard_map/pallas_call | solution.py:469
  (83 shorter events, 6.0 us)
Async XLA Ops:
  1.6 15.1 %collective-permute-start.3 = (bf16[256,512]{1,0:T(8,128)(2,1)S(1)}, bf16[256,512]{1,0:T(8,128)(2,1)S(1)}, u32[]{:S(2)}, u32[]{:S(2)}) collective-permute-start(bf16[256,512]{1,0:T(8,128)(2,1)S(1)} %dynamic-slice_bitcast_fusion.4), channel_id=1, source_target_pairs={{0,2},{1,3},{2,0},{3,1},{4,6},{5,7},{6,4},{7,5},{8,10},{9,11},{10,... | collective-permute-start | bytes 786440 | tf_op jit(solution)/shard_map/ppermute | solution.py:457
  6.2 10.5 %copy-start.2 = (bf16[16,2176]{1,0:T(8,128)(2,1)S(1)}, bf16[16,2176]{1,0:T(8,128)(2,1)}, u32[]{:S(2)}) copy-start(bf16[16,2176]{1,0:T(8,128)(2,1)} %shard_map.262) | copy-start | bytes 208900
  6.2 6.4 %collective-permute-start = (bf16[16,2176]{1,0:T(8,128)(2,1)}, bf16[16,2176]{1,0:T(8,128)(2,1)S(1)}, u32[]{:S(2)}, u32[]{:S(2)}) collective-permute-start(bf16[16,2176]{1,0:T(8,128)(2,1)} %shard_map.262), channel_id=1, source_target_pairs={{0,8},{1,9},{2,10},{3,11},{4,12},{5,13},{6,14},{7,15},{8,0},{9,1},... | collective-permute-start | bytes 208904 | tf_op jit(solution)/shard_map/ppermute | solution.py:457
  7.8 7.5 %collective-permute-start.1 = (bf16[16,2176]{1,0:T(8,128)(2,1)}, bf16[16,2176]{1,0:T(8,128)(2,1)S(1)}, u32[]{:S(2)}, u32[]{:S(2)}) collective-permute-start(bf16[16,2176]{1,0:T(8,128)(2,1)} %shard_map.262), channel_id=1, source_target_pairs={{0,16},{1,17},{2,18},{3,19},{4,20},{5,21},{6,22},{7,23},{8,24},{9,... | collective-permute-start | bytes 208904 | tf_op jit(solution)/shard_map/ppermute | solution.py:457
  10.3 6.4 %collective-permute-start.2 = (bf16[16,2176]{1,0:T(8,128)(2,1)}, bf16[16,2176]{1,0:T(8,128)(2,1)S(1)}, u32[]{:S(2)}, u32[]{:S(2)}) collective-permute-start(bf16[16,2176]{1,0:T(8,128)(2,1)} %shard_map.262), channel_id=1, source_target_pairs={{0,24},{1,25},{2,26},{3,27},{4,28},{5,29},{6,30},{7,31},{8,16},{9,... | collective-permute-start | bytes 208904 | tf_op jit(solution)/shard_map/ppermute | solution.py:457
  12.2 7.4 %collective-permute-start.7 = (bf16[272,512]{1,0:T(8,128)(2,1)S(1)}, bf16[272,512]{1,0:T(8,128)(2,1)S(1)}, u32[]{:S(2)}, u32[]{:S(2)}) collective-permute-start(bf16[272,512]{1,0:T(8,128)(2,1)S(1)} %fusion.4), channel_id=1, source_target_pairs={{0,2},{1,3},{2,0},{3,1},{4,6},{5,7},{6,4},{7,5},{8,10},{9,11},{10,... | collective-permute-start | bytes 835592 | tf_op jit(solution)/shard_map/ppermute | solution.py:457
  16.7 9.2 %collective-permute-start.9 = (bf16[256,512]{1,0:T(8,128)(2,1)S(1)}, bf16[256,512]{1,0:T(8,128)(2,1)S(1)}, u32[]{:S(2)}, u32[]{:S(2)}) collective-permute-start(bf16[256,512]{1,0:T(8,128)(2,1)S(1)} %collective-permute-done.3), channel_id=1, source_target_pairs={{0,8},{4,12},{8,0},{12,4},{16,24},{20,28},{24,16},{28,20},{1,9},{5... | collective-permute-start | bytes 786440 | tf_op jit(solution)/shard_map/ppermute | solution.py:457
  16.9 9.3 %collective-permute-start.4 = (bf16[64,2176]{1,0:T(8,128)(2,1)S(1)}, bf16[64,2176]{1,0:T(8,128)(2,1)}, u32[]{:S(2)}, u32[]{:S(2)}) collective-permute-start(bf16[64,2176]{1,0:T(8,128)(2,1)S(1)} %constant_dynamic-update-slice_fusion.refs_0_), channel_id=1, source_target_pairs={{0,4},{1,5},{2,6},{3,7},{4,0},{5,1},{6,2},{7,3},{8,12},{9,13},{10,... | collective-permute-start | bytes 835592 | tf_op jit(solution)/shard_map/ppermute | solution.py:457
  19.6 9.2 %collective-permute-start.8 = (bf16[272,512]{1,0:T(8,128)(2,1)S(1)}, bf16[272,512]{1,0:T(8,128)(2,1)S(1)}, u32[]{:S(2)}, u32[]{:S(2)}) collective-permute-start(bf16[272,512]{1,0:T(8,128)(2,1)S(1)} %collective-permute-done.7), channel_id=1, source_target_pairs={{0,8},{4,12},{8,0},{12,4},{16,24},{20,28},{24,16},{28,20},{1,9},{5... | collective-permute-start | bytes 835592 | tf_op jit(solution)/shard_map/ppermute | solution.py:457
  20.4 12.0 %collective-permute-start.5 = (bf16[64,2176]{1,0:T(8,128)(2,1)S(1)}, bf16[64,2176]{1,0:T(8,128)(2,1)}, u32[]{:S(2)}, u32[]{:S(2)}) collective-permute-start(bf16[64,2176]{1,0:T(8,128)(2,1)S(1)} %constant_dynamic-update-slice_fusion.refs_0_), channel_id=1, source_target_pairs={{0,2},{1,3},{2,0},{3,1},{4,6},{5,7},{6,4},{7,5},{8,10},{9,11},{10,... | collective-permute-start | bytes 835592 | tf_op jit(solution)/shard_map/ppermute | solution.py:457
  20.9 11.5 %collective-permute-start.6 = (bf16[64,2176]{1,0:T(8,128)(2,1)S(1)}, bf16[64,2176]{1,0:T(8,128)(2,1)}, u32[]{:S(2)}, u32[]{:S(2)}) collective-permute-start(bf16[64,2176]{1,0:T(8,128)(2,1)S(1)} %constant_dynamic-update-slice_fusion.refs_0_), channel_id=1, source_target_pairs={{0,6},{1,7},{2,4},{3,5},{4,2},{5,3},{6,0},{7,1},{8,14},{9,15},{10,... | collective-permute-start | bytes 835592 | tf_op jit(solution)/shard_map/ppermute | solution.py:457
  26.1 7.3 %copy-start = (bf16[512,512]{1,0:T(8,128)(2,1)S(1)}, bf16[512,512]{1,0:T(8,128)(2,1)}, u32[]{:S(2)}) copy-start(bf16[512,512]{1,0:T(8,128)(2,1)} %wi0.3) | copy-start | bytes 1572868
  32.4 2.4 %collective-permute-start.10 = (bf16[64,2176]{1,0:T(8,128)(2,1)S(1)}, bf16[64,2176]{1,0:T(8,128)(2,1)}, u32[]{:S(2)}, u32[]{:S(2)}) collective-permute-start(bf16[64,2176]{1,0:T(8,128)(2,1)S(1)} %constant_dynamic-update-slice_fusion.refs_0_), channel_id=1, source_target_pairs={{0,1},{1,0},{2,3},{3,2},{4,5},{5,4},{6,7},{7,6},{8,9},{9,8},{10,11... | collective-permute-start | bytes 835592 | tf_op jit(solution)/shard_map/ppermute | solution.py:457
  32.4 3.0 %collective-permute-start.11 = (bf16[64,2176]{1,0:T(8,128)(2,1)}, bf16[64,2176]{1,0:T(8,128)(2,1)}, u32[]{:S(2)}, u32[]{:S(2)}) collective-permute-start(bf16[64,2176]{1,0:T(8,128)(2,1)} %collective-permute-done.5.refs_1_), channel_id=1, source_target_pairs={{0,1},{1,0},{2,3},{3,2},{4,5},{5,4},{6,7},{7,6},{8,9},{9,8},{10,11... | collective-permute-start | bytes 835592 | tf_op jit(solution)/shard_map/ppermute | solution.py:457
  32.9 2.6 %collective-permute-start.12 = (bf16[64,2176]{1,0:T(8,128)(2,1)}, bf16[64,2176]{1,0:T(8,128)(2,1)}, u32[]{:S(2)}, u32[]{:S(2)}) collective-permute-start(bf16[64,2176]{1,0:T(8,128)(2,1)} %collective-permute-done.4.refs_2_), channel_id=1, source_target_pairs={{0,1},{1,0},{2,3},{3,2},{4,5},{5,4},{6,7},{7,6},{8,9},{9,8},{10,11... | collective-permute-start | bytes 835592 | tf_op jit(solution)/shard_map/ppermute | solution.py:457
  32.9 3.0 %collective-permute-start.13 = (bf16[64,2176]{1,0:T(8,128)(2,1)}, bf16[64,2176]{1,0:T(8,128)(2,1)}, u32[]{:S(2)}, u32[]{:S(2)}) collective-permute-start(bf16[64,2176]{1,0:T(8,128)(2,1)} %collective-permute-done.6.refs_3_), channel_id=1, source_target_pairs={{0,1},{1,0},{2,3},{3,2},{4,5},{5,4},{6,7},{7,6},{8,9},{9,8},{10,11... | collective-permute-start | bytes 835592 | tf_op jit(solution)/shard_map/ppermute | solution.py:457
  33.4 11.0 %collective-permute-start.14 = (bf16[512,512]{1,0:T(8,128)(2,1)S(1)}, bf16[512,512]{1,0:T(8,128)(2,1)S(1)}, u32[]{:S(2)}, u32[]{:S(2)}) collective-permute-start(bf16[512,512]{1,0:T(8,128)(2,1)S(1)} %copy-done), channel_id=1, source_target_pairs={{0,1},{1,0},{2,3},{3,2},{4,5},{5,4},{6,7},{7,6},{8,9},{9,8},{10,11... | collective-permute-start | bytes 1572872 | tf_op jit(solution)/shard_map/ppermute | solution.py:457
  34.8 3.8 %copy-start.1 = (bf16[512,512]{1,0:T(8,128)(2,1)S(1)}, bf16[512,512]{1,0:T(8,128)(2,1)}, u32[]{:S(2)}) copy-start(bf16[512,512]{1,0:T(8,128)(2,1)} %get-tuple-element.143.x1_ref) | copy-start | bytes 1572868
  34.9 9.6 %collective-permute-start.16 = (bf16[528,512]{1,0:T(8,128)(2,1)S(1)}, bf16[528,512]{1,0:T(8,128)(2,1)S(1)}, u32[]{:S(2)}, u32[]{:S(2)}) collective-permute-start(bf16[528,512]{1,0:T(8,128)(2,1)S(1)} %maximum_maximum_fusion.wo0), channel_id=1, source_target_pairs={{0,1},{1,0},{2,3},{3,2},{4,5},{5,4},{6,7},{7,6},{8,9},{9,8},{10,11... | collective-permute-start | bytes 1622024 | tf_op jit(solution)/shard_map/ppermute | solution.py:457
  35.4 9.1 %collective-permute-start.15 = (bf16[512,512]{1,0:T(8,128)(2,1)S(1)}, bf16[512,512]{1,0:T(8,128)(2,1)S(1)}, u32[]{:S(2)}, u32[]{:S(2)}) collective-permute-start(bf16[512,512]{1,0:T(8,128)(2,1)S(1)} %maximum_select_fusion.1.wi2), channel_id=1, source_target_pairs={{0,1},{1,0},{2,3},{3,2},{4,5},{5,4},{6,7},{7,6},{8,9},{9,8},{10,11... | collective-permute-start | bytes 1572872 | tf_op jit(solution)/shard_map/ppermute | solution.py:457
  35.5 9.0 %collective-permute-start.17 = (bf16[528,512]{1,0:T(8,128)(2,1)S(1)}, bf16[528,512]{1,0:T(8,128)(2,1)S(1)}, u32[]{:S(2)}, u32[]{:S(2)}) collective-permute-start(bf16[528,512]{1,0:T(8,128)(2,1)S(1)} %maximum_select_fusion.wo2), channel_id=1, source_target_pairs={{0,1},{1,0},{2,3},{3,2},{4,5},{5,4},{6,7},{7,6},{8,9},{9,8},{10,11... | collective-permute-start | bytes 1622024 | tf_op jit(solution)/shard_map/ppermute | solution.py:457
  54.1 3.2 %collective-permute-start.18 = (bf16[2,4,128,512]{3,2,1,0:T(8,128)(2,1)S(1)}, bf16[2,4,128,512]{3,2,1,0:T(8,128)(2,1)S(1)}, u32[]{:S(2)}, u32[]{:S(2)}) collective-permute-start(bf16[2,4,128,512]{3,2,1,0:T(8,128)(2,1)S(1)} %get-tuple-element.168), channel_id=1, source_target_pairs={{0,1},{1,0},{2,3},{3,2},{4,5},{5,4},{6,7},{7,6},{8,9},{9,8},{10,11... | collective-permute-start | bytes 3145736 | tf_op jit(solution)/shard_map/ppermute | solution.py:457
  56.8 3.9 %collective-permute-start.20 = (bf16[2,4,136,512]{3,2,1,0:T(8,128)(2,1)S(1)}, bf16[2,4,136,512]{3,2,1,0:T(8,128)(2,1)S(1)}, u32[]{:S(2)}, u32[]{:S(2)}) collective-permute-start(bf16[2,4,136,512]{3,2,1,0:T(8,128)(2,1)S(1)} %get-tuple-element.175), channel_id=1, source_target_pairs={{0,1},{1,0},{2,3},{3,2},{4,5},{5,4},{6,7},{7,6},{8,9},{9,8},{10,11... | collective-permute-start | bytes 3342344 | tf_op jit(solution)/shard_map/ppermute | solution.py:457
  57.6 15.1 %collective-permute-start.19 = (bf16[4,128,512]{2,1,0:T(8,128)(2,1)S(1)}, bf16[4,128,512]{2,1,0:T(8,128)(2,1)S(1)}, u32[]{:S(2)}, u32[]{:S(2)}) collective-permute-start(bf16[4,128,512]{2,1,0:T(8,128)(2,1)S(1)} %get-tuple-element.266.after_ref), channel_id=1, source_target_pairs={{0,2},{1,3},{2,0},{3,1},{4,6},{5,7},{6,4},{7,5},{8,10},{9,11},{10,... | collective-permute-start | bytes 1572872 | tf_op jit(solution)/shard_map/ppermute | solution.py:457
  61.1 14.4 %collective-permute-start.21 = (bf16[2,2,136,512]{3,2,1,0:T(8,128)(2,1)S(1)}, bf16[2,2,136,512]{3,2,1,0:T(8,128)(2,1)S(1)}, u32[]{:S(2)}, u32[]{:S(2)}) collective-permute-start(bf16[2,2,136,512]{3,2,1,0:T(8,128)(2,1)S(1)} %get-tuple-element.264.after_ref), channel_id=1, source_target_pairs={{0,4},{4,0},{8,12},{12,8},{16,20},{20,16},{24,28},{28,24},{1,5},{5... | collective-permute-start | bytes 1671176 | tf_op jit(solution)/shard_map/ppermute | solution.py:457
  72.0 5.1 %collective-permute-start.23 = (bf16[4,16,2176]{2,1,0:T(8,128)(2,1)S(1)}, bf16[4,16,2176]{2,1,0:T(8,128)(2,1)S(1)}, u32[]{:S(2)}, u32[]{:S(2)}) collective-permute-start(bf16[4,16,2176]{2,1,0:T(8,128)(2,1)S(1)} %bitcast.74), channel_id=1, source_target_pairs={{0,1},{1,0},{2,3},{3,2},{4,5},{5,4},{6,7},{7,6},{8,9},{9,8},{10,11... | collective-permute-start | bytes 835592 | tf_op jit(solution)/shard_map/ppermute | solution.py:457
  72.1 5.0 %collective-permute-start.24 = (bf16[4,16,2176]{2,1,0:T(8,128)(2,1)S(1)}, bf16[4,16,2176]{2,1,0:T(8,128)(2,1)S(1)}, u32[]{:S(2)}, u32[]{:S(2)}) collective-permute-start(bf16[4,16,2176]{2,1,0:T(8,128)(2,1)S(1)} %bitcast.73), channel_id=1, source_target_pairs={{0,1},{1,0},{2,3},{3,2},{4,5},{5,4},{6,7},{7,6},{8,9},{9,8},{10,11... | collective-permute-start | bytes 835592 | tf_op jit(solution)/shard_map/ppermute | solution.py:457
  72.6 4.5 %collective-permute-start.25 = (bf16[4,16,2176]{2,1,0:T(8,128)(2,1)S(1)}, bf16[4,16,2176]{2,1,0:T(8,128)(2,1)S(1)}, u32[]{:S(2)}, u32[]{:S(2)}) collective-permute-start(bf16[4,16,2176]{2,1,0:T(8,128)(2,1)S(1)} %bitcast.72), channel_id=1, source_target_pairs={{0,1},{1,0},{2,3},{3,2},{4,5},{5,4},{6,7},{7,6},{8,9},{9,8},{10,11... | collective-permute-start | bytes 835592 | tf_op jit(solution)/shard_map/ppermute | solution.py:457
  72.7 4.4 %collective-permute-start.26 = (bf16[4,16,2176]{2,1,0:T(8,128)(2,1)S(1)}, bf16[4,16,2176]{2,1,0:T(8,128)(2,1)S(1)}, u32[]{:S(2)}, u32[]{:S(2)}) collective-permute-start(bf16[4,16,2176]{2,1,0:T(8,128)(2,1)S(1)} %bitcast.71), channel_id=1, source_target_pairs={{0,1},{1,0},{2,3},{3,2},{4,5},{5,4},{6,7},{7,6},{8,9},{9,8},{10,11... | collective-permute-start | bytes 835592 | tf_op jit(solution)/shard_map/ppermute | solution.py:457
  75.5 9.2 %collective-permute-start.22 = (bf16[2,128,512]{2,1,0:T(8,128)(2,1)S(1)}, bf16[2,128,512]{2,1,0:T(8,128)(2,1)S(1)}, u32[]{:S(2)}, u32[]{:S(2)}) collective-permute-start(bf16[2,128,512]{2,1,0:T(8,128)(2,1)S(1)} %get-tuple-element.276), channel_id=1, source_target_pairs={{0,4},{4,0},{8,12},{12,8},{16,20},{20,16},{24,28},{28,24},{1,5},{5... | collective-permute-start | bytes 786440 | tf_op jit(solution)/shard_map/ppermute | solution.py:457
  77.2 10.7 %collective-permute-start.29 = (bf16[2,136,512]{2,1,0:T(8,128)(2,1)S(1)}, bf16[2,136,512]{2,1,0:T(8,128)(2,1)S(1)}, u32[]{:S(2)}, u32[]{:S(2)}) collective-permute-start(bf16[2,136,512]{2,1,0:T(8,128)(2,1)S(1)} %get-tuple-element.273), channel_id=1, source_target_pairs={{0,2},{1,3},{2,0},{3,1},{4,6},{5,7},{6,4},{7,5},{8,10},{9,11},{10,... | collective-permute-start | bytes 835592 | tf_op jit(solution)/shard_map/ppermute | solution.py:457
  79.0 16.0 %collective-permute-start.31 = (bf16[8,16,2176]{2,1,0:T(8,128)(2,1)S(1)}, bf16[8,16,2176]{2,1,0:T(8,128)(2,1)S(1)}, u32[]{:S(2)}, u32[]{:S(2)}) collective-permute-start(bf16[8,16,2176]{2,1,0:T(8,128)(2,1)S(1)} %get-tuple-element.271), channel_id=1, source_target_pairs={{0,4},{1,5},{2,6},{3,7},{4,0},{5,1},{6,2},{7,3},{8,12},{9,13},{10,... | collective-permute-start | bytes 1671176 | tf_op jit(solution)/shard_map/ppermute | solution.py:457
  84.8 16.2 %collective-permute-start.27 = (bf16[512,512]{1,0:T(8,128)(2,1)S(1)}, bf16[512,512]{1,0:T(8,128)(2,1)S(1)}, u32[]{:S(2)}, u32[]{:S(2)}) collective-permute-start(bf16[512,512]{1,0:T(8,128)(2,1)S(1)} %shard_map.272.r0), channel_id=1, source_target_pairs={{0,2},{1,3},{2,0},{3,1},{4,6},{5,7},{6,4},{7,5},{8,10},{9,11},{10,... | collective-permute-start | bytes 1572872 | tf_op jit(solution)/shard_map/ppermute | solution.py:457
  86.4 5.1 %collective-permute-start.28 = (bf16[128,512]{1,0:T(8,128)(2,1)S(1)}, bf16[128,512]{1,0:T(8,128)(2,1)S(1)}, u32[]{:S(2)}, u32[]{:S(2)}) collective-permute-start(bf16[128,512]{1,0:T(8,128)(2,1)S(1)} %get-tuple-element.281), channel_id=1, source_target_pairs={{0,8},{4,12},{8,0},{12,4},{16,24},{20,28},{24,16},{28,20},{1,9},{5... | collective-permute-start | bytes 393224 | tf_op jit(solution)/shard_map/ppermute | solution.py:457
  87.9 7.0 %collective-permute-start.32 = (bf16[136,512]{1,0:T(8,128)(2,1)S(1)}, bf16[136,512]{1,0:T(8,128)(2,1)S(1)}, u32[]{:S(2)}, u32[]{:S(2)}) collective-permute-start(bf16[136,512]{1,0:T(8,128)(2,1)S(1)} %get-tuple-element.279), channel_id=1, source_target_pairs={{0,8},{4,12},{8,0},{12,4},{16,24},{20,28},{24,16},{28,20},{1,9},{5... | collective-permute-start | bytes 417800 | tf_op jit(solution)/shard_map/ppermute | solution.py:457
  91.5 7.8 %collective-permute-start.30 = (bf16[128,512]{1,0:T(8,128)(2,1)S(1)}, bf16[128,512]{1,0:T(8,128)(2,1)S(1)}, u32[]{:S(2)}, u32[]{:S(2)}) collective-permute-start(bf16[128,512]{1,0:T(8,128)(2,1)S(1)} %add_convert_fusion.17), channel_id=1, source_target_pairs={{0,16},{4,20},{8,24},{12,28},{16,0},{20,4},{24,8},{28,12},{1,17},{... | collective-permute-start | bytes 393224 | tf_op jit(solution)/shard_map/ppermute | solution.py:457
  95.1 9.7 %collective-permute-start.36 = (bf16[4,16,2176]{2,1,0:T(8,128)(2,1)S(1)}, bf16[4,16,2176]{2,1,0:T(8,128)(2,1)S(1)}, u32[]{:S(2)}, u32[]{:S(2)}) collective-permute-start(bf16[4,16,2176]{2,1,0:T(8,128)(2,1)S(1)} %get-tuple-element.269), channel_id=1, source_target_pairs={{0,2},{1,3},{2,0},{3,1},{4,6},{5,7},{6,4},{7,5},{8,10},{9,11},{10,... | collective-permute-start | bytes 835592 | tf_op jit(solution)/shard_map/ppermute | solution.py:457
  96.3 16.6 %collective-permute-start.40 = (bf16[512,512]{1,0:T(8,128)(2,1)S(1)}, bf16[512,512]{1,0:T(8,128)(2,1)S(1)}, u32[]{:S(2)}, u32[]{:S(2)}) collective-permute-start(bf16[512,512]{1,0:T(8,128)(2,1)S(1)} %get-tuple-element.235.r0), channel_id=1, source_target_pairs={{0,2},{1,3},{2,0},{3,1},{4,6},{5,7},{6,4},{7,5},{8,10},{9,11},{10,... | collective-permute-start | bytes 1572872 | tf_op jit(solution)/shard_map/ppermute | solution.py:457
  97.2 18.7 %collective-permute-start.42 = (bf16[512,512]{1,0:T(8,128)(2,1)S(1)}, bf16[512,512]{1,0:T(8,128)(2,1)S(1)}, u32[]{:S(2)}, u32[]{:S(2)}) collective-permute-start(bf16[512,512]{1,0:T(8,128)(2,1)S(1)} %get-tuple-element.235.r0), channel_id=1, source_target_pairs={{0,1},{1,0},{2,3},{3,2},{4,5},{5,4},{6,7},{7,6},{8,9},{9,8},{10,11... | collective-permute-start | bytes 1572872 | tf_op jit(solution)/shard_map/ppermute | solution.py:457
  99.3 8.5 %collective-permute-start.35 = (bf16[136,512]{1,0:T(8,128)(2,1)S(1)}, bf16[136,512]{1,0:T(8,128)(2,1)S(1)}, u32[]{:S(2)}, u32[]{:S(2)}) collective-permute-start(bf16[136,512]{1,0:T(8,128)(2,1)S(1)} %add_convert_fusion.13), channel_id=1, source_target_pairs={{0,16},{4,20},{8,24},{12,28},{16,0},{20,4},{24,8},{28,12},{1,17},{... | collective-permute-start | bytes 417800 | tf_op jit(solution)/shard_map/ppermute | solution.py:457
  100.9 7.4 %collective-permute-start.34 = (bf16[128,512]{1,0:T(8,128)(2,1)S(1)}, bf16[128,512]{1,0:T(8,128)(2,1)S(1)}, u32[]{:S(2)}, u32[]{:S(2)}) collective-permute-start(bf16[128,512]{1,0:T(8,128)(2,1)S(1)} %add_convert_fusion.16), channel_id=1, source_target_pairs={{0,8},{4,12},{8,0},{12,4},{16,24},{20,28},{24,16},{28,20},{1,9},{5... | collective-permute-start | bytes 393224 | tf_op jit(solution)/shard_map/ppermute | solution.py:457
  107.8 6.5 %collective-permute-start.39 = (bf16[136,512]{1,0:T(8,128)(2,1)S(1)}, bf16[136,512]{1,0:T(8,128)(2,1)S(1)}, u32[]{:S(2)}, u32[]{:S(2)}) collective-permute-start(bf16[136,512]{1,0:T(8,128)(2,1)S(1)} %add_convert_fusion.11), channel_id=1, source_target_pairs={{0,8},{4,12},{8,0},{12,4},{16,24},{20,28},{24,16},{28,20},{1,9},{5... | collective-permute-start | bytes 417800 | tf_op jit(solution)/shard_map/ppermute | solution.py:457
  107.9 16.1 %collective-permute-start.44 = (bf16[512,512]{1,0:T(8,128)(2,1)S(1)}, bf16[512,512]{1,0:T(8,128)(2,1)S(1)}, u32[]{:S(2)}, u32[]{:S(2)}) collective-permute-start(bf16[512,512]{1,0:T(8,128)(2,1)S(1)} %shard_map.272.r0), channel_id=1, source_target_pairs={{0,1},{1,0},{2,3},{3,2},{4,5},{5,4},{6,7},{7,6},{8,9},{9,8},{10,11... | collective-permute-start | bytes 1572872 | tf_op jit(solution)/shard_map/ppermute | solution.py:457
  108.4 7.4 %collective-permute-start.38 = (bf16[2,16,2176]{2,1,0:T(8,128)(2,1)S(1)}, bf16[2,16,2176]{2,1,0:T(8,128)(2,1)S(1)}, u32[]{:S(2)}, u32[]{:S(2)}) collective-permute-start(bf16[2,16,2176]{2,1,0:T(8,128)(2,1)S(1)} %get-tuple-element.277), channel_id=1, source_target_pairs={{0,8},{1,9},{2,10},{3,11},{4,12},{5,13},{6,14},{7,15},{8,0},{9,1},... | collective-permute-start | bytes 417800 | tf_op jit(solution)/shard_map/ppermute | solution.py:457
  112.9 11.1 %collective-permute-start.33 = (bf16[512,512]{1,0:T(8,128)(2,1)S(1)}, bf16[512,512]{1,0:T(8,128)(2,1)S(1)}, u32[]{:S(2)}, u32[]{:S(2)}) collective-permute-start(bf16[512,512]{1,0:T(8,128)(2,1)S(1)} %collective-permute-done.27.r2), channel_id=1, source_target_pairs={{0,1},{1,0},{2,3},{3,2},{4,5},{5,4},{6,7},{7,6},{8,9},{9,8},{10,11... | collective-permute-start | bytes 1572872 | tf_op jit(solution)/shard_map/ppermute | solution.py:457
  114.2 9.7 %collective-permute-start.37 = (bf16[2,128,512]{2,1,0:T(8,128)(2,1)S(1)}, bf16[2,128,512]{2,1,0:T(8,128)(2,1)S(1)}, u32[]{:S(2)}, u32[]{:S(2)}) collective-permute-start(bf16[2,128,512]{2,1,0:T(8,128)(2,1)S(1)} %pad_maximum_fusion.1.own_ref), channel_id=1, source_target_pairs={{0,4},{4,0},{8,12},{12,8},{16,20},{20,16},{24,28},{28,24},{1,5},{5... | collective-permute-start | bytes 786440 | tf_op jit(solution)/shard_map/ppermute | solution.py:457
  115.8 2.0 %collective-permute-start.43 = (bf16[512,512]{1,0:T(8,128)(2,1)S(1)}, bf16[512,512]{1,0:T(8,128)(2,1)S(1)}, u32[]{:S(2)}, u32[]{:S(2)}) collective-permute-start(bf16[512,512]{1,0:T(8,128)(2,1)S(1)} %collective-permute-done.40.r2), channel_id=1, source_target_pairs={{0,1},{1,0},{2,3},{3,2},{4,5},{5,4},{6,7},{7,6},{8,9},{9,8},{10,11... | collective-permute-start | bytes 1572872 | tf_op jit(solution)/shard_map/ppermute | solution.py:457
  115.9 11.7 %collective-permute-start.45 = (bf16[2,136,512]{2,1,0:T(8,128)(2,1)S(1)}, bf16[2,136,512]{2,1,0:T(8,128)(2,1)S(1)}, u32[]{:S(2)}, u32[]{:S(2)}) collective-permute-start(bf16[2,136,512]{2,1,0:T(8,128)(2,1)S(1)} %pad_maximum_fusion.own_ref), channel_id=1, source_target_pairs={{0,4},{4,0},{8,12},{12,8},{16,20},{20,16},{24,28},{28,24},{1,5},{5... | collective-permute-start | bytes 835592 | tf_op jit(solution)/shard_map/ppermute | solution.py:457
  117.8 6.2 %collective-permute-start.41 = (bf16[1,16,2176]{2,1,0:T(8,128)(2,1)S(1)}, bf16[1,16,2176]{2,1,0:T(8,128)(2,1)S(1)}, u32[]{:S(2)}, u32[]{:S(2)}) collective-permute-start(bf16[1,16,2176]{2,1,0:T(8,128)(2,1)S(1)} %get-tuple-element.284), channel_id=1, source_target_pairs={{0,16},{1,17},{2,18},{3,19},{4,20},{5,21},{6,22},{7,23},{8,24},{9,... | collective-permute-start | bytes 208904 | tf_op jit(solution)/shard_map/ppermute | solution.py:457

commit v6 on v5

--- a/solution.py
+++ b/solution.py
@@ -522,19 +522,19 @@
     wo_halves = outer_weight.reshape(2, D // 2, D)
     wo_near = swap(jnp.concatenate([pick(wo_halves, z), outer_rows[D:]]), "mp", 2)
     if by_bits:
-        line = [local] + [swap(local, ALL, 8 * j) for j in range(1, 4)]
+        line = [local] + [swap(local, ALL, 8 * j) for j in (2, 1, 3)]
         *line, wi_near = tie(*line, wi_near)
         wi_far = swap(wi_near, "dp", 2)
         line = jnp.concatenate(line, axis=0)
-        plane = [line] + [swap(line, ALL, 2 * b) for b in range(1, 4)]
+        plane = [line] + [swap(line, ALL, 2 * b) for b in (1, 3, 2)]
         wi2 = jnp.where(z == 0, jnp.concatenate([wi_near, wi_far]), jnp.concatenate([wi_far, wi_near]))
         wo_far = swap(wo_near, "dp", 2)
         top, bottom, biases = wo_near[: D // 2], wo_far[: D // 2], wo_near[D // 2 :]
         wo2 = jnp.where(z == 0, jnp.concatenate([top, bottom, biases]), jnp.concatenate([bottom, top, biases]))
-        plane[2], own, start, cot = tie(plane[2], own, start, cot)
+        plane[3], own, start, cot = tie(plane[3], own, start, cot)
         *plane, wo2, wi2 = tie(*plane, wo2, wi2)
         pieces = plane + [swap(piece, ALL, 1) for piece in plane]
-        bits = [[2 * b + c + 8 * j for j in range(4)] for c in range(2) for b in range(4)]
+        bits = [[2 * b + c + 8 * j for j in (0, 2, 1, 3)] for c in range(2) for b in (0, 1, 3, 2)]
     else:
         pieces = [lax.all_gather(local, ALL, axis=0, tiled=True)]
         bits = [None]
@@ -549,6 +549,7 @@
         [VMEM] * 2,
         flops=2 * 10**9,
         bytes_=5 * 2**20,
+        mib=32,
     )(at, *pieces, own)
     p, o, m, l = call(
         attend_kernel,
@@ -560,7 +561,7 @@
         ],
         [VMEM],
         [VMEM] * 4,
-        flops=5 * 10**9,
+        flops=9 * 10**9,
         bytes_=7 * 2**20,
     )(qkv)
 
@@ -569,7 +570,7 @@
         [sds((PAD, D), F32), sds((PAD, D), F32)],
         [VMEM] * 2,
         [VMEM] * 2,
-        flops=3 * 10**9,
+        flops=1 * 10**9,
         bytes_=4 * 2**20,
         mib=16,
     )(start, w)
@@ -603,7 +604,8 @@
         [SMEM] + [VMEM] * 17,
         [VMEM] * 16,
         [pltpu.VMEM((4, SPAN, D), LOW)],
-        flops=10 * 10**9,
+        flops=5 * 10**9,
+        mib=28,
         bytes_=14 * 2**20,
     )(
         at, nm, small, own, w, qkv, o, m, l, inner_weight, wi1, wi2, wi3, outer_rows, wo1, wo2, wo3, cot,

time: 130 us -> 130 us (level)
  transfers between devices with their start and end apart: 46 -> 46, of which waited for: 19 -> 18; matrix products, arithmetic and copies ran while one was open for 6% -> 6% of each run, Pallas kernels for 23% -> 23%
where the time goes in v6:
time: 130 us; the launch traced here: 129 us
  starting transfers between devices  42.6 us (33%)
  Pallas kernels  40.5 us (31%)
  waiting for transfers between devices  36.5 us (28%)
  local copies, waits for them, and re-layouts  5.14 us (4%)
  other arithmetic  3.39 us (3%)
    ppermute x46, starting transfers between devices, swap(): return lax.ppermute(value, axis, [(i, i ^ bit) for i in range(n)])  42.6 us
    ppermute x46, waiting for transfers between devices, swap(): return lax.ppermute(value, axis, [(i, i ^ bit) for i in range(n)])  36.5 us
    pallas_call x1, Pallas kernels, shards(): call(forward_kernel, [square_low, outer_shape, outer_shape, sds((4, SPAN,...  9.55 us
    pallas_call x2, Pallas kernels, heads_backward(): call(functools.partial(heads_kernel, low_h, low_h + half), [sds((3, some,...  4.48 us
    squeeze x3, local copies, waits for them, and re-layouts, shards(): pick = lambda v, i: lax.dynamic_index_in_dim(v, i, 0, keepdims=False)  4.19 us
    pallas_call x1, Pallas kernels, shards(): call(attend_kernel, [sds((HEADS, SPAN, SPAN), LOW), sds((D, SPAN), F32),...  3.56 us
    pallas_call x1, Pallas kernels, closing(): call(closing_kernel, shapes, [SMEM] + [VMEM] * 8, [ANY] + [VMEM] * (len(s...  2.92 us
    pallas_call x1, Pallas kernels, shards(): call(functools.partial(project_kernel, bits), [sds((D, WIDE), LOW), sds((...  2.63 us
  transfers between devices with their start and end apart: 46, of which 18 were waited for; matrix products, arithmetic and copies ran while one was open for 6% of the time, Pallas kernels for 23%

profile of v6, /device:TPU:0, one launch (start us, length us, event | category | flops | bytes accessed | tf_op | source)
XLA Modules:
  0.0 129.3 jit_solution(5553959870475122724)
XLA Ops:
  0.7 1.0 dynamic-slice_bitcast_fusion.4
  1.6 3.0 %collective-permute-start.3 = (bf16[256,512]{1,0:T(8,128)(2,1)S(1)}, bf16[256,512]{1,0:T(8,128)(2,1)S(1)}, u32[]{:S(2)}, u32[]{:S(2)}) collective-permute-start(bf16[256,512]{1,0:T(8,128)(2,1)S(1)} %dynamic-slice_bitcast_fusion.4), channel_id=1, source_target_pairs={{0,2},{1,3},{2,0},{3,1},{4,6},{5,7},{6,4},{7,5},{8,10},{9,11},{10,... | collective-permute-start | bytes 786440 | tf_op jit(solution)/shard_map/ppermute | solution.py:457
  4.7 1.5 %shard_map.262 = bf16[16,2176]{1,0:T(8,128)(2,1)} custom-call(bf16[16,512]{1,0:T(8,128)(2,1)} %q_ref.1, bf16[16,512]{1,0:T(8,128)(2,1)} %k_ref.1, bf16[16,512]{1,0:T(8,128)(2,1)} %v_ref.1, bf16[16,512]{1,0:T(8,128)(2,1)} %o_ref.1, bf16[16,20]{1,0:T(8,128)(2,1)} %bitcast.83, bf16[1,16]{1,0:T(2,128)(2,1)} %bitcast.84, bf16[1,16]{1,0:T(2,128)(2,1)} %bitcast.85, ...), custom_call_target="tpu_custom_call" | custom-call | flops 1 | bytes 1 | tf_op jit(solution)/shard_map/pallas_call | solution.py:513
  6.2 2.6 %collective-permute-start = (bf16[16,2176]{1,0:T(8,128)(2,1)}, bf16[16,2176]{1,0:T(8,128)(2,1)S(1)}, u32[]{:S(2)}, u32[]{:S(2)}) collective-permute-start(bf16[16,2176]{1,0:T(8,128)(2,1)} %shard_map.262), channel_id=1, source_target_pairs={{0,16},{1,17},{2,18},{3,19},{4,20},{5,21},{6,22},{7,23},{8,24},{9,... | collective-permute-start | bytes 208904 | tf_op jit(solution)/shard_map/ppermute | solution.py:457
  8.8 1.6 %collective-permute-start.1 = (bf16[16,2176]{1,0:T(8,128)(2,1)}, bf16[16,2176]{1,0:T(8,128)(2,1)S(1)}, u32[]{:S(2)}, u32[]{:S(2)}) collective-permute-start(bf16[16,2176]{1,0:T(8,128)(2,1)} %shard_map.262), channel_id=1, source_target_pairs={{0,8},{1,9},{2,10},{3,11},{4,12},{5,13},{6,14},{7,15},{8,0},{9,1},... | collective-permute-start | bytes 208904 | tf_op jit(solution)/shard_map/ppermute | solution.py:457
  10.6 0.7 reshape.127
  11.2 1.0 dynamic-slice_bitcast_fusion.3
  12.6 0.7 collective-permute-done.1
  13.3 3.4 %collective-permute-done.2 = bf16[16,2176]{1,0:T(8,128)(2,1)S(1)} collective-permute-done((bf16[16,2176]{1,0:T(8,128)(2,1)}, bf16[16,2176]{1,0:T(8,128)(2,1)S(1)}, u32[]{:S(2)}, u32[]{:S(2)}) %collective-permute-start.2) | collective-permute-done | bytes 69664 | tf_op jit(solution)/shard_map/ppermute | solution.py:457
  16.8 1.6 %collective-permute-start.4 = (bf16[64,2176]{1,0:T(8,128)(2,1)S(1)}, bf16[64,2176]{1,0:T(8,128)(2,1)}, u32[]{:S(2)}, u32[]{:S(2)}) collective-permute-start(bf16[64,2176]{1,0:T(8,128)(2,1)S(1)} %constant_dynamic-update-slice_fusion.refs_0_), channel_id=1, source_target_pairs={{0,4},{1,5},{2,6},{3,7},{4,0},{5,1},{6,2},{7,3},{8,12},{9,13},{10,... | collective-permute-start | bytes 835592 | tf_op jit(solution)/shard_map/ppermute | solution.py:457
  18.4 1.3 collective-permute-done.7
  19.6 0.7 collective-permute-start.8
  20.4 0.5 collective-permute-start.5
  20.9 2.4 %collective-permute-start.6 = (bf16[64,2176]{1,0:T(8,128)(2,1)S(1)}, bf16[64,2176]{1,0:T(8,128)(2,1)}, u32[]{:S(2)}, u32[]{:S(2)}) collective-permute-start(bf16[64,2176]{1,0:T(8,128)(2,1)S(1)} %constant_dynamic-update-slice_fusion.refs_0_), channel_id=1, source_target_pairs={{0,6},{1,7},{2,4},{3,5},{4,2},{5,3},{6,0},{7,1},{8,14},{9,15},{10,... | collective-permute-start | bytes 835592 | tf_op jit(solution)/shard_map/ppermute | solution.py:457
  23.2 2.3 %dynamic-slice_bitcast_fusion.1 = (bf16[512,512]{1,0:T(8,128)(2,1)}, bf16[512,512]{1,0:T(8,128)(2,1)S(1)}, bf16[512,512]{1,0:T(8,128)(2,1)S(1)}) fusion(bf16[4,512,512]{2,1,0:T(8,128)(2,1)} %bitcast.78, s32[]{:T(128)S(6)} %select_n.44, s32[]{:T(128)S(6)} %select_n.43, bf16[4,512,512]{2,1,0:T(8,128)(2,1)} %bitcast.81), kind=kLoop, calls=%fused_computation.21 | loop fusion | bytes 3145736 | tf_op jit(solution)/shard_map/jit(dynamic_index_in_dim)/squeeze | solution.py:501
  26.1 2.7 %collective-permute-done.8 = bf16[272,512]{1,0:T(8,128)(2,1)S(1)} collective-permute-done((bf16[272,512]{1,0:T(8,128)(2,1)S(1)}, bf16[272,512]{1,0:T(8,128)(2,1)S(1)}, u32[]{:S(2)}, u32[]{:S(2)}) %collective-permute-start.8) | collective-permute-done | bytes 278560 | tf_op jit(solution)/shard_map/ppermute | solution.py:457
  29.0 3.4 %collective-permute-done.5.refs_1_ = bf16[64,2176]{1,0:T(8,128)(2,1)} collective-permute-done((bf16[64,2176]{1,0:T(8,128)(2,1)S(1)}, bf16[64,2176]{1,0:T(8,128)(2,1)}, u32[]{:S(2)}, u32[]{:S(2)}) %collective-permute-start.5) | collective-permute-done | bytes 278560 | tf_op jit(solution)/shard_map/ppermute | solution.py:457
  32.5 0.5 collective-permute-start.11
  33.0 0.5 collective-permute-start.13
  33.6 1.2 maximum_maximum_fusion.wo0
  34.9 0.6 collective-permute-start.16
  36.0 2.6 %shard_map.263 = (bf16[512,2176]{1,0:T(8,128)(2,1)S(1)}, bf16[1536,512]{1,0:T(8,128)(2,1)S(1)}) custom-call(s32[7]{0:T(128)S(1)} %stack.49.at_ref, bf16[64,2176]{1,0:T(8,128)(2,1)S(1)} %constant_dynamic-update-slice_fusion.refs_0_, bf16[64,2176]{1,0:T(8,128)(2,1)} %collective-permute-done.5.refs_1_, bf16[64,2176]{1,0:T(8,128)(2,1)} %collective-permute-done.6.refs_2_, ...), custom_call_target="tpu_custom_call" | custom-call | flops 2000000000 | bytes 5242880 | tf_op jit(solution)/shard_map/pallas_call | solution.py:545
  38.6 2.3 %shard_map.264 = (f32[32,512]{1,0:T(8,128)S(1)}, f32[32,512]{1,0:T(8,128)S(1)}) custom-call(bf16[512,512]{1,0:T(8,128)(2,1)S(1)} %copy-done.1, bf16[512,2176]{1,0:T(8,128)(2,1)S(1)} %get-tuple-element.151.w_ref), custom_call_target="tpu_custom_call" | custom-call | flops 1000000000 | bytes 4194304 | tf_op jit(solution)/shard_map/pallas_call | solution.py:568
  41.0 3.6 %shard_map.265 = (bf16[8,512,512]{2,1,0:T(8,128)(2,1)S(1)}, f32[512,512]{1,0:T(8,128)S(1)}, f32[8,512]{1,0:T(8,128)S(1)}, f32[8,512]{1,0:T(8,128)S(1)}) custom-call(bf16[1536,512]{1,0:T(8,128)(2,1)S(1)} %get-tuple-element.153.qkv_ref), custom_call_target="tpu_custom_call" | custom-call | flops 8999999488 | bytes 7340032 | tf_op jit(solution)/shard_map/pallas_call | solution.py:554
  44.6 9.5 %shard_map.266 = (bf16[512,512]{1,0:T(8,128)(2,1)S(1)}, bf16[2,4,128,512]{3,2,1,0:T(8,128)(2,1)S(1)}, bf16[2,4,128,512]{3,2,1,0:T(8,128)(2,1)S(1)}, bf16[4,512,5...) custom-call(s32[7]{0:T(128)S(1)} %stack.49.at_ref, ...), custom_call_target="tpu_custom_call" | custom-call | flops 5000000000 | bytes 14680064 | tf_op jit(solution)/shard_map/pallas_call | solution.py:584
  54.3 2.5 %shard_map.267 = (bf16[2,4,136,512]{3,2,1,0:T(8,128)(2,1)S(1)}, f32[512,512]{1,0:T(8,128)S(1)}) custom-call(s32[7]{0:T(128)S(1)} %stack.49.at_ref, bf16[512,512]{1,0:T(8,128)(2,1)S(1)} %collective-permute-done.14.wi1, bf16[512,512]{1,0:T(8,128)(2,1)S(1)} %collective-permute-done.15.wi3, bf16[528,512]{1,0:T(8,128)(2,1)S(1)} %collective-permute-done.16.wo1, ...), custom_call_target="tpu_custom_call" | custom-call | flops 1 | bytes 1 | tf_op jit(solution)/shard_map/pallas_call | solution.py:617
  57.6 0.6 collective-permute-start.19
  58.2 2.5 %shard_map.268 = (bf16[2,4,136,512]{3,2,1,0:T(8,128)(2,1)S(1)}, f32[512,512]{1,0:T(8,128)S(1)}) custom-call(s32[7]{0:T(128)S(1)} %stack.49.at_ref, bf16[4,128,512]{2,1,0:T(8,128)(2,1)S(1)} %get-tuple-element.266.after_ref, bf16[512,512]{1,0:T(8,128)(2,1)S(1)} %copy-done, bf16[512,512]{1,0:T(8,128)(2,1)S(1)} %maximum_select_fusion.1.wi2, ...), custom_call_target="tpu_custom_call" | custom-call | flops 1 | bytes 1 | tf_op jit(solution)/shard_map/pallas_call | solution.py:628
  61.1 1.6 %collective-permute-start.21 = (bf16[2,2,136,512]{3,2,1,0:T(8,128)(2,1)S(1)}, bf16[2,2,136,512]{3,2,1,0:T(8,128)(2,1)S(1)}, u32[]{:S(2)}, u32[]{:S(2)}) collective-permute-start(bf16[2,2,136,512]{3,2,1,0:T(8,128)(2,1)S(1)} %get-tuple-element.264.after_ref), channel_id=1, source_target_pairs={{0,4},{4,0},{8,12},{12,8},{16,20},{20,16},{24,28},{28,24},{1,5},{5... | collective-permute-start | bytes 1671176 | tf_op jit(solution)/shard_map/ppermute | solution.py:457
  62.6 1.2 shard_map.269
  63.8 2.2 %shard_map.270 = (bf16[3,256,512]{2,1,0:T(8,128)(2,1)S(1)}, f32[2,32,256]{2,1,0:T(8,128)S(1)}) custom-call(bf16[2,2,136,512]{3,2,1,0:T(8,128)(2,1)S(1)} %get-tuple-element.264.after_ref, bf16[1536,512]{1,0:T(8,128)(2,1)S(1)} %get-tuple-element.153.qkv_ref, bf16[8,512,512]{2,1,0:T(8,128)(2,1)S(1)} %get-tuple-element.176.p_ref, ...), custom_call_target="tpu_custom_call" | custom-call | flops 1 | bytes 1 | tf_op jit(solution)/shard_map/pallas_call | solution.py:645
  66.1 2.2 %shard_map.271 = (bf16[3,256,512]{2,1,0:T(8,128)(2,1)S(1)}, f32[2,32,256]{2,1,0:T(8,128)S(1)}) custom-call(bf16[2,2,136,512]{3,2,1,0:T(8,128)(2,1)S(1)} %get-tuple-element.264.after_ref, bf16[1536,512]{1,0:T(8,128)(2,1)S(1)} %get-tuple-element.153.qkv_ref, bf16[8,512,512]{2,1,0:T(8,128)(2,1)S(1)} %get-tuple-element.176.p_ref, ...), custom_call_target="tpu_custom_call" | custom-call | flops 1 | bytes 1 | tf_op jit(solution)/shard_map/pallas_call | solution.py:645
  68.3 1.2 shard_map.272.r0
  69.5 2.6 %shard_map.273 = (bf16[256,2176]{1,0:T(8,128)(2,1)S(1)}, bf16[64,2176]{1,0:T(8,128)(2,1)S(1)}, bf16[64,2176]{1,0:T(8,128)(2,1)S(1)}, bf16[64,2176]{1,0:T(8,128)(2,1)S(1)}, bf16[64,2176]{1,0:T(8,128)(2,1)S(1)}) custom-call(bf16[2,2,136,512]{3,2,1,0:T(8,128)(2,1)S(1)} %get-tuple-element.264.after_ref, s32[7]{0:T(128)S(1)} %stack.49.at_ref, ...), custom_call_target="tpu_custom_call" | custom-call | flops 1 | bytes 1 | tf_op jit(solution)/shard_map/pallas_call | solution.py:672
  72.2 0.5 collective-permute-start.24
  73.3 2.2 %collective-permute-done.21 = bf16[2,2,136,512]{3,2,1,0:T(8,128)(2,1)S(1)} collective-permute-done((bf16[2,2,136,512]{3,2,1,0:T(8,128)(2,1)S(1)}, bf16[2,2,136,512]{3,2,1,0:T(8,128)(2,1)S(1)}, u32[]{:S(2)}, u32[]{:S(2)}) %collective-permute-start.21) | collective-permute-done | bytes 557088 | tf_op jit(solution)/shard_map/ppermute | solution.py:457
  75.5 1.5 %collective-permute-start.22 = (bf16[2,128,512]{2,1,0:T(8,128)(2,1)S(1)}, bf16[2,128,512]{2,1,0:T(8,128)(2,1)S(1)}, u32[]{:S(2)}, u32[]{:S(2)}) collective-permute-start(bf16[2,128,512]{2,1,0:T(8,128)(2,1)S(1)} %get-tuple-element.276), channel_id=1, source_target_pairs={{0,4},{4,0},{8,12},{12,8},{16,20},{20,16},{24,28},{28,24},{1,5},{5... | collective-permute-start | bytes 786440 | tf_op jit(solution)/shard_map/ppermute | solution.py:457
  77.2 1.6 %collective-permute-start.29 = (bf16[2,136,512]{2,1,0:T(8,128)(2,1)S(1)}, bf16[2,136,512]{2,1,0:T(8,128)(2,1)S(1)}, u32[]{:S(2)}, u32[]{:S(2)}) collective-permute-start(bf16[2,136,512]{2,1,0:T(8,128)(2,1)S(1)} %get-tuple-element.273), channel_id=1, source_target_pairs={{0,2},{1,3},{2,0},{3,1},{4,6},{5,7},{6,4},{7,5},{8,10},{9,11},{10,... | collective-permute-start | bytes 835592 | tf_op jit(solution)/shard_map/ppermute | solution.py:457
  79.0 0.6 collective-permute-start.31
  79.6 5.1 %collective-permute-done.22 = bf16[2,128,512]{2,1,0:T(8,128)(2,1)S(1)} collective-permute-done((bf16[2,128,512]{2,1,0:T(8,128)(2,1)S(1)}, bf16[2,128,512]{2,1,0:T(8,128)(2,1)S(1)}, u32[]{:S(2)}, u32[]{:S(2)}) %collective-permute-start.22) | collective-permute-done | bytes 262176 | tf_op jit(solution)/shard_map/ppermute | solution.py:457
  84.8 1.6 %collective-permute-start.27 = (bf16[512,512]{1,0:T(8,128)(2,1)S(1)}, bf16[512,512]{1,0:T(8,128)(2,1)S(1)}, u32[]{:S(2)}, u32[]{:S(2)}) collective-permute-start(bf16[512,512]{1,0:T(8,128)(2,1)S(1)} %shard_map.272.r0), channel_id=1, source_target_pairs={{0,2},{1,3},{2,0},{3,1},{4,6},{5,7},{6,4},{7,5},{8,10},{9,11},{10,... | collective-permute-start | bytes 1572872 | tf_op jit(solution)/shard_map/ppermute | solution.py:457
  86.4 1.4 %collective-permute-start.28 = (bf16[128,512]{1,0:T(8,128)(2,1)S(1)}, bf16[128,512]{1,0:T(8,128)(2,1)S(1)}, u32[]{:S(2)}, u32[]{:S(2)}) collective-permute-start(bf16[128,512]{1,0:T(8,128)(2,1)S(1)} %get-tuple-element.281), channel_id=1, source_target_pairs={{0,8},{4,12},{8,0},{12,4},{16,24},{20,28},{24,16},{28,20},{1,9},{5... | collective-permute-start | bytes 393224 | tf_op jit(solution)/shard_map/ppermute | solution.py:457
  87.9 0.7 collective-permute-start.32
  88.6 2.9 %collective-permute-done.28 = bf16[128,512]{1,0:T(8,128)(2,1)S(1)} collective-permute-done((bf16[128,512]{1,0:T(8,128)(2,1)S(1)}, bf16[128,512]{1,0:T(8,128)(2,1)S(1)}, u32[]{:S(2)}, u32[]{:S(2)}) %collective-permute-start.28) | collective-permute-done | bytes 131104 | tf_op jit(solution)/shard_map/ppermute | solution.py:457
  91.6 3.4 %collective-permute-start.30 = (bf16[128,512]{1,0:T(8,128)(2,1)S(1)}, bf16[128,512]{1,0:T(8,128)(2,1)S(1)}, u32[]{:S(2)}, u32[]{:S(2)}) collective-permute-start(bf16[128,512]{1,0:T(8,128)(2,1)S(1)} %add_convert_fusion.17), channel_id=1, source_target_pairs={{0,16},{4,20},{8,24},{12,28},{16,0},{20,4},{24,8},{28,12},{1,17},{... | collective-permute-start | bytes 393224 | tf_op jit(solution)/shard_map/ppermute | solution.py:457
  95.1 1.2 collective-permute-start.36
  96.3 0.9 collective-permute-start.40
  97.2 2.1 %collective-permute-done.30 = bf16[128,512]{1,0:T(8,128)(2,1)S(1)} collective-permute-done((bf16[128,512]{1,0:T(8,128)(2,1)S(1)}, bf16[128,512]{1,0:T(8,128)(2,1)S(1)}, u32[]{:S(2)}, u32[]{:S(2)}) %collective-permute-start.30) | collective-permute-done | bytes 131104 | tf_op jit(solution)/shard_map/ppermute | solution.py:457
  99.3 1.6 %collective-permute-start.35 = (bf16[136,512]{1,0:T(8,128)(2,1)S(1)}, bf16[136,512]{1,0:T(8,128)(2,1)S(1)}, u32[]{:S(2)}, u32[]{:S(2)}) collective-permute-start(bf16[136,512]{1,0:T(8,128)(2,1)S(1)} %add_convert_fusion.13), channel_id=1, source_target_pairs={{0,16},{4,20},{8,24},{12,28},{16,0},{20,4},{24,8},{28,12},{1,17},{... | collective-permute-start | bytes 417800 | tf_op jit(solution)/shard_map/ppermute | solution.py:457
  100.9 2.8 %collective-permute-start.34 = (bf16[128,512]{1,0:T(8,128)(2,1)S(1)}, bf16[128,512]{1,0:T(8,128)(2,1)S(1)}, u32[]{:S(2)}, u32[]{:S(2)}) collective-permute-start(bf16[128,512]{1,0:T(8,128)(2,1)S(1)} %add_convert_fusion.16), channel_id=1, source_target_pairs={{0,8},{4,12},{8,0},{12,4},{16,24},{20,28},{24,16},{28,20},{1,9},{5... | collective-permute-start | bytes 393224 | tf_op jit(solution)/shard_map/ppermute | solution.py:457
  103.8 1.0 collective-permute-done.36
  104.9 2.9 %collective-permute-done.35 = bf16[136,512]{1,0:T(8,128)(2,1)S(1)} collective-permute-done((bf16[136,512]{1,0:T(8,128)(2,1)S(1)}, bf16[136,512]{1,0:T(8,128)(2,1)S(1)}, u32[]{:S(2)}, u32[]{:S(2)}) %collective-permute-start.35) | collective-permute-done | bytes 139296 | tf_op jit(solution)/shard_map/ppermute | solution.py:457
  108.4 1.5 %collective-permute-start.38 = (bf16[2,16,2176]{2,1,0:T(8,128)(2,1)S(1)}, bf16[2,16,2176]{2,1,0:T(8,128)(2,1)S(1)}, u32[]{:S(2)}, u32[]{:S(2)}) collective-permute-start(bf16[2,16,2176]{2,1,0:T(8,128)(2,1)S(1)} %get-tuple-element.277), channel_id=1, source_target_pairs={{0,8},{1,9},{2,10},{3,11},{4,12},{5,13},{6,14},{7,15},{8,0},{9,1},... | collective-permute-start | bytes 417800 | tf_op jit(solution)/shard_map/ppermute | solution.py:457
  109.9 3.0 %collective-permute-done.40.r2 = bf16[512,512]{1,0:T(8,128)(2,1)S(1)} collective-permute-done((bf16[512,512]{1,0:T(8,128)(2,1)S(1)}, bf16[512,512]{1,0:T(8,128)(2,1)S(1)}, u32[]{:S(2)}, u32[]{:S(2)}) %collective-permute-start.40) | collective-permute-done | bytes 524320 | tf_op jit(solution)/shard_map/ppermute | solution.py:457
  112.9 1.3 %collective-permute-done.39 = bf16[136,512]{1,0:T(8,128)(2,1)S(1)} collective-permute-done((bf16[136,512]{1,0:T(8,128)(2,1)S(1)}, bf16[136,512]{1,0:T(8,128)(2,1)S(1)}, u32[]{:S(2)}, u32[]{:S(2)}) %collective-permute-start.39) | collective-permute-done | bytes 139296 | tf_op jit(solution)/shard_map/ppermute | solution.py:457
  114.2 1.5 %collective-permute-start.37 = (bf16[2,128,512]{2,1,0:T(8,128)(2,1)S(1)}, bf16[2,128,512]{2,1,0:T(8,128)(2,1)S(1)}, u32[]{:S(2)}, u32[]{:S(2)}) collective-permute-start(bf16[2,128,512]{2,1,0:T(8,128)(2,1)S(1)} %pad_maximum_fusion.1.own_ref), channel_id=1, source_target_pairs={{0,4},{4,0},{8,12},{12,8},{16,20},{20,16},{24,28},{28,24},{1,5},{5... | collective-permute-start | bytes 786440 | tf_op jit(solution)/shard_map/ppermute | solution.py:457
  115.9 1.4 %collective-permute-start.45 = (bf16[2,136,512]{2,1,0:T(8,128)(2,1)S(1)}, bf16[2,136,512]{2,1,0:T(8,128)(2,1)S(1)}, u32[]{:S(2)}, u32[]{:S(2)}) collective-permute-start(bf16[2,136,512]{2,1,0:T(8,128)(2,1)S(1)} %pad_maximum_fusion.own_ref), channel_id=1, source_target_pairs={{0,4},{4,0},{8,12},{12,8},{16,20},{20,16},{24,28},{28,24},{1,5},{5... | collective-permute-start | bytes 835592 | tf_op jit(solution)/shard_map/ppermute | solution.py:457
  117.3 0.5 collective-permute-done.43.r3
  117.8 1.8 %collective-permute-start.41 = (bf16[1,16,2176]{2,1,0:T(8,128)(2,1)S(1)}, bf16[1,16,2176]{2,1,0:T(8,128)(2,1)S(1)}, u32[]{:S(2)}, u32[]{:S(2)}) collective-permute-start(bf16[1,16,2176]{2,1,0:T(8,128)(2,1)S(1)} %get-tuple-element.284), channel_id=1, source_target_pairs={{0,16},{1,17},{2,18},{3,19},{4,20},{5,21},{6,22},{7,23},{8,24},{9,... | collective-permute-start | bytes 208904 | tf_op jit(solution)/shard_map/ppermute | solution.py:457
  119.6 1.9 %shard_map.274 = bf16[4,512,512]{2,1,0:T(8,128)(2,1)} custom-call(s32[7]{0:T(128)S(1)} %stack.49.at_ref, bf16[512,512]{1,0:T(8,128)(2,1)S(1)} %get-tuple-element.235.r0, bf16[512,512]{1,0:T(8,128)(2,1)S(1)} %collective-permute-done.42.r1, bf16[512,512]{1,0:T(8,128)(2,1)S(1)} %collective-permute-done.40.r2, bf16[512,512]{1,0:T(8,128)(2,1)S(1)} %collective-permute-done.43.r3), custom_call_target="tpu_custom_call" | custom-call | flops 1 | bytes 1 | tf_op jit(solution)/shard_map/pallas_call | solution.py:392
  121.5 2.5 %collective-permute-done.41.got_ref = bf16[1,16,2176]{2,1,0:T(8,128)(2,1)S(1)} collective-permute-done((bf16[1,16,2176]{2,1,0:T(8,128)(2,1)S(1)}, bf16[1,16,2176]{2,1,0:T(8,128)(2,1)S(1)}, u32[]{:S(2)}, u32[]{:S(2)}) %collective-permute-start.41) | collective-permute-done | bytes 69664 | tf_op jit(solution)/shard_map/ppermute | solution.py:457
  124.0 2.9 %shard_map.275 = (bf16[4,512,512]{2,1,0:T(8,128)(2,1)}, f32[512,512]{1,0:T(8,128)}, f32[16,20]{1,0:T(8,128)}, f32[16,512]{1,0:T(8,128)}, f32[16,512]{1,0:T(8,128...) custom-call(s32[7]{0:T(128)S(1)} %stack.49.at_ref, ...), custom_call_target="tpu_custom_call" | custom-call | flops 1 | bytes 1 | tf_op jit(solution)/shard_map/pallas_call | solution.py:443
  126.9 0.7 collective-permute-done.45.other_ref
  127.6 1.7 %shard_map.276 = (f32[512,512]{1,0:T(8,128)}, f32[1,512]{1,0:T(1,128)}) custom-call(s32[7]{0:T(128)S(1)} %stack.49.at_ref, bf16[2,136,512]{2,1,0:T(8,128)(2,1)S(1)} %pad_maximum_fusion.own_ref, bf16[2,136,512]{2,1,0:T(8,128)(2,1)S(1)} %collective-permute-done.45.other_ref), custom_call_target="tpu_custom_call" | custom-call | flops 1 | bytes 2097152 | tf_op jit(solution)/shard_map/pallas_call | solution.py:469
  (83 shorter events, 6.0 us)
Async XLA Ops:
  1.6 15.0 %collective-permute-start.3 = (bf16[256,512]{1,0:T(8,128)(2,1)S(1)}, bf16[256,512]{1,0:T(8,128)(2,1)S(1)}, u32[]{:S(2)}, u32[]{:S(2)}) collective-permute-start(bf16[256,512]{1,0:T(8,128)(2,1)S(1)} %dynamic-slice_bitcast_fusion.4), channel_id=1, source_target_pairs={{0,2},{1,3},{2,0},{3,1},{4,6},{5,7},{6,4},{7,5},{8,10},{9,11},{10,... | collective-permute-start | bytes 786440 | tf_op jit(solution)/shard_map/ppermute | solution.py:457
  6.2 10.5 %copy-start.2 = (bf16[16,2176]{1,0:T(8,128)(2,1)S(1)}, bf16[16,2176]{1,0:T(8,128)(2,1)}, u32[]{:S(2)}) copy-start(bf16[16,2176]{1,0:T(8,128)(2,1)} %shard_map.262) | copy-start | bytes 208900
  6.2 6.4 %collective-permute-start = (bf16[16,2176]{1,0:T(8,128)(2,1)}, bf16[16,2176]{1,0:T(8,128)(2,1)S(1)}, u32[]{:S(2)}, u32[]{:S(2)}) collective-permute-start(bf16[16,2176]{1,0:T(8,128)(2,1)} %shard_map.262), channel_id=1, source_target_pairs={{0,16},{1,17},{2,18},{3,19},{4,20},{5,21},{6,22},{7,23},{8,24},{9,... | collective-permute-start | bytes 208904 | tf_op jit(solution)/shard_map/ppermute | solution.py:457
  8.8 4.5 %collective-permute-start.1 = (bf16[16,2176]{1,0:T(8,128)(2,1)}, bf16[16,2176]{1,0:T(8,128)(2,1)S(1)}, u32[]{:S(2)}, u32[]{:S(2)}) collective-permute-start(bf16[16,2176]{1,0:T(8,128)(2,1)} %shard_map.262), channel_id=1, source_target_pairs={{0,8},{1,9},{2,10},{3,11},{4,12},{5,13},{6,14},{7,15},{8,0},{9,1},... | collective-permute-start | bytes 208904 | tf_op jit(solution)/shard_map/ppermute | solution.py:457
  10.3 6.3 %collective-permute-start.2 = (bf16[16,2176]{1,0:T(8,128)(2,1)}, bf16[16,2176]{1,0:T(8,128)(2,1)S(1)}, u32[]{:S(2)}, u32[]{:S(2)}) collective-permute-start(bf16[16,2176]{1,0:T(8,128)(2,1)} %shard_map.262), channel_id=1, source_target_pairs={{0,24},{1,25},{2,26},{3,27},{4,28},{5,29},{6,30},{7,31},{8,16},{9,... | collective-permute-start | bytes 208904 | tf_op jit(solution)/shard_map/ppermute | solution.py:457
  12.2 7.4 %collective-permute-start.7 = (bf16[272,512]{1,0:T(8,128)(2,1)S(1)}, bf16[272,512]{1,0:T(8,128)(2,1)S(1)}, u32[]{:S(2)}, u32[]{:S(2)}) collective-permute-start(bf16[272,512]{1,0:T(8,128)(2,1)S(1)} %fusion.4), channel_id=1, source_target_pairs={{0,2},{1,3},{2,0},{3,1},{4,6},{5,7},{6,4},{7,5},{8,10},{9,11},{10,... | collective-permute-start | bytes 835592 | tf_op jit(solution)/shard_map/ppermute | solution.py:457
  16.7 9.2 %collective-permute-start.9 = (bf16[256,512]{1,0:T(8,128)(2,1)S(1)}, bf16[256,512]{1,0:T(8,128)(2,1)S(1)}, u32[]{:S(2)}, u32[]{:S(2)}) collective-permute-start(bf16[256,512]{1,0:T(8,128)(2,1)S(1)} %collective-permute-done.3), channel_id=1, source_target_pairs={{0,8},{4,12},{8,0},{12,4},{16,24},{20,28},{24,16},{28,20},{1,9},{5... | collective-permute-start | bytes 786440 | tf_op jit(solution)/shard_map/ppermute | solution.py:457
  16.8 9.3 %collective-permute-start.4 = (bf16[64,2176]{1,0:T(8,128)(2,1)S(1)}, bf16[64,2176]{1,0:T(8,128)(2,1)}, u32[]{:S(2)}, u32[]{:S(2)}) collective-permute-start(bf16[64,2176]{1,0:T(8,128)(2,1)S(1)} %constant_dynamic-update-slice_fusion.refs_0_), channel_id=1, source_target_pairs={{0,4},{1,5},{2,6},{3,7},{4,0},{5,1},{6,2},{7,3},{8,12},{9,13},{10,... | collective-permute-start | bytes 835592 | tf_op jit(solution)/shard_map/ppermute | solution.py:457
  19.6 9.2 %collective-permute-start.8 = (bf16[272,512]{1,0:T(8,128)(2,1)S(1)}, bf16[272,512]{1,0:T(8,128)(2,1)S(1)}, u32[]{:S(2)}, u32[]{:S(2)}) collective-permute-start(bf16[272,512]{1,0:T(8,128)(2,1)S(1)} %collective-permute-done.7), channel_id=1, source_target_pairs={{0,8},{4,12},{8,0},{12,4},{16,24},{20,28},{24,16},{28,20},{1,9},{5... | collective-permute-start | bytes 835592 | tf_op jit(solution)/shard_map/ppermute | solution.py:457
  20.4 12.1 %collective-permute-start.5 = (bf16[64,2176]{1,0:T(8,128)(2,1)S(1)}, bf16[64,2176]{1,0:T(8,128)(2,1)}, u32[]{:S(2)}, u32[]{:S(2)}) collective-permute-start(bf16[64,2176]{1,0:T(8,128)(2,1)S(1)} %constant_dynamic-update-slice_fusion.refs_0_), channel_id=1, source_target_pairs={{0,2},{1,3},{2,0},{3,1},{4,6},{5,7},{6,4},{7,5},{8,10},{9,11},{10,... | collective-permute-start | bytes 835592 | tf_op jit(solution)/shard_map/ppermute | solution.py:457
  20.9 11.6 %collective-permute-start.6 = (bf16[64,2176]{1,0:T(8,128)(2,1)S(1)}, bf16[64,2176]{1,0:T(8,128)(2,1)}, u32[]{:S(2)}, u32[]{:S(2)}) collective-permute-start(bf16[64,2176]{1,0:T(8,128)(2,1)S(1)} %constant_dynamic-update-slice_fusion.refs_0_), channel_id=1, source_target_pairs={{0,6},{1,7},{2,4},{3,5},{4,2},{5,3},{6,0},{7,1},{8,14},{9,15},{10,... | collective-permute-start | bytes 835592 | tf_op jit(solution)/shard_map/ppermute | solution.py:457
  26.1 7.4 %copy-start = (bf16[512,512]{1,0:T(8,128)(2,1)S(1)}, bf16[512,512]{1,0:T(8,128)(2,1)}, u32[]{:S(2)}) copy-start(bf16[512,512]{1,0:T(8,128)(2,1)} %wi0.3) | copy-start | bytes 1572868
  32.4 2.4 %collective-permute-start.10 = (bf16[64,2176]{1,0:T(8,128)(2,1)S(1)}, bf16[64,2176]{1,0:T(8,128)(2,1)}, u32[]{:S(2)}, u32[]{:S(2)}) collective-permute-start(bf16[64,2176]{1,0:T(8,128)(2,1)S(1)} %constant_dynamic-update-slice_fusion.refs_0_), channel_id=1, source_target_pairs={{0,1},{1,0},{2,3},{3,2},{4,5},{5,4},{6,7},{7,6},{8,9},{9,8},{10,11... | collective-permute-start | bytes 835592 | tf_op jit(solution)/shard_map/ppermute | solution.py:457
  32.5 3.0 %collective-permute-start.11 = (bf16[64,2176]{1,0:T(8,128)(2,1)}, bf16[64,2176]{1,0:T(8,128)(2,1)}, u32[]{:S(2)}, u32[]{:S(2)}) collective-permute-start(bf16[64,2176]{1,0:T(8,128)(2,1)} %collective-permute-done.5.refs_1_), channel_id=1, source_target_pairs={{0,1},{1,0},{2,3},{3,2},{4,5},{5,4},{6,7},{7,6},{8,9},{9,8},{10,11... | collective-permute-start | bytes 835592 | tf_op jit(solution)/shard_map/ppermute | solution.py:457
  33.0 2.6 %collective-permute-start.12 = (bf16[64,2176]{1,0:T(8,128)(2,1)}, bf16[64,2176]{1,0:T(8,128)(2,1)}, u32[]{:S(2)}, u32[]{:S(2)}) collective-permute-start(bf16[64,2176]{1,0:T(8,128)(2,1)} %collective-permute-done.6.refs_2_), channel_id=1, source_target_pairs={{0,1},{1,0},{2,3},{3,2},{4,5},{5,4},{6,7},{7,6},{8,9},{9,8},{10,11... | collective-permute-start | bytes 835592 | tf_op jit(solution)/shard_map/ppermute | solution.py:457
  33.0 3.0 %collective-permute-start.13 = (bf16[64,2176]{1,0:T(8,128)(2,1)}, bf16[64,2176]{1,0:T(8,128)(2,1)}, u32[]{:S(2)}, u32[]{:S(2)}) collective-permute-start(bf16[64,2176]{1,0:T(8,128)(2,1)} %collective-permute-done.4.refs_3_), channel_id=1, source_target_pairs={{0,1},{1,0},{2,3},{3,2},{4,5},{5,4},{6,7},{7,6},{8,9},{9,8},{10,11... | collective-permute-start | bytes 835592 | tf_op jit(solution)/shard_map/ppermute | solution.py:457
  33.5 11.0 %collective-permute-start.14 = (bf16[512,512]{1,0:T(8,128)(2,1)S(1)}, bf16[512,512]{1,0:T(8,128)(2,1)S(1)}, u32[]{:S(2)}, u32[]{:S(2)}) collective-permute-start(bf16[512,512]{1,0:T(8,128)(2,1)S(1)} %copy-done), channel_id=1, source_target_pairs={{0,1},{1,0},{2,3},{3,2},{4,5},{5,4},{6,7},{7,6},{8,9},{9,8},{10,11... | collective-permute-start | bytes 1572872 | tf_op jit(solution)/shard_map/ppermute | solution.py:457
  34.9 3.8 %copy-start.1 = (bf16[512,512]{1,0:T(8,128)(2,1)S(1)}, bf16[512,512]{1,0:T(8,128)(2,1)}, u32[]{:S(2)}) copy-start(bf16[512,512]{1,0:T(8,128)(2,1)} %get-tuple-element.143.x1_ref) | copy-start | bytes 1572868
  34.9 9.6 %collective-permute-start.16 = (bf16[528,512]{1,0:T(8,128)(2,1)S(1)}, bf16[528,512]{1,0:T(8,128)(2,1)S(1)}, u32[]{:S(2)}, u32[]{:S(2)}) collective-permute-start(bf16[528,512]{1,0:T(8,128)(2,1)S(1)} %maximum_maximum_fusion.wo0), channel_id=1, source_target_pairs={{0,1},{1,0},{2,3},{3,2},{4,5},{5,4},{6,7},{7,6},{8,9},{9,8},{10,11... | collective-permute-start | bytes 1622024 | tf_op jit(solution)/shard_map/ppermute | solution.py:457
  35.5 9.1 %collective-permute-start.15 = (bf16[512,512]{1,0:T(8,128)(2,1)S(1)}, bf16[512,512]{1,0:T(8,128)(2,1)S(1)}, u32[]{:S(2)}, u32[]{:S(2)}) collective-permute-start(bf16[512,512]{1,0:T(8,128)(2,1)S(1)} %maximum_select_fusion.1.wi2), channel_id=1, source_target_pairs={{0,1},{1,0},{2,3},{3,2},{4,5},{5,4},{6,7},{7,6},{8,9},{9,8},{10,11... | collective-permute-start | bytes 1572872 | tf_op jit(solution)/shard_map/ppermute | solution.py:457
  35.6 9.0 %collective-permute-start.17 = (bf16[528,512]{1,0:T(8,128)(2,1)S(1)}, bf16[528,512]{1,0:T(8,128)(2,1)S(1)}, u32[]{:S(2)}, u32[]{:S(2)}) collective-permute-start(bf16[528,512]{1,0:T(8,128)(2,1)S(1)} %maximum_select_fusion.wo2), channel_id=1, source_target_pairs={{0,1},{1,0},{2,3},{3,2},{4,5},{5,4},{6,7},{7,6},{8,9},{9,8},{10,11... | collective-permute-start | bytes 1622024 | tf_op jit(solution)/shard_map/ppermute | solution.py:457
  54.1 3.2 %collective-permute-start.18 = (bf16[2,4,128,512]{3,2,1,0:T(8,128)(2,1)S(1)}, bf16[2,4,128,512]{3,2,1,0:T(8,128)(2,1)S(1)}, u32[]{:S(2)}, u32[]{:S(2)}) collective-permute-start(bf16[2,4,128,512]{3,2,1,0:T(8,128)(2,1)S(1)} %get-tuple-element.168), channel_id=1, source_target_pairs={{0,1},{1,0},{2,3},{3,2},{4,5},{5,4},{6,7},{7,6},{8,9},{9,8},{10,11... | collective-permute-start | bytes 3145736 | tf_op jit(solution)/shard_map/ppermute | solution.py:457
  56.8 3.9 %collective-permute-start.20 = (bf16[2,4,136,512]{3,2,1,0:T(8,128)(2,1)S(1)}, bf16[2,4,136,512]{3,2,1,0:T(8,128)(2,1)S(1)}, u32[]{:S(2)}, u32[]{:S(2)}) collective-permute-start(bf16[2,4,136,512]{3,2,1,0:T(8,128)(2,1)S(1)} %get-tuple-element.175), channel_id=1, source_target_pairs={{0,1},{1,0},{2,3},{3,2},{4,5},{5,4},{6,7},{7,6},{8,9},{9,8},{10,11... | collective-permute-start | bytes 3342344 | tf_op jit(solution)/shard_map/ppermute | solution.py:457
  57.6 15.1 %collective-permute-start.19 = (bf16[4,128,512]{2,1,0:T(8,128)(2,1)S(1)}, bf16[4,128,512]{2,1,0:T(8,128)(2,1)S(1)}, u32[]{:S(2)}, u32[]{:S(2)}) collective-permute-start(bf16[4,128,512]{2,1,0:T(8,128)(2,1)S(1)} %get-tuple-element.266.after_ref), channel_id=1, source_target_pairs={{0,2},{1,3},{2,0},{3,1},{4,6},{5,7},{6,4},{7,5},{8,10},{9,11},{10,... | collective-permute-start | bytes 1572872 | tf_op jit(solution)/shard_map/ppermute | solution.py:457
  61.1 14.4 %collective-permute-start.21 = (bf16[2,2,136,512]{3,2,1,0:T(8,128)(2,1)S(1)}, bf16[2,2,136,512]{3,2,1,0:T(8,128)(2,1)S(1)}, u32[]{:S(2)}, u32[]{:S(2)}) collective-permute-start(bf16[2,2,136,512]{3,2,1,0:T(8,128)(2,1)S(1)} %get-tuple-element.264.after_ref), channel_id=1, source_target_pairs={{0,4},{4,0},{8,12},{12,8},{16,20},{20,16},{24,28},{28,24},{1,5},{5... | collective-permute-start | bytes 1671176 | tf_op jit(solution)/shard_map/ppermute | solution.py:457
  72.1 5.1 %collective-permute-start.23 = (bf16[4,16,2176]{2,1,0:T(8,128)(2,1)S(1)}, bf16[4,16,2176]{2,1,0:T(8,128)(2,1)S(1)}, u32[]{:S(2)}, u32[]{:S(2)}) collective-permute-start(bf16[4,16,2176]{2,1,0:T(8,128)(2,1)S(1)} %bitcast.74), channel_id=1, source_target_pairs={{0,1},{1,0},{2,3},{3,2},{4,5},{5,4},{6,7},{7,6},{8,9},{9,8},{10,11... | collective-permute-start | bytes 835592 | tf_op jit(solution)/shard_map/ppermute | solution.py:457
  72.2 5.0 %collective-permute-start.24 = (bf16[4,16,2176]{2,1,0:T(8,128)(2,1)S(1)}, bf16[4,16,2176]{2,1,0:T(8,128)(2,1)S(1)}, u32[]{:S(2)}, u32[]{:S(2)}) collective-permute-start(bf16[4,16,2176]{2,1,0:T(8,128)(2,1)S(1)} %bitcast.73), channel_id=1, source_target_pairs={{0,1},{1,0},{2,3},{3,2},{4,5},{5,4},{6,7},{7,6},{8,9},{9,8},{10,11... | collective-permute-start | bytes 835592 | tf_op jit(solution)/shard_map/ppermute | solution.py:457
  72.6 4.5 %collective-permute-start.25 = (bf16[4,16,2176]{2,1,0:T(8,128)(2,1)S(1)}, bf16[4,16,2176]{2,1,0:T(8,128)(2,1)S(1)}, u32[]{:S(2)}, u32[]{:S(2)}) collective-permute-start(bf16[4,16,2176]{2,1,0:T(8,128)(2,1)S(1)} %bitcast.72), channel_id=1, source_target_pairs={{0,1},{1,0},{2,3},{3,2},{4,5},{5,4},{6,7},{7,6},{8,9},{9,8},{10,11... | collective-permute-start | bytes 835592 | tf_op jit(solution)/shard_map/ppermute | solution.py:457
  72.7 4.4 %collective-permute-start.26 = (bf16[4,16,2176]{2,1,0:T(8,128)(2,1)S(1)}, bf16[4,16,2176]{2,1,0:T(8,128)(2,1)S(1)}, u32[]{:S(2)}, u32[]{:S(2)}) collective-permute-start(bf16[4,16,2176]{2,1,0:T(8,128)(2,1)S(1)} %bitcast.71), channel_id=1, source_target_pairs={{0,1},{1,0},{2,3},{3,2},{4,5},{5,4},{6,7},{7,6},{8,9},{9,8},{10,11... | collective-permute-start | bytes 835592 | tf_op jit(solution)/shard_map/ppermute | solution.py:457
  75.5 9.2 %collective-permute-start.22 = (bf16[2,128,512]{2,1,0:T(8,128)(2,1)S(1)}, bf16[2,128,512]{2,1,0:T(8,128)(2,1)S(1)}, u32[]{:S(2)}, u32[]{:S(2)}) collective-permute-start(bf16[2,128,512]{2,1,0:T(8,128)(2,1)S(1)} %get-tuple-element.276), channel_id=1, source_target_pairs={{0,4},{4,0},{8,12},{12,8},{16,20},{20,16},{24,28},{28,24},{1,5},{5... | collective-permute-start | bytes 786440 | tf_op jit(solution)/shard_map/ppermute | solution.py:457
  77.2 10.7 %collective-permute-start.29 = (bf16[2,136,512]{2,1,0:T(8,128)(2,1)S(1)}, bf16[2,136,512]{2,1,0:T(8,128)(2,1)S(1)}, u32[]{:S(2)}, u32[]{:S(2)}) collective-permute-start(bf16[2,136,512]{2,1,0:T(8,128)(2,1)S(1)} %get-tuple-element.273), channel_id=1, source_target_pairs={{0,2},{1,3},{2,0},{3,1},{4,6},{5,7},{6,4},{7,5},{8,10},{9,11},{10,... | collective-permute-start | bytes 835592 | tf_op jit(solution)/shard_map/ppermute | solution.py:457
  79.0 15.9 %collective-permute-start.31 = (bf16[8,16,2176]{2,1,0:T(8,128)(2,1)S(1)}, bf16[8,16,2176]{2,1,0:T(8,128)(2,1)S(1)}, u32[]{:S(2)}, u32[]{:S(2)}) collective-permute-start(bf16[8,16,2176]{2,1,0:T(8,128)(2,1)S(1)} %get-tuple-element.271), channel_id=1, source_target_pairs={{0,4},{1,5},{2,6},{3,7},{4,0},{5,1},{6,2},{7,3},{8,12},{9,13},{10,... | collective-permute-start | bytes 1671176 | tf_op jit(solution)/shard_map/ppermute | solution.py:457
  84.8 16.1 %collective-permute-start.27 = (bf16[512,512]{1,0:T(8,128)(2,1)S(1)}, bf16[512,512]{1,0:T(8,128)(2,1)S(1)}, u32[]{:S(2)}, u32[]{:S(2)}) collective-permute-start(bf16[512,512]{1,0:T(8,128)(2,1)S(1)} %shard_map.272.r0), channel_id=1, source_target_pairs={{0,2},{1,3},{2,0},{3,1},{4,6},{5,7},{6,4},{7,5},{8,10},{9,11},{10,... | collective-permute-start | bytes 1572872 | tf_op jit(solution)/shard_map/ppermute | solution.py:457
  86.4 5.1 %collective-permute-start.28 = (bf16[128,512]{1,0:T(8,128)(2,1)S(1)}, bf16[128,512]{1,0:T(8,128)(2,1)S(1)}, u32[]{:S(2)}, u32[]{:S(2)}) collective-permute-start(bf16[128,512]{1,0:T(8,128)(2,1)S(1)} %get-tuple-element.281), channel_id=1, source_target_pairs={{0,8},{4,12},{8,0},{12,4},{16,24},{20,28},{24,16},{28,20},{1,9},{5... | collective-permute-start | bytes 393224 | tf_op jit(solution)/shard_map/ppermute | solution.py:457
  87.9 7.0 %collective-permute-start.32 = (bf16[136,512]{1,0:T(8,128)(2,1)S(1)}, bf16[136,512]{1,0:T(8,128)(2,1)S(1)}, u32[]{:S(2)}, u32[]{:S(2)}) collective-permute-start(bf16[136,512]{1,0:T(8,128)(2,1)S(1)} %get-tuple-element.279), channel_id=1, source_target_pairs={{0,8},{4,12},{8,0},{12,4},{16,24},{20,28},{24,16},{28,20},{1,9},{5... | collective-permute-start | bytes 417800 | tf_op jit(solution)/shard_map/ppermute | solution.py:457
  91.6 7.7 %collective-permute-start.30 = (bf16[128,512]{1,0:T(8,128)(2,1)S(1)}, bf16[128,512]{1,0:T(8,128)(2,1)S(1)}, u32[]{:S(2)}, u32[]{:S(2)}) collective-permute-start(bf16[128,512]{1,0:T(8,128)(2,1)S(1)} %add_convert_fusion.17), channel_id=1, source_target_pairs={{0,16},{4,20},{8,24},{12,28},{16,0},{20,4},{24,8},{28,12},{1,17},{... | collective-permute-start | bytes 393224 | tf_op jit(solution)/shard_map/ppermute | solution.py:457
  95.1 9.7 %collective-permute-start.36 = (bf16[4,16,2176]{2,1,0:T(8,128)(2,1)S(1)}, bf16[4,16,2176]{2,1,0:T(8,128)(2,1)S(1)}, u32[]{:S(2)}, u32[]{:S(2)}) collective-permute-start(bf16[4,16,2176]{2,1,0:T(8,128)(2,1)S(1)} %get-tuple-element.269), channel_id=1, source_target_pairs={{0,2},{1,3},{2,0},{3,1},{4,6},{5,7},{6,4},{7,5},{8,10},{9,11},{10,... | collective-permute-start | bytes 835592 | tf_op jit(solution)/shard_map/ppermute | solution.py:457
  96.3 16.6 %collective-permute-start.40 = (bf16[512,512]{1,0:T(8,128)(2,1)S(1)}, bf16[512,512]{1,0:T(8,128)(2,1)S(1)}, u32[]{:S(2)}, u32[]{:S(2)}) collective-permute-start(bf16[512,512]{1,0:T(8,128)(2,1)S(1)} %get-tuple-element.235.r0), channel_id=1, source_target_pairs={{0,2},{1,3},{2,0},{3,1},{4,6},{5,7},{6,4},{7,5},{8,10},{9,11},{10,... | collective-permute-start | bytes 1572872 | tf_op jit(solution)/shard_map/ppermute | solution.py:457
  97.2 18.7 %collective-permute-start.42 = (bf16[512,512]{1,0:T(8,128)(2,1)S(1)}, bf16[512,512]{1,0:T(8,128)(2,1)S(1)}, u32[]{:S(2)}, u32[]{:S(2)}) collective-permute-start(bf16[512,512]{1,0:T(8,128)(2,1)S(1)} %get-tuple-element.235.r0), channel_id=1, source_target_pairs={{0,1},{1,0},{2,3},{3,2},{4,5},{5,4},{6,7},{7,6},{8,9},{9,8},{10,11... | collective-permute-start | bytes 1572872 | tf_op jit(solution)/shard_map/ppermute | solution.py:457
  99.3 8.5 %collective-permute-start.35 = (bf16[136,512]{1,0:T(8,128)(2,1)S(1)}, bf16[136,512]{1,0:T(8,128)(2,1)S(1)}, u32[]{:S(2)}, u32[]{:S(2)}) collective-permute-start(bf16[136,512]{1,0:T(8,128)(2,1)S(1)} %add_convert_fusion.13), channel_id=1, source_target_pairs={{0,16},{4,20},{8,24},{12,28},{16,0},{20,4},{24,8},{28,12},{1,17},{... | collective-permute-start | bytes 417800 | tf_op jit(solution)/shard_map/ppermute | solution.py:457
  100.9 7.4 %collective-permute-start.34 = (bf16[128,512]{1,0:T(8,128)(2,1)S(1)}, bf16[128,512]{1,0:T(8,128)(2,1)S(1)}, u32[]{:S(2)}, u32[]{:S(2)}) collective-permute-start(bf16[128,512]{1,0:T(8,128)(2,1)S(1)} %add_convert_fusion.16), channel_id=1, source_target_pairs={{0,8},{4,12},{8,0},{12,4},{16,24},{20,28},{24,16},{28,20},{1,9},{5... | collective-permute-start | bytes 393224 | tf_op jit(solution)/shard_map/ppermute | solution.py:457
  107.8 6.5 %collective-permute-start.39 = (bf16[136,512]{1,0:T(8,128)(2,1)S(1)}, bf16[136,512]{1,0:T(8,128)(2,1)S(1)}, u32[]{:S(2)}, u32[]{:S(2)}) collective-permute-start(bf16[136,512]{1,0:T(8,128)(2,1)S(1)} %add_convert_fusion.11), channel_id=1, source_target_pairs={{0,8},{4,12},{8,0},{12,4},{16,24},{20,28},{24,16},{28,20},{1,9},{5... | collective-permute-start | bytes 417800 | tf_op jit(solution)/shard_map/ppermute | solution.py:457
  107.9 16.1 %collective-permute-start.44 = (bf16[512,512]{1,0:T(8,128)(2,1)S(1)}, bf16[512,512]{1,0:T(8,128)(2,1)S(1)}, u32[]{:S(2)}, u32[]{:S(2)}) collective-permute-start(bf16[512,512]{1,0:T(8,128)(2,1)S(1)} %shard_map.272.r0), channel_id=1, source_target_pairs={{0,1},{1,0},{2,3},{3,2},{4,5},{5,4},{6,7},{7,6},{8,9},{9,8},{10,11... | collective-permute-start | bytes 1572872 | tf_op jit(solution)/shard_map/ppermute | solution.py:457
  108.4 7.4 %collective-permute-start.38 = (bf16[2,16,2176]{2,1,0:T(8,128)(2,1)S(1)}, bf16[2,16,2176]{2,1,0:T(8,128)(2,1)S(1)}, u32[]{:S(2)}, u32[]{:S(2)}) collective-permute-start(bf16[2,16,2176]{2,1,0:T(8,128)(2,1)S(1)} %get-tuple-element.277), channel_id=1, source_target_pairs={{0,8},{1,9},{2,10},{3,11},{4,12},{5,13},{6,14},{7,15},{8,0},{9,1},... | collective-permute-start | bytes 417800 | tf_op jit(solution)/shard_map/ppermute | solution.py:457
  112.9 11.1 %collective-permute-start.33 = (bf16[512,512]{1,0:T(8,128)(2,1)S(1)}, bf16[512,512]{1,0:T(8,128)(2,1)S(1)}, u32[]{:S(2)}, u32[]{:S(2)}) collective-permute-start(bf16[512,512]{1,0:T(8,128)(2,1)S(1)} %collective-permute-done.27.r2), channel_id=1, source_target_pairs={{0,1},{1,0},{2,3},{3,2},{4,5},{5,4},{6,7},{7,6},{8,9},{9,8},{10,11... | collective-permute-start | bytes 1572872 | tf_op jit(solution)/shard_map/ppermute | solution.py:457
  114.2 9.7 %collective-permute-start.37 = (bf16[2,128,512]{2,1,0:T(8,128)(2,1)S(1)}, bf16[2,128,512]{2,1,0:T(8,128)(2,1)S(1)}, u32[]{:S(2)}, u32[]{:S(2)}) collective-permute-start(bf16[2,128,512]{2,1,0:T(8,128)(2,1)S(1)} %pad_maximum_fusion.1.own_ref), channel_id=1, source_target_pairs={{0,4},{4,0},{8,12},{12,8},{16,20},{20,16},{24,28},{28,24},{1,5},{5... | collective-permute-start | bytes 786440 | tf_op jit(solution)/shard_map/ppermute | solution.py:457
  115.8 2.0 %collective-permute-start.43 = (bf16[512,512]{1,0:T(8,128)(2,1)S(1)}, bf16[512,512]{1,0:T(8,128)(2,1)S(1)}, u32[]{:S(2)}, u32[]{:S(2)}) collective-permute-start(bf16[512,512]{1,0:T(8,128)(2,1)S(1)} %collective-permute-done.40.r2), channel_id=1, source_target_pairs={{0,1},{1,0},{2,3},{3,2},{4,5},{5,4},{6,7},{7,6},{8,9},{9,8},{10,11... | collective-permute-start | bytes 1572872 | tf_op jit(solution)/shard_map/ppermute | solution.py:457
  115.9 11.7 %collective-permute-start.45 = (bf16[2,136,512]{2,1,0:T(8,128)(2,1)S(1)}, bf16[2,136,512]{2,1,0:T(8,128)(2,1)S(1)}, u32[]{:S(2)}, u32[]{:S(2)}) collective-permute-start(bf16[2,136,512]{2,1,0:T(8,128)(2,1)S(1)} %pad_maximum_fusion.own_ref), channel_id=1, source_target_pairs={{0,4},{4,0},{8,12},{12,8},{16,20},{20,16},{24,28},{28,24},{1,5},{5... | collective-permute-start | bytes 835592 | tf_op jit(solution)/shard_map/ppermute | solution.py:457
  117.8 6.2 %collective-permute-start.41 = (bf16[1,16,2176]{2,1,0:T(8,128)(2,1)S(1)}, bf16[1,16,2176]{2,1,0:T(8,128)(2,1)S(1)}, u32[]{:S(2)}, u32[]{:S(2)}) collective-permute-start(bf16[1,16,2176]{2,1,0:T(8,128)(2,1)S(1)} %get-tuple-element.284), channel_id=1, source_target_pairs={{0,16},{1,17},{2,18},{3,19},{4,20},{5,21},{6,22},{7,23},{8,24},{9,... | collective-permute-start | bytes 208904 | tf_op jit(solution)/shard_map/ppermute | solution.py:457

commit v7 on v5

--- a/solution.py
+++ b/solution.py
@@ -661,7 +661,7 @@
     gp1, gm1 = heads_backward(half, inner_give)
 
     if by_bits:
-        out_bits = [[[2 * b + c + 8 * j for j in (0, 2, 1, 3)] for b in range(4)] for c in range(2)]
+        out_bits = [[[4 * (b >> 1) + 8 * (b & 1) + c + j for j in (0, 16, 2, 18)] for b in range(4)] for c in range(2)]
         out_bits = [sum(out_bits[0], []), *out_bits[1]]
     else:
         out_bits = [None]
@@ -724,7 +724,7 @@
 
         a_got, p_mine = tie(a_got, p_mine)
         a_mine, a_give = both(a_mine, a_got)
-        a_got = swap(a_give, ALL, 2)
+        a_got = swap(a_give, ALL, 8)
 
         q_got, a_mine = tie(q_got, a_mine)
         q_mine = add_low(q_mine, q_got)
@@ -735,7 +735,7 @@
 
         a_got, rows_across = tie(a_got, rows_across)
         a_mine, a_give = both(a_mine, a_got)
-        a_got = swap(a_give, ALL, 8)
+        a_got = swap(a_give, ALL, 2)
 
         p_got, a_mine = tie(p_got, a_mine)
         p_mine = add_low(p_mine, p_got)

time: 130 us -> 129 us (level)
  starting transfers between devices: 42.6 us -> 46.7 us
  waiting for transfers between devices: 36.5 us -> 32.4 us
    ppermute x46, waiting for transfers between devices: 36.5 us -> 32.4 us  [swap(): return lax.ppermute(value, axis, [(i, i ^ bit) for i in range(n)])]
    ppermute x46, starting transfers between devices: 42.6 us -> 46.7 us  [swap(): return lax.ppermute(value, axis, [(i, i ^ bit) for i in range(n)])]
  transfers between devices with their start and end apart: 46 -> 46, of which waited for: 19 -> 16; matrix products, arithmetic and copies ran while one was open for 6% -> 6% of each run, Pallas kernels for 23% -> 23%
where the time goes in v7:
time: 129 us
  starting transfers between devices  46.7 us (36%)
  Pallas kernels  40.5 us (31%)
  waiting for transfers between devices  32.4 us (25%)
  local copies, waits for them, and re-layouts  5.14 us (4%)
  other arithmetic  3.4 us (3%)
    ppermute x46, starting transfers between devices, swap(): return lax.ppermute(value, axis, [(i, i ^ bit) for i in range(n)])  46.7 us
    ppermute x46, waiting for transfers between devices, swap(): return lax.ppermute(value, axis, [(i, i ^ bit) for i in range(n)])  32.4 us
    pallas_call x1, Pallas kernels, shards(): call(forward_kernel, [square_low, outer_shape, outer_shape, sds((4, SPAN,...  9.54 us
    pallas_call x2, Pallas kernels, heads_backward(): call(functools.partial(heads_kernel, low_h, low_h + half), [sds((3, some,...  4.48 us
    squeeze x3, local copies, waits for them, and re-layouts, shards(): pick = lambda v, i: lax.dynamic_index_in_dim(v, i, 0, keepdims=False)  4.19 us
    pallas_call x1, Pallas kernels, shards(): call(attend_kernel, [sds((HEADS, SPAN, SPAN), LOW), sds((D, SPAN), F32),...  3.56 us
    pallas_call x1, Pallas kernels, closing(): call(closing_kernel, shapes, [SMEM] + [VMEM] * 8, [ANY] + [VMEM] * (len(s...  2.92 us
    pallas_call x1, Pallas kernels, shards(): call(functools.partial(project_kernel, bits), [sds((D, WIDE), LOW), sds((...  2.63 us
  transfers between devices with their start and end apart: 46, of which 16 were waited for; matrix products, arithmetic and copies ran while one was open for 6% of the time, Pallas kernels for 23%

profile of v7, /device:TPU:0, one launch (start us, length us, event | category | flops | bytes accessed | tf_op | source)
XLA Modules:
  0.0 129.1 jit_solution(9934914861025558101)
XLA Ops:
  0.7 1.0 dynamic-slice_bitcast_fusion.4
  1.6 3.0 %collective-permute-start.3 = (bf16[256,512]{1,0:T(8,128)(2,1)S(1)}, bf16[256,512]{1,0:T(8,128)(2,1)S(1)}, u32[]{:S(2)}, u32[]{:S(2)}) collective-permute-start(bf16[256,512]{1,0:T(8,128)(2,1)S(1)} %dynamic-slice_bitcast_fusion.4), channel_id=1, source_target_pairs={{0,2},{1,3},{2,0},{3,1},{4,6},{5,7},{6,4},{7,5},{8,10},{9,11},{10,... | collective-permute-start | bytes 786440 | tf_op jit(solution)/shard_map/ppermute | solution.py:457
  4.7 1.5 %shard_map.262 = bf16[16,2176]{1,0:T(8,128)(2,1)} custom-call(bf16[16,512]{1,0:T(8,128)(2,1)} %q_ref.1, bf16[16,512]{1,0:T(8,128)(2,1)} %k_ref.1, bf16[16,512]{1,0:T(8,128)(2,1)} %v_ref.1, bf16[16,512]{1,0:T(8,128)(2,1)} %o_ref.1, bf16[16,20]{1,0:T(8,128)(2,1)} %bitcast.83, bf16[1,16]{1,0:T(2,128)(2,1)} %bitcast.84, bf16[1,16]{1,0:T(2,128)(2,1)} %bitcast.85, ...), custom_call_target="tpu_custom_call" | custom-call | flops 1 | bytes 1 | tf_op jit(solution)/shard_map/pallas_call | solution.py:513
  6.2 1.6 %collective-permute-start = (bf16[16,2176]{1,0:T(8,128)(2,1)}, bf16[16,2176]{1,0:T(8,128)(2,1)S(1)}, u32[]{:S(2)}, u32[]{:S(2)}) collective-permute-start(bf16[16,2176]{1,0:T(8,128)(2,1)} %shard_map.262), channel_id=1, source_target_pairs={{0,8},{1,9},{2,10},{3,11},{4,12},{5,13},{6,14},{7,15},{8,0},{9,1},... | collective-permute-start | bytes 208904 | tf_op jit(solution)/shard_map/ppermute | solution.py:457
  7.8 2.6 %collective-permute-start.1 = (bf16[16,2176]{1,0:T(8,128)(2,1)}, bf16[16,2176]{1,0:T(8,128)(2,1)S(1)}, u32[]{:S(2)}, u32[]{:S(2)}) collective-permute-start(bf16[16,2176]{1,0:T(8,128)(2,1)} %shard_map.262), channel_id=1, source_target_pairs={{0,16},{1,17},{2,18},{3,19},{4,20},{5,21},{6,22},{7,23},{8,24},{9,... | collective-permute-start | bytes 208904 | tf_op jit(solution)/shard_map/ppermute | solution.py:457
  10.6 0.7 reshape.127
  11.2 1.0 dynamic-slice_bitcast_fusion.3
  12.6 2.6 %collective-permute-done.1 = bf16[16,2176]{1,0:T(8,128)(2,1)S(1)} collective-permute-done((bf16[16,2176]{1,0:T(8,128)(2,1)}, bf16[16,2176]{1,0:T(8,128)(2,1)S(1)}, u32[]{:S(2)}, u32[]{:S(2)}) %collective-permute-start.1) | collective-permute-done | bytes 69664 | tf_op jit(solution)/shard_map/ppermute | solution.py:457
  15.2 1.5 %collective-permute-done.2 = bf16[16,2176]{1,0:T(8,128)(2,1)S(1)} collective-permute-done((bf16[16,2176]{1,0:T(8,128)(2,1)}, bf16[16,2176]{1,0:T(8,128)(2,1)S(1)}, u32[]{:S(2)}, u32[]{:S(2)}) %collective-permute-start.2) | collective-permute-done | bytes 69664 | tf_op jit(solution)/shard_map/ppermute | solution.py:457
  16.9 1.6 %collective-permute-start.4 = (bf16[64,2176]{1,0:T(8,128)(2,1)S(1)}, bf16[64,2176]{1,0:T(8,128)(2,1)}, u32[]{:S(2)}, u32[]{:S(2)}) collective-permute-start(bf16[64,2176]{1,0:T(8,128)(2,1)S(1)} %constant_dynamic-update-slice_fusion.refs_0_), channel_id=1, source_target_pairs={{0,4},{1,5},{2,6},{3,7},{4,0},{5,1},{6,2},{7,3},{8,12},{9,13},{10,... | collective-permute-start | bytes 835592 | tf_op jit(solution)/shard_map/ppermute | solution.py:457
  18.4 1.2 collective-permute-done.7
  19.6 0.8 collective-permute-start.8
  20.4 0.5 collective-permute-start.5
  20.9 2.3 %collective-permute-start.6 = (bf16[64,2176]{1,0:T(8,128)(2,1)S(1)}, bf16[64,2176]{1,0:T(8,128)(2,1)}, u32[]{:S(2)}, u32[]{:S(2)}) collective-permute-start(bf16[64,2176]{1,0:T(8,128)(2,1)S(1)} %constant_dynamic-update-slice_fusion.refs_0_), channel_id=1, source_target_pairs={{0,6},{1,7},{2,4},{3,5},{4,2},{5,3},{6,0},{7,1},{8,14},{9,15},{10,... | collective-permute-start | bytes 835592 | tf_op jit(solution)/shard_map/ppermute | solution.py:457
  23.2 2.3 %dynamic-slice_bitcast_fusion.1 = (bf16[512,512]{1,0:T(8,128)(2,1)}, bf16[512,512]{1,0:T(8,128)(2,1)S(1)}, bf16[512,512]{1,0:T(8,128)(2,1)S(1)}) fusion(bf16[4,512,512]{2,1,0:T(8,128)(2,1)} %bitcast.78, s32[]{:T(128)S(6)} %select_n.44, s32[]{:T(128)S(6)} %select_n.43, bf16[4,512,512]{2,1,0:T(8,128)(2,1)} %bitcast.81), kind=kLoop, calls=%fused_computation.21 | loop fusion | bytes 3145736 | tf_op jit(solution)/shard_map/jit(dynamic_index_in_dim)/squeeze | solution.py:501
  26.2 2.7 %collective-permute-done.8 = bf16[272,512]{1,0:T(8,128)(2,1)S(1)} collective-permute-done((bf16[272,512]{1,0:T(8,128)(2,1)S(1)}, bf16[272,512]{1,0:T(8,128)(2,1)S(1)}, u32[]{:S(2)}, u32[]{:S(2)}) %collective-permute-start.8) | collective-permute-done | bytes 278560 | tf_op jit(solution)/shard_map/ppermute | solution.py:457
  29.0 3.4 %collective-permute-done.5.refs_1_ = bf16[64,2176]{1,0:T(8,128)(2,1)} collective-permute-done((bf16[64,2176]{1,0:T(8,128)(2,1)S(1)}, bf16[64,2176]{1,0:T(8,128)(2,1)}, u32[]{:S(2)}, u32[]{:S(2)}) %collective-permute-start.5) | collective-permute-done | bytes 278560 | tf_op jit(solution)/shard_map/ppermute | solution.py:457
  32.4 0.5 collective-permute-start.11
  32.9 0.5 collective-permute-start.13
  33.6 1.2 maximum_maximum_fusion.wo0
  34.9 0.6 collective-permute-start.16
  36.0 2.6 %shard_map.263 = (bf16[512,2176]{1,0:T(8,128)(2,1)S(1)}, bf16[1536,512]{1,0:T(8,128)(2,1)S(1)}) custom-call(s32[7]{0:T(128)S(1)} %stack.49.at_ref, bf16[64,2176]{1,0:T(8,128)(2,1)S(1)} %constant_dynamic-update-slice_fusion.refs_0_, bf16[64,2176]{1,0:T(8,128)(2,1)} %collective-permute-done.5.refs_1_, bf16[64,2176]{1,0:T(8,128)(2,1)} %collective-permute-done.4.refs_2_, ...), custom_call_target="tpu_custom_call" | custom-call | flops 2000000000 | bytes 5242880 | tf_op jit(solution)/shard_map/pallas_call | solution.py:545
  38.6 2.3 %shard_map.264 = (f32[32,512]{1,0:T(8,128)S(1)}, f32[32,512]{1,0:T(8,128)S(1)}) custom-call(bf16[512,512]{1,0:T(8,128)(2,1)S(1)} %copy-done.1, bf16[512,2176]{1,0:T(8,128)(2,1)S(1)} %get-tuple-element.151.w_ref), custom_call_target="tpu_custom_call" | custom-call | flops 3000000000 | bytes 4194304 | tf_op jit(solution)/shard_map/pallas_call | solution.py:567
  40.9 3.6 %shard_map.265 = (bf16[8,512,512]{2,1,0:T(8,128)(2,1)S(1)}, f32[512,512]{1,0:T(8,128)S(1)}, f32[8,512]{1,0:T(8,128)S(1)}, f32[8,512]{1,0:T(8,128)S(1)}) custom-call(bf16[1536,512]{1,0:T(8,128)(2,1)S(1)} %get-tuple-element.153.qkv_ref), custom_call_target="tpu_custom_call" | custom-call | flops 5000000000 | bytes 7340032 | tf_op jit(solution)/shard_map/pallas_call | solution.py:553
  44.5 9.5 %shard_map.266 = (bf16[512,512]{1,0:T(8,128)(2,1)S(1)}, bf16[2,4,128,512]{3,2,1,0:T(8,128)(2,1)S(1)}, bf16[2,4,128,512]{3,2,1,0:T(8,128)(2,1)S(1)}, bf16[4,512,5...) custom-call(s32[7]{0:T(128)S(1)} %stack.49.at_ref, ...), custom_call_target="tpu_custom_call" | custom-call | flops 10000000000 | bytes 14680064 | tf_op jit(solution)/shard_map/pallas_call | solution.py:583
  54.2 2.5 %shard_map.267 = (bf16[2,4,136,512]{3,2,1,0:T(8,128)(2,1)S(1)}, f32[512,512]{1,0:T(8,128)S(1)}) custom-call(s32[7]{0:T(128)S(1)} %stack.49.at_ref, bf16[512,512]{1,0:T(8,128)(2,1)S(1)} %collective-permute-done.14.wi1, bf16[512,512]{1,0:T(8,128)(2,1)S(1)} %collective-permute-done.15.wi3, bf16[528,512]{1,0:T(8,128)(2,1)S(1)} %collective-permute-done.16.wo1, ...), custom_call_target="tpu_custom_call" | custom-call | flops 1 | bytes 1 | tf_op jit(solution)/shard_map/pallas_call | solution.py:615
  56.8 0.5 collective-permute-start.20
  57.6 0.6 collective-permute-start.19
  58.2 2.5 %shard_map.268 = (bf16[2,4,136,512]{3,2,1,0:T(8,128)(2,1)S(1)}, f32[512,512]{1,0:T(8,128)S(1)}) custom-call(s32[7]{0:T(128)S(1)} %stack.49.at_ref, bf16[4,128,512]{2,1,0:T(8,128)(2,1)S(1)} %get-tuple-element.266.after_ref, bf16[512,512]{1,0:T(8,128)(2,1)S(1)} %copy-done, bf16[512,512]{1,0:T(8,128)(2,1)S(1)} %maximum_select_fusion.1.wi2, ...), custom_call_target="tpu_custom_call" | custom-call | flops 1 | bytes 1 | tf_op jit(solution)/shard_map/pallas_call | solution.py:626
  61.1 1.6 %collective-permute-start.21 = (bf16[2,2,136,512]{3,2,1,0:T(8,128)(2,1)S(1)}, bf16[2,2,136,512]{3,2,1,0:T(8,128)(2,1)S(1)}, u32[]{:S(2)}, u32[]{:S(2)}) collective-permute-start(bf16[2,2,136,512]{3,2,1,0:T(8,128)(2,1)S(1)} %get-tuple-element.264.after_ref), channel_id=1, source_target_pairs={{0,4},{4,0},{8,12},{12,8},{16,20},{20,16},{24,28},{28,24},{1,5},{5... | collective-permute-start | bytes 1671176 | tf_op jit(solution)/shard_map/ppermute | solution.py:457
  62.6 1.2 shard_map.269
  63.8 2.2 %shard_map.270 = (bf16[3,256,512]{2,1,0:T(8,128)(2,1)S(1)}, f32[2,32,256]{2,1,0:T(8,128)S(1)}) custom-call(bf16[2,2,136,512]{3,2,1,0:T(8,128)(2,1)S(1)} %get-tuple-element.264.after_ref, bf16[1536,512]{1,0:T(8,128)(2,1)S(1)} %get-tuple-element.153.qkv_ref, bf16[8,512,512]{2,1,0:T(8,128)(2,1)S(1)} %get-tuple-element.176.p_ref, ...), custom_call_target="tpu_custom_call" | custom-call | flops 1 | bytes 1 | tf_op jit(solution)/shard_map/pallas_call | solution.py:643
  66.0 2.2 %shard_map.271 = (bf16[3,256,512]{2,1,0:T(8,128)(2,1)S(1)}, f32[2,32,256]{2,1,0:T(8,128)S(1)}) custom-call(bf16[2,2,136,512]{3,2,1,0:T(8,128)(2,1)S(1)} %get-tuple-element.264.after_ref, bf16[1536,512]{1,0:T(8,128)(2,1)S(1)} %get-tuple-element.153.qkv_ref, bf16[8,512,512]{2,1,0:T(8,128)(2,1)S(1)} %get-tuple-element.176.p_ref, ...), custom_call_target="tpu_custom_call" | custom-call | flops 1 | bytes 1 | tf_op jit(solution)/shard_map/pallas_call | solution.py:643
  68.3 1.2 shard_map.272.r0
  69.5 2.6 %shard_map.273 = (bf16[256,2176]{1,0:T(8,128)(2,1)S(1)}, bf16[64,2176]{1,0:T(8,128)(2,1)S(1)}, bf16[64,2176]{1,0:T(8,128)(2,1)S(1)}, bf16[64,2176]{1,0:T(8,128)(2,1)S(1)}, bf16[64,2176]{1,0:T(8,128)(2,1)S(1)}) custom-call(bf16[2,2,136,512]{3,2,1,0:T(8,128)(2,1)S(1)} %get-tuple-element.264.after_ref, s32[7]{0:T(128)S(1)} %stack.49.at_ref, ...), custom_call_target="tpu_custom_call" | custom-call | flops 1 | bytes 1 | tf_op jit(solution)/shard_map/pallas_call | solution.py:670
  72.1 0.5 collective-permute-start.24
  72.7 0.4 collective-permute-start.26
  73.3 2.2 %collective-permute-done.21 = bf16[2,2,136,512]{3,2,1,0:T(8,128)(2,1)S(1)} collective-permute-done((bf16[2,2,136,512]{3,2,1,0:T(8,128)(2,1)S(1)}, bf16[2,2,136,512]{3,2,1,0:T(8,128)(2,1)S(1)}, u32[]{:S(2)}, u32[]{:S(2)}) %collective-permute-start.21) | collective-permute-done | bytes 557088 | tf_op jit(solution)/shard_map/ppermute | solution.py:457
  75.5 1.5 %collective-permute-start.22 = (bf16[2,128,512]{2,1,0:T(8,128)(2,1)S(1)}, bf16[2,128,512]{2,1,0:T(8,128)(2,1)S(1)}, u32[]{:S(2)}, u32[]{:S(2)}) collective-permute-start(bf16[2,128,512]{2,1,0:T(8,128)(2,1)S(1)} %get-tuple-element.276), channel_id=1, source_target_pairs={{0,4},{4,0},{8,12},{12,8},{16,20},{20,16},{24,28},{28,24},{1,5},{5... | collective-permute-start | bytes 786440 | tf_op jit(solution)/shard_map/ppermute | solution.py:457
  77.2 1.6 %collective-permute-start.29 = (bf16[2,136,512]{2,1,0:T(8,128)(2,1)S(1)}, bf16[2,136,512]{2,1,0:T(8,128)(2,1)S(1)}, u32[]{:S(2)}, u32[]{:S(2)}) collective-permute-start(bf16[2,136,512]{2,1,0:T(8,128)(2,1)S(1)} %get-tuple-element.273), channel_id=1, source_target_pairs={{0,2},{1,3},{2,0},{3,1},{4,6},{5,7},{6,4},{7,5},{8,10},{9,11},{10,... | collective-permute-start | bytes 835592 | tf_op jit(solution)/shard_map/ppermute | solution.py:457
  79.0 0.6 collective-permute-start.31
  79.6 5.1 %collective-permute-done.22 = bf16[2,128,512]{2,1,0:T(8,128)(2,1)S(1)} collective-permute-done((bf16[2,128,512]{2,1,0:T(8,128)(2,1)S(1)}, bf16[2,128,512]{2,1,0:T(8,128)(2,1)S(1)}, u32[]{:S(2)}, u32[]{:S(2)}) %collective-permute-start.22) | collective-permute-done | bytes 262176 | tf_op jit(solution)/shard_map/ppermute | solution.py:457
  84.8 1.6 %collective-permute-start.27 = (bf16[512,512]{1,0:T(8,128)(2,1)S(1)}, bf16[512,512]{1,0:T(8,128)(2,1)S(1)}, u32[]{:S(2)}, u32[]{:S(2)}) collective-permute-start(bf16[512,512]{1,0:T(8,128)(2,1)S(1)} %shard_map.272.r0), channel_id=1, source_target_pairs={{0,2},{1,3},{2,0},{3,1},{4,6},{5,7},{6,4},{7,5},{8,10},{9,11},{10,... | collective-permute-start | bytes 1572872 | tf_op jit(solution)/shard_map/ppermute | solution.py:457
  86.4 1.5 %collective-permute-start.28 = (bf16[128,512]{1,0:T(8,128)(2,1)S(1)}, bf16[128,512]{1,0:T(8,128)(2,1)S(1)}, u32[]{:S(2)}, u32[]{:S(2)}) collective-permute-start(bf16[128,512]{1,0:T(8,128)(2,1)S(1)} %get-tuple-element.281), channel_id=1, source_target_pairs={{0,8},{4,12},{8,0},{12,4},{16,24},{20,28},{24,16},{28,20},{1,9},{5... | collective-permute-start | bytes 393224 | tf_op jit(solution)/shard_map/ppermute | solution.py:457
  87.9 0.6 collective-permute-start.32
  88.5 2.9 %collective-permute-done.28 = bf16[128,512]{1,0:T(8,128)(2,1)S(1)} collective-permute-done((bf16[128,512]{1,0:T(8,128)(2,1)S(1)}, bf16[128,512]{1,0:T(8,128)(2,1)S(1)}, u32[]{:S(2)}, u32[]{:S(2)}) %collective-permute-start.28) | collective-permute-done | bytes 131104 | tf_op jit(solution)/shard_map/ppermute | solution.py:457
  91.5 3.4 %collective-permute-start.30 = (bf16[128,512]{1,0:T(8,128)(2,1)S(1)}, bf16[128,512]{1,0:T(8,128)(2,1)S(1)}, u32[]{:S(2)}, u32[]{:S(2)}) collective-permute-start(bf16[128,512]{1,0:T(8,128)(2,1)S(1)} %add_convert_fusion.17), channel_id=1, source_target_pairs={{0,16},{4,20},{8,24},{12,28},{16,0},{20,4},{24,8},{28,12},{1,17},{... | collective-permute-start | bytes 393224 | tf_op jit(solution)/shard_map/ppermute | solution.py:457
  95.1 1.6 %collective-permute-start.36 = (bf16[4,16,2176]{2,1,0:T(8,128)(2,1)S(1)}, bf16[4,16,2176]{2,1,0:T(8,128)(2,1)S(1)}, u32[]{:S(2)}, u32[]{:S(2)}) collective-permute-start(bf16[4,16,2176]{2,1,0:T(8,128)(2,1)S(1)} %get-tuple-element.269), channel_id=1, source_target_pairs={{0,8},{1,9},{2,10},{3,11},{4,12},{5,13},{6,14},{7,15},{8,0},{9,1},... | collective-permute-start | bytes 835592 | tf_op jit(solution)/shard_map/ppermute | solution.py:457
  96.7 1.1 collective-permute-start.40
  97.8 1.4 %collective-permute-done.30 = bf16[128,512]{1,0:T(8,128)(2,1)S(1)} collective-permute-done((bf16[128,512]{1,0:T(8,128)(2,1)S(1)}, bf16[128,512]{1,0:T(8,128)(2,1)S(1)}, u32[]{:S(2)}, u32[]{:S(2)}) %collective-permute-start.30) | collective-permute-done | bytes 131104 | tf_op jit(solution)/shard_map/ppermute | solution.py:457
  99.2 3.1 %collective-permute-start.35 = (bf16[136,512]{1,0:T(8,128)(2,1)S(1)}, bf16[136,512]{1,0:T(8,128)(2,1)S(1)}, u32[]{:S(2)}, u32[]{:S(2)}) collective-permute-start(bf16[136,512]{1,0:T(8,128)(2,1)S(1)} %add_convert_fusion.13), channel_id=1, source_target_pairs={{0,16},{4,20},{8,24},{12,28},{16,0},{20,4},{24,8},{28,12},{1,17},{... | collective-permute-start | bytes 417800 | tf_op jit(solution)/shard_map/ppermute | solution.py:457
  102.3 1.5 %collective-permute-start.34 = (bf16[128,512]{1,0:T(8,128)(2,1)S(1)}, bf16[128,512]{1,0:T(8,128)(2,1)S(1)}, u32[]{:S(2)}, u32[]{:S(2)}) collective-permute-start(bf16[128,512]{1,0:T(8,128)(2,1)S(1)} %add_convert_fusion.16), channel_id=1, source_target_pairs={{0,8},{4,12},{8,0},{12,4},{16,24},{20,28},{24,16},{28,20},{1,9},{5... | collective-permute-start | bytes 393224 | tf_op jit(solution)/shard_map/ppermute | solution.py:457
  103.8 2.6 %collective-permute-done.36 = bf16[4,16,2176]{2,1,0:T(8,128)(2,1)S(1)} collective-permute-done((bf16[4,16,2176]{2,1,0:T(8,128)(2,1)S(1)}, bf16[4,16,2176]{2,1,0:T(8,128)(2,1)S(1)}, u32[]{:S(2)}, u32[]{:S(2)}) %collective-permute-start.36) | collective-permute-done | bytes 278560 | tf_op jit(solution)/shard_map/ppermute | solution.py:457
  106.5 3.3 %collective-permute-start.39 = (bf16[136,512]{1,0:T(8,128)(2,1)S(1)}, bf16[136,512]{1,0:T(8,128)(2,1)S(1)}, u32[]{:S(2)}, u32[]{:S(2)}) collective-permute-start(bf16[136,512]{1,0:T(8,128)(2,1)S(1)} %add_convert_fusion.11), channel_id=1, source_target_pairs={{0,8},{4,12},{8,0},{12,4},{16,24},{20,28},{24,16},{28,20},{1,9},{5... | collective-permute-start | bytes 417800 | tf_op jit(solution)/shard_map/ppermute | solution.py:457
  109.9 1.3 collective-permute-start.38
  111.4 1.5 %collective-permute-done.39 = bf16[136,512]{1,0:T(8,128)(2,1)S(1)} collective-permute-done((bf16[136,512]{1,0:T(8,128)(2,1)S(1)}, bf16[136,512]{1,0:T(8,128)(2,1)S(1)}, u32[]{:S(2)}, u32[]{:S(2)}) %collective-permute-start.39) | collective-permute-done | bytes 139296 | tf_op jit(solution)/shard_map/ppermute | solution.py:457
  112.9 1.5 %collective-permute-start.37 = (bf16[2,128,512]{2,1,0:T(8,128)(2,1)S(1)}, bf16[2,128,512]{2,1,0:T(8,128)(2,1)S(1)}, u32[]{:S(2)}, u32[]{:S(2)}) collective-permute-start(bf16[2,128,512]{2,1,0:T(8,128)(2,1)S(1)} %pad_maximum_fusion.1.own_ref), channel_id=1, source_target_pairs={{0,4},{4,0},{8,12},{12,8},{16,20},{20,16},{24,28},{28,24},{1,5},{5... | collective-permute-start | bytes 786440 | tf_op jit(solution)/shard_map/ppermute | solution.py:457
  114.4 1.6 %collective-permute-done.38 = bf16[2,16,2176]{2,1,0:T(8,128)(2,1)S(1)} collective-permute-done((bf16[2,16,2176]{2,1,0:T(8,128)(2,1)S(1)}, bf16[2,16,2176]{2,1,0:T(8,128)(2,1)S(1)}, u32[]{:S(2)}, u32[]{:S(2)}) %collective-permute-start.38) | collective-permute-done | bytes 139296 | tf_op jit(solution)/shard_map/ppermute | solution.py:457
  116.0 1.5 %collective-permute-start.45 = (bf16[2,136,512]{2,1,0:T(8,128)(2,1)S(1)}, bf16[2,136,512]{2,1,0:T(8,128)(2,1)S(1)}, u32[]{:S(2)}, u32[]{:S(2)}) collective-permute-start(bf16[2,136,512]{2,1,0:T(8,128)(2,1)S(1)} %pad_maximum_fusion.own_ref), channel_id=1, source_target_pairs={{0,4},{4,0},{8,12},{12,8},{16,20},{20,16},{24,28},{28,24},{1,5},{5... | collective-permute-start | bytes 835592 | tf_op jit(solution)/shard_map/ppermute | solution.py:457
  117.9 2.0 %collective-permute-start.41 = (bf16[1,16,2176]{2,1,0:T(8,128)(2,1)S(1)}, bf16[1,16,2176]{2,1,0:T(8,128)(2,1)S(1)}, u32[]{:S(2)}, u32[]{:S(2)}) collective-permute-start(bf16[1,16,2176]{2,1,0:T(8,128)(2,1)S(1)} %get-tuple-element.284), channel_id=1, source_target_pairs={{0,16},{1,17},{2,18},{3,19},{4,20},{5,21},{6,22},{7,23},{8,24},{9,... | collective-permute-start | bytes 208904 | tf_op jit(solution)/shard_map/ppermute | solution.py:457
  119.8 1.9 %shard_map.274 = bf16[4,512,512]{2,1,0:T(8,128)(2,1)} custom-call(s32[7]{0:T(128)S(1)} %stack.49.at_ref, bf16[512,512]{1,0:T(8,128)(2,1)S(1)} %get-tuple-element.235.r0, bf16[512,512]{1,0:T(8,128)(2,1)S(1)} %collective-permute-done.42.r1, bf16[512,512]{1,0:T(8,128)(2,1)S(1)} %collective-permute-done.40.r2, bf16[512,512]{1,0:T(8,128)(2,1)S(1)} %collective-permute-done.43.r3), custom_call_target="tpu_custom_call" | custom-call | flops 1 | bytes 1 | tf_op jit(solution)/shard_map/pallas_call | solution.py:392
  121.7 2.7 %collective-permute-done.41.got_ref = bf16[1,16,2176]{2,1,0:T(8,128)(2,1)S(1)} collective-permute-done((bf16[1,16,2176]{2,1,0:T(8,128)(2,1)S(1)}, bf16[1,16,2176]{2,1,0:T(8,128)(2,1)S(1)}, u32[]{:S(2)}, u32[]{:S(2)}) %collective-permute-start.41) | collective-permute-done | bytes 69664 | tf_op jit(solution)/shard_map/ppermute | solution.py:457
  124.5 2.9 %shard_map.275 = (bf16[4,512,512]{2,1,0:T(8,128)(2,1)}, f32[512,512]{1,0:T(8,128)}, f32[16,20]{1,0:T(8,128)}, f32[16,512]{1,0:T(8,128)}, f32[16,512]{1,0:T(8,128...) custom-call(s32[7]{0:T(128)S(1)} %stack.49.at_ref, ...), custom_call_target="tpu_custom_call" | custom-call | flops 1 | bytes 1 | tf_op jit(solution)/shard_map/pallas_call | solution.py:443
  127.4 1.7 %shard_map.276 = (f32[512,512]{1,0:T(8,128)}, f32[1,512]{1,0:T(1,128)}) custom-call(s32[7]{0:T(128)S(1)} %stack.49.at_ref, bf16[2,136,512]{2,1,0:T(8,128)(2,1)S(1)} %pad_maximum_fusion.own_ref, bf16[2,136,512]{2,1,0:T(8,128)(2,1)S(1)} %collective-permute-done.45.other_ref), custom_call_target="tpu_custom_call" | custom-call | flops 1 | bytes 2097152 | tf_op jit(solution)/shard_map/pallas_call | solution.py:469
  (83 shorter events, 5.1 us)
Async XLA Ops:
  1.6 15.1 %collective-permute-start.3 = (bf16[256,512]{1,0:T(8,128)(2,1)S(1)}, bf16[256,512]{1,0:T(8,128)(2,1)S(1)}, u32[]{:S(2)}, u32[]{:S(2)}) collective-permute-start(bf16[256,512]{1,0:T(8,128)(2,1)S(1)} %dynamic-slice_bitcast_fusion.4), channel_id=1, source_target_pairs={{0,2},{1,3},{2,0},{3,1},{4,6},{5,7},{6,4},{7,5},{8,10},{9,11},{10,... | collective-permute-start | bytes 786440 | tf_op jit(solution)/shard_map/ppermute | solution.py:457
  6.2 10.5 %copy-start.2 = (bf16[16,2176]{1,0:T(8,128)(2,1)S(1)}, bf16[16,2176]{1,0:T(8,128)(2,1)}, u32[]{:S(2)}) copy-start(bf16[16,2176]{1,0:T(8,128)(2,1)} %shard_map.262) | copy-start | bytes 208900
  6.2 6.4 %collective-permute-start = (bf16[16,2176]{1,0:T(8,128)(2,1)}, bf16[16,2176]{1,0:T(8,128)(2,1)S(1)}, u32[]{:S(2)}, u32[]{:S(2)}) collective-permute-start(bf16[16,2176]{1,0:T(8,128)(2,1)} %shard_map.262), channel_id=1, source_target_pairs={{0,8},{1,9},{2,10},{3,11},{4,12},{5,13},{6,14},{7,15},{8,0},{9,1},... | collective-permute-start | bytes 208904 | tf_op jit(solution)/shard_map/ppermute | solution.py:457
  7.8 7.5 %collective-permute-start.1 = (bf16[16,2176]{1,0:T(8,128)(2,1)}, bf16[16,2176]{1,0:T(8,128)(2,1)S(1)}, u32[]{:S(2)}, u32[]{:S(2)}) collective-permute-start(bf16[16,2176]{1,0:T(8,128)(2,1)} %shard_map.262), channel_id=1, source_target_pairs={{0,16},{1,17},{2,18},{3,19},{4,20},{5,21},{6,22},{7,23},{8,24},{9,... | collective-permute-start | bytes 208904 | tf_op jit(solution)/shard_map/ppermute | solution.py:457
  10.3 6.4 %collective-permute-start.2 = (bf16[16,2176]{1,0:T(8,128)(2,1)}, bf16[16,2176]{1,0:T(8,128)(2,1)S(1)}, u32[]{:S(2)}, u32[]{:S(2)}) collective-permute-start(bf16[16,2176]{1,0:T(8,128)(2,1)} %shard_map.262), channel_id=1, source_target_pairs={{0,24},{1,25},{2,26},{3,27},{4,28},{5,29},{6,30},{7,31},{8,16},{9,... | collective-permute-start | bytes 208904 | tf_op jit(solution)/shard_map/ppermute | solution.py:457
  12.2 7.4 %collective-permute-start.7 = (bf16[272,512]{1,0:T(8,128)(2,1)S(1)}, bf16[272,512]{1,0:T(8,128)(2,1)S(1)}, u32[]{:S(2)}, u32[]{:S(2)}) collective-permute-start(bf16[272,512]{1,0:T(8,128)(2,1)S(1)} %fusion.4), channel_id=1, source_target_pairs={{0,2},{1,3},{2,0},{3,1},{4,6},{5,7},{6,4},{7,5},{8,10},{9,11},{10,... | collective-permute-start | bytes 835592 | tf_op jit(solution)/shard_map/ppermute | solution.py:457
  16.7 9.2 %collective-permute-start.9 = (bf16[256,512]{1,0:T(8,128)(2,1)S(1)}, bf16[256,512]{1,0:T(8,128)(2,1)S(1)}, u32[]{:S(2)}, u32[]{:S(2)}) collective-permute-start(bf16[256,512]{1,0:T(8,128)(2,1)S(1)} %collective-permute-done.3), channel_id=1, source_target_pairs={{0,8},{4,12},{8,0},{12,4},{16,24},{20,28},{24,16},{28,20},{1,9},{5... | collective-permute-start | bytes 786440 | tf_op jit(solution)/shard_map/ppermute | solution.py:457
  16.9 9.3 %collective-permute-start.4 = (bf16[64,2176]{1,0:T(8,128)(2,1)S(1)}, bf16[64,2176]{1,0:T(8,128)(2,1)}, u32[]{:S(2)}, u32[]{:S(2)}) collective-permute-start(bf16[64,2176]{1,0:T(8,128)(2,1)S(1)} %constant_dynamic-update-slice_fusion.refs_0_), channel_id=1, source_target_pairs={{0,4},{1,5},{2,6},{3,7},{4,0},{5,1},{6,2},{7,3},{8,12},{9,13},{10,... | collective-permute-start | bytes 835592 | tf_op jit(solution)/shard_map/ppermute | solution.py:457
  19.6 9.2 %collective-permute-start.8 = (bf16[272,512]{1,0:T(8,128)(2,1)S(1)}, bf16[272,512]{1,0:T(8,128)(2,1)S(1)}, u32[]{:S(2)}, u32[]{:S(2)}) collective-permute-start(bf16[272,512]{1,0:T(8,128)(2,1)S(1)} %collective-permute-done.7), channel_id=1, source_target_pairs={{0,8},{4,12},{8,0},{12,4},{16,24},{20,28},{24,16},{28,20},{1,9},{5... | collective-permute-start | bytes 835592 | tf_op jit(solution)/shard_map/ppermute | solution.py:457
  20.4 12.0 %collective-permute-start.5 = (bf16[64,2176]{1,0:T(8,128)(2,1)S(1)}, bf16[64,2176]{1,0:T(8,128)(2,1)}, u32[]{:S(2)}, u32[]{:S(2)}) collective-permute-start(bf16[64,2176]{1,0:T(8,128)(2,1)S(1)} %constant_dynamic-update-slice_fusion.refs_0_), channel_id=1, source_target_pairs={{0,2},{1,3},{2,0},{3,1},{4,6},{5,7},{6,4},{7,5},{8,10},{9,11},{10,... | collective-permute-start | bytes 835592 | tf_op jit(solution)/shard_map/ppermute | solution.py:457
  20.9 11.5 %collective-permute-start.6 = (bf16[64,2176]{1,0:T(8,128)(2,1)S(1)}, bf16[64,2176]{1,0:T(8,128)(2,1)}, u32[]{:S(2)}, u32[]{:S(2)}) collective-permute-start(bf16[64,2176]{1,0:T(8,128)(2,1)S(1)} %constant_dynamic-update-slice_fusion.refs_0_), channel_id=1, source_target_pairs={{0,6},{1,7},{2,4},{3,5},{4,2},{5,3},{6,0},{7,1},{8,14},{9,15},{10,... | collective-permute-start | bytes 835592 | tf_op jit(solution)/shard_map/ppermute | solution.py:457
  26.1 7.3 %copy-start = (bf16[512,512]{1,0:T(8,128)(2,1)S(1)}, bf16[512,512]{1,0:T(8,128)(2,1)}, u32[]{:S(2)}) copy-start(bf16[512,512]{1,0:T(8,128)(2,1)} %wi0.3) | copy-start | bytes 1572868
  32.4 2.4 %collective-permute-start.10 = (bf16[64,2176]{1,0:T(8,128)(2,1)S(1)}, bf16[64,2176]{1,0:T(8,128)(2,1)}, u32[]{:S(2)}, u32[]{:S(2)}) collective-permute-start(bf16[64,2176]{1,0:T(8,128)(2,1)S(1)} %constant_dynamic-update-slice_fusion.refs_0_), channel_id=1, source_target_pairs={{0,1},{1,0},{2,3},{3,2},{4,5},{5,4},{6,7},{7,6},{8,9},{9,8},{10,11... | collective-permute-start | bytes 835592 | tf_op jit(solution)/shard_map/ppermute | solution.py:457
  32.4 3.0 %collective-permute-start.11 = (bf16[64,2176]{1,0:T(8,128)(2,1)}, bf16[64,2176]{1,0:T(8,128)(2,1)}, u32[]{:S(2)}, u32[]{:S(2)}) collective-permute-start(bf16[64,2176]{1,0:T(8,128)(2,1)} %collective-permute-done.5.refs_1_), channel_id=1, source_target_pairs={{0,1},{1,0},{2,3},{3,2},{4,5},{5,4},{6,7},{7,6},{8,9},{9,8},{10,11... | collective-permute-start | bytes 835592 | tf_op jit(solution)/shard_map/ppermute | solution.py:457
  32.9 2.6 %collective-permute-start.12 = (bf16[64,2176]{1,0:T(8,128)(2,1)}, bf16[64,2176]{1,0:T(8,128)(2,1)}, u32[]{:S(2)}, u32[]{:S(2)}) collective-permute-start(bf16[64,2176]{1,0:T(8,128)(2,1)} %collective-permute-done.4.refs_2_), channel_id=1, source_target_pairs={{0,1},{1,0},{2,3},{3,2},{4,5},{5,4},{6,7},{7,6},{8,9},{9,8},{10,11... | collective-permute-start | bytes 835592 | tf_op jit(solution)/shard_map/ppermute | solution.py:457
  32.9 3.0 %collective-permute-start.13 = (bf16[64,2176]{1,0:T(8,128)(2,1)}, bf16[64,2176]{1,0:T(8,128)(2,1)}, u32[]{:S(2)}, u32[]{:S(2)}) collective-permute-start(bf16[64,2176]{1,0:T(8,128)(2,1)} %collective-permute-done.6.refs_3_), channel_id=1, source_target_pairs={{0,1},{1,0},{2,3},{3,2},{4,5},{5,4},{6,7},{7,6},{8,9},{9,8},{10,11... | collective-permute-start | bytes 835592 | tf_op jit(solution)/shard_map/ppermute | solution.py:457
  33.4 11.0 %collective-permute-start.14 = (bf16[512,512]{1,0:T(8,128)(2,1)S(1)}, bf16[512,512]{1,0:T(8,128)(2,1)S(1)}, u32[]{:S(2)}, u32[]{:S(2)}) collective-permute-start(bf16[512,512]{1,0:T(8,128)(2,1)S(1)} %copy-done), channel_id=1, source_target_pairs={{0,1},{1,0},{2,3},{3,2},{4,5},{5,4},{6,7},{7,6},{8,9},{9,8},{10,11... | collective-permute-start | bytes 1572872 | tf_op jit(solution)/shard_map/ppermute | solution.py:457
  34.8 3.8 %copy-start.1 = (bf16[512,512]{1,0:T(8,128)(2,1)S(1)}, bf16[512,512]{1,0:T(8,128)(2,1)}, u32[]{:S(2)}) copy-start(bf16[512,512]{1,0:T(8,128)(2,1)} %get-tuple-element.143.x1_ref) | copy-start | bytes 1572868
  34.9 9.6 %collective-permute-start.16 = (bf16[528,512]{1,0:T(8,128)(2,1)S(1)}, bf16[528,512]{1,0:T(8,128)(2,1)S(1)}, u32[]{:S(2)}, u32[]{:S(2)}) collective-permute-start(bf16[528,512]{1,0:T(8,128)(2,1)S(1)} %maximum_maximum_fusion.wo0), channel_id=1, source_target_pairs={{0,1},{1,0},{2,3},{3,2},{4,5},{5,4},{6,7},{7,6},{8,9},{9,8},{10,11... | collective-permute-start | bytes 1622024 | tf_op jit(solution)/shard_map/ppermute | solution.py:457
  35.4 9.1 %collective-permute-start.15 = (bf16[512,512]{1,0:T(8,128)(2,1)S(1)}, bf16[512,512]{1,0:T(8,128)(2,1)S(1)}, u32[]{:S(2)}, u32[]{:S(2)}) collective-permute-start(bf16[512,512]{1,0:T(8,128)(2,1)S(1)} %maximum_select_fusion.1.wi2), channel_id=1, source_target_pairs={{0,1},{1,0},{2,3},{3,2},{4,5},{5,4},{6,7},{7,6},{8,9},{9,8},{10,11... | collective-permute-start | bytes 1572872 | tf_op jit(solution)/shard_map/ppermute | solution.py:457
  35.5 9.0 %collective-permute-start.17 = (bf16[528,512]{1,0:T(8,128)(2,1)S(1)}, bf16[528,512]{1,0:T(8,128)(2,1)S(1)}, u32[]{:S(2)}, u32[]{:S(2)}) collective-permute-start(bf16[528,512]{1,0:T(8,128)(2,1)S(1)} %maximum_select_fusion.wo2), channel_id=1, source_target_pairs={{0,1},{1,0},{2,3},{3,2},{4,5},{5,4},{6,7},{7,6},{8,9},{9,8},{10,11... | collective-permute-start | bytes 1622024 | tf_op jit(solution)/shard_map/ppermute | solution.py:457
  54.1 3.2 %collective-permute-start.18 = (bf16[2,4,128,512]{3,2,1,0:T(8,128)(2,1)S(1)}, bf16[2,4,128,512]{3,2,1,0:T(8,128)(2,1)S(1)}, u32[]{:S(2)}, u32[]{:S(2)}) collective-permute-start(bf16[2,4,128,512]{3,2,1,0:T(8,128)(2,1)S(1)} %get-tuple-element.168), channel_id=1, source_target_pairs={{0,1},{1,0},{2,3},{3,2},{4,5},{5,4},{6,7},{7,6},{8,9},{9,8},{10,11... | collective-permute-start | bytes 3145736 | tf_op jit(solution)/shard_map/ppermute | solution.py:457
  56.8 3.9 %collective-permute-start.20 = (bf16[2,4,136,512]{3,2,1,0:T(8,128)(2,1)S(1)}, bf16[2,4,136,512]{3,2,1,0:T(8,128)(2,1)S(1)}, u32[]{:S(2)}, u32[]{:S(2)}) collective-permute-start(bf16[2,4,136,512]{3,2,1,0:T(8,128)(2,1)S(1)} %get-tuple-element.175), channel_id=1, source_target_pairs={{0,1},{1,0},{2,3},{3,2},{4,5},{5,4},{6,7},{7,6},{8,9},{9,8},{10,11... | collective-permute-start | bytes 3342344 | tf_op jit(solution)/shard_map/ppermute | solution.py:457
  57.6 15.1 %collective-permute-start.19 = (bf16[4,128,512]{2,1,0:T(8,128)(2,1)S(1)}, bf16[4,128,512]{2,1,0:T(8,128)(2,1)S(1)}, u32[]{:S(2)}, u32[]{:S(2)}) collective-permute-start(bf16[4,128,512]{2,1,0:T(8,128)(2,1)S(1)} %get-tuple-element.266.after_ref), channel_id=1, source_target_pairs={{0,2},{1,3},{2,0},{3,1},{4,6},{5,7},{6,4},{7,5},{8,10},{9,11},{10,... | collective-permute-start | bytes 1572872 | tf_op jit(solution)/shard_map/ppermute | solution.py:457
  61.1 14.4 %collective-permute-start.21 = (bf16[2,2,136,512]{3,2,1,0:T(8,128)(2,1)S(1)}, bf16[2,2,136,512]{3,2,1,0:T(8,128)(2,1)S(1)}, u32[]{:S(2)}, u32[]{:S(2)}) collective-permute-start(bf16[2,2,136,512]{3,2,1,0:T(8,128)(2,1)S(1)} %get-tuple-element.264.after_ref), channel_id=1, source_target_pairs={{0,4},{4,0},{8,12},{12,8},{16,20},{20,16},{24,28},{28,24},{1,5},{5... | collective-permute-start | bytes 1671176 | tf_op jit(solution)/shard_map/ppermute | solution.py:457
  72.0 5.1 %collective-permute-start.23 = (bf16[4,16,2176]{2,1,0:T(8,128)(2,1)S(1)}, bf16[4,16,2176]{2,1,0:T(8,128)(2,1)S(1)}, u32[]{:S(2)}, u32[]{:S(2)}) collective-permute-start(bf16[4,16,2176]{2,1,0:T(8,128)(2,1)S(1)} %bitcast.74), channel_id=1, source_target_pairs={{0,1},{1,0},{2,3},{3,2},{4,5},{5,4},{6,7},{7,6},{8,9},{9,8},{10,11... | collective-permute-start | bytes 835592 | tf_op jit(solution)/shard_map/ppermute | solution.py:457
  72.1 5.0 %collective-permute-start.24 = (bf16[4,16,2176]{2,1,0:T(8,128)(2,1)S(1)}, bf16[4,16,2176]{2,1,0:T(8,128)(2,1)S(1)}, u32[]{:S(2)}, u32[]{:S(2)}) collective-permute-start(bf16[4,16,2176]{2,1,0:T(8,128)(2,1)S(1)} %bitcast.73), channel_id=1, source_target_pairs={{0,1},{1,0},{2,3},{3,2},{4,5},{5,4},{6,7},{7,6},{8,9},{9,8},{10,11... | collective-permute-start | bytes 835592 | tf_op jit(solution)/shard_map/ppermute | solution.py:457
  72.6 4.5 %collective-permute-start.25 = (bf16[4,16,2176]{2,1,0:T(8,128)(2,1)S(1)}, bf16[4,16,2176]{2,1,0:T(8,128)(2,1)S(1)}, u32[]{:S(2)}, u32[]{:S(2)}) collective-permute-start(bf16[4,16,2176]{2,1,0:T(8,128)(2,1)S(1)} %bitcast.72), channel_id=1, source_target_pairs={{0,1},{1,0},{2,3},{3,2},{4,5},{5,4},{6,7},{7,6},{8,9},{9,8},{10,11... | collective-permute-start | bytes 835592 | tf_op jit(solution)/shard_map/ppermute | solution.py:457
  72.7 4.4 %collective-permute-start.26 = (bf16[4,16,2176]{2,1,0:T(8,128)(2,1)S(1)}, bf16[4,16,2176]{2,1,0:T(8,128)(2,1)S(1)}, u32[]{:S(2)}, u32[]{:S(2)}) collective-permute-start(bf16[4,16,2176]{2,1,0:T(8,128)(2,1)S(1)} %bitcast.71), channel_id=1, source_target_pairs={{0,1},{1,0},{2,3},{3,2},{4,5},{5,4},{6,7},{7,6},{8,9},{9,8},{10,11... | collective-permute-start | bytes 835592 | tf_op jit(solution)/shard_map/ppermute | solution.py:457
  75.5 9.2 %collective-permute-start.22 = (bf16[2,128,512]{2,1,0:T(8,128)(2,1)S(1)}, bf16[2,128,512]{2,1,0:T(8,128)(2,1)S(1)}, u32[]{:S(2)}, u32[]{:S(2)}) collective-permute-start(bf16[2,128,512]{2,1,0:T(8,128)(2,1)S(1)} %get-tuple-element.276), channel_id=1, source_target_pairs={{0,4},{4,0},{8,12},{12,8},{16,20},{20,16},{24,28},{28,24},{1,5},{5... | collective-permute-start | bytes 786440 | tf_op jit(solution)/shard_map/ppermute | solution.py:457
  77.2 10.7 %collective-permute-start.29 = (bf16[2,136,512]{2,1,0:T(8,128)(2,1)S(1)}, bf16[2,136,512]{2,1,0:T(8,128)(2,1)S(1)}, u32[]{:S(2)}, u32[]{:S(2)}) collective-permute-start(bf16[2,136,512]{2,1,0:T(8,128)(2,1)S(1)} %get-tuple-element.273), channel_id=1, source_target_pairs={{0,2},{1,3},{2,0},{3,1},{4,6},{5,7},{6,4},{7,5},{8,10},{9,11},{10,... | collective-permute-start | bytes 835592 | tf_op jit(solution)/shard_map/ppermute | solution.py:457
  79.0 16.0 %collective-permute-start.31 = (bf16[8,16,2176]{2,1,0:T(8,128)(2,1)S(1)}, bf16[8,16,2176]{2,1,0:T(8,128)(2,1)S(1)}, u32[]{:S(2)}, u32[]{:S(2)}) collective-permute-start(bf16[8,16,2176]{2,1,0:T(8,128)(2,1)S(1)} %get-tuple-element.271), channel_id=1, source_target_pairs={{0,4},{1,5},{2,6},{3,7},{4,0},{5,1},{6,2},{7,3},{8,12},{9,13},{10,... | collective-permute-start | bytes 1671176 | tf_op jit(solution)/shard_map/ppermute | solution.py:457
  84.8 17.5 %collective-permute-start.27 = (bf16[512,512]{1,0:T(8,128)(2,1)S(1)}, bf16[512,512]{1,0:T(8,128)(2,1)S(1)}, u32[]{:S(2)}, u32[]{:S(2)}) collective-permute-start(bf16[512,512]{1,0:T(8,128)(2,1)S(1)} %shard_map.272.r0), channel_id=1, source_target_pairs={{0,2},{1,3},{2,0},{3,1},{4,6},{5,7},{6,4},{7,5},{8,10},{9,11},{10,... | collective-permute-start | bytes 1572872 | tf_op jit(solution)/shard_map/ppermute | solution.py:457
  86.4 5.1 %collective-permute-start.28 = (bf16[128,512]{1,0:T(8,128)(2,1)S(1)}, bf16[128,512]{1,0:T(8,128)(2,1)S(1)}, u32[]{:S(2)}, u32[]{:S(2)}) collective-permute-start(bf16[128,512]{1,0:T(8,128)(2,1)S(1)} %get-tuple-element.281), channel_id=1, source_target_pairs={{0,8},{4,12},{8,0},{12,4},{16,24},{20,28},{24,16},{28,20},{1,9},{5... | collective-permute-start | bytes 393224 | tf_op jit(solution)/shard_map/ppermute | solution.py:457
  87.9 7.0 %collective-permute-start.32 = (bf16[136,512]{1,0:T(8,128)(2,1)S(1)}, bf16[136,512]{1,0:T(8,128)(2,1)S(1)}, u32[]{:S(2)}, u32[]{:S(2)}) collective-permute-start(bf16[136,512]{1,0:T(8,128)(2,1)S(1)} %get-tuple-element.279), channel_id=1, source_target_pairs={{0,8},{4,12},{8,0},{12,4},{16,24},{20,28},{24,16},{28,20},{1,9},{5... | collective-permute-start | bytes 417800 | tf_op jit(solution)/shard_map/ppermute | solution.py:457
  91.5 7.7 %collective-permute-start.30 = (bf16[128,512]{1,0:T(8,128)(2,1)S(1)}, bf16[128,512]{1,0:T(8,128)(2,1)S(1)}, u32[]{:S(2)}, u32[]{:S(2)}) collective-permute-start(bf16[128,512]{1,0:T(8,128)(2,1)S(1)} %add_convert_fusion.17), channel_id=1, source_target_pairs={{0,16},{4,20},{8,24},{12,28},{16,0},{20,4},{24,8},{28,12},{1,17},{... | collective-permute-start | bytes 393224 | tf_op jit(solution)/shard_map/ppermute | solution.py:457
  95.1 11.3 %collective-permute-start.36 = (bf16[4,16,2176]{2,1,0:T(8,128)(2,1)S(1)}, bf16[4,16,2176]{2,1,0:T(8,128)(2,1)S(1)}, u32[]{:S(2)}, u32[]{:S(2)}) collective-permute-start(bf16[4,16,2176]{2,1,0:T(8,128)(2,1)S(1)} %get-tuple-element.269), channel_id=1, source_target_pairs={{0,8},{1,9},{2,10},{3,11},{4,12},{5,13},{6,14},{7,15},{8,0},{9,1},... | collective-permute-start | bytes 835592 | tf_op jit(solution)/shard_map/ppermute | solution.py:457
  96.7 14.5 %collective-permute-start.40 = (bf16[512,512]{1,0:T(8,128)(2,1)S(1)}, bf16[512,512]{1,0:T(8,128)(2,1)S(1)}, u32[]{:S(2)}, u32[]{:S(2)}) collective-permute-start(bf16[512,512]{1,0:T(8,128)(2,1)S(1)} %get-tuple-element.235.r0), channel_id=1, source_target_pairs={{0,2},{1,3},{2,0},{3,1},{4,6},{5,7},{6,4},{7,5},{8,10},{9,11},{10,... | collective-permute-start | bytes 1572872 | tf_op jit(solution)/shard_map/ppermute | solution.py:457
  97.8 18.2 %collective-permute-start.42 = (bf16[512,512]{1,0:T(8,128)(2,1)S(1)}, bf16[512,512]{1,0:T(8,128)(2,1)S(1)}, u32[]{:S(2)}, u32[]{:S(2)}) collective-permute-start(bf16[512,512]{1,0:T(8,128)(2,1)S(1)} %get-tuple-element.235.r0), channel_id=1, source_target_pairs={{0,1},{1,0},{2,3},{3,2},{4,5},{5,4},{6,7},{7,6},{8,9},{9,8},{10,11... | collective-permute-start | bytes 1572872 | tf_op jit(solution)/shard_map/ppermute | solution.py:457
  99.2 7.3 %collective-permute-start.35 = (bf16[136,512]{1,0:T(8,128)(2,1)S(1)}, bf16[136,512]{1,0:T(8,128)(2,1)S(1)}, u32[]{:S(2)}, u32[]{:S(2)}) collective-permute-start(bf16[136,512]{1,0:T(8,128)(2,1)S(1)} %add_convert_fusion.13), channel_id=1, source_target_pairs={{0,16},{4,20},{8,24},{12,28},{16,0},{20,4},{24,8},{28,12},{1,17},{... | collective-permute-start | bytes 417800 | tf_op jit(solution)/shard_map/ppermute | solution.py:457
  102.3 7.6 %collective-permute-start.34 = (bf16[128,512]{1,0:T(8,128)(2,1)S(1)}, bf16[128,512]{1,0:T(8,128)(2,1)S(1)}, u32[]{:S(2)}, u32[]{:S(2)}) collective-permute-start(bf16[128,512]{1,0:T(8,128)(2,1)S(1)} %add_convert_fusion.16), channel_id=1, source_target_pairs={{0,8},{4,12},{8,0},{12,4},{16,24},{20,28},{24,16},{28,20},{1,9},{5... | collective-permute-start | bytes 393224 | tf_op jit(solution)/shard_map/ppermute | solution.py:457
  106.5 6.3 %collective-permute-start.39 = (bf16[136,512]{1,0:T(8,128)(2,1)S(1)}, bf16[136,512]{1,0:T(8,128)(2,1)S(1)}, u32[]{:S(2)}, u32[]{:S(2)}) collective-permute-start(bf16[136,512]{1,0:T(8,128)(2,1)S(1)} %add_convert_fusion.11), channel_id=1, source_target_pairs={{0,8},{4,12},{8,0},{12,4},{16,24},{20,28},{24,16},{28,20},{1,9},{5... | collective-permute-start | bytes 417800 | tf_op jit(solution)/shard_map/ppermute | solution.py:457
  109.9 14.6 %collective-permute-start.44 = (bf16[512,512]{1,0:T(8,128)(2,1)S(1)}, bf16[512,512]{1,0:T(8,128)(2,1)S(1)}, u32[]{:S(2)}, u32[]{:S(2)}) collective-permute-start(bf16[512,512]{1,0:T(8,128)(2,1)S(1)} %shard_map.272.r0), channel_id=1, source_target_pairs={{0,1},{1,0},{2,3},{3,2},{4,5},{5,4},{6,7},{7,6},{8,9},{9,8},{10,11... | collective-permute-start | bytes 1572872 | tf_op jit(solution)/shard_map/ppermute | solution.py:457
  109.9 6.1 %collective-permute-start.38 = (bf16[2,16,2176]{2,1,0:T(8,128)(2,1)S(1)}, bf16[2,16,2176]{2,1,0:T(8,128)(2,1)S(1)}, u32[]{:S(2)}, u32[]{:S(2)}) collective-permute-start(bf16[2,16,2176]{2,1,0:T(8,128)(2,1)S(1)} %get-tuple-element.277), channel_id=1, source_target_pairs={{0,2},{1,3},{2,0},{3,1},{4,6},{5,7},{6,4},{7,5},{8,10},{9,11},{10,... | collective-permute-start | bytes 417800 | tf_op jit(solution)/shard_map/ppermute | solution.py:457
  111.2 13.3 %collective-permute-start.33 = (bf16[512,512]{1,0:T(8,128)(2,1)S(1)}, bf16[512,512]{1,0:T(8,128)(2,1)S(1)}, u32[]{:S(2)}, u32[]{:S(2)}) collective-permute-start(bf16[512,512]{1,0:T(8,128)(2,1)S(1)} %collective-permute-done.27.r2), channel_id=1, source_target_pairs={{0,1},{1,0},{2,3},{3,2},{4,5},{5,4},{6,7},{7,6},{8,9},{9,8},{10,11... | collective-permute-start | bytes 1572872 | tf_op jit(solution)/shard_map/ppermute | solution.py:457
  112.9 11.6 %collective-permute-start.37 = (bf16[2,128,512]{2,1,0:T(8,128)(2,1)S(1)}, bf16[2,128,512]{2,1,0:T(8,128)(2,1)S(1)}, u32[]{:S(2)}, u32[]{:S(2)}) collective-permute-start(bf16[2,128,512]{2,1,0:T(8,128)(2,1)S(1)} %pad_maximum_fusion.1.own_ref), channel_id=1, source_target_pairs={{0,4},{4,0},{8,12},{12,8},{16,20},{20,16},{24,28},{28,24},{1,5},{5... | collective-permute-start | bytes 786440 | tf_op jit(solution)/shard_map/ppermute | solution.py:457
  115.9 1.9 %collective-permute-start.43 = (bf16[512,512]{1,0:T(8,128)(2,1)S(1)}, bf16[512,512]{1,0:T(8,128)(2,1)S(1)}, u32[]{:S(2)}, u32[]{:S(2)}) collective-permute-start(bf16[512,512]{1,0:T(8,128)(2,1)S(1)} %collective-permute-done.40.r2), channel_id=1, source_target_pairs={{0,1},{1,0},{2,3},{3,2},{4,5},{5,4},{6,7},{7,6},{8,9},{9,8},{10,11... | collective-permute-start | bytes 1572872 | tf_op jit(solution)/shard_map/ppermute | solution.py:457
  116.0 11.5 %collective-permute-start.45 = (bf16[2,136,512]{2,1,0:T(8,128)(2,1)S(1)}, bf16[2,136,512]{2,1,0:T(8,128)(2,1)S(1)}, u32[]{:S(2)}, u32[]{:S(2)}) collective-permute-start(bf16[2,136,512]{2,1,0:T(8,128)(2,1)S(1)} %pad_maximum_fusion.own_ref), channel_id=1, source_target_pairs={{0,4},{4,0},{8,12},{12,8},{16,20},{20,16},{24,28},{28,24},{1,5},{5... | collective-permute-start | bytes 835592 | tf_op jit(solution)/shard_map/ppermute | solution.py:457
  117.9 6.6 %collective-permute-start.41 = (bf16[1,16,2176]{2,1,0:T(8,128)(2,1)S(1)}, bf16[1,16,2176]{2,1,0:T(8,128)(2,1)S(1)}, u32[]{:S(2)}, u32[]{:S(2)}) collective-permute-start(bf16[1,16,2176]{2,1,0:T(8,128)(2,1)S(1)} %get-tuple-element.284), channel_id=1, source_target_pairs={{0,16},{1,17},{2,18},{3,19},{4,20},{5,21},{6,22},{7,23},{8,24},{9,... | collective-permute-start | bytes 208904 | tf_op jit(solution)/shard_map/ppermute | solution.py:457
